TPU v7x, 32 devices: a whole 2x2x4 slice. The times are simulated.
32 devices in a mesh: seq: 2 (over y), head: 4 (over z), dp: 4 (over x, core).
Axes of the slice: x: 2, y: 2, z: 4, core: 2. Of those that a mesh axis runs over, the one named last changes fastest.
Arguments:
- queries: bfloat16 [2304, 8192], P(('dp', 'seq', 'head')), parts along dimension 0, may hold values from -20 to 20
- routed_keys: bfloat16 [2304, 1024], P(('dp', 'seq', 'head')), parts along dimension 0, may hold values from -4 to 4
- routed_values: bfloat16 [2304, 1024], P(('dp', 'seq', 'head')), parts along dimension 0, may hold values from -6 to 6
- output_gradient: bfloat16 [2304, 8192], P(('dp', 'seq', 'head')), parts along dimension 0, may hold values from -6 to 6
- positions: int32 [2304], P('dp'), parts along dimension 0, may hold values from 0 to 3071, as said below
- counts: int32 [8], P('dp'), parts along dimension 0, may hold values from 1 to 288, as said below
Outputs:
- attended: bfloat16 [2304, 8192], P(('dp', 'seq', 'head')), parts along dimension 0
- grad_query: bfloat16 [2304, 8192], P(('dp', 'seq', 'head')), parts along dimension 0
- key_state_gradient: bfloat16 [2304, 1024], P(('dp', 'seq', 'head')), parts along dimension 0
- value_state_gradient: bfloat16 [2304, 1024], P(('dp', 'seq', 'head')), parts along dimension 0
There are 4 independent parts, one for each index of `dp`. A program takes and returns all parts, laid end to end along the dimension named above; each array names one. Nothing has to cross between parts.
Inputs may be any that keep to these rules, and one draw needn't show every extreme that they name: `counts`: one sequence shard has exactly 288; every other shard has 96 or more. Within shard s all positions lie in s * 1536 to (s + 1) * 1536 - 1 and are distinct; the live slots of a shard are strictly increasing.
All inputs are finite; a program needn't handle non-finite values.
Results may differ from a plain program's by a relative error of at most 0.018.
Values may be sent and summed in bfloat16 or wider, within the bound.
No kernel may reach another device: no remote copies, remote signals or barrier semaphores. Data moves between devices by JAX's collectives and lax.ppermute only.
A program may use at most 128 MiB of HBM per device.

v0:
```python
import jax
import jax.numpy as jnp
from jax import lax
from jax.sharding import PartitionSpec as P

QUERY_HEADS = 64
KEY_VALUE_HEADS = 8
HEAD_WIDTH = 128


ROPE_BASE = 500000.0


def rope_angles(position):
    inverse_freq = jnp.float32(ROPE_BASE) ** (
        -(jnp.arange(HEAD_WIDTH // 2, dtype=jnp.float32) * 2.0 / HEAD_WIDTH)
    )
    angle_table = position.astype(jnp.float32)[:, None] * inverse_freq[None, :]
    return (jnp.cos(angle_table), jnp.sin(angle_table))


def apply_rotary(vectors, cosine_table, sine_values):
    half_size = vectors.shape[-1] // 2
    lower_half = vectors[..., :half_size]
    upper_half = vectors[..., half_size:]
    cosine_table = cosine_table[:, None, :]
    sine_values = sine_values[:, None, :]
    return jnp.concatenate(
        [
            lower_half * cosine_table - upper_half * sine_values,
            upper_half * cosine_table + lower_half * sine_values,
        ],
        -1,
    )


def invert_rotary(vectors, cosine_table, sine_values):
    half_size = vectors.shape[-1] // 2
    lower_half = vectors[..., :half_size]
    upper_half = vectors[..., half_size:]
    cosine_table = cosine_table[:, None, :]
    sine_values = sine_values[:, None, :]
    return jnp.concatenate(
        [
            lower_half * cosine_table + upper_half * sine_values,
            upper_half * cosine_table - lower_half * sine_values,
        ],
        -1,
    )


def pick_rows(routed_count):
    for block_size in (1024, 768, 512, 384, 256):
        if routed_count % block_size == 0:
            return block_size
    return routed_count


def attend(query_in, grad_in, key_block, value_block, query_pos, query_live, key_pos, key_live):
    routed_count = query_in.shape[0]
    head_count = query_in.shape[1] // HEAD_WIDTH
    block_rows = pick_rows(routed_count)
    block_count = routed_count // block_rows
    score_scale = 1.0 / jnp.sqrt(jnp.float32(HEAD_WIDTH))
    query_blocks = query_in.reshape(block_count, block_rows, head_count, HEAD_WIDTH)
    grad_blocks = grad_in.reshape(block_count, block_rows, head_count, HEAD_WIDTH)
    pos_blocks = query_pos.reshape(block_count, block_rows)
    live_blocks = query_live.reshape(block_count, block_rows)

    def block_step(totals, pieces):
        query_part, grad_part, pos_part, live_part = pieces
        scores = (
            jnp.einsum("bhd,kd->hbk", query_part, key_block, preferred_element_type=jnp.float32)
            * score_scale
        )
        allowed = (key_pos[None, :] <= pos_part[:, None]) & key_live[None, :]
        scores = jnp.where(allowed[None], scores, -1e30)
        row_max = jnp.max(scores, -1, keepdims=True)
        weights = jnp.exp(scores - row_max)
        row_total = jnp.sum(weights, -1, keepdims=True)
        probs = weights / row_total * live_part.astype(jnp.float32)[None, :, None]
        probs_low = probs.astype(jnp.bfloat16)
        out_part = jnp.einsum(
            "hbk,kd->bhd", probs_low, value_block, preferred_element_type=jnp.float32
        ).astype(jnp.bfloat16)
        dprob = jnp.einsum(
            "bhd,kd->hbk", grad_part, value_block, preferred_element_type=jnp.float32
        )
        delta = jnp.sum(grad_part.astype(jnp.float32) * out_part.astype(jnp.float32), -1).T
        dscore = (probs * (dprob - delta[:, :, None])).astype(jnp.bfloat16)
        grad_q = (
            jnp.einsum("hbk,kd->bhd", dscore, key_block, preferred_element_type=jnp.float32)
            * score_scale
        )
        cosine_table, sine_values = rope_angles(pos_part)
        grad_q = invert_rotary(grad_q, cosine_table, sine_values).astype(jnp.bfloat16)
        key_total = (
            totals[0]
            + jnp.einsum("hbk,bhd->kd", dscore, query_part, preferred_element_type=jnp.float32)
            * score_scale
        )
        value_total = totals[1] + jnp.einsum(
            "hbk,bhd->kd", probs_low, grad_part, preferred_element_type=jnp.float32
        )
        totals = (key_total, value_total)
        return (totals, (out_part, grad_q, row_max[:, :, 0].T, row_total[:, :, 0].T, delta.T))

    zeros = jnp.zeros((routed_count, HEAD_WIDTH), jnp.float32)
    sums, stacked = lax.scan(
        block_step, (zeros, zeros), (query_blocks, grad_blocks, pos_blocks, live_blocks)
    )
    out_heads = stacked[0].reshape(routed_count, head_count * HEAD_WIDTH)
    grad_heads = stacked[1].reshape(routed_count, head_count * HEAD_WIDTH)
    row_stats = (
        stacked[2].reshape(routed_count, head_count),
        stacked[3].reshape(routed_count, head_count),
        stacked[4].reshape(routed_count, head_count),
    )
    return (out_heads, grad_heads, sums[0], sums[1], row_stats)


def shards(queries, routed_keys, routed_values, output_gradient, positions, counts):
    seq_count = lax.axis_size("seq")
    head_count = lax.axis_size("head")
    seq_index = lax.axis_index("seq")
    head_index = lax.axis_index("head")
    routed_count = positions.shape[0]
    capacity = routed_count // seq_count
    slot_rows = queries.shape[0]
    heads_per_group = QUERY_HEADS // KEY_VALUE_HEADS
    query_heads = QUERY_HEADS // (seq_count * head_count)
    is_valid = jnp.arange(routed_count) % capacity < jnp.repeat(
        counts, capacity, total_repeat_length=routed_count
    )
    row_start = seq_index * capacity + head_index * slot_rows
    local_pos = lax.dynamic_slice_in_dim(positions, row_start, slot_rows)
    cosine_table, sine_values = rope_angles(local_pos)
    query_rotated = apply_rotary(
        queries.astype(jnp.float32).reshape(slot_rows, QUERY_HEADS, HEAD_WIDTH),
        cosine_table,
        sine_values,
    )
    query_rotated = query_rotated.astype(jnp.bfloat16).reshape(slot_rows, QUERY_HEADS * HEAD_WIDTH)
    key_rotated = apply_rotary(
        routed_keys.astype(jnp.float32).reshape(slot_rows, KEY_VALUE_HEADS, HEAD_WIDTH),
        cosine_table,
        sine_values,
    )
    key_rotated = key_rotated.astype(jnp.bfloat16).reshape(slot_rows, KEY_VALUE_HEADS * HEAD_WIDTH)
    key_split, value_split = (
        lax.all_to_all(key_rotated, "seq", split_axis=1, concat_axis=0, tiled=True),
        lax.all_to_all(routed_values, "seq", split_axis=1, concat_axis=0, tiled=True),
    )
    key_all, value_all = (
        lax.all_gather(key_split, "head", axis=0, tiled=True),
        lax.all_gather(value_split, "head", axis=0, tiled=True),
    )

    def by_head(vector):
        return (
            vector.reshape(seq_count, head_count, slot_rows)
            .transpose(1, 0, 2)
            .reshape(routed_count)
        )

    key_pos = by_head(positions)
    key_live = by_head(is_valid)
    kv_index = head_index * query_heads // heads_per_group
    key_block = lax.dynamic_slice_in_dim(key_all, kv_index * HEAD_WIDTH, HEAD_WIDTH, 1)
    value_block = lax.dynamic_slice_in_dim(value_all, kv_index * HEAD_WIDTH, HEAD_WIDTH, 1)
    query_in, grad_in = (
        lax.all_to_all(query_rotated, ("seq", "head"), split_axis=1, concat_axis=0, tiled=True),
        lax.all_to_all(output_gradient, ("seq", "head"), split_axis=1, concat_axis=0, tiled=True),
    )
    out_heads, grad_heads, key_grad, value_grad, row_stats = attend(
        query_in, grad_in, key_block, value_block, positions, is_valid, key_pos, key_live
    )
    wide_zeros = jnp.zeros((routed_count, KEY_VALUE_HEADS // seq_count * HEAD_WIDTH), jnp.float32)
    key_wide = lax.dynamic_update_slice_in_dim(wide_zeros, key_grad, kv_index * HEAD_WIDTH, 1)
    value_wide = lax.dynamic_update_slice_in_dim(wide_zeros, value_grad, kv_index * HEAD_WIDTH, 1)
    key_summed, value_summed = (
        lax.psum_scatter(key_wide, "head", scatter_dimension=0, tiled=True),
        lax.psum_scatter(value_wide, "head", scatter_dimension=0, tiled=True),
    )
    key_unrotated, value_back = (
        lax.all_to_all(
            key_summed.astype(jnp.bfloat16), "seq", split_axis=0, concat_axis=1, tiled=True
        ).astype(key_summed.dtype),
        lax.all_to_all(
            value_summed.astype(jnp.bfloat16), "seq", split_axis=0, concat_axis=1, tiled=True
        ).astype(value_summed.dtype),
    )
    key_state_gradient = invert_rotary(
        key_unrotated.reshape(slot_rows, KEY_VALUE_HEADS, HEAD_WIDTH), cosine_table, sine_values
    )
    key_state_gradient = key_state_gradient.astype(jnp.bfloat16).reshape(
        slot_rows, KEY_VALUE_HEADS * HEAD_WIDTH
    )
    value_state_gradient = value_back.astype(jnp.bfloat16)
    attended, grad_query = (
        lax.all_to_all(out_heads, ("seq", "head"), split_axis=0, concat_axis=1, tiled=True),
        lax.all_to_all(grad_heads, ("seq", "head"), split_axis=0, concat_axis=1, tiled=True),
    )
    return (attended, grad_query, key_state_gradient, value_state_gradient)


def solution(mesh):
    in_specs = (
        P(("dp", "seq", "head"), None),
        P(("dp", "seq", "head"), None),
        P(("dp", "seq", "head"), None),
        P(("dp", "seq", "head"), None),
        P("dp"),
        P("dp"),
    )
    out_specs = (
        P(("dp", "seq", "head"), None),
        P(("dp", "seq", "head"), None),
        P(("dp", "seq", "head"), None),
        P(("dp", "seq", "head"), None),
    )
    return jax.shard_map(shards, mesh=mesh, in_specs=in_specs, out_specs=out_specs, check_vma=False)
```

profile of v0, /device:TPU:0, one launch (start us, length us, event | category | flops | bytes accessed | tf_op | source)
XLA Modules:
  0.0 282.8 jit_solution(16258995990798832955)
XLA Ops:
  7.2 1.7 copy.99
  8.9 4.2 %all-to-all-start = ((bf16[72,2,512]{2,0,1:T(8,128)(2,1)}), bf16[72,2,512]{2,0,1:T(8,128)(2,1)S(1)}, u32[]{:S(2)}, u32[]{:S(2)}) async-start(bf16[72,2,512]{2,0,1:T(8,128)(2,1)} %bitcast.105), calls=%async_computation | async-start | bytes 294912 | tf_op jit(solution)/shard_map/all_to_all | solution.py:152
  16.1 1.6 all-to-all-done
  17.8 3.4 %all-to-all-start.1 = ((bf16[72,2,512]{2,0,1:T(8,128)(2,1)}), bf16[72,2,512]{2,0,1:T(8,128)(2,1)S(1)}, u32[]{:S(2)}, u32[]{:S(2)}) async-start(bf16[72,2,512]{2,0,1:T(8,128)(2,1)} %copy.47), calls=%async_computation.1 | async-start | bytes 294912 | tf_op jit(solution)/shard_map/all_to_all | solution.py:151
  22.3 3.4 %all-to-all-done.1 = bf16[72,2,512]{2,0,1:T(8,128)(2,1)S(1)} async-done(((bf16[72,2,512]{2,0,1:T(8,128)(2,1)}), bf16[72,2,512]{2,0,1:T(8,128)(2,1)S(1)}, u32[]{:S(2)}, u32[]{:S(2)}) %all-to-all-start.1) | async-done | bytes 147488 | tf_op jit(solution)/shard_map/all_to_all | solution.py:151
  26.4 5.4 %all-to-all-start.4 = ((bf16[72,8,1024]{2,0,1:T(8,128)(2,1)}), bf16[72,8,1024]{2,0,1:T(8,128)(2,1)S(1)}, u32[]{:S(2)}, u32[]{:S(2)}) async-start(bf16[72,8,1024]{2,0,1:T(8,128)(2,1)} %bitcast.103), calls=%async_computation.4 | async-start | bytes 2359296 | tf_op jit(solution)/shard_map/all_to_all | solution.py:173
  35.0 1.7 copy.48
  36.7 22.3 %all-to-all-done.4 = bf16[72,8,1024]{2,0,1:T(8,128)(2,1)S(1)} async-done(((bf16[72,8,1024]{2,0,1:T(8,128)(2,1)}), bf16[72,8,1024]{2,0,1:T(8,128)(2,1)S(1)}, u32[]{:S(2)}, u32[]{:S(2)}) %all-to-all-start.4) | async-done | bytes 1179680 | tf_op jit(solution)/shard_map/all_to_all | solution.py:173
  58.9 3.6 %all-to-all-start.2 = ((bf16[72,8,1024]{2,0,1:T(8,128)(2,1)}), bf16[72,8,1024]{2,0,1:T(8,128)(2,1)S(1)}, u32[]{:S(2)}, u32[]{:S(2)}) async-start(bf16[72,8,1024]{2,0,1:T(8,128)(2,1)} %copy.48), calls=%async_computation.2 | async-start | bytes 2359296 | tf_op jit(solution)/shard_map/all_to_all | solution.py:172
  67.2 1.9 multiply_cosine_fusion
  69.2 31.7 %all_gather.7 = bf16[576,512]{1,0:T(8,128)(2,1)} all-gather(bf16[144,512]{1,0:T(8,128)(2,1)S(1)} %bitcast.123), channel_id=1, replica_groups=mesh['seq'=2,'head'=4,'dp'=4] {'head'}, dimensions={0}, use_global_device_ids=true | all-gather | bytes 737280 | tf_op jit(solution)/shard_map/all_gather | solution.py:155
  100.8 17.3 %all_gather.6 = bf16[576,512]{1,0:T(8,128)(2,1)} all-gather(bf16[144,512]{1,0:T(8,128)(2,1)S(1)} %bitcast.122), channel_id=1, replica_groups=mesh['seq'=2,'head'=4,'dp'=4] {'head'}, dimensions={0}, use_global_device_ids=true | all-gather | bytes 737280 | tf_op jit(solution)/shard_map/all_gather | solution.py:156
  118.8 10.1 %fusion.55 = (f32[8,576]{1,0:T(8,128)S(1)}, f32[8,576,576]{1,2,0:T(8,128)}) fusion(pred[576,576]{0,1:T(8,128)(4,1)} %compare_and_fusion, bf16[576,8,128]{2,1,0:T(8,128)(2,1)S(1)} %bitcast.116, bf16[576,512]{1,0:T(8,128)(2,1)} %all_gather.7, s32[]{:T(128)S(6)} %select_n.41), kind=kOutput, calls=%fused_computation.83 | convolution fusion | flops 690094656 | bytes 12331012 | tf_op jit(solution)/shard_map/while/body/eval_jaxpr/sub | solution.py:79
  128.8 5.5 %fusion.7 = bf16[8,576,576]{1,2,0:T(8,128)(2,1)S(1)} fusion(f32[576]{0:T(1024)S(1)} %fusion.43, f32[8,576,576]{1,2,0:T(8,128)} %get-tuple-element.70, f32[8,576]{1,0:T(8,128)S(1)} %get-tuple-element.69), kind=kLoop, calls=%fused_computation.11 | loop fusion | flops 7962624 | bytes 15945984 | tf_op jit(solution)/shard_map/while/body/eval_jaxpr/convert_element_type | solution.py:82
  134.5 2.3 copy-done
  136.9 1.6 fusion.11
  138.5 6.5 %multiply_reduce_fusion = (f32[576,8]{0,1:T(8,128)S(1)}, bf16[576,8,128]{2,0,1:T(8,128)(2,1)S(1)}) fusion(bf16[576,8,128]{2,1,0:T(8,128)(2,1)} %bitcast.112, bf16[8,576,576]{1,2,0:T(8,128)(2,1)} %copy-done, bf16[576,512]{1,0:T(8,128)(2,1)} %all_gather.6, s32[]{:T(128)S(6)} %select_n.41), kind=kOutput, calls=%fused_computation.16 | convolution fusion | flops 682421760 | bytes 8423428 | tf_op jit(solution)/shard_map/while/body/eval_jaxpr/hbk,kd->bhd/dot_general | solution.py:83
  145.0 7.5 %fusion.2 = bf16[8,576,576]{1,2,0:T(8,128)(2,1)} fusion(f32[8,576]{1,0:T(8,128)S(1)} %bitcast.127, f32[576]{0:T(1024)S(1)} %fusion.43, f32[8,576,576]{1,2,0:T(8,128)} %get-tuple-element.70, f32[8,576]{1,0:T(8,128)S(1)} %copy-done.22, bf16[576,8,128]{2,1,0:T(8,128)(2,1)S(1)} %bitcast.113, bf16[576,512]{1,0:T(8,128)(2,1)} %all_gather.6, s32[]{:T(128)S(6)} %select_n.41), kind=kOutput, calls=%fused_computation.3 | convolution fusion | flops 692748288 | bytes 18471172 | tf_op jit(solution)/shard_map/while/body/eval_jaxpr/bhd,kd->hbk/dot_general | solution.py:86
  152.5 5.2 %multiply_bitcast_fusion = f32[576,8,128]{2,0,1:T(8,128)S(1)} fusion(bf16[8,576,576]{1,2,0:T(8,128)(2,1)} %fusion.2, bf16[576,512]{1,0:T(8,128)(2,1)} %all_gather.7, s32[]{:T(128)S(6)} %select_n.41), kind=kOutput, calls=%fused_computation.15 | convolution fusion | flops 680067072 | bytes 8404996 | tf_op jit(solution)/shard_map/while/body/eval_jaxpr/hbk,kd->bhd/dot_general | solution.py:92
  160.0 1.4 convert_element_type.91
  161.4 5.4 %all-to-all-start.5 = ((bf16[8,72,1024]{2,1,0:T(8,128)(2,1)}), bf16[8,72,1024]{2,1,0:T(8,128)(2,1)S(1)}, u32[]{:S(2)}, u32[]{:S(2)}) async-start(bf16[8,72,1024]{2,1,0:T(8,128)(2,1)} %convert_element_type.91), calls=%async_computation.5 | async-start | bytes 2359296 | tf_op jit(solution)/shard_map/all_to_all | solution.py:202
  167.0 4.6 %fusion.13 = f32[576,512]{1,0:T(8,128)S(1)} fusion(f32[576,512]{1,0:T(8,128)S(1)} %broadcast_in_dim.61.clone, s32[]{:T(128)S(6)} %select_n.41, bf16[8,576,576]{1,2,0:T(8,128)(2,1)} %fusion.2, bf16[576,8,128]{2,1,0:T(8,128)(2,1)} %bitcast.117), kind=kOutput, calls=%fused_computation.30 | convolution fusion | flops 679550976 | bytes 6782980 | tf_op jit(solution)/shard_map/while/body/eval_jaxpr/hbk,bhd->kd/dot_general | solution.py:99
  173.4 1.4 all_to_all.107
  174.8 32.8 %all-to-all-done.5 = bf16[8,72,1024]{2,1,0:T(8,128)(2,1)S(1)} async-done(((bf16[8,72,1024]{2,1,0:T(8,128)(2,1)}), bf16[8,72,1024]{2,1,0:T(8,128)(2,1)S(1)}, u32[]{:S(2)}, u32[]{:S(2)}) %all-to-all-start.5) | async-done | bytes 1179680 | tf_op jit(solution)/shard_map/all_to_all | solution.py:202
  207.6 3.6 %all-to-all-start.3 = ((bf16[8,72,1024]{2,1,0:T(8,128)(2,1)}), bf16[8,72,1024]{2,1,0:T(8,128)(2,1)S(1)}, u32[]{:S(2)}, u32[]{:S(2)}) async-start(bf16[8,72,1024]{2,1,0:T(8,128)(2,1)} %all_to_all.107), calls=%async_computation.3 | async-start | bytes 2359296 | tf_op jit(solution)/shard_map/all_to_all | solution.py:201
  211.2 1.6 convert_element_type.97
  212.8 45.7 %all-to-all-done.3 = bf16[8,72,1024]{2,1,0:T(8,128)(2,1)S(1)} async-done(((bf16[8,72,1024]{2,1,0:T(8,128)(2,1)}), bf16[8,72,1024]{2,1,0:T(8,128)(2,1)S(1)}, u32[]{:S(2)}, u32[]{:S(2)}) %all-to-all-start.3) | async-done | bytes 1179680 | tf_op jit(solution)/shard_map/all_to_all | solution.py:201
  258.5 3.4 %all-to-all-start.7 = ((bf16[2,72,512]{2,1,0:T(8,128)(2,1)}), bf16[2,72,512]{2,1,0:T(8,128)(2,1)S(1)}, u32[]{:S(2)}, u32[]{:S(2)}) async-start(bf16[2,72,512]{2,1,0:T(8,128)(2,1)} %bitcast.23), calls=%async_computation.9 | async-start | bytes 294912 | tf_op jit(solution)/shard_map/all_to_all | solution.py:189
  262.0 1.6 convert_element_type.92
  263.6 2.9 %all-to-all-done.7 = bf16[2,72,512]{2,1,0:T(8,128)(2,1)S(1)} async-done(((bf16[2,72,512]{2,1,0:T(8,128)(2,1)}), bf16[2,72,512]{2,1,0:T(8,128)(2,1)S(1)}, u32[]{:S(2)}, u32[]{:S(2)}) %all-to-all-start.7) | async-done | bytes 147488 | tf_op jit(solution)/shard_map/all_to_all | solution.py:189
  266.5 3.4 %all-to-all-start.6 = ((bf16[2,72,512]{2,1,0:T(8,128)(2,1)}), bf16[2,72,512]{2,1,0:T(8,128)(2,1)S(1)}, u32[]{:S(2)}, u32[]{:S(2)}) async-start(bf16[2,72,512]{2,1,0:T(8,128)(2,1)} %bitcast.20), calls=%async_computation.7 | async-start | bytes 294912 | tf_op jit(solution)/shard_map/all_to_all | solution.py:186
  272.8 1.6 all-to-all-done.6
  (100 shorter events, 22.0 us)
Async XLA Ops:
  7.2 14.1 %copy-start.6 = (bf16[72,8192]{1,0:T(8,128)(2,1)S(1)}, bf16[72,8192]{1,0:T(8,128)(2,1)}, u32[]{:S(2)}) copy-start(bf16[72,8192]{1,0:T(8,128)(2,1)} %param.11) | copy-start | bytes 3538948
  8.9 8.9 %all-to-all-start = ((bf16[72,2,512]{2,0,1:T(8,128)(2,1)}), bf16[72,2,512]{2,0,1:T(8,128)(2,1)S(1)}, u32[]{:S(2)}, u32[]{:S(2)}) async-start(bf16[72,2,512]{2,0,1:T(8,128)(2,1)} %bitcast.105), calls=%async_computation | async-start | bytes 294912 | tf_op jit(solution)/shard_map/all_to_all | solution.py:152
  15.1 2.7 copy-start.14
  15.1 2.7 copy-start.17
  17.8 8.0 %copy-start.10 = (bf16[72,2,512]{2,0,1:T(8,128)(2,1)}, bf16[72,2,512]{2,0,1:T(8,128)(2,1)S(1)}, u32[]{:S(2)}) copy-start(bf16[72,2,512]{2,0,1:T(8,128)(2,1)S(1)} %all-to-all-done) | copy-start | bytes 442372
  17.8 8.0 %all-to-all-start.1 = ((bf16[72,2,512]{2,0,1:T(8,128)(2,1)}), bf16[72,2,512]{2,0,1:T(8,128)(2,1)S(1)}, u32[]{:S(2)}, u32[]{:S(2)}) async-start(bf16[72,2,512]{2,0,1:T(8,128)(2,1)} %copy.47), calls=%async_computation.1 | async-start | bytes 294912 | tf_op jit(solution)/shard_map/all_to_all | solution.py:151
  21.2 10.6 %copy-start.5 = (bf16[72,8192]{1,0:T(8,128)(2,1)S(1)}, bf16[72,8192]{1,0:T(8,128)(2,1)}, u32[]{:S(2)}) copy-start(bf16[72,8192]{1,0:T(8,128)(2,1)} %param.8) | copy-start | bytes 3538948
  26.4 32.5 %all-to-all-start.4 = ((bf16[72,8,1024]{2,0,1:T(8,128)(2,1)}), bf16[72,8,1024]{2,0,1:T(8,128)(2,1)S(1)}, u32[]{:S(2)}, u32[]{:S(2)}) async-start(bf16[72,8,1024]{2,0,1:T(8,128)(2,1)} %bitcast.103), calls=%async_computation.4 | async-start | bytes 2359296 | tf_op jit(solution)/shard_map/all_to_all | solution.py:173
  35.0 27.6 %copy-start.20 = (s32[576]{0:T(1024)S(1)}, s32[576]{0:T(1024)}, u32[]{:S(2)}) copy-start(s32[576]{0:T(1024)} %param.12) | copy-start | bytes 6916
  35.0 27.7 %copy-start.24 = (s32[2]{0:T(128)S(1)}, s32[2]{0:T(128)}, u32[]{:S(2)}) copy-start(s32[2]{0:T(128)} %param.13) | copy-start | bytes 28
  35.0 28.3 %copy-start.23 = (pred[576]{0:T(1024)(128)(4,1)S(1)}, pred[576]{0:T(1024)(128)(4,1)}, u32[]{:S(2)}) copy-start(pred[576]{0:T(1024)(128)(4,1)} %constant.196) | copy-start | bytes 1732
  36.7 32.5 %copy-start.13 = (bf16[72,2,512]{2,0,1:T(8,128)(2,1)S(1)}, bf16[72,2,512]{2,0,1:T(8,128)(2,1)}, u32[]{:S(2)}) copy-start(bf16[72,2,512]{2,0,1:T(8,128)(2,1)} %copy-done.12) | copy-start | bytes 442372
  36.7 64.1 %copy-start.11 = (bf16[72,2,512]{2,0,1:T(8,128)(2,1)S(1)}, bf16[72,2,512]{2,0,1:T(8,128)(2,1)}, u32[]{:S(2)}) copy-start(bf16[72,2,512]{2,0,1:T(8,128)(2,1)} %copy-done.10) | copy-start | bytes 442372
  58.9 59.5 %all-to-all-start.2 = ((bf16[72,8,1024]{2,0,1:T(8,128)(2,1)}), bf16[72,8,1024]{2,0,1:T(8,128)(2,1)S(1)}, u32[]{:S(2)}, u32[]{:S(2)}) async-start(bf16[72,8,1024]{2,0,1:T(8,128)(2,1)} %copy.48), calls=%async_computation.2 | async-start | bytes 2359296 | tf_op jit(solution)/shard_map/all_to_all | solution.py:172
  62.5 148.6 %reduce-scatter.5.cloned.1.call-start = ((), (), s32[]{:S(2)}) async-start(), calls=%async_computation.11 | async-start | bytes 1474560 | tf_op jit(solution)/shard_map/reduce_scatter | solution.py:183
  118.4 16.1 %copy-start.3 = (bf16[72,8,8,128]{3,2,1,0:T(8,128)(2,1)}, bf16[72,8,8,128]{3,2,1,0:T(8,128)(2,1)S(1)}, u32[]{:S(2)}) copy-start(bf16[72,8,8,128]{3,2,1,0:T(8,128)(2,1)S(1)} %copy.73) | copy-start | bytes 3538948
  118.8 10.1 %copy-start.7 = (bf16[72,8,8,128]{3,2,1,0:T(8,128)(2,1)}, bf16[72,8,8,128]{3,2,1,0:T(8,128)(2,1)S(1)}, u32[]{:S(2)}) copy-start(bf16[72,8,8,128]{3,2,1,0:T(8,128)(2,1)S(1)} %copy.72) | copy-start | bytes 3538948
  128.8 5.6 %copy-start.21 = (f32[8,576]{1,0:T(8,128)}, f32[8,576]{1,0:T(8,128)S(1)}, u32[]{:S(2)}) copy-start(f32[8,576]{1,0:T(8,128)S(1)} %get-tuple-element.69) | copy-start | bytes 55300
  134.4 2.5 copy-start
  138.5 6.5 %copy-start.2 = (f32[576,512]{1,0:T(8,128)}, f32[576,512]{1,0:T(8,128)S(1)}, u32[]{:S(2)}) copy-start(f32[576,512]{1,0:T(8,128)S(1)} %fusion.11) | copy-start | bytes 3538948
  138.5 6.5 %copy-start.4 = (bf16[72,8,8,128]{3,2,1,0:T(8,128)(2,1)S(1)}, bf16[72,8,8,128]{3,2,1,0:T(8,128)(2,1)}, u32[]{:S(2)}) copy-start(bf16[72,8,8,128]{3,2,1,0:T(8,128)(2,1)} %copy-done.3) | copy-start | bytes 3538948
  138.5 6.5 %copy-start.22 = (f32[8,576]{1,0:T(8,128)S(1)}, f32[8,576]{1,0:T(8,128)}, u32[]{:S(2)}) copy-start(f32[8,576]{1,0:T(8,128)} %copy-done.21) | copy-start | bytes 55300
  152.5 5.3 %copy-start.8 = (f32[576,64]{1,0:T(8,128)S(1)}, f32[576,64]{1,0:T(8,128)}, u32[]{:S(2)}) copy-start(f32[576,64]{1,0:T(8,128)} %get-tuple-element.63) | copy-start | bytes 442372
  152.5 5.3 %copy-start.9 = (f32[576,64]{1,0:T(8,128)S(1)}, f32[576,64]{1,0:T(8,128)}, u32[]{:S(2)}) copy-start(f32[576,64]{1,0:T(8,128)} %get-tuple-element.64) | copy-start | bytes 442372
  161.4 46.2 %all-to-all-start.5 = ((bf16[8,72,1024]{2,1,0:T(8,128)(2,1)}), bf16[8,72,1024]{2,1,0:T(8,128)(2,1)S(1)}, u32[]{:S(2)}, u32[]{:S(2)}) async-start(bf16[8,72,1024]{2,1,0:T(8,128)(2,1)} %convert_element_type.91), calls=%async_computation.5 | async-start | bytes 2359296 | tf_op jit(solution)/shard_map/all_to_all | solution.py:202
  166.8 95.1 %reduce-scatter.3.cloned.1.call-start = ((), (), s32[]{:S(2)}) async-start(), calls=%async_computation.10 | async-start | bytes 1474560 | tf_op jit(solution)/shard_map/reduce_scatter | solution.py:182
  171.6 1.0 copy-start.1
  207.6 51.0 %all-to-all-start.3 = ((bf16[8,72,1024]{2,1,0:T(8,128)(2,1)}), bf16[8,72,1024]{2,1,0:T(8,128)(2,1)S(1)}, u32[]{:S(2)}, u32[]{:S(2)}) async-start(bf16[8,72,1024]{2,1,0:T(8,128)(2,1)} %all_to_all.107), calls=%async_computation.3 | async-start | bytes 2359296 | tf_op jit(solution)/shard_map/all_to_all | solution.py:201
  258.5 8.0 %all-to-all-start.7 = ((bf16[2,72,512]{2,1,0:T(8,128)(2,1)}), bf16[2,72,512]{2,1,0:T(8,128)(2,1)S(1)}, u32[]{:S(2)}, u32[]{:S(2)}) async-start(bf16[2,72,512]{2,1,0:T(8,128)(2,1)} %bitcast.23), calls=%async_computation.9 | async-start | bytes 294912 | tf_op jit(solution)/shard_map/all_to_all | solution.py:189
  266.5 8.0 %all-to-all-start.6 = ((bf16[2,72,512]{2,1,0:T(8,128)(2,1)}), bf16[2,72,512]{2,1,0:T(8,128)(2,1)S(1)}, u32[]{:S(2)}, u32[]{:S(2)}) async-start(bf16[2,72,512]{2,1,0:T(8,128)(2,1)} %bitcast.20), calls=%async_computation.7 | async-start | bytes 294912 | tf_op jit(solution)/shard_map/all_to_all | solution.py:186
  271.1 3.9 %copy-start.16 = (f32[72,64]{1,0:T(8,128)S(1)}, f32[72,64]{1,0:T(8,128)}, u32[]{:S(2)}) copy-start(f32[72,64]{1,0:T(8,128)} %copy-done.14) | copy-start | bytes 55300
  271.1 3.9 %copy-start.19 = (f32[72,64]{1,0:T(8,128)S(1)}, f32[72,64]{1,0:T(8,128)}, u32[]{:S(2)}) copy-start(f32[72,64]{1,0:T(8,128)} %copy-done.17) | copy-start | bytes 55300
  (3 other events, 2.2 us)
Sparse Core Ops, SparseCore 0:
  152.6 45.9 reduce-scatter.4
  201.0 53.8 reduce-scatter.2
where the time goes:
time: 284 us; the launch traced here: 283 us
  waiting for transfers between devices  110 us (39%)
  blocking collectives  48.9 us (17%)
  matrix products  35.4 us (12%)
  starting transfers between devices  32.5 us (11%)
  local copies, waits for them, and re-layouts  20.8 us (7%)
  other arithmetic  20.2 us (7%)
  between operations  14.6 us (5%)
    all_to_all x1, waiting for transfers between devices, shards(): lax.all_to_all(out_heads, ('seq', 'head'), split_axis=0, concat_axis=1, t...  45.7 us
    all_to_all x1, waiting for transfers between devices, shards(): lax.all_to_all(grad_heads, ('seq', 'head'), split_axis=0, concat_axis=1,...  32.8 us
    all_gather x1, blocking collectives, shards(): lax.all_gather(key_split, 'head', axis=0, tiled=True)  31.7 us
    all_to_all x1, waiting for transfers between devices, shards(): lax.all_to_all(output_gradient, ('seq', 'head'), split_axis=1, concat_axi...  22.3 us
    all_gather x1, blocking collectives, shards(): lax.all_gather(value_split, 'head', axis=0, tiled=True)  17.3 us
    sub x1, matrix products, block_step(): weights = jnp.exp(scores - row_max)  10.1 us
    dot_general x1, matrix products, block_step(): jnp.einsum('bhd,kd->hbk', grad_part, value_block, preferred_element_type=...  7.47 us
    dot_general x1, matrix products, block_step(): jnp.einsum('hbk,kd->bhd', probs_low, value_block, preferred_element_type=...  6.46 us
  transfers between devices with their start and end apart: 10, of which 7 were waited for; matrix products, arithmetic and copies ran while one was open for 13% of the time, Pallas kernels for 0%

commit v1 on v0

v1 whole, which is shorter than its diff:
```python
import functools

import jax
import jax.numpy as jnp
import numpy as np
from jax import lax
from jax.experimental import pallas as pl
from jax.experimental.pallas import tpu as pltpu
from jax.sharding import PartitionSpec as P

QUERY_HEADS = 64
KEY_VALUE_HEADS = 8
HEAD_WIDTH = 128
GROUP = QUERY_HEADS // KEY_VALUE_HEADS
ROPE_BASE = 500000.0
SCORE_SCALE = 1.0 / float(np.sqrt(HEAD_WIDTH))
LOG2_E = 1.4426950408889634
CHUNKS = 2
HEADS_PER_CHUNK = KEY_VALUE_HEADS // CHUNKS
CHUNK_COLS = HEADS_PER_CHUNK * HEAD_WIDTH
VMEM = pl.BlockSpec(memory_space=pltpu.VMEM)
SMEM = pl.BlockSpec(memory_space=pltpu.SMEM)


def inverse_freq_row():
    half = HEAD_WIDTH // 2
    place = lax.rem(lax.broadcasted_iota(jnp.int32, (8, HEAD_WIDTH), 1), half)
    row = jnp.ones((8, HEAD_WIDTH), jnp.float32)
    for i in range(1, half):
        row = jnp.where(place == i, np.float32(ROPE_BASE ** (-2.0 * i / HEAD_WIDTH)), row)
    return row[0:1]


def rope(vectors, cosine, sine):
    return vectors * cosine + pltpu.roll(vectors, HEAD_WIDTH // 2, 1) * sine


def rope_back(vectors, cosine, sine):
    return vectors * cosine - pltpu.roll(vectors, HEAD_WIDTH // 2, 1) * sine


def head_cols(index):
    return slice(index * HEAD_WIDTH, (index + 1) * HEAD_WIDTH)


def prepare_keys(rows, pos_ref, key_ref, value_ref, *out_refs):
    kv_refs, (cos_ref, sin_ref) = out_refs[:CHUNKS], out_refs[CHUNKS:]
    padded = key_ref.shape[0]
    start = (lax.axis_index("seq") * lax.axis_size("head") + lax.axis_index("head")) * rows
    sublane = lax.broadcasted_iota(jnp.int32, (8, HEAD_WIDTH), 0)
    pieces = []
    for base in range(0, padded, 8):
        piece = jnp.zeros((8, HEAD_WIDTH), jnp.int32)
        for offset in range(min(8, rows - base)):
            piece = jnp.where(sublane == offset, pos_ref[start + (base + offset)], piece)
        pieces.append(piece)
    angle = jnp.concatenate(pieces, 0).astype(jnp.float32) * inverse_freq_row()
    lane = lax.broadcasted_iota(jnp.int32, angle.shape, 1)
    cosine = jnp.cos(angle)
    sine = jnp.sin(angle) * jnp.where(lane < HEAD_WIDTH // 2, -1.0, 1.0)
    cos_ref[...] = cosine
    sin_ref[...] = sine
    for head in range(KEY_VALUE_HEADS):
        chunk, place = divmod(head, HEADS_PER_CHUNK)
        rotated = rope(key_ref[:, head_cols(head)].astype(jnp.float32), cosine, sine)
        kv_refs[chunk][:, head_cols(place)] = rotated.astype(jnp.bfloat16)
        kv_refs[chunk][:, head_cols(HEADS_PER_CHUNK + place)] = value_ref[:, head_cols(head)]


def prepare_queries(query_ref, grad_ref, cos_ref, sin_ref, q_ref, qt_ref, g_ref, gt_ref, table_ref):
    cosine, sine = cos_ref[...], sin_ref[...]
    queries = jnp.concatenate(
        [
            rope(query_ref[:, head_cols(h)].astype(jnp.float32), cosine, sine)
            for h in range(GROUP)
        ],
        0,
    )
    grads = jnp.concatenate(
        [grad_ref[:, head_cols(h)].astype(jnp.float32) for h in range(GROUP)], 0
    )
    q_ref[0] = queries.astype(jnp.bfloat16)
    qt_ref[0] = queries.T.astype(jnp.bfloat16)
    g_ref[0] = grads.astype(jnp.bfloat16)
    gt_ref[0] = grads.T.astype(jnp.bfloat16)
    table_ref[...] = cosine


def dot(left, right):
    return jnp.dot(left, right, preferred_element_type=jnp.float32)


def attend(seq_count, head_count, rows, has_alias, counts_ref, *refs):
    blocks = seq_count * head_count
    kv_refs = refs[:blocks]
    q_ref, qt_ref, g_ref, gt_ref, cos_ref, sin_ref = refs[blocks : blocks + 6]
    outs = refs[blocks + 6 + 2 * has_alias :]
    out_ref, grad_ref = outs[:2]
    part_refs = outs[2 : 2 + seq_count]
    bias_ref, live_ref = outs[2 + seq_count :]
    padded = kv_refs[0].shape[0]
    query_rows = GROUP * padded
    step = pl.program_id(0)
    seq_index, head_index = lax.axis_index("seq"), lax.axis_index("head")
    my_rank = seq_index * head_count + head_index

    @pl.when(step == 0)
    def _():
        key_row = lax.broadcasted_iota(jnp.int32, (padded, query_rows), 0)
        query_row = lax.rem(lax.broadcasted_iota(jnp.int32, (padded, query_rows), 1), padded)
        for block in range(blocks):
            seq_offset, head_offset = divmod(block, head_count)
            seq_from = jnp.bitwise_xor(seq_index, seq_offset)
            head_from = jnp.bitwise_xor(head_index, head_offset)
            rank = seq_from * head_count + head_from
            limit = jnp.minimum(counts_ref[seq_from] - head_from * rows, rows)
            limit = jnp.where(rank <= my_rank, limit, 0)
            allowed = key_row < limit
            if block == 0:
                allowed = allowed & (key_row <= query_row)
                live_ref[...] = (query_row[:8] < limit).astype(jnp.float32)
            bias_ref[block * padded : (block + 1) * padded, :] = jnp.where(allowed, 0.0, -1e30)

    cols = pl.ds(pl.multiple_of(step * HEAD_WIDTH, HEAD_WIDTH), HEAD_WIDTH)
    far_cols = pl.ds(pl.multiple_of(CHUNK_COLS + step * HEAD_WIDTH, HEAD_WIDTH), HEAD_WIDTH)
    keys_wide = jnp.concatenate([ref[:, cols].astype(jnp.float32) for ref in kv_refs], 0)
    values_wide = jnp.concatenate([ref[:, far_cols].astype(jnp.float32) for ref in kv_refs], 0)
    keys, keys_t = keys_wide.astype(jnp.bfloat16), keys_wide.T.astype(jnp.bfloat16)
    values, values_t = values_wide.astype(jnp.bfloat16), values_wide.T.astype(jnp.bfloat16)
    queries, queries_t = q_ref[0], qt_ref[0]
    grads, grads_t = g_ref[0], gt_ref[0]

    scores = dot(keys, queries_t) * (SCORE_SCALE * LOG2_E) + bias_ref[...]
    weights = jnp.exp2(scores - jnp.max(scores, 0, keepdims=True))
    row_total = jnp.sum(weights, 0, keepdims=True)
    probs = weights * (live_ref[0:1, :] / row_total)
    probs_low = probs.astype(jnp.bfloat16)
    out_t = dot(values_t, probs_low)
    delta = jnp.sum(
        grads_t.astype(jnp.float32) * out_t.astype(jnp.bfloat16).astype(jnp.float32),
        0,
        keepdims=True,
    )
    dscore = (probs * (dot(values, grads_t) - delta)).astype(jnp.bfloat16)
    grad_t = dot(keys_t, dscore) * SCORE_SCALE
    key_part = dot(dscore, queries) * SCORE_SCALE
    value_part = dot(probs_low, grads)

    cosine, sine = cos_ref[...], sin_ref[...]
    out_heads, grad_heads = out_t.T, grad_t.T
    for h in range(GROUP):
        piece = slice(h * padded, (h + 1) * padded)
        out_ref[:, head_cols(h)] = out_heads[piece].astype(jnp.bfloat16)
        grad_ref[:, head_cols(h)] = rope_back(grad_heads[piece], cosine, sine).astype(jnp.bfloat16)
    for block in range(blocks):
        seq_offset, head_offset = divmod(block, head_count)
        piece = slice(block * padded, (block + 1) * padded)
        part_refs[seq_offset][head_offset, :, cols] = key_part[piece].astype(jnp.bfloat16)
        part_refs[seq_offset][head_offset, :, far_cols] = value_part[piece].astype(jnp.bfloat16)


def combine(seq_count, head_count, *refs):
    part_refs, base_ref, send_refs = refs[:seq_count], refs[seq_count], refs[seq_count + 1 :]
    for offset in range(head_count):
        total = part_refs[0][offset].astype(jnp.float32)
        for ref in part_refs[1:]:
            total = total + ref[offset].astype(jnp.float32)
        if offset == 0:
            base_ref[...] = total
        else:
            send_refs[offset - 1][...] = total.astype(jnp.bfloat16)


def finish(head_count, *refs):
    cosine, sine = refs[0][...], refs[1][...]
    key_ref, value_ref = refs[-2:]
    for chunk in range(CHUNKS):
        mine = refs[2 + chunk * head_count : 2 + (chunk + 1) * head_count]
        for place in range(HEADS_PER_CHUNK):
            here, there = head_cols(place), head_cols(HEADS_PER_CHUNK + place)
            key_total, value_total = mine[0][:, here], mine[0][:, there]
            for ref in mine[1:]:
                key_total = key_total + ref[:, here].astype(jnp.float32)
                value_total = value_total + ref[:, there].astype(jnp.float32)
            cols = head_cols(chunk * HEADS_PER_CHUNK + place)
            key_ref[:, cols] = rope_back(key_total, cosine, sine).astype(jnp.bfloat16)
            value_ref[:, cols] = value_total.astype(jnp.bfloat16)


def params(mebibytes):
    return pltpu.CompilerParams(vmem_limit_bytes=mebibytes << 20)


def cost(microseconds):
    return pl.CostEstimate(
        flops=microseconds * 1153 * 10**6,
        bytes_accessed=microseconds * 3690 * 10**3,
        transcendentals=0,
    )


def shards(queries, routed_keys, routed_values, output_gradient, positions, counts):
    seq_count = lax.axis_size("seq")
    head_count = lax.axis_size("head")
    blocks = seq_count * head_count
    rows = queries.shape[0]
    padded = -(-rows // 8) * 8
    if padded != rows:
        extra = ((0, padded - rows), (0, 0))
        queries, routed_keys, routed_values, output_gradient = (
            jnp.pad(x, extra) for x in (queries, routed_keys, routed_values, output_gradient)
        )
    query_rows = GROUP * padded
    shape = jax.ShapeDtypeStruct
    bf16, f32 = jnp.bfloat16, jnp.float32
    ranks = [(s, z) for s in range(seq_count) for z in range(head_count)]

    def rank_of(s, z):
        return s * head_count + z

    def along_head(x, offset, upward, held=0):
        pairs = []
        for s, z in ranks:
            other = z ^ offset
            if s < seq_count - 1 or ((z ^ held) < other) == upward:
                pairs.append((rank_of(s, z), rank_of(s, other)))
        return lax.ppermute(x, ("seq", "head"), pairs)

    def along_seq(x, offset, upward):
        pairs = [
            (rank_of(s, z), rank_of(s ^ offset, z))
            for s, z in ranks
            if (s < (s ^ offset)) == upward
        ]
        return lax.ppermute(x, ("seq", "head"), pairs)

    table = shape((padded, HEAD_WIDTH), f32)
    piece = shape((padded, 2 * CHUNK_COLS), bf16)
    *own, cosine, sine = pl.pallas_call(
        functools.partial(prepare_keys, rows),
        out_shape=[piece] * CHUNKS + [table, table],
        in_specs=[SMEM, VMEM, VMEM],
        out_specs=[VMEM] * (CHUNKS + 2),
        compiler_params=params(56),
        name="prepare_keys",
    )(positions, routed_keys, routed_values)

    wide = GROUP * HEAD_WIDTH
    row_block = pl.BlockSpec((padded, wide), lambda g: (0, g))
    table_block = pl.BlockSpec((padded, HEAD_WIDTH), lambda g: (0, 0))
    tall_block = pl.BlockSpec((1, query_rows, HEAD_WIDTH), lambda g: (g, 0, 0))
    flat_block = pl.BlockSpec((1, HEAD_WIDTH, query_rows), lambda g: (g, 0, 0))
    tall = shape((KEY_VALUE_HEADS, query_rows, HEAD_WIDTH), bf16)
    flat = shape((KEY_VALUE_HEADS, HEAD_WIDTH, query_rows), bf16)
    *stacked, cosine_later = pl.pallas_call(
        prepare_queries,
        grid=(KEY_VALUE_HEADS,),
        out_shape=[tall, flat, tall, flat, table],
        in_specs=[row_block, row_block, table_block, table_block],
        out_specs=[tall_block, flat_block, tall_block, flat_block]
        + [table_block],
        cost_estimate=cost(7),
        compiler_params=params(16),
        name="prepare_queries",
    )(queries, output_gradient, cosine, sine)

    bits = [1 << b for b in reversed(range((head_count - 1).bit_length()))]
    far = [[[along_seq(x, a, True)] for a in range(1, seq_count)] for x in own]
    gathered = []
    for chunk in range(CHUNKS):
        near = {0: own[chunk]}
        for bit in bits:
            near.update({j ^ bit: along_head(x, bit, True, j) for j, x in near.items()})
            if bit == bits[0] and chunk == 0:
                near[bit], cosine_later, far = lax.optimization_barrier(
                    (near[bit], cosine_later, far)
                )
            if bit == bits[0] and chunk + 1 < CHUNKS:
                own[chunk + 1], near[bit] = lax.optimization_barrier((own[chunk + 1], near[bit]))
        near = [near[j] for j in range(head_count)]
        for a in range(1, seq_count):
            far[chunk][a - 1] += [along_seq(x, a, True) for x in near[1:]]
        gathered.append(near + [x for group in far[chunk] for x in group])

    wide_outs = ()
    summed = []
    for chunk in range(CHUNKS):
        first = chunk * HEADS_PER_CHUNK
        has_alias = int(chunk > 0)
        tall_part = pl.BlockSpec((1, query_rows, HEAD_WIDTH), lambda g, f=first: (f + g, 0, 0))
        flat_part = pl.BlockSpec((1, HEAD_WIDTH, query_rows), lambda g, f=first: (f + g, 0, 0))
        row_part = pl.BlockSpec((padded, wide), lambda g, f=first: (0, f + g))
        kv_block = pl.BlockSpec((padded, 2 * CHUNK_COLS), lambda g: (0, 0))
        part_block = pl.BlockSpec((head_count, padded, 2 * CHUNK_COLS), lambda g: (0, 0, 0))
        out = pl.pallas_call(
            functools.partial(attend, seq_count, head_count, rows, has_alias),
            grid=(HEADS_PER_CHUNK,),
            out_shape=[shape((padded, QUERY_HEADS * HEAD_WIDTH), bf16)] * 2
            + [shape((head_count, padded, 2 * CHUNK_COLS), bf16)] * seq_count,
            in_specs=[SMEM]
            + [kv_block] * blocks
            + [tall_part, flat_part, tall_part, flat_part, table_block, table_block]
            + [pl.BlockSpec(memory_space=pl.ANY)] * (2 * has_alias),
            out_specs=[row_part, row_part] + [part_block] * seq_count,
            scratch_shapes=[
                pltpu.VMEM((blocks * padded, query_rows), f32),
                pltpu.VMEM((8, query_rows), f32),
            ],
            input_output_aliases={blocks + 7: 0, blocks + 8: 1} if has_alias else {},
            cost_estimate=cost(10),
            compiler_params=params(32),
            name="attend",
        )(counts, *gathered[chunk], *stacked, cosine_later, sine, *wide_outs)
        wide_outs = out[:2]
        parts = [out[2]] + [along_seq(out[2 + a], a, False) for a in range(1, seq_count)]
        base, *sends = pl.pallas_call(
            functools.partial(combine, seq_count, head_count),
            out_shape=[shape((padded, 2 * CHUNK_COLS), f32)] + [piece] * (head_count - 1),
            in_specs=[VMEM] * seq_count,
            out_specs=[VMEM] * head_count,
            cost_estimate=cost(2),
            compiler_params=params(8),
            name="combine",
        )(*parts)
        summed += [base] + [along_head(x, j + 1, False) for j, x in enumerate(sends)]

    narrow = shape((padded, KEY_VALUE_HEADS * HEAD_WIDTH), bf16)
    key_grad, value_grad = pl.pallas_call(
        functools.partial(finish, head_count),
        out_shape=[narrow, narrow],
        in_specs=[VMEM] * (2 + CHUNKS * head_count),
        out_specs=[VMEM, VMEM],
        cost_estimate=cost(2),
        compiler_params=params(8),
        name="finish",
    )(cosine, sine, *summed)
    results = (*wide_outs, key_grad, value_grad)
    if padded != rows:
        results = tuple(x[:rows] for x in results)
    return results


def solution(mesh):
    rows = P(("dp", "seq", "head"), None)
    return jax.shard_map(
        shards,
        mesh=mesh,
        in_specs=(rows, rows, rows, rows, P("dp"), P("dp")),
        out_specs=(rows, rows, rows, rows),
        check_vma=False,
    )
```

time: 284 us -> 99.5 us (0.35)
  waiting for transfers between devices: 110 us -> 16.1 us
  blocking collectives: 48.9 us -> 0 us
  matrix products: 35.4 us -> 0 us
  Pallas kernels: 0 us -> 22.6 us
  starting transfers between devices: 32.5 us -> 54.9 us
  other arithmetic: 20.2 us -> 0 us
  local copies, waits for them, and re-layouts: 20.8 us -> 4.09 us
  between operations: 14.6 us -> 0.99 us
    all_to_all x8 -> x0, waiting for transfers between devices: 110 us -> none  [the longest x1 45.7 us: shards(): lax.all_to_all(out_heads, ('seq', 'head'), split_axis=0, concat_axis=1, t...]
    ppermute x0 -> x22, starting transfers between devices: none -> 54.9 us  [the longest x12 39.8 us: along_head(): return lax.ppermute(x, ('seq', 'head'), pairs)]
    all_gather x2 -> x0, blocking collectives: 48.9 us -> none  [the longest x1 31.7 us: shards(): lax.all_gather(key_split, 'head', axis=0, tiled=True)]
    all_to_all x8 -> x0, starting transfers between devices: 32.5 us -> none  [the longest x1 5.45 us: shards(): lax.all_to_all(grad_heads, ('seq', 'head'), split_axis=0, concat_axis=1,...]
    dot_general x5 -> x0, matrix products: 25.3 us -> none  [the longest x1 7.47 us: block_step(): jnp.einsum('bhd,kd->hbk', grad_part, value_block, preferred_element_type=...]
    pallas_call x0 -> x7, Pallas kernels: none -> 22.6 us  [the longest x2 17 us: shards(): pl.pallas_call(functools.partial(attend, seq_count, head_count, rows, has...]
    ppermute x0 -> x22, waiting for transfers between devices: none -> 16.1 us  [the longest x10 8.41 us: along_seq(): return lax.ppermute(x, ('seq', 'head'), pairs)]
    convert_element_type x7 -> x0, other arithmetic: 10.9 us -> none  [the longest x1 5.54 us: block_step(): probs_low = probs.astype(jnp.bfloat16)]
  transfers between devices with their start and end apart: 10 -> 22, of which waited for: 7 -> 5; matrix products, arithmetic and copies ran while one was open for 13% -> 0% of each run, Pallas kernels for 0% -> 20%
where the time goes in v1:
time: 99.5 us; the launch traced here: 98.6 us
  starting transfers between devices  54.9 us (55%)
  Pallas kernels  22.6 us (23%)
  waiting for transfers between devices  16.1 us (16%)
  local copies, waits for them, and re-layouts  4.09 us (4%)
    ppermute x12, starting transfers between devices, along_head(): return lax.ppermute(x, ('seq', 'head'), pairs)  39.8 us
    pallas_call x2, Pallas kernels, shards(): pl.pallas_call(functools.partial(attend, seq_count, head_count, rows, has...  17 us
    ppermute x10, starting transfers between devices, along_seq(): return lax.ppermute(x, ('seq', 'head'), pairs)  15.1 us
    ppermute x10, waiting for transfers between devices, along_seq(): return lax.ppermute(x, ('seq', 'head'), pairs)  8.41 us
    ppermute x12, waiting for transfers between devices, along_head(): return lax.ppermute(x, ('seq', 'head'), pairs)  7.66 us
    unnamed x18, local copies, waits for them, and re-layouts  4.09 us
    pallas_call x1, Pallas kernels, shards(): pl.pallas_call(prepare_queries, grid=(KEY_VALUE_HEADS,), out_shape=[tall,...  2.53 us
  transfers between devices with their start and end apart: 22, of which 5 were waited for; matrix products, arithmetic and copies ran while one was open for 0% of the time, Pallas kernels for 20%

profile of v1, /device:TPU:0, one launch (start us, length us, event | category | flops | bytes accessed | tf_op | source)
XLA Modules:
  0.0 98.6 jit_solution(10958653637332047870)
XLA Ops:
  0.6 1.9 %prepare_keys.1 = (bf16[72,1024]{1,0:T(8,128)(2,1)}, bf16[72,1024]{1,0:T(8,128)(2,1)}, f32[72,128]{1,0:T(8,128)}, f32[72,128]{1,0:T(8,128)}) custom-call(s32[576]{0:T(1024)} %pos_ref.1, bf16[72,1024]{1,0:T(8,128)(2,1)} %key_ref.1, bf16[72,1024]{1,0:T(8,128)(2,1)} %value_ref.1), custom_call_target="tpu_custom_call" | custom-call | tf_op jit(solution)/shard_map/prepare_keys/pallas_call | solution.py:239
  2.6 4.9 %collective-permute-start.9 = (bf16[72,1024]{1,0:T(8,128)(2,1)}, bf16[72,1024]{1,0:T(8,128)(2,1)S(1)}, u32[]{:S(2)}, u32[]{:S(2)}) collective-permute-start(bf16[72,1024]{1,0:T(8,128)(2,1)} %get-tuple-element.38.refs_0_), channel_id=1, source_target_pairs={{0,4},{4,0},{8,12},{12,8},{16,20},{24,28},{1,5},{5,1},{9,13},{13,9... | collective-permute-start | bytes 442376 | tf_op jit(solution)/shard_map/ppermute | solution.py:227
  7.5 3.4 %collective-permute-start.1 = (bf16[72,1024]{1,0:T(8,128)(2,1)}, bf16[72,1024]{1,0:T(8,128)(2,1)S(1)}, u32[]{:S(2)}, u32[]{:S(2)}) collective-permute-start(bf16[72,1024]{1,0:T(8,128)(2,1)} %get-tuple-element.38.refs_0_), channel_id=1, source_target_pairs={{0,16},{4,20},{8,24},{12,28},{1,17},{5,21},{9,25},{13,29},{2,18},{... | collective-permute-start | bytes 442376 | tf_op jit(solution)/shard_map/ppermute | solution.py:235
  11.0 4.5 %collective-permute-start = (bf16[72,1024]{1,0:T(8,128)(2,1)}, bf16[72,1024]{1,0:T(8,128)(2,1)S(1)}, u32[]{:S(2)}, u32[]{:S(2)}) collective-permute-start(bf16[72,1024]{1,0:T(8,128)(2,1)} %get-tuple-element.38.refs_0_), channel_id=1, source_target_pairs={{0,8},{4,12},{8,0},{12,4},{16,24},{20,28},{1,9},{5,13},{9,1},{13,5... | collective-permute-start | bytes 442376 | tf_op jit(solution)/shard_map/ppermute | solution.py:227
  15.5 1.3 %collective-permute-start.2 = (bf16[72,1024]{1,0:T(8,128)(2,1)}, bf16[72,1024]{1,0:T(8,128)(2,1)S(1)}, u32[]{:S(2)}, u32[]{:S(2)}) collective-permute-start(bf16[72,1024]{1,0:T(8,128)(2,1)} %get-tuple-element.43.refs_0_), channel_id=1, source_target_pairs={{0,16},{4,20},{8,24},{12,28},{1,17},{5,21},{9,25},{13,29},{2,18},{... | collective-permute-start | bytes 442376 | tf_op jit(solution)/shard_map/ppermute | solution.py:235
  16.8 1.3 %copy-done = bf16[72,8192]{1,0:T(8,128)(2,1)S(1)} copy-done((bf16[72,8192]{1,0:T(8,128)(2,1)S(1)}, bf16[72,8192]{1,0:T(8,128)(2,1)}, u32[]{:S(2)}) %copy-start) | copy-done | bytes 1179672
  18.0 1.3 %copy-done.1 = bf16[72,8192]{1,0:T(8,128)(2,1)S(1)} copy-done((bf16[72,8192]{1,0:T(8,128)(2,1)S(1)}, bf16[72,8192]{1,0:T(8,128)(2,1)}, u32[]{:S(2)}) %copy-start.1) | copy-done | bytes 1179672
  20.9 2.5 %prepare_queries.1 = (bf16[8,576,128]{2,1,0:T(8,128)(2,1)S(1)}, bf16[8,128,576]{2,1,0:T(8,128)(2,1)S(1)}, bf16[8,576,128]{2,1,0:T(8,128)(2,1)S(1)}, bf16[8,128,576]{2,1,0:T(8,128)(2,1)S(1)}, f32[72,128]{1,0:T(8,128)S(1)}) custom-call(bf16[72,8192]{1,0:T(8,128)(2,1)S(1)} %copy-done, bf16[72,8192]{1,0:T(8,128)(2,1)S(1)} %copy-done.1, f32[72,128]{1,0:T(8,128)S(1)} %copy-done.4, ...), custom_call_target="tpu_custom_call" | custom-call | flops 8071000064 | bytes 25830000 | tf_op jit(solution)/shard_map/prepare_queries/pallas_call | solution.py:255
  23.4 2.2 %collective-permute-start.4 = (bf16[72,1024]{1,0:T(8,128)(2,1)S(1)}, bf16[72,1024]{1,0:T(8,128)(2,1)S(1)}, u32[]{:S(2)}, u32[]{:S(2)}) collective-permute-start(bf16[72,1024]{1,0:T(8,128)(2,1)S(1)} %copy-done.2), channel_id=1, source_target_pairs={{0,8},{4,12},{8,0},{12,4},{16,24},{20,28},{1,9},{5,13},{9,1},{13,5... | collective-permute-start | bytes 442376 | tf_op jit(solution)/shard_map/ppermute | solution.py:227
  25.7 2.5 %collective-permute-start.10 = (bf16[72,1024]{1,0:T(8,128)(2,1)S(1)}, bf16[72,1024]{1,0:T(8,128)(2,1)S(1)}, u32[]{:S(2)}, u32[]{:S(2)}) collective-permute-start(bf16[72,1024]{1,0:T(8,128)(2,1)S(1)} %collective-permute-done.refs_2_), channel_id=1, source_target_pairs={{0,4},{4,0},{8,12},{12,8},{24,28},{28,24},{1,5},{5,1},{9,13},{13,9... | collective-permute-start | bytes 442376 | tf_op jit(solution)/shard_map/ppermute | solution.py:227
  28.2 1.3 %collective-permute-start.11 = (bf16[72,1024]{1,0:T(8,128)(2,1)S(1)}, bf16[72,1024]{1,0:T(8,128)(2,1)S(1)}, u32[]{:S(2)}, u32[]{:S(2)}) collective-permute-start(bf16[72,1024]{1,0:T(8,128)(2,1)S(1)} %collective-permute-done.9.refs_1_), channel_id=1, source_target_pairs={{0,16},{4,20},{8,24},{12,28},{1,17},{5,21},{9,25},{13,29},{2,18},{... | collective-permute-start | bytes 442376 | tf_op jit(solution)/shard_map/ppermute | solution.py:235
  29.5 3.3 %collective-permute-start.3 = (bf16[72,1024]{1,0:T(8,128)(2,1)S(1)}, bf16[72,1024]{1,0:T(8,128)(2,1)S(1)}, u32[]{:S(2)}, u32[]{:S(2)}) collective-permute-start(bf16[72,1024]{1,0:T(8,128)(2,1)S(1)} %copy-done.2), channel_id=1, source_target_pairs={{0,4},{4,0},{8,12},{12,8},{16,20},{24,28},{1,5},{5,1},{9,13},{13,9... | collective-permute-start | bytes 442376 | tf_op jit(solution)/shard_map/ppermute | solution.py:227
  33.3 2.1 %collective-permute-start.5 = (bf16[72,1024]{1,0:T(8,128)(2,1)S(1)}, bf16[72,1024]{1,0:T(8,128)(2,1)S(1)}, u32[]{:S(2)}, u32[]{:S(2)}) collective-permute-start(bf16[72,1024]{1,0:T(8,128)(2,1)S(1)} %collective-permute-done.4.refs_2_), channel_id=1, source_target_pairs={{0,4},{4,0},{8,12},{12,8},{24,28},{28,24},{1,5},{5,1},{9,13},{13,9... | collective-permute-start | bytes 442376 | tf_op jit(solution)/shard_map/ppermute | solution.py:227
  35.4 1.3 %collective-permute-start.12 = (bf16[72,1024]{1,0:T(8,128)(2,1)S(1)}, bf16[72,1024]{1,0:T(8,128)(2,1)S(1)}, u32[]{:S(2)}, u32[]{:S(2)}) collective-permute-start(bf16[72,1024]{1,0:T(8,128)(2,1)S(1)} %collective-permute-done.refs_2_), channel_id=1, source_target_pairs={{0,16},{4,20},{8,24},{12,28},{1,17},{5,21},{9,25},{13,29},{2,18},{... | collective-permute-start | bytes 442376 | tf_op jit(solution)/shard_map/ppermute | solution.py:235
  36.7 1.3 %collective-permute-start.13 = (bf16[72,1024]{1,0:T(8,128)(2,1)S(1)}, bf16[72,1024]{1,0:T(8,128)(2,1)S(1)}, u32[]{:S(2)}, u32[]{:S(2)}) collective-permute-start(bf16[72,1024]{1,0:T(8,128)(2,1)S(1)} %collective-permute-done.10.refs_3_), channel_id=1, source_target_pairs={{0,16},{4,20},{8,24},{12,28},{1,17},{5,21},{9,25},{13,29},{2,18},{... | collective-permute-start | bytes 442376 | tf_op jit(solution)/shard_map/ppermute | solution.py:235
  38.0 1.3 %collective-permute-start.7 = (bf16[72,1024]{1,0:T(8,128)(2,1)S(1)}, bf16[72,1024]{1,0:T(8,128)(2,1)S(1)}, u32[]{:S(2)}, u32[]{:S(2)}) collective-permute-start(bf16[72,1024]{1,0:T(8,128)(2,1)S(1)} %collective-permute-done.4.refs_2_), channel_id=1, source_target_pairs={{0,16},{4,20},{8,24},{12,28},{1,17},{5,21},{9,25},{13,29},{2,18},{... | collective-permute-start | bytes 442376 | tf_op jit(solution)/shard_map/ppermute | solution.py:235
  39.4 1.3 %collective-permute-start.6 = (bf16[72,1024]{1,0:T(8,128)(2,1)S(1)}, bf16[72,1024]{1,0:T(8,128)(2,1)S(1)}, u32[]{:S(2)}, u32[]{:S(2)}) collective-permute-start(bf16[72,1024]{1,0:T(8,128)(2,1)S(1)} %collective-permute-done.3.refs_1_), channel_id=1, source_target_pairs={{0,16},{4,20},{8,24},{12,28},{1,17},{5,21},{9,25},{13,29},{2,18},{... | collective-permute-start | bytes 442376 | tf_op jit(solution)/shard_map/ppermute | solution.py:235
  41.4 1.3 %collective-permute-start.8 = (bf16[72,1024]{1,0:T(8,128)(2,1)S(1)}, bf16[72,1024]{1,0:T(8,128)(2,1)S(1)}, u32[]{:S(2)}, u32[]{:S(2)}) collective-permute-start(bf16[72,1024]{1,0:T(8,128)(2,1)S(1)} %collective-permute-done.5.refs_3_), channel_id=1, source_target_pairs={{0,16},{4,20},{8,24},{12,28},{1,17},{5,21},{9,25},{13,29},{2,18},{... | collective-permute-start | bytes 442376 | tf_op jit(solution)/shard_map/ppermute | solution.py:235
  42.7 1.4 %collective-permute-done.13.refs_7_ = bf16[72,1024]{1,0:T(8,128)(2,1)S(1)} collective-permute-done((bf16[72,1024]{1,0:T(8,128)(2,1)S(1)}, bf16[72,1024]{1,0:T(8,128)(2,1)S(1)}, u32[]{:S(2)}, u32[]{:S(2)}) %collective-permute-start.13) | collective-permute-done | bytes 147488 | tf_op jit(solution)/shard_map/ppermute | solution.py:235
  44.1 8.5 %attend.2 = (bf16[72,8192]{1,0:T(8,128)(2,1)}, bf16[72,8192]{1,0:T(8,128)(2,1)}, bf16[4,72,1024]{2,1,0:T(8,128)(2,1)S(1)}, bf16[4,72,1024]{2,1,0:T(8,128)(2,1)S(1)}) custom-call(s32[2]{0:T(128)S(1)} %copy-done.8, bf16[72,1024]{1,0:T(8,128)(2,1)S(1)} %copy-done.3, bf16[72,1024]{1,0:T(8,128)(2,1)S(1)} %collective-permute-done.9.refs_1_, ...), custom_call_target="tpu_custom_call" | custom-call | flops 11530000384 | bytes 36900000 | tf_op jit(solution)/shard_map/attend/pallas_call | solution.py:295
  52.6 1.3 %collective-permute-start.14 = (bf16[4,72,1024]{2,1,0:T(8,128)(2,1)S(1)}, bf16[4,72,1024]{2,1,0:T(8,128)(2,1)S(1)}, u32[]{:S(2)}, u32[]{:S(2)}) collective-permute-start(bf16[4,72,1024]{2,1,0:T(8,128)(2,1)S(1)} %get-tuple-element.57), channel_id=1, source_target_pairs={{16,0},{20,4},{24,8},{28,12},{17,1},{21,5},{25,9},{29,13},{18,2},{... | collective-permute-start | bytes 1769480 | tf_op jit(solution)/shard_map/ppermute | solution.py:235
  53.9 8.5 %attend.3 = (bf16[72,8192]{1,0:T(8,128)(2,1)}, bf16[72,8192]{1,0:T(8,128)(2,1)}, bf16[4,72,1024]{2,1,0:T(8,128)(2,1)S(1)}, bf16[4,72,1024]{2,1,0:T(8,128)(2,1)S(1)}) custom-call(s32[2]{0:T(128)S(1)} %copy-done.8, bf16[72,1024]{1,0:T(8,128)(2,1)S(1)} %copy-done.2, ...), custom_call_target="tpu_custom_call", output_to_operand_aliasing={{0}: (15, {}), {1}: (16, {})} | custom-call | flops 11530000384 | bytes 36900000 | tf_op jit(solution)/shard_map/attend/pallas_call | solution.py:295
  62.4 1.3 %collective-permute-start.18 = (bf16[4,72,1024]{2,1,0:T(8,128)(2,1)S(1)}, bf16[4,72,1024]{2,1,0:T(8,128)(2,1)S(1)}, u32[]{:S(2)}, u32[]{:S(2)}) collective-permute-start(bf16[4,72,1024]{2,1,0:T(8,128)(2,1)S(1)} %get-tuple-element.63), channel_id=1, source_target_pairs={{16,0},{20,4},{24,8},{28,12},{17,1},{21,5},{25,9},{29,13},{18,2},{... | collective-permute-start | bytes 1769480 | tf_op jit(solution)/shard_map/ppermute | solution.py:235
  63.7 7.0 %collective-permute-done.14.refs_1_ = bf16[4,72,1024]{2,1,0:T(8,128)(2,1)S(1)} collective-permute-done((bf16[4,72,1024]{2,1,0:T(8,128)(2,1)S(1)}, bf16[4,72,1024]{2,1,0:T(8,128)(2,1)S(1)}, u32[]{:S(2)}, u32[]{:S(2)}) %collective-permute-start.14) | collective-permute-done | bytes 589856 | tf_op jit(solution)/shard_map/ppermute | solution.py:235
  70.8 3.7 %collective-permute-start.15 = (bf16[72,1024]{1,0:T(8,128)(2,1)S(1)}, bf16[72,1024]{1,0:T(8,128)(2,1)S(1)}, u32[]{:S(2)}, u32[]{:S(2)}) collective-permute-start(bf16[72,1024]{1,0:T(8,128)(2,1)S(1)} %get-tuple-element.59), channel_id=1, source_target_pairs={{0,4},{4,0},{8,12},{12,8},{20,16},{28,24},{1,5},{5,1},{9,13},{13,9... | collective-permute-start | bytes 442376 | tf_op jit(solution)/shard_map/ppermute | solution.py:227
  74.5 1.9 %collective-permute-start.16 = (bf16[72,1024]{1,0:T(8,128)(2,1)S(1)}, bf16[72,1024]{1,0:T(8,128)(2,1)S(1)}, u32[]{:S(2)}, u32[]{:S(2)}) collective-permute-start(bf16[72,1024]{1,0:T(8,128)(2,1)S(1)} %get-tuple-element.60), channel_id=1, source_target_pairs={{0,8},{4,12},{8,0},{12,4},{24,16},{28,20},{1,9},{5,13},{9,1},{13,5... | collective-permute-start | bytes 442376 | tf_op jit(solution)/shard_map/ppermute | solution.py:227
  76.4 4.5 %collective-permute-start.17 = (bf16[72,1024]{1,0:T(8,128)(2,1)S(1)}, bf16[72,1024]{1,0:T(8,128)(2,1)S(1)}, u32[]{:S(2)}, u32[]{:S(2)}) collective-permute-start(bf16[72,1024]{1,0:T(8,128)(2,1)S(1)} %get-tuple-element.61), channel_id=1, source_target_pairs={{0,12},{4,8},{8,4},{12,0},{24,20},{28,16},{1,13},{5,9},{9,5},{13,1... | collective-permute-start | bytes 442376 | tf_op jit(solution)/shard_map/ppermute | solution.py:227
  81.1 3.3 %collective-permute-start.19 = (bf16[72,1024]{1,0:T(8,128)(2,1)S(1)}, bf16[72,1024]{1,0:T(8,128)(2,1)S(1)}, u32[]{:S(2)}, u32[]{:S(2)}) collective-permute-start(bf16[72,1024]{1,0:T(8,128)(2,1)S(1)} %get-tuple-element.65), channel_id=1, source_target_pairs={{0,4},{4,0},{8,12},{12,8},{20,16},{28,24},{1,5},{5,1},{9,13},{13,9... | collective-permute-start | bytes 442376 | tf_op jit(solution)/shard_map/ppermute | solution.py:227
  84.4 2.3 %collective-permute-start.20 = (bf16[72,1024]{1,0:T(8,128)(2,1)S(1)}, bf16[72,1024]{1,0:T(8,128)(2,1)S(1)}, u32[]{:S(2)}, u32[]{:S(2)}) collective-permute-start(bf16[72,1024]{1,0:T(8,128)(2,1)S(1)} %get-tuple-element.66), channel_id=1, source_target_pairs={{0,8},{4,12},{8,0},{12,4},{24,16},{28,20},{1,9},{5,13},{9,1},{13,5... | collective-permute-start | bytes 442376 | tf_op jit(solution)/shard_map/ppermute | solution.py:227
  86.7 4.5 %collective-permute-start.21 = (bf16[72,1024]{1,0:T(8,128)(2,1)S(1)}, bf16[72,1024]{1,0:T(8,128)(2,1)S(1)}, u32[]{:S(2)}, u32[]{:S(2)}) collective-permute-start(bf16[72,1024]{1,0:T(8,128)(2,1)S(1)} %get-tuple-element.67), channel_id=1, source_target_pairs={{0,12},{4,8},{8,4},{12,0},{24,20},{28,16},{1,13},{5,9},{9,5},{13,1... | collective-permute-start | bytes 442376 | tf_op jit(solution)/shard_map/ppermute | solution.py:227
  91.3 6.4 %collective-permute-done.20.refs_8_ = bf16[72,1024]{1,0:T(8,128)(2,1)S(1)} collective-permute-done((bf16[72,1024]{1,0:T(8,128)(2,1)S(1)}, bf16[72,1024]{1,0:T(8,128)(2,1)S(1)}, u32[]{:S(2)}, u32[]{:S(2)}) %collective-permute-start.20) | collective-permute-done | bytes 147488 | tf_op jit(solution)/shard_map/ppermute | solution.py:227
  97.7 0.9 finish.1
  (37 shorter events, 3.1 us)
Async XLA Ops:
  2.6 25.6 %collective-permute-start.9 = (bf16[72,1024]{1,0:T(8,128)(2,1)}, bf16[72,1024]{1,0:T(8,128)(2,1)S(1)}, u32[]{:S(2)}, u32[]{:S(2)}) collective-permute-start(bf16[72,1024]{1,0:T(8,128)(2,1)} %get-tuple-element.38.refs_0_), channel_id=1, source_target_pairs={{0,4},{4,0},{8,12},{12,8},{16,20},{24,28},{1,5},{5,1},{9,13},{13,9... | collective-permute-start | bytes 442376 | tf_op jit(solution)/shard_map/ppermute | solution.py:227
  7.5 15.9 %collective-permute-start.1 = (bf16[72,1024]{1,0:T(8,128)(2,1)}, bf16[72,1024]{1,0:T(8,128)(2,1)S(1)}, u32[]{:S(2)}, u32[]{:S(2)}) collective-permute-start(bf16[72,1024]{1,0:T(8,128)(2,1)} %get-tuple-element.38.refs_0_), channel_id=1, source_target_pairs={{0,16},{4,20},{8,24},{12,28},{1,17},{5,21},{9,25},{13,29},{2,18},{... | collective-permute-start | bytes 442376 | tf_op jit(solution)/shard_map/ppermute | solution.py:235
  11.0 12.5 %collective-permute-start = (bf16[72,1024]{1,0:T(8,128)(2,1)}, bf16[72,1024]{1,0:T(8,128)(2,1)S(1)}, u32[]{:S(2)}, u32[]{:S(2)}) collective-permute-start(bf16[72,1024]{1,0:T(8,128)(2,1)} %get-tuple-element.38.refs_0_), channel_id=1, source_target_pairs={{0,8},{4,12},{8,0},{12,4},{16,24},{20,28},{1,9},{5,13},{9,1},{13,5... | collective-permute-start | bytes 442376 | tf_op jit(solution)/shard_map/ppermute | solution.py:227
  15.5 7.9 %collective-permute-start.2 = (bf16[72,1024]{1,0:T(8,128)(2,1)}, bf16[72,1024]{1,0:T(8,128)(2,1)S(1)}, u32[]{:S(2)}, u32[]{:S(2)}) collective-permute-start(bf16[72,1024]{1,0:T(8,128)(2,1)} %get-tuple-element.43.refs_0_), channel_id=1, source_target_pairs={{0,16},{4,20},{8,24},{12,28},{1,17},{5,21},{9,25},{13,29},{2,18},{... | collective-permute-start | bytes 442376 | tf_op jit(solution)/shard_map/ppermute | solution.py:235
  16.8 1.3 %copy-start = (bf16[72,8192]{1,0:T(8,128)(2,1)S(1)}, bf16[72,8192]{1,0:T(8,128)(2,1)}, u32[]{:S(2)}) copy-start(bf16[72,8192]{1,0:T(8,128)(2,1)} %query_ref.1) | copy-start | bytes 3538948
  18.0 1.3 %copy-start.1 = (bf16[72,8192]{1,0:T(8,128)(2,1)S(1)}, bf16[72,8192]{1,0:T(8,128)(2,1)}, u32[]{:S(2)}) copy-start(bf16[72,8192]{1,0:T(8,128)(2,1)} %grad_ref.1) | copy-start | bytes 3538948
  19.3 0.8 copy-start.4
  20.1 0.8 copy-start.6
  20.8 2.6 %copy-start.2 = (bf16[72,1024]{1,0:T(8,128)(2,1)S(1)}, bf16[72,1024]{1,0:T(8,128)(2,1)}, u32[]{:S(2)}) copy-start(bf16[72,1024]{1,0:T(8,128)(2,1)} %get-tuple-element.43.refs_0_) | copy-start | bytes 442372
  20.8 23.2 %copy-start.3 = (bf16[72,1024]{1,0:T(8,128)(2,1)S(1)}, bf16[72,1024]{1,0:T(8,128)(2,1)}, u32[]{:S(2)}) copy-start(bf16[72,1024]{1,0:T(8,128)(2,1)} %get-tuple-element.38.refs_0_) | copy-start | bytes 442372
  20.8 23.2 %copy-start.7 = (f32[72,128]{1,0:T(8,128)S(1)}, f32[72,128]{1,0:T(8,128)}, u32[]{:S(2)}) copy-start(f32[72,128]{1,0:T(8,128)} %get-tuple-element.40.sin_ref.refs_13_.refs_1_) | copy-start | bytes 110596
  20.9 23.2 %copy-start.8 = (s32[2]{0:T(128)S(1)}, s32[2]{0:T(128)}, u32[]{:S(2)}) copy-start(s32[2]{0:T(128)} %counts_ref.3) | copy-start | bytes 28
  23.4 9.9 %collective-permute-start.4 = (bf16[72,1024]{1,0:T(8,128)(2,1)S(1)}, bf16[72,1024]{1,0:T(8,128)(2,1)S(1)}, u32[]{:S(2)}, u32[]{:S(2)}) collective-permute-start(bf16[72,1024]{1,0:T(8,128)(2,1)S(1)} %copy-done.2), channel_id=1, source_target_pairs={{0,8},{4,12},{8,0},{12,4},{16,24},{20,28},{1,9},{5,13},{9,1},{13,5... | collective-permute-start | bytes 442376 | tf_op jit(solution)/shard_map/ppermute | solution.py:227
  25.7 11.0 %collective-permute-start.10 = (bf16[72,1024]{1,0:T(8,128)(2,1)S(1)}, bf16[72,1024]{1,0:T(8,128)(2,1)S(1)}, u32[]{:S(2)}, u32[]{:S(2)}) collective-permute-start(bf16[72,1024]{1,0:T(8,128)(2,1)S(1)} %collective-permute-done.refs_2_), channel_id=1, source_target_pairs={{0,4},{4,0},{8,12},{12,8},{24,28},{28,24},{1,5},{5,1},{9,13},{13,9... | collective-permute-start | bytes 442376 | tf_op jit(solution)/shard_map/ppermute | solution.py:227
  28.2 9.8 %collective-permute-start.11 = (bf16[72,1024]{1,0:T(8,128)(2,1)S(1)}, bf16[72,1024]{1,0:T(8,128)(2,1)S(1)}, u32[]{:S(2)}, u32[]{:S(2)}) collective-permute-start(bf16[72,1024]{1,0:T(8,128)(2,1)S(1)} %collective-permute-done.9.refs_1_), channel_id=1, source_target_pairs={{0,16},{4,20},{8,24},{12,28},{1,17},{5,21},{9,25},{13,29},{2,18},{... | collective-permute-start | bytes 442376 | tf_op jit(solution)/shard_map/ppermute | solution.py:235
  29.5 9.8 %collective-permute-start.3 = (bf16[72,1024]{1,0:T(8,128)(2,1)S(1)}, bf16[72,1024]{1,0:T(8,128)(2,1)S(1)}, u32[]{:S(2)}, u32[]{:S(2)}) collective-permute-start(bf16[72,1024]{1,0:T(8,128)(2,1)S(1)} %copy-done.2), channel_id=1, source_target_pairs={{0,4},{4,0},{8,12},{12,8},{16,20},{24,28},{1,5},{5,1},{9,13},{13,9... | collective-permute-start | bytes 442376 | tf_op jit(solution)/shard_map/ppermute | solution.py:227
  33.3 8.1 %collective-permute-start.5 = (bf16[72,1024]{1,0:T(8,128)(2,1)S(1)}, bf16[72,1024]{1,0:T(8,128)(2,1)S(1)}, u32[]{:S(2)}, u32[]{:S(2)}) collective-permute-start(bf16[72,1024]{1,0:T(8,128)(2,1)S(1)} %collective-permute-done.4.refs_2_), channel_id=1, source_target_pairs={{0,4},{4,0},{8,12},{12,8},{24,28},{28,24},{1,5},{5,1},{9,13},{13,9... | collective-permute-start | bytes 442376 | tf_op jit(solution)/shard_map/ppermute | solution.py:227
  35.4 7.3 %collective-permute-start.12 = (bf16[72,1024]{1,0:T(8,128)(2,1)S(1)}, bf16[72,1024]{1,0:T(8,128)(2,1)S(1)}, u32[]{:S(2)}, u32[]{:S(2)}) collective-permute-start(bf16[72,1024]{1,0:T(8,128)(2,1)S(1)} %collective-permute-done.refs_2_), channel_id=1, source_target_pairs={{0,16},{4,20},{8,24},{12,28},{1,17},{5,21},{9,25},{13,29},{2,18},{... | collective-permute-start | bytes 442376 | tf_op jit(solution)/shard_map/ppermute | solution.py:235
  36.7 7.3 %collective-permute-start.13 = (bf16[72,1024]{1,0:T(8,128)(2,1)S(1)}, bf16[72,1024]{1,0:T(8,128)(2,1)S(1)}, u32[]{:S(2)}, u32[]{:S(2)}) collective-permute-start(bf16[72,1024]{1,0:T(8,128)(2,1)S(1)} %collective-permute-done.10.refs_3_), channel_id=1, source_target_pairs={{0,16},{4,20},{8,24},{12,28},{1,17},{5,21},{9,25},{13,29},{2,18},{... | collective-permute-start | bytes 442376 | tf_op jit(solution)/shard_map/ppermute | solution.py:235
  38.0 15.8 %collective-permute-start.7 = (bf16[72,1024]{1,0:T(8,128)(2,1)S(1)}, bf16[72,1024]{1,0:T(8,128)(2,1)S(1)}, u32[]{:S(2)}, u32[]{:S(2)}) collective-permute-start(bf16[72,1024]{1,0:T(8,128)(2,1)S(1)} %collective-permute-done.4.refs_2_), channel_id=1, source_target_pairs={{0,16},{4,20},{8,24},{12,28},{1,17},{5,21},{9,25},{13,29},{2,18},{... | collective-permute-start | bytes 442376 | tf_op jit(solution)/shard_map/ppermute | solution.py:235
  39.4 14.5 %collective-permute-start.6 = (bf16[72,1024]{1,0:T(8,128)(2,1)S(1)}, bf16[72,1024]{1,0:T(8,128)(2,1)S(1)}, u32[]{:S(2)}, u32[]{:S(2)}) collective-permute-start(bf16[72,1024]{1,0:T(8,128)(2,1)S(1)} %collective-permute-done.3.refs_1_), channel_id=1, source_target_pairs={{0,16},{4,20},{8,24},{12,28},{1,17},{5,21},{9,25},{13,29},{2,18},{... | collective-permute-start | bytes 442376 | tf_op jit(solution)/shard_map/ppermute | solution.py:235
  41.4 12.5 %collective-permute-start.8 = (bf16[72,1024]{1,0:T(8,128)(2,1)S(1)}, bf16[72,1024]{1,0:T(8,128)(2,1)S(1)}, u32[]{:S(2)}, u32[]{:S(2)}) collective-permute-start(bf16[72,1024]{1,0:T(8,128)(2,1)S(1)} %collective-permute-done.5.refs_3_), channel_id=1, source_target_pairs={{0,16},{4,20},{8,24},{12,28},{1,17},{5,21},{9,25},{13,29},{2,18},{... | collective-permute-start | bytes 442376 | tf_op jit(solution)/shard_map/ppermute | solution.py:235
  52.6 18.1 %collective-permute-start.14 = (bf16[4,72,1024]{2,1,0:T(8,128)(2,1)S(1)}, bf16[4,72,1024]{2,1,0:T(8,128)(2,1)S(1)}, u32[]{:S(2)}, u32[]{:S(2)}) collective-permute-start(bf16[4,72,1024]{2,1,0:T(8,128)(2,1)S(1)} %get-tuple-element.57), channel_id=1, source_target_pairs={{16,0},{20,4},{24,8},{28,12},{17,1},{21,5},{25,9},{29,13},{18,2},{... | collective-permute-start | bytes 1769480 | tf_op jit(solution)/shard_map/ppermute | solution.py:235
  62.4 18.6 %collective-permute-start.18 = (bf16[4,72,1024]{2,1,0:T(8,128)(2,1)S(1)}, bf16[4,72,1024]{2,1,0:T(8,128)(2,1)S(1)}, u32[]{:S(2)}, u32[]{:S(2)}) collective-permute-start(bf16[4,72,1024]{2,1,0:T(8,128)(2,1)S(1)} %get-tuple-element.63), channel_id=1, source_target_pairs={{16,0},{20,4},{24,8},{28,12},{17,1},{21,5},{25,9},{29,13},{18,2},{... | collective-permute-start | bytes 1769480 | tf_op jit(solution)/shard_map/ppermute | solution.py:235
  70.8 15.9 %collective-permute-start.15 = (bf16[72,1024]{1,0:T(8,128)(2,1)S(1)}, bf16[72,1024]{1,0:T(8,128)(2,1)S(1)}, u32[]{:S(2)}, u32[]{:S(2)}) collective-permute-start(bf16[72,1024]{1,0:T(8,128)(2,1)S(1)} %get-tuple-element.59), channel_id=1, source_target_pairs={{0,4},{4,0},{8,12},{12,8},{20,16},{28,24},{1,5},{5,1},{9,13},{13,9... | collective-permute-start | bytes 442376 | tf_op jit(solution)/shard_map/ppermute | solution.py:227
  74.5 16.8 %collective-permute-start.16 = (bf16[72,1024]{1,0:T(8,128)(2,1)S(1)}, bf16[72,1024]{1,0:T(8,128)(2,1)S(1)}, u32[]{:S(2)}, u32[]{:S(2)}) collective-permute-start(bf16[72,1024]{1,0:T(8,128)(2,1)S(1)} %get-tuple-element.60), channel_id=1, source_target_pairs={{0,8},{4,12},{8,0},{12,4},{24,16},{28,20},{1,9},{5,13},{9,1},{13,5... | collective-permute-start | bytes 442376 | tf_op jit(solution)/shard_map/ppermute | solution.py:227
  76.4 14.9 %collective-permute-start.17 = (bf16[72,1024]{1,0:T(8,128)(2,1)S(1)}, bf16[72,1024]{1,0:T(8,128)(2,1)S(1)}, u32[]{:S(2)}, u32[]{:S(2)}) collective-permute-start(bf16[72,1024]{1,0:T(8,128)(2,1)S(1)} %get-tuple-element.61), channel_id=1, source_target_pairs={{0,12},{4,8},{8,4},{12,0},{24,20},{28,16},{1,13},{5,9},{9,5},{13,1... | collective-permute-start | bytes 442376 | tf_op jit(solution)/shard_map/ppermute | solution.py:227
  81.0 16.8 %copy-start.5 = (f32[72,128]{1,0:T(8,128)S(1)}, f32[72,128]{1,0:T(8,128)}, u32[]{:S(2)}) copy-start(f32[72,128]{1,0:T(8,128)} %get-tuple-element.39.cos_ref.refs_0_) | copy-start | bytes 110596
  81.1 10.2 %collective-permute-start.19 = (bf16[72,1024]{1,0:T(8,128)(2,1)S(1)}, bf16[72,1024]{1,0:T(8,128)(2,1)S(1)}, u32[]{:S(2)}, u32[]{:S(2)}) collective-permute-start(bf16[72,1024]{1,0:T(8,128)(2,1)S(1)} %get-tuple-element.65), channel_id=1, source_target_pairs={{0,4},{4,0},{8,12},{12,8},{20,16},{28,24},{1,5},{5,1},{9,13},{13,9... | collective-permute-start | bytes 442376 | tf_op jit(solution)/shard_map/ppermute | solution.py:227
  84.4 13.3 %collective-permute-start.20 = (bf16[72,1024]{1,0:T(8,128)(2,1)S(1)}, bf16[72,1024]{1,0:T(8,128)(2,1)S(1)}, u32[]{:S(2)}, u32[]{:S(2)}) collective-permute-start(bf16[72,1024]{1,0:T(8,128)(2,1)S(1)} %get-tuple-element.66), channel_id=1, source_target_pairs={{0,8},{4,12},{8,0},{12,4},{24,16},{28,20},{1,9},{5,13},{9,1},{13,5... | collective-permute-start | bytes 442376 | tf_op jit(solution)/shard_map/ppermute | solution.py:227
  86.7 11.0 %collective-permute-start.21 = (bf16[72,1024]{1,0:T(8,128)(2,1)S(1)}, bf16[72,1024]{1,0:T(8,128)(2,1)S(1)}, u32[]{:S(2)}, u32[]{:S(2)}) collective-permute-start(bf16[72,1024]{1,0:T(8,128)(2,1)S(1)} %get-tuple-element.67), channel_id=1, source_target_pairs={{0,12},{4,8},{8,4},{12,0},{24,20},{28,16},{1,13},{5,9},{9,5},{13,1... | collective-permute-start | bytes 442376 | tf_op jit(solution)/shard_map/ppermute | solution.py:227

commit v2 on v1

--- a/solution.py
+++ b/solution.py
@@ -43,8 +43,7 @@
     return slice(index * HEAD_WIDTH, (index + 1) * HEAD_WIDTH)
 
 
-def prepare_keys(rows, pos_ref, key_ref, value_ref, *out_refs):
-    kv_refs, (cos_ref, sin_ref) = out_refs[:CHUNKS], out_refs[CHUNKS:]
+def prepare_keys(rows, pos_ref, key_ref, value_ref, kv_ref, cos_ref, sin_ref):
     padded = key_ref.shape[0]
     start = (lax.axis_index("seq") * lax.axis_size("head") + lax.axis_index("head")) * rows
     sublane = lax.broadcasted_iota(jnp.int32, (8, HEAD_WIDTH), 0)
@@ -62,9 +61,10 @@
     sin_ref[...] = sine
     for head in range(KEY_VALUE_HEADS):
         chunk, place = divmod(head, HEADS_PER_CHUNK)
+        place += 2 * chunk * HEADS_PER_CHUNK
         rotated = rope(key_ref[:, head_cols(head)].astype(jnp.float32), cosine, sine)
-        kv_refs[chunk][:, head_cols(place)] = rotated.astype(jnp.bfloat16)
-        kv_refs[chunk][:, head_cols(HEADS_PER_CHUNK + place)] = value_ref[:, head_cols(head)]
+        kv_ref[:, head_cols(place)] = rotated.astype(jnp.bfloat16)
+        kv_ref[:, head_cols(HEADS_PER_CHUNK + place)] = value_ref[:, head_cols(head)]
 
 
 def prepare_queries(query_ref, grad_ref, cos_ref, sin_ref, q_ref, qt_ref, g_ref, gt_ref, table_ref):
@@ -159,32 +159,27 @@
         part_refs[seq_offset][head_offset, :, far_cols] = value_part[piece].astype(jnp.bfloat16)
 
 
-def combine(seq_count, head_count, *refs):
-    part_refs, base_ref, send_refs = refs[:seq_count], refs[seq_count], refs[seq_count + 1 :]
-    for offset in range(head_count):
+def combine(*refs):
+    *part_refs, send_ref = refs
+    for offset in range(send_ref.shape[0]):
         total = part_refs[0][offset].astype(jnp.float32)
         for ref in part_refs[1:]:
             total = total + ref[offset].astype(jnp.float32)
-        if offset == 0:
-            base_ref[...] = total
-        else:
-            send_refs[offset - 1][...] = total.astype(jnp.bfloat16)
-
-
-def finish(head_count, *refs):
-    cosine, sine = refs[0][...], refs[1][...]
-    key_ref, value_ref = refs[-2:]
-    for chunk in range(CHUNKS):
-        mine = refs[2 + chunk * head_count : 2 + (chunk + 1) * head_count]
+        send_ref[jnp.bitwise_xor(lax.axis_index("head"), offset)] = total.astype(jnp.bfloat16)
+
+
+def finish(cos_ref, sin_ref, *refs):
+    cosine, sine = cos_ref[...], sin_ref[...]
+    *sum_refs, key_ref, value_ref = refs
+
+    def total(ref, place):
+        return sum(ref[z, :, head_cols(place)].astype(jnp.float32) for z in range(ref.shape[0]))
+
+    for chunk, ref in enumerate(sum_refs):
         for place in range(HEADS_PER_CHUNK):
-            here, there = head_cols(place), head_cols(HEADS_PER_CHUNK + place)
-            key_total, value_total = mine[0][:, here], mine[0][:, there]
-            for ref in mine[1:]:
-                key_total = key_total + ref[:, here].astype(jnp.float32)
-                value_total = value_total + ref[:, there].astype(jnp.float32)
             cols = head_cols(chunk * HEADS_PER_CHUNK + place)
-            key_ref[:, cols] = rope_back(key_total, cosine, sine).astype(jnp.bfloat16)
-            value_ref[:, cols] = value_total.astype(jnp.bfloat16)
+            key_ref[:, cols] = rope_back(total(ref, place), cosine, sine).astype(jnp.bfloat16)
+            value_ref[:, cols] = total(ref, HEADS_PER_CHUNK + place).astype(jnp.bfloat16)
 
 
 def params(mebibytes):
@@ -235,12 +230,11 @@
         return lax.ppermute(x, ("seq", "head"), pairs)
 
     table = shape((padded, HEAD_WIDTH), f32)
-    piece = shape((padded, 2 * CHUNK_COLS), bf16)
-    *own, cosine, sine = pl.pallas_call(
+    own, cosine, sine = pl.pallas_call(
         functools.partial(prepare_keys, rows),
-        out_shape=[piece] * CHUNKS + [table, table],
+        out_shape=[shape((padded, 2 * KEY_VALUE_HEADS * HEAD_WIDTH), bf16), table, table],
         in_specs=[SMEM, VMEM, VMEM],
-        out_specs=[VMEM] * (CHUNKS + 2),
+        out_specs=[VMEM] * 3,
         compiler_params=params(56),
         name="prepare_keys",
     )(positions, routed_keys, routed_values)
@@ -265,22 +259,30 @@
     )(queries, output_gradient, cosine, sine)
 
     bits = [1 << b for b in reversed(range((head_count - 1).bit_length()))]
-    far = [[[along_seq(x, a, True)] for a in range(1, seq_count)] for x in own]
+    later = range(1, seq_count)
+    whole = {0: own, **{bit: along_head(own, bit, True) for bit in {bits[0], 1}}}
+    far = {(a, 0): along_seq(own, a, True) for a in later}
+    whole[1], cosine_later, far = lax.optimization_barrier((whole[1], cosine_later, far))
+    far.update({(a, 1): along_seq(whole[1], a, True) for a in later})
+    chunked = [
+        {j: x[:, 2 * c * CHUNK_COLS : 2 * (c + 1) * CHUNK_COLS] for j, x in whole.items()}
+        for c in range(CHUNKS)
+    ]
     gathered = []
-    for chunk in range(CHUNKS):
-        near = {0: own[chunk]}
-        for bit in bits:
-            near.update({j ^ bit: along_head(x, bit, True, j) for j, x in near.items()})
-            if bit == bits[0] and chunk == 0:
-                near[bit], cosine_later, far = lax.optimization_barrier(
-                    (near[bit], cosine_later, far)
-                )
-            if bit == bits[0] and chunk + 1 < CHUNKS:
-                own[chunk + 1], near[bit] = lax.optimization_barrier((own[chunk + 1], near[bit]))
-        near = [near[j] for j in range(head_count)]
-        for a in range(1, seq_count):
-            far[chunk][a - 1] += [along_seq(x, a, True) for x in near[1:]]
-        gathered.append(near + [x for group in far[chunk] for x in group])
+    for c, near in enumerate(chunked):
+        for bit in bits[1:]:
+            near.update(
+                {j ^ bit: along_head(x, bit, True, j) for j, x in near.items() if j ^ bit not in near}
+            )
+        if c + 1 < CHUNKS:
+            chunked[c + 1][bits[0]], near[head_count - 1], far = lax.optimization_barrier(
+                (chunked[c + 1][bits[0]], near[head_count - 1], far)
+            )
+        blocks_here = [whole[0], whole[1]] + [near[j] for j in range(2, head_count)]
+        for a in later:
+            blocks_here += [far[a, 0], far[a, 1]]
+            blocks_here += [along_seq(near[j], a, True) for j in range(2, head_count)]
+        gathered.append(blocks_here)
 
     wide_outs = ()
     summed = []
@@ -290,7 +292,8 @@
         tall_part = pl.BlockSpec((1, query_rows, HEAD_WIDTH), lambda g, f=first: (f + g, 0, 0))
         flat_part = pl.BlockSpec((1, HEAD_WIDTH, query_rows), lambda g, f=first: (f + g, 0, 0))
         row_part = pl.BlockSpec((padded, wide), lambda g, f=first: (0, f + g))
-        kv_block = pl.BlockSpec((padded, 2 * CHUNK_COLS), lambda g: (0, 0))
+        kv_whole = pl.BlockSpec((padded, 2 * CHUNK_COLS), lambda g, c=chunk: (0, c))
+        kv_chunk = pl.BlockSpec((padded, 2 * CHUNK_COLS), lambda g: (0, 0))
         part_block = pl.BlockSpec((head_count, padded, 2 * CHUNK_COLS), lambda g: (0, 0, 0))
         out = pl.pallas_call(
             functools.partial(attend, seq_count, head_count, rows, has_alias),
@@ -298,7 +301,7 @@
             out_shape=[shape((padded, QUERY_HEADS * HEAD_WIDTH), bf16)] * 2
             + [shape((head_count, padded, 2 * CHUNK_COLS), bf16)] * seq_count,
             in_specs=[SMEM]
-            + [kv_block] * blocks
+            + ([kv_whole] * 2 + [kv_chunk] * (head_count - 2)) * seq_count
             + [tall_part, flat_part, tall_part, flat_part, table_block, table_block]
             + [pl.BlockSpec(memory_space=pl.ANY)] * (2 * has_alias),
             out_specs=[row_part, row_part] + [part_block] * seq_count,
@@ -313,22 +316,24 @@
         )(counts, *gathered[chunk], *stacked, cosine_later, sine, *wide_outs)
         wide_outs = out[:2]
         parts = [out[2]] + [along_seq(out[2 + a], a, False) for a in range(1, seq_count)]
-        base, *sends = pl.pallas_call(
-            functools.partial(combine, seq_count, head_count),
-            out_shape=[shape((padded, 2 * CHUNK_COLS), f32)] + [piece] * (head_count - 1),
+        if chunk:
+            parts[-1], sums = lax.optimization_barrier((parts[-1], sums))
+        sums = pl.pallas_call(
+            combine,
+            out_shape=shape((head_count, padded, 2 * CHUNK_COLS), bf16),
             in_specs=[VMEM] * seq_count,
-            out_specs=[VMEM] * head_count,
+            out_specs=VMEM,
             cost_estimate=cost(2),
             compiler_params=params(8),
             name="combine",
         )(*parts)
-        summed += [base] + [along_head(x, j + 1, False) for j, x in enumerate(sends)]
+        summed.append(lax.all_to_all(sums, "head", split_axis=0, concat_axis=0, tiled=True))
 
     narrow = shape((padded, KEY_VALUE_HEADS * HEAD_WIDTH), bf16)
     key_grad, value_grad = pl.pallas_call(
-        functools.partial(finish, head_count),
+        finish,
         out_shape=[narrow, narrow],
-        in_specs=[VMEM] * (2 + CHUNKS * head_count),
+        in_specs=[VMEM] * (2 + CHUNKS),
         out_specs=[VMEM, VMEM],
         cost_estimate=cost(2),
         compiler_params=params(8),

time: 99.5 us -> 113 us (1.14)
  starting transfers between devices: 54.9 us -> 31.3 us
  blocking collectives: 0 us -> 16.3 us
  waiting for transfers between devices: 16.1 us -> 30.8 us
  local copies, waits for them, and re-layouts: 4.09 us -> 9.29 us
    ppermute x12 -> x4, starting transfers between devices: 39.8 us -> 13.3 us  [along_head(): return lax.ppermute(x, ('seq', 'head'), pairs)]
    all_to_all x0 -> x1, blocking collectives: none -> 16.3 us  [shards(): lax.all_to_all(sums, 'head', split_axis=0, concat_axis=0, tiled=True)]
    ppermute x10 -> x8, waiting for transfers between devices: 8.41 us -> 20.2 us  [along_seq(): return lax.ppermute(x, ('seq', 'head'), pairs)]
    unnamed x18 -> x32, local copies, waits for them, and re-layouts: 4.09 us -> 9.27 us
    all_to_all x0 -> x1, starting transfers between devices: none -> 3.48 us  [shards(): lax.all_to_all(sums, 'head', split_axis=0, concat_axis=0, tiled=True)]
    ppermute x12 -> x4, waiting for transfers between devices: 7.66 us -> 10.5 us  [along_head(): return lax.ppermute(x, ('seq', 'head'), pairs)]
    ppermute x10 -> x8, starting transfers between devices: 15.1 us -> 14.5 us  [along_seq(): return lax.ppermute(x, ('seq', 'head'), pairs)]
  transfers between devices with their start and end apart: 22 -> 13, of which waited for: 5 -> 6; matrix products, arithmetic and copies ran while one was open for 0% -> 0% of each run, Pallas kernels for 20% -> 11%
where the time goes in v2:
time: 113 us; the launch traced here: 112 us
  starting transfers between devices  31.3 us (28%)
  waiting for transfers between devices  30.8 us (27%)
  Pallas kernels  23.5 us (21%)
  blocking collectives  16.3 us (14%)
  local copies, waits for them, and re-layouts  9.29 us (8%)
    ppermute x8, waiting for transfers between devices, along_seq(): return lax.ppermute(x, ('seq', 'head'), pairs)  20.2 us
    pallas_call x2, Pallas kernels, shards(): pl.pallas_call(functools.partial(attend, seq_count, head_count, rows, has...  17 us
    all_to_all x1, blocking collectives, shards(): lax.all_to_all(sums, 'head', split_axis=0, concat_axis=0, tiled=True)  16.3 us
    ppermute x8, starting transfers between devices, along_seq(): return lax.ppermute(x, ('seq', 'head'), pairs)  14.5 us
    ppermute x4, starting transfers between devices, along_head(): return lax.ppermute(x, ('seq', 'head'), pairs)  13.3 us
    ppermute x4, waiting for transfers between devices, along_head(): return lax.ppermute(x, ('seq', 'head'), pairs)  10.5 us
    unnamed x32, local copies, waits for them, and re-layouts  9.27 us
    all_to_all x1, starting transfers between devices, shards(): lax.all_to_all(sums, 'head', split_axis=0, concat_axis=0, tiled=True)  3.48 us
  transfers between devices with their start and end apart: 13, of which 6 were waited for; matrix products, arithmetic and copies ran while one was open for 0% of the time, Pallas kernels for 11%

profile of v2, /device:TPU:0, one launch (start us, length us, event | category | flops | bytes accessed | tf_op | source)
XLA Modules:
  0.0 112.0 jit_solution(13397140041930297679)
XLA Ops:
  0.6 2.0 %prepare_keys.1 = (bf16[72,2048]{1,0:T(8,128)(2,1)}, f32[72,128]{1,0:T(8,128)}, f32[72,128]{1,0:T(8,128)}) custom-call(s32[576]{0:T(1024)} %pos_ref.1, bf16[72,1024]{1,0:T(8,128)(2,1)} %key_ref.1, bf16[72,1024]{1,0:T(8,128)(2,1)} %value_ref.1), custom_call_target="tpu_custom_call" | custom-call | tf_op jit(solution)/shard_map/prepare_keys/pallas_call | solution.py:233
  2.6 4.9 %collective-permute-start = (bf16[72,2048]{1,0:T(8,128)(2,1)}, bf16[72,2048]{1,0:T(8,128)(2,1)S(1)}, u32[]{:S(2)}, u32[]{:S(2)}) collective-permute-start(bf16[72,2048]{1,0:T(8,128)(2,1)} %get-tuple-element.30.refs_0_), channel_id=1, source_target_pairs={{0,4},{4,0},{8,12},{12,8},{16,20},{24,28},{1,5},{5,1},{9,13},{13,9... | collective-permute-start | bytes 884744 | tf_op jit(solution)/shard_map/ppermute | solution.py:222
  7.5 3.5 %collective-permute-start.1 = (bf16[72,2048]{1,0:T(8,128)(2,1)}, bf16[72,2048]{1,0:T(8,128)(2,1)S(1)}, u32[]{:S(2)}, u32[]{:S(2)}) collective-permute-start(bf16[72,2048]{1,0:T(8,128)(2,1)} %get-tuple-element.30.refs_0_), channel_id=1, source_target_pairs={{0,16},{4,20},{8,24},{12,28},{1,17},{5,21},{9,25},{13,29},{2,18},{... | collective-permute-start | bytes 884744 | tf_op jit(solution)/shard_map/ppermute | solution.py:230
  11.0 4.5 %collective-permute-start.2 = (bf16[72,2048]{1,0:T(8,128)(2,1)}, bf16[72,2048]{1,0:T(8,128)(2,1)S(1)}, u32[]{:S(2)}, u32[]{:S(2)}) collective-permute-start(bf16[72,2048]{1,0:T(8,128)(2,1)} %get-tuple-element.30.refs_0_), channel_id=1, source_target_pairs={{0,8},{4,12},{8,0},{12,4},{16,24},{20,28},{1,9},{5,13},{9,1},{13,5... | collective-permute-start | bytes 884744 | tf_op jit(solution)/shard_map/ppermute | solution.py:222
  15.5 1.3 %copy-done = bf16[72,8192]{1,0:T(8,128)(2,1)S(1)} copy-done((bf16[72,8192]{1,0:T(8,128)(2,1)S(1)}, bf16[72,8192]{1,0:T(8,128)(2,1)}, u32[]{:S(2)}) %copy-start) | copy-done | bytes 1179672
  16.8 1.3 %copy-done.1 = bf16[72,8192]{1,0:T(8,128)(2,1)S(1)} copy-done((bf16[72,8192]{1,0:T(8,128)(2,1)S(1)}, bf16[72,8192]{1,0:T(8,128)(2,1)}, u32[]{:S(2)}) %copy-start.1) | copy-done | bytes 1179672
  19.6 2.5 %prepare_queries.1 = (bf16[8,576,128]{2,1,0:T(8,128)(2,1)S(1)}, bf16[8,128,576]{2,1,0:T(8,128)(2,1)S(1)}, bf16[8,576,128]{2,1,0:T(8,128)(2,1)S(1)}, bf16[8,128,576]{2,1,0:T(8,128)(2,1)S(1)}, f32[72,128]{1,0:T(8,128)S(1)}) custom-call(bf16[72,8192]{1,0:T(8,128)(2,1)S(1)} %copy-done, bf16[72,8192]{1,0:T(8,128)(2,1)S(1)} %copy-done.1, f32[72,128]{1,0:T(8,128)S(1)} %copy-done.3, ...), custom_call_target="tpu_custom_call" | custom-call | flops 8071000064 | bytes 25830000 | tf_op jit(solution)/shard_map/prepare_queries/pallas_call | solution.py:249
  22.2 1.3 %collective-permute-start.4 = (bf16[72,2048]{1,0:T(8,128)(2,1)S(1)}, bf16[72,2048]{1,0:T(8,128)(2,1)S(1)}, u32[]{:S(2)}, u32[]{:S(2)}) collective-permute-start(bf16[72,2048]{1,0:T(8,128)(2,1)S(1)} %collective-permute-done.refs_1_), channel_id=1, source_target_pairs={{0,16},{4,20},{8,24},{12,28},{1,17},{5,21},{9,25},{13,29},{2,18},{... | collective-permute-start | bytes 884744 | tf_op jit(solution)/shard_map/ppermute | solution.py:230
  23.5 5.0 %collective-permute-done.2 = bf16[72,2048]{1,0:T(8,128)(2,1)S(1)} collective-permute-done((bf16[72,2048]{1,0:T(8,128)(2,1)}, bf16[72,2048]{1,0:T(8,128)(2,1)S(1)}, u32[]{:S(2)}, u32[]{:S(2)}) %collective-permute-start.2) | collective-permute-done | bytes 294944 | tf_op jit(solution)/shard_map/ppermute | solution.py:222
  28.5 1.9 %collective-permute-start.3 = (bf16[72,1024]{1,0:T(8,128)(2,1)S(1)}, bf16[72,1024]{1,0:T(8,128)(2,1)S(1)}, u32[]{:S(2)}, u32[]{:S(2)}) collective-permute-start(bf16[72,1024]{1,0:T(8,128)(2,1)S(1)} %get-tuple-element.56.refs_2_), channel_id=1, source_target_pairs={{0,4},{4,0},{8,12},{12,8},{24,28},{28,24},{1,5},{5,1},{9,13},{13,9... | collective-permute-start | bytes 442376 | tf_op jit(solution)/shard_map/ppermute | solution.py:222
  30.4 1.3 %collective-permute-start.8 = (bf16[72,1024]{1,0:T(8,128)(2,1)S(1)}, bf16[72,1024]{1,0:T(8,128)(2,1)S(1)}, u32[]{:S(2)}, u32[]{:S(2)}) collective-permute-start(bf16[72,1024]{1,0:T(8,128)(2,1)S(1)} %get-tuple-element.56.refs_2_), channel_id=1, source_target_pairs={{0,16},{4,20},{8,24},{12,28},{1,17},{5,21},{9,25},{13,29},{2,18},{... | collective-permute-start | bytes 442376 | tf_op jit(solution)/shard_map/ppermute | solution.py:230
  31.7 3.8 %collective-permute-done.3.refs_3_ = bf16[72,1024]{1,0:T(8,128)(2,1)S(1)} collective-permute-done((bf16[72,1024]{1,0:T(8,128)(2,1)S(1)}, bf16[72,1024]{1,0:T(8,128)(2,1)S(1)}, u32[]{:S(2)}, u32[]{:S(2)}) %collective-permute-start.3) | collective-permute-done | bytes 147488 | tf_op jit(solution)/shard_map/ppermute | solution.py:222
  35.5 1.3 %collective-permute-start.9 = (bf16[72,1024]{1,0:T(8,128)(2,1)S(1)}, bf16[72,1024]{1,0:T(8,128)(2,1)S(1)}, u32[]{:S(2)}, u32[]{:S(2)}) collective-permute-start(bf16[72,1024]{1,0:T(8,128)(2,1)S(1)} %collective-permute-done.3.refs_3_), channel_id=1, source_target_pairs={{0,16},{4,20},{8,24},{12,28},{1,17},{5,21},{9,25},{13,29},{2,18},{... | collective-permute-start | bytes 442376 | tf_op jit(solution)/shard_map/ppermute | solution.py:230
  36.8 2.6 %collective-permute-done.9.refs_7_ = bf16[72,1024]{1,0:T(8,128)(2,1)S(1)} collective-permute-done((bf16[72,1024]{1,0:T(8,128)(2,1)S(1)}, bf16[72,1024]{1,0:T(8,128)(2,1)S(1)}, u32[]{:S(2)}, u32[]{:S(2)}) %collective-permute-start.9) | collective-permute-done | bytes 147488 | tf_op jit(solution)/shard_map/ppermute | solution.py:230
  39.5 8.5 %attend.2 = (bf16[72,8192]{1,0:T(8,128)(2,1)}, bf16[72,8192]{1,0:T(8,128)(2,1)}, bf16[4,72,1024]{2,1,0:T(8,128)(2,1)S(1)}, bf16[4,72,1024]{2,1,0:T(8,128)(2,1)S(1)}) custom-call(s32[2]{0:T(128)S(1)} %copy-done.7, bf16[72,2048]{1,0:T(8,128)(2,1)S(1)} %copy-done.2, bf16[72,2048]{1,0:T(8,128)(2,1)S(1)} %collective-permute-done.refs_1_, ...), custom_call_target="tpu_custom_call" | custom-call | flops 11530000384 | bytes 36900000 | tf_op jit(solution)/shard_map/attend/pallas_call | solution.py:298
  48.0 1.3 %collective-permute-start.10 = (bf16[4,72,1024]{2,1,0:T(8,128)(2,1)S(1)}, bf16[4,72,1024]{2,1,0:T(8,128)(2,1)S(1)}, u32[]{:S(2)}, u32[]{:S(2)}) collective-permute-start(bf16[4,72,1024]{2,1,0:T(8,128)(2,1)S(1)} %get-tuple-element.50), channel_id=1, source_target_pairs={{16,0},{20,4},{24,8},{28,12},{17,1},{21,5},{25,9},{29,13},{18,2},{... | collective-permute-start | bytes 1769480 | tf_op jit(solution)/shard_map/ppermute | solution.py:230
  49.3 2.0 %collective-permute-start.5 = (bf16[72,1024]{1,0:T(8,128)(2,1)S(1)}, bf16[72,1024]{1,0:T(8,128)(2,1)S(1)}, u32[]{:S(2)}, u32[]{:S(2)}) collective-permute-start(bf16[72,1024]{1,0:T(8,128)(2,1)S(1)} %get-tuple-element.36.refs_2_), channel_id=1, source_target_pairs={{0,4},{4,0},{8,12},{12,8},{24,28},{28,24},{1,5},{5,1},{9,13},{13,9... | collective-permute-start | bytes 442376 | tf_op jit(solution)/shard_map/ppermute | solution.py:222
  51.3 3.2 %collective-permute-start.6 = (bf16[72,1024]{1,0:T(8,128)(2,1)S(1)}, bf16[72,1024]{1,0:T(8,128)(2,1)S(1)}, u32[]{:S(2)}, u32[]{:S(2)}) collective-permute-start(bf16[72,1024]{1,0:T(8,128)(2,1)S(1)} %get-tuple-element.36.refs_2_), channel_id=1, source_target_pairs={{0,16},{4,20},{8,24},{12,28},{1,17},{5,21},{9,25},{13,29},{2,18},{... | collective-permute-start | bytes 442376 | tf_op jit(solution)/shard_map/ppermute | solution.py:230
  54.6 1.8 %collective-permute-done.5.refs_3_ = bf16[72,1024]{1,0:T(8,128)(2,1)S(1)} collective-permute-done((bf16[72,1024]{1,0:T(8,128)(2,1)S(1)}, bf16[72,1024]{1,0:T(8,128)(2,1)S(1)}, u32[]{:S(2)}, u32[]{:S(2)}) %collective-permute-start.5) | collective-permute-done | bytes 147488 | tf_op jit(solution)/shard_map/ppermute | solution.py:222
  56.3 1.3 %collective-permute-start.7 = (bf16[72,1024]{1,0:T(8,128)(2,1)S(1)}, bf16[72,1024]{1,0:T(8,128)(2,1)S(1)}, u32[]{:S(2)}, u32[]{:S(2)}) collective-permute-start(bf16[72,1024]{1,0:T(8,128)(2,1)S(1)} %collective-permute-done.5.refs_3_), channel_id=1, source_target_pairs={{0,16},{4,20},{8,24},{12,28},{1,17},{5,21},{9,25},{13,29},{2,18},{... | collective-permute-start | bytes 442376 | tf_op jit(solution)/shard_map/ppermute | solution.py:230
  57.6 5.0 %collective-permute-done.10.refs_1_ = bf16[4,72,1024]{2,1,0:T(8,128)(2,1)S(1)} collective-permute-done((bf16[4,72,1024]{2,1,0:T(8,128)(2,1)S(1)}, bf16[4,72,1024]{2,1,0:T(8,128)(2,1)S(1)}, u32[]{:S(2)}, u32[]{:S(2)}) %collective-permute-start.10) | collective-permute-done | bytes 589856 | tf_op jit(solution)/shard_map/ppermute | solution.py:230
  62.6 1.0 combine.2
  63.6 3.5 %all-to-all-start = ((bf16[4,72,1024]{2,1,0:T(8,128)(2,1)}), bf16[4,72,1024]{2,1,0:T(8,128)(2,1)S(1)}, u32[]{:S(2)}, u32[]{:S(2)}) async-start(bf16[4,72,1024]{2,1,0:T(8,128)(2,1)} %combine.2), calls=%async_computation | async-start | bytes 1179648 | tf_op jit(solution)/shard_map/all_to_all | solution.py:330
  67.1 1.3 %copy-done.9 = bf16[8,128,576]{2,1,0:T(8,128)(2,1)S(1)} copy-done((bf16[8,128,576]{2,1,0:T(8,128)(2,1)S(1)}, bf16[8,128,576]{2,1,0:T(8,128)(2,1)}, u32[]{:S(2)}) %copy-start.9) | copy-done | bytes 1179672
  68.4 1.3 %copy-done.11 = bf16[8,128,576]{2,1,0:T(8,128)(2,1)S(1)} copy-done((bf16[8,128,576]{2,1,0:T(8,128)(2,1)S(1)}, bf16[8,128,576]{2,1,0:T(8,128)(2,1)}, u32[]{:S(2)}) %copy-start.11) | copy-done | bytes 1179672
  69.7 1.3 %copy-done.13 = bf16[8,576,128]{2,1,0:T(8,128)(2,1)S(1)} copy-done((bf16[8,576,128]{2,1,0:T(8,128)(2,1)S(1)}, bf16[8,576,128]{2,1,0:T(8,128)(2,1)}, u32[]{:S(2)}) %copy-start.13) | copy-done | bytes 1179672
  71.0 1.3 %copy-done.15 = bf16[8,576,128]{2,1,0:T(8,128)(2,1)S(1)} copy-done((bf16[8,576,128]{2,1,0:T(8,128)(2,1)S(1)}, bf16[8,576,128]{2,1,0:T(8,128)(2,1)}, u32[]{:S(2)}) %copy-start.15) | copy-done | bytes 1179672
  72.2 8.5 %attend.3 = (bf16[72,8192]{1,0:T(8,128)(2,1)}, bf16[72,8192]{1,0:T(8,128)(2,1)}, bf16[4,72,1024]{2,1,0:T(8,128)(2,1)S(1)}, bf16[4,72,1024]{2,1,0:T(8,128)(2,1)S(1)}) custom-call(s32[2]{0:T(128)S(1)} %copy-done.7, bf16[72,2048]{1,0:T(8,128)(2,1)S(1)} %copy-done.2, ...), custom_call_target="tpu_custom_call", output_to_operand_aliasing={{0}: (15, {}), {1}: (16, {})} | custom-call | flops 11530000384 | bytes 36900000 | tf_op jit(solution)/shard_map/attend/pallas_call | solution.py:298
  80.7 1.3 %collective-permute-start.11 = (bf16[4,72,1024]{2,1,0:T(8,128)(2,1)S(1)}, bf16[4,72,1024]{2,1,0:T(8,128)(2,1)S(1)}, u32[]{:S(2)}, u32[]{:S(2)}) collective-permute-start(bf16[4,72,1024]{2,1,0:T(8,128)(2,1)S(1)} %get-tuple-element.52), channel_id=1, source_target_pairs={{16,0},{20,4},{24,8},{28,12},{17,1},{21,5},{25,9},{29,13},{18,2},{... | collective-permute-start | bytes 1769480 | tf_op jit(solution)/shard_map/ppermute | solution.py:230
  82.0 12.6 %collective-permute-done.11.refs_1_ = bf16[4,72,1024]{2,1,0:T(8,128)(2,1)S(1)} collective-permute-done((bf16[4,72,1024]{2,1,0:T(8,128)(2,1)S(1)}, bf16[4,72,1024]{2,1,0:T(8,128)(2,1)S(1)}, u32[]{:S(2)}, u32[]{:S(2)}) %collective-permute-start.11) | collective-permute-done | bytes 589856 | tf_op jit(solution)/shard_map/ppermute | solution.py:230
  94.8 16.3 %all_to_all.10.refs_1_ = bf16[4,72,1024]{2,1,0:T(8,128)(2,1)S(1)} all-to-all(bf16[4,72,1024]{2,1,0:T(8,128)(2,1)S(1)} %combine.3), channel_id=1, replica_groups=mesh['seq'=2,'head'=4,'dp'=4] {'head'}, dimensions={0} | all-to-all | bytes 1179648 | tf_op jit(solution)/shard_map/all_to_all | solution.py:330
  111.1 0.9 finish.1
  (35 shorter events, 1.8 us)
Async XLA Ops:
  2.6 19.6 %collective-permute-start = (bf16[72,2048]{1,0:T(8,128)(2,1)}, bf16[72,2048]{1,0:T(8,128)(2,1)S(1)}, u32[]{:S(2)}, u32[]{:S(2)}) collective-permute-start(bf16[72,2048]{1,0:T(8,128)(2,1)} %get-tuple-element.30.refs_0_), channel_id=1, source_target_pairs={{0,4},{4,0},{8,12},{12,8},{16,20},{24,28},{1,5},{5,1},{9,13},{13,9... | collective-permute-start | bytes 884744 | tf_op jit(solution)/shard_map/ppermute | solution.py:222
  7.5 14.6 %collective-permute-start.1 = (bf16[72,2048]{1,0:T(8,128)(2,1)}, bf16[72,2048]{1,0:T(8,128)(2,1)S(1)}, u32[]{:S(2)}, u32[]{:S(2)}) collective-permute-start(bf16[72,2048]{1,0:T(8,128)(2,1)} %get-tuple-element.30.refs_0_), channel_id=1, source_target_pairs={{0,16},{4,20},{8,24},{12,28},{1,17},{5,21},{9,25},{13,29},{2,18},{... | collective-permute-start | bytes 884744 | tf_op jit(solution)/shard_map/ppermute | solution.py:230
  11.0 17.5 %collective-permute-start.2 = (bf16[72,2048]{1,0:T(8,128)(2,1)}, bf16[72,2048]{1,0:T(8,128)(2,1)S(1)}, u32[]{:S(2)}, u32[]{:S(2)}) collective-permute-start(bf16[72,2048]{1,0:T(8,128)(2,1)} %get-tuple-element.30.refs_0_), channel_id=1, source_target_pairs={{0,8},{4,12},{8,0},{12,4},{16,24},{20,28},{1,9},{5,13},{9,1},{13,5... | collective-permute-start | bytes 884744 | tf_op jit(solution)/shard_map/ppermute | solution.py:222
  15.5 1.3 %copy-start = (bf16[72,8192]{1,0:T(8,128)(2,1)S(1)}, bf16[72,8192]{1,0:T(8,128)(2,1)}, u32[]{:S(2)}) copy-start(bf16[72,8192]{1,0:T(8,128)(2,1)} %query_ref.1) | copy-start | bytes 3538948
  16.8 1.3 %copy-start.1 = (bf16[72,8192]{1,0:T(8,128)(2,1)S(1)}, bf16[72,8192]{1,0:T(8,128)(2,1)}, u32[]{:S(2)}) copy-start(bf16[72,8192]{1,0:T(8,128)(2,1)} %grad_ref.1) | copy-start | bytes 3538948
  18.0 0.8 copy-start.3
  18.8 0.8 copy-start.5
  19.6 19.9 %copy-start.2 = (bf16[72,2048]{1,0:T(8,128)(2,1)S(1)}, bf16[72,2048]{1,0:T(8,128)(2,1)}, u32[]{:S(2)}) copy-start(bf16[72,2048]{1,0:T(8,128)(2,1)} %get-tuple-element.30.refs_0_) | copy-start | bytes 884740
  19.6 19.9 %copy-start.6 = (f32[72,128]{1,0:T(8,128)S(1)}, f32[72,128]{1,0:T(8,128)}, u32[]{:S(2)}) copy-start(f32[72,128]{1,0:T(8,128)} %get-tuple-element.32.sin_ref.refs_13_) | copy-start | bytes 110596
  19.6 19.9 %copy-start.7 = (s32[2]{0:T(128)S(1)}, s32[2]{0:T(128)}, u32[]{:S(2)}) copy-start(s32[2]{0:T(128)} %counts_ref.3) | copy-start | bytes 28
  22.1 25.9 %copy-start.8 = (bf16[8,128,576]{2,1,0:T(8,128)(2,1)}, bf16[8,128,576]{2,1,0:T(8,128)(2,1)S(1)}, u32[]{:S(2)}) copy-start(bf16[8,128,576]{2,1,0:T(8,128)(2,1)S(1)} %get-tuple-element.40.refs_9_) | copy-start | bytes 3538948
  22.1 25.9 %copy-start.10 = (bf16[8,128,576]{2,1,0:T(8,128)(2,1)}, bf16[8,128,576]{2,1,0:T(8,128)(2,1)S(1)}, u32[]{:S(2)}) copy-start(bf16[8,128,576]{2,1,0:T(8,128)(2,1)S(1)} %get-tuple-element.42.refs_11_) | copy-start | bytes 3538948
  22.1 25.8 %copy-start.12 = (bf16[8,576,128]{2,1,0:T(8,128)(2,1)}, bf16[8,576,128]{2,1,0:T(8,128)(2,1)S(1)}, u32[]{:S(2)}) copy-start(bf16[8,576,128]{2,1,0:T(8,128)(2,1)S(1)} %get-tuple-element.39.refs_8_) | copy-start | bytes 3538948
  22.1 25.8 %copy-start.14 = (bf16[8,576,128]{2,1,0:T(8,128)(2,1)}, bf16[8,576,128]{2,1,0:T(8,128)(2,1)S(1)}, u32[]{:S(2)}) copy-start(bf16[8,576,128]{2,1,0:T(8,128)(2,1)S(1)} %get-tuple-element.41.refs_10_) | copy-start | bytes 3538948
  22.2 13.3 %collective-permute-start.4 = (bf16[72,2048]{1,0:T(8,128)(2,1)S(1)}, bf16[72,2048]{1,0:T(8,128)(2,1)S(1)}, u32[]{:S(2)}, u32[]{:S(2)}) collective-permute-start(bf16[72,2048]{1,0:T(8,128)(2,1)S(1)} %collective-permute-done.refs_1_), channel_id=1, source_target_pairs={{0,16},{4,20},{8,24},{12,28},{1,17},{5,21},{9,25},{13,29},{2,18},{... | collective-permute-start | bytes 884744 | tf_op jit(solution)/shard_map/ppermute | solution.py:230
  28.5 7.0 %collective-permute-start.3 = (bf16[72,1024]{1,0:T(8,128)(2,1)S(1)}, bf16[72,1024]{1,0:T(8,128)(2,1)S(1)}, u32[]{:S(2)}, u32[]{:S(2)}) collective-permute-start(bf16[72,1024]{1,0:T(8,128)(2,1)S(1)} %get-tuple-element.56.refs_2_), channel_id=1, source_target_pairs={{0,4},{4,0},{8,12},{12,8},{24,28},{28,24},{1,5},{5,1},{9,13},{13,9... | collective-permute-start | bytes 442376 | tf_op jit(solution)/shard_map/ppermute | solution.py:222
  30.4 6.4 %collective-permute-start.8 = (bf16[72,1024]{1,0:T(8,128)(2,1)S(1)}, bf16[72,1024]{1,0:T(8,128)(2,1)S(1)}, u32[]{:S(2)}, u32[]{:S(2)}) collective-permute-start(bf16[72,1024]{1,0:T(8,128)(2,1)S(1)} %get-tuple-element.56.refs_2_), channel_id=1, source_target_pairs={{0,16},{4,20},{8,24},{12,28},{1,17},{5,21},{9,25},{13,29},{2,18},{... | collective-permute-start | bytes 442376 | tf_op jit(solution)/shard_map/ppermute | solution.py:230
  35.5 3.9 %collective-permute-start.9 = (bf16[72,1024]{1,0:T(8,128)(2,1)S(1)}, bf16[72,1024]{1,0:T(8,128)(2,1)S(1)}, u32[]{:S(2)}, u32[]{:S(2)}) collective-permute-start(bf16[72,1024]{1,0:T(8,128)(2,1)S(1)} %collective-permute-done.3.refs_3_), channel_id=1, source_target_pairs={{0,16},{4,20},{8,24},{12,28},{1,17},{5,21},{9,25},{13,29},{2,18},{... | collective-permute-start | bytes 442376 | tf_op jit(solution)/shard_map/ppermute | solution.py:230
  48.0 14.6 %collective-permute-start.10 = (bf16[4,72,1024]{2,1,0:T(8,128)(2,1)S(1)}, bf16[4,72,1024]{2,1,0:T(8,128)(2,1)S(1)}, u32[]{:S(2)}, u32[]{:S(2)}) collective-permute-start(bf16[4,72,1024]{2,1,0:T(8,128)(2,1)S(1)} %get-tuple-element.50), channel_id=1, source_target_pairs={{16,0},{20,4},{24,8},{28,12},{17,1},{21,5},{25,9},{29,13},{18,2},{... | collective-permute-start | bytes 1769480 | tf_op jit(solution)/shard_map/ppermute | solution.py:230
  49.3 7.0 %collective-permute-start.5 = (bf16[72,1024]{1,0:T(8,128)(2,1)S(1)}, bf16[72,1024]{1,0:T(8,128)(2,1)S(1)}, u32[]{:S(2)}, u32[]{:S(2)}) collective-permute-start(bf16[72,1024]{1,0:T(8,128)(2,1)S(1)} %get-tuple-element.36.refs_2_), channel_id=1, source_target_pairs={{0,4},{4,0},{8,12},{12,8},{24,28},{28,24},{1,5},{5,1},{9,13},{13,9... | collective-permute-start | bytes 442376 | tf_op jit(solution)/shard_map/ppermute | solution.py:222
  51.3 15.7 %collective-permute-start.6 = (bf16[72,1024]{1,0:T(8,128)(2,1)S(1)}, bf16[72,1024]{1,0:T(8,128)(2,1)S(1)}, u32[]{:S(2)}, u32[]{:S(2)}) collective-permute-start(bf16[72,1024]{1,0:T(8,128)(2,1)S(1)} %get-tuple-element.36.refs_2_), channel_id=1, source_target_pairs={{0,16},{4,20},{8,24},{12,28},{1,17},{5,21},{9,25},{13,29},{2,18},{... | collective-permute-start | bytes 442376 | tf_op jit(solution)/shard_map/ppermute | solution.py:230
  56.3 10.7 %collective-permute-start.7 = (bf16[72,1024]{1,0:T(8,128)(2,1)S(1)}, bf16[72,1024]{1,0:T(8,128)(2,1)S(1)}, u32[]{:S(2)}, u32[]{:S(2)}) collective-permute-start(bf16[72,1024]{1,0:T(8,128)(2,1)S(1)} %collective-permute-done.5.refs_3_), channel_id=1, source_target_pairs={{0,16},{4,20},{8,24},{12,28},{1,17},{5,21},{9,25},{13,29},{2,18},{... | collective-permute-start | bytes 442376 | tf_op jit(solution)/shard_map/ppermute | solution.py:230
  63.6 31.2 %all-to-all-start = ((bf16[4,72,1024]{2,1,0:T(8,128)(2,1)}), bf16[4,72,1024]{2,1,0:T(8,128)(2,1)S(1)}, u32[]{:S(2)}, u32[]{:S(2)}) async-start(bf16[4,72,1024]{2,1,0:T(8,128)(2,1)} %combine.2), calls=%async_computation | async-start | bytes 1179648 | tf_op jit(solution)/shard_map/all_to_all | solution.py:330
  67.1 1.3 %copy-start.9 = (bf16[8,128,576]{2,1,0:T(8,128)(2,1)S(1)}, bf16[8,128,576]{2,1,0:T(8,128)(2,1)}, u32[]{:S(2)}) copy-start(bf16[8,128,576]{2,1,0:T(8,128)(2,1)} %copy-done.8) | copy-start | bytes 3538948
  68.4 1.3 %copy-start.11 = (bf16[8,128,576]{2,1,0:T(8,128)(2,1)S(1)}, bf16[8,128,576]{2,1,0:T(8,128)(2,1)}, u32[]{:S(2)}) copy-start(bf16[8,128,576]{2,1,0:T(8,128)(2,1)} %copy-done.10) | copy-start | bytes 3538948
  69.7 1.3 %copy-start.13 = (bf16[8,576,128]{2,1,0:T(8,128)(2,1)S(1)}, bf16[8,576,128]{2,1,0:T(8,128)(2,1)}, u32[]{:S(2)}) copy-start(bf16[8,576,128]{2,1,0:T(8,128)(2,1)} %copy-done.12) | copy-start | bytes 3538948
  71.0 1.3 %copy-start.15 = (bf16[8,576,128]{2,1,0:T(8,128)(2,1)S(1)}, bf16[8,576,128]{2,1,0:T(8,128)(2,1)}, u32[]{:S(2)}) copy-start(bf16[8,576,128]{2,1,0:T(8,128)(2,1)} %copy-done.14) | copy-start | bytes 3538948
  80.7 13.9 %collective-permute-start.11 = (bf16[4,72,1024]{2,1,0:T(8,128)(2,1)S(1)}, bf16[4,72,1024]{2,1,0:T(8,128)(2,1)S(1)}, u32[]{:S(2)}, u32[]{:S(2)}) collective-permute-start(bf16[4,72,1024]{2,1,0:T(8,128)(2,1)S(1)} %get-tuple-element.52), channel_id=1, source_target_pairs={{16,0},{20,4},{24,8},{28,12},{17,1},{21,5},{25,9},{29,13},{18,2},{... | collective-permute-start | bytes 1769480 | tf_op jit(solution)/shard_map/ppermute | solution.py:230
  94.6 16.5 %copy-start.4 = (f32[72,128]{1,0:T(8,128)S(1)}, f32[72,128]{1,0:T(8,128)}, u32[]{:S(2)}) copy-start(f32[72,128]{1,0:T(8,128)} %get-tuple-element.31.cos_ref) | copy-start | bytes 110596

commit v3 on v1

--- a/solution.py
+++ b/solution.py
@@ -18,6 +18,7 @@
 CHUNKS = 2
 HEADS_PER_CHUNK = KEY_VALUE_HEADS // CHUNKS
 CHUNK_COLS = HEADS_PER_CHUNK * HEAD_WIDTH
+STEP_HEADS = 2
 VMEM = pl.BlockSpec(memory_space=pltpu.VMEM)
 SMEM = pl.BlockSpec(memory_space=pltpu.SMEM)
 
@@ -43,7 +44,7 @@
     return slice(index * HEAD_WIDTH, (index + 1) * HEAD_WIDTH)
 
 
-def prepare_keys(rows, pos_ref, key_ref, value_ref, *out_refs):
+def prepare_keys(rows, pos_ref, key_ref, value_ref, whole_ref, *out_refs):
     kv_refs, (cos_ref, sin_ref) = out_refs[:CHUNKS], out_refs[CHUNKS:]
     padded = key_ref.shape[0]
     start = (lax.axis_index("seq") * lax.axis_size("head") + lax.axis_index("head")) * rows
@@ -63,8 +64,13 @@
     for head in range(KEY_VALUE_HEADS):
         chunk, place = divmod(head, HEADS_PER_CHUNK)
         rotated = rope(key_ref[:, head_cols(head)].astype(jnp.float32), cosine, sine)
-        kv_refs[chunk][:, head_cols(place)] = rotated.astype(jnp.bfloat16)
-        kv_refs[chunk][:, head_cols(HEADS_PER_CHUNK + place)] = value_ref[:, head_cols(head)]
+        columns = {
+            place: rotated.astype(jnp.bfloat16),
+            HEADS_PER_CHUNK + place: value_ref[:, head_cols(head)],
+        }
+        for column, x in columns.items():
+            kv_refs[chunk][:, head_cols(column)] = x
+            whole_ref[:, head_cols(2 * chunk * HEADS_PER_CHUNK + column)] = x
 
 
 def prepare_queries(query_ref, grad_ref, cos_ref, sin_ref, q_ref, qt_ref, g_ref, gt_ref, table_ref):
@@ -121,42 +127,50 @@
                 live_ref[...] = (query_row[:8] < limit).astype(jnp.float32)
             bias_ref[block * padded : (block + 1) * padded, :] = jnp.where(allowed, 0.0, -1e30)
 
-    cols = pl.ds(pl.multiple_of(step * HEAD_WIDTH, HEAD_WIDTH), HEAD_WIDTH)
-    far_cols = pl.ds(pl.multiple_of(CHUNK_COLS + step * HEAD_WIDTH, HEAD_WIDTH), HEAD_WIDTH)
-    keys_wide = jnp.concatenate([ref[:, cols].astype(jnp.float32) for ref in kv_refs], 0)
-    values_wide = jnp.concatenate([ref[:, far_cols].astype(jnp.float32) for ref in kv_refs], 0)
-    keys, keys_t = keys_wide.astype(jnp.bfloat16), keys_wide.T.astype(jnp.bfloat16)
-    values, values_t = values_wide.astype(jnp.bfloat16), values_wide.T.astype(jnp.bfloat16)
-    queries, queries_t = q_ref[0], qt_ref[0]
-    grads, grads_t = g_ref[0], gt_ref[0]
-
-    scores = dot(keys, queries_t) * (SCORE_SCALE * LOG2_E) + bias_ref[...]
-    weights = jnp.exp2(scores - jnp.max(scores, 0, keepdims=True))
-    row_total = jnp.sum(weights, 0, keepdims=True)
-    probs = weights * (live_ref[0:1, :] / row_total)
-    probs_low = probs.astype(jnp.bfloat16)
-    out_t = dot(values_t, probs_low)
-    delta = jnp.sum(
-        grads_t.astype(jnp.float32) * out_t.astype(jnp.bfloat16).astype(jnp.float32),
-        0,
-        keepdims=True,
-    )
-    dscore = (probs * (dot(values, grads_t) - delta)).astype(jnp.bfloat16)
-    grad_t = dot(keys_t, dscore) * SCORE_SCALE
-    key_part = dot(dscore, queries) * SCORE_SCALE
-    value_part = dot(probs_low, grads)
+    def lanes(first, place):
+        start = pl.multiple_of((first + step * STEP_HEADS + place) * HEAD_WIDTH, HEAD_WIDTH)
+        return pl.ds(start, HEAD_WIDTH)
+
+    def gathered(first, place):
+        cols = lanes(first, place)
+        wide = jnp.concatenate([ref[:, cols].astype(jnp.float32) for ref in kv_refs], 0)
+        return wide.astype(jnp.bfloat16), wide.T.astype(jnp.bfloat16)
+
+    heads = range(STEP_HEADS)
+    keys, values = [gathered(0, p) for p in heads], [gathered(HEADS_PER_CHUNK, p) for p in heads]
+    bias, live = bias_ref[...], live_ref[0:1, :]
+    scores = [dot(keys[p][0], qt_ref[p]) * (SCORE_SCALE * LOG2_E) + bias for p in heads]
+    dprobs, probs, probs_low = [], [], []
+    for p in heads:
+        weights = jnp.exp2(scores[p] - jnp.max(scores[p], 0, keepdims=True))
+        probs.append(weights * (live / jnp.sum(weights, 0, keepdims=True)))
+        probs_low.append(probs[p].astype(jnp.bfloat16))
+        dprobs.append(dot(values[p][0], gt_ref[p]))
+    outs_t, value_parts, dscores = [], [], []
+    for p in heads:
+        outs_t.append(dot(values[p][1], probs_low[p]))
+        value_parts.append(dot(probs_low[p], g_ref[p]))
+        out_low = outs_t[p].astype(jnp.bfloat16).astype(jnp.float32)
+        delta = jnp.sum(gt_ref[p].astype(jnp.float32) * out_low, 0, keepdims=True)
+        dscores.append((probs[p] * (dprobs[p] - delta)).astype(jnp.bfloat16))
+    grads_t = [dot(keys[p][1], dscores[p]) * SCORE_SCALE for p in heads]
+    key_parts = [dot(dscores[p], q_ref[p]) * SCORE_SCALE for p in heads]
 
     cosine, sine = cos_ref[...], sin_ref[...]
-    out_heads, grad_heads = out_t.T, grad_t.T
-    for h in range(GROUP):
-        piece = slice(h * padded, (h + 1) * padded)
-        out_ref[:, head_cols(h)] = out_heads[piece].astype(jnp.bfloat16)
-        grad_ref[:, head_cols(h)] = rope_back(grad_heads[piece], cosine, sine).astype(jnp.bfloat16)
-    for block in range(blocks):
-        seq_offset, head_offset = divmod(block, head_count)
-        piece = slice(block * padded, (block + 1) * padded)
-        part_refs[seq_offset][head_offset, :, cols] = key_part[piece].astype(jnp.bfloat16)
-        part_refs[seq_offset][head_offset, :, far_cols] = value_part[piece].astype(jnp.bfloat16)
+    for p in heads:
+        out_heads, grad_heads = outs_t[p].T, grads_t[p].T
+        for h in range(GROUP):
+            piece, cols = slice(h * padded, (h + 1) * padded), head_cols(p * GROUP + h)
+            out_ref[:, cols] = out_heads[piece].astype(jnp.bfloat16)
+            grad_ref[:, cols] = rope_back(grad_heads[piece], cosine, sine).astype(jnp.bfloat16)
+        for block in range(blocks):
+            seq_offset, head_offset = divmod(block, head_count)
+            piece = slice(block * padded, (block + 1) * padded)
+            part_ref = part_refs[seq_offset]
+            part_ref[head_offset, :, lanes(0, p)] = key_parts[p][piece].astype(jnp.bfloat16)
+            part_ref[head_offset, :, lanes(HEADS_PER_CHUNK, p)] = value_parts[p][piece].astype(
+                jnp.bfloat16
+            )
 
 
 def combine(seq_count, head_count, *refs):
@@ -236,11 +250,13 @@
 
     table = shape((padded, HEAD_WIDTH), f32)
     piece = shape((padded, 2 * CHUNK_COLS), bf16)
-    *own, cosine, sine = pl.pallas_call(
+    whole, *own, cosine, sine = pl.pallas_call(
         functools.partial(prepare_keys, rows),
-        out_shape=[piece] * CHUNKS + [table, table],
+        out_shape=[shape((padded, CHUNKS * 2 * CHUNK_COLS), bf16)]
+        + [piece] * CHUNKS
+        + [table, table],
         in_specs=[SMEM, VMEM, VMEM],
-        out_specs=[VMEM] * (CHUNKS + 2),
+        out_specs=[VMEM] * (CHUNKS + 3),
         compiler_params=params(56),
         name="prepare_keys",
     )(positions, routed_keys, routed_values)
@@ -265,40 +281,46 @@
     )(queries, output_gradient, cosine, sine)
 
     bits = [1 << b for b in reversed(range((head_count - 1).bit_length()))]
-    far = [[[along_seq(x, a, True)] for a in range(1, seq_count)] for x in own]
+    later = range(1, seq_count)
+    chunked = [{bits[0]: along_head(own[0], bits[0], True)}]
+    far = {(a, 0): along_seq(whole, a, True) for a in later}
+    nearest = along_head(whole, 1, True)
+    chunked[0][bits[0]], own[1:], cosine_later, far = lax.optimization_barrier(
+        (chunked[0][bits[0]], own[1:], cosine_later, far)
+    )
+    chunked += [{bits[0]: along_head(x, bits[0], True)} for x in own[1:]]
+    far.update({(a, 1): along_seq(nearest, a, True) for a in later})
     gathered = []
-    for chunk in range(CHUNKS):
-        near = {0: own[chunk]}
-        for bit in bits:
-            near.update({j ^ bit: along_head(x, bit, True, j) for j, x in near.items()})
-            if bit == bits[0] and chunk == 0:
-                near[bit], cosine_later, far = lax.optimization_barrier(
-                    (near[bit], cosine_later, far)
-                )
-            if bit == bits[0] and chunk + 1 < CHUNKS:
-                own[chunk + 1], near[bit] = lax.optimization_barrier((own[chunk + 1], near[bit]))
-        near = [near[j] for j in range(head_count)]
-        for a in range(1, seq_count):
-            far[chunk][a - 1] += [along_seq(x, a, True) for x in near[1:]]
-        gathered.append(near + [x for group in far[chunk] for x in group])
+    for c, near in enumerate(chunked):
+        near[0] = own[c]
+        for bit in bits[1:]:
+            near.update(
+                {j ^ bit: along_head(x, bit, True, j) for j, x in near.items() if j ^ bit > 1}
+            )
+        blocks_here = [whole, nearest] + [near[j] for j in range(2, head_count)]
+        for a in later:
+            blocks_here += [far[a, 0], far[a, 1]]
+            blocks_here += [along_seq(near[j], a, True) for j in range(2, head_count)]
+        gathered.append(blocks_here)
 
     wide_outs = ()
     summed = []
     for chunk in range(CHUNKS):
-        first = chunk * HEADS_PER_CHUNK
+        first = chunk * HEADS_PER_CHUNK // STEP_HEADS
         has_alias = int(chunk > 0)
-        tall_part = pl.BlockSpec((1, query_rows, HEAD_WIDTH), lambda g, f=first: (f + g, 0, 0))
-        flat_part = pl.BlockSpec((1, HEAD_WIDTH, query_rows), lambda g, f=first: (f + g, 0, 0))
-        row_part = pl.BlockSpec((padded, wide), lambda g, f=first: (0, f + g))
-        kv_block = pl.BlockSpec((padded, 2 * CHUNK_COLS), lambda g: (0, 0))
+        tall_part = pl.BlockSpec((STEP_HEADS, query_rows, HEAD_WIDTH), lambda g, f=first: (f + g, 0, 0))
+        flat_part = pl.BlockSpec((STEP_HEADS, HEAD_WIDTH, query_rows), lambda g, f=first: (f + g, 0, 0))
+        row_part = pl.BlockSpec((padded, STEP_HEADS * wide), lambda g, f=first: (0, f + g))
+        kv_whole = pl.BlockSpec((padded, 2 * CHUNK_COLS), lambda g, c=chunk: (0, c))
+        kv_chunk = pl.BlockSpec((padded, 2 * CHUNK_COLS), lambda g: (0, 0))
         part_block = pl.BlockSpec((head_count, padded, 2 * CHUNK_COLS), lambda g: (0, 0, 0))
         out = pl.pallas_call(
             functools.partial(attend, seq_count, head_count, rows, has_alias),
-            grid=(HEADS_PER_CHUNK,),
+            grid=(HEADS_PER_CHUNK // STEP_HEADS,),
             out_shape=[shape((padded, QUERY_HEADS * HEAD_WIDTH), bf16)] * 2
             + [shape((head_count, padded, 2 * CHUNK_COLS), bf16)] * seq_count,
             in_specs=[SMEM]
-            + [kv_block] * blocks
+            + ([kv_whole] * 2 + [kv_chunk] * (head_count - 2)) * seq_count
             + [tall_part, flat_part, tall_part, flat_part, table_block, table_block]
             + [pl.BlockSpec(memory_space=pl.ANY)] * (2 * has_alias),
             out_specs=[row_part, row_part] + [part_block] * seq_count,

time: 99.5 us -> 97.9 us (0.984)
  starting transfers between devices: 54.9 us -> 51.1 us
  waiting for transfers between devices: 16.1 us -> 19.5 us
  Pallas kernels: 22.6 us -> 21.5 us
    ppermute x12 -> x11, starting transfers between devices: 39.8 us -> 37 us  [along_head(): return lax.ppermute(x, ('seq', 'head'), pairs)]
    ppermute x12 -> x11, waiting for transfers between devices: 7.66 us -> 10.2 us  [along_head(): return lax.ppermute(x, ('seq', 'head'), pairs)]
    pallas_call x2, Pallas kernels: 17 us -> 15.7 us  [shards(): pl.pallas_call(functools.partial(attend, seq_count, head_count, rows, has...]
    ppermute x10 -> x8, starting transfers between devices: 15.1 us -> 14.1 us  [along_seq(): return lax.ppermute(x, ('seq', 'head'), pairs)]
    ppermute x10 -> x8, waiting for transfers between devices: 8.41 us -> 9.26 us  [along_seq(): return lax.ppermute(x, ('seq', 'head'), pairs)]
  transfers between devices with their start and end apart: 22 -> 19, of which waited for: 5 -> 5; matrix products, arithmetic and copies ran while one was open for 0% -> 0% of each run, Pallas kernels for 20% -> 19%
where the time goes in v3:
time: 97.9 us; the launch traced here: 97.1 us
  starting transfers between devices  51.1 us (52%)
  Pallas kernels  21.5 us (22%)
  waiting for transfers between devices  19.5 us (20%)
  local copies, waits for them, and re-layouts  4.09 us (4%)
    ppermute x11, starting transfers between devices, along_head(): return lax.ppermute(x, ('seq', 'head'), pairs)  37 us
    pallas_call x2, Pallas kernels, shards(): pl.pallas_call(functools.partial(attend, seq_count, head_count, rows, has...  15.7 us
    ppermute x8, starting transfers between devices, along_seq(): return lax.ppermute(x, ('seq', 'head'), pairs)  14.1 us
    ppermute x11, waiting for transfers between devices, along_head(): return lax.ppermute(x, ('seq', 'head'), pairs)  10.2 us
    ppermute x8, waiting for transfers between devices, along_seq(): return lax.ppermute(x, ('seq', 'head'), pairs)  9.26 us
    unnamed x18, local copies, waits for them, and re-layouts  4.09 us
    pallas_call x1, Pallas kernels, shards(): pl.pallas_call(prepare_queries, grid=(KEY_VALUE_HEADS,), out_shape=[tall,...  2.53 us
    pallas_call x1, Pallas kernels, shards(): pl.pallas_call(functools.partial(prepare_keys, rows), out_shape=[shape((p...  2.1 us
  transfers between devices with their start and end apart: 19, of which 5 were waited for; matrix products, arithmetic and copies ran while one was open for 0% of the time, Pallas kernels for 19%

profile of v3, /device:TPU:0, one launch (start us, length us, event | category | flops | bytes accessed | tf_op | source)
XLA Modules:
  0.0 97.1 jit_solution(8979614453586393977)
XLA Ops:
  0.6 2.1 %prepare_keys.1 = (bf16[72,2048]{1,0:T(8,128)(2,1)}, bf16[72,1024]{1,0:T(8,128)(2,1)}, bf16[72,1024]{1,0:T(8,128)(2,1)}, f32[72,128]{1,0:T(8,128)}, f32[72,128]{1,0:T(8,128)}) custom-call(s32[576]{0:T(1024)} %pos_ref.1, bf16[72,1024]{1,0:T(8,128)(2,1)} %key_ref.1, bf16[72,1024]{1,0:T(8,128)(2,1)} %value_ref.1), custom_call_target="tpu_custom_call" | custom-call | tf_op jit(solution)/shard_map/prepare_keys/pallas_call | solution.py:253
  2.7 4.9 %collective-permute-start.2 = (bf16[72,2048]{1,0:T(8,128)(2,1)}, bf16[72,2048]{1,0:T(8,128)(2,1)S(1)}, u32[]{:S(2)}, u32[]{:S(2)}) collective-permute-start(bf16[72,2048]{1,0:T(8,128)(2,1)} %get-tuple-element.36.refs_0_), channel_id=1, source_target_pairs={{0,16},{4,20},{8,24},{12,28},{1,17},{5,21},{9,25},{13,29},{2,18},{... | collective-permute-start | bytes 884744 | tf_op jit(solution)/shard_map/ppermute | solution.py:249
  7.6 3.5 %collective-permute-start = (bf16[72,2048]{1,0:T(8,128)(2,1)}, bf16[72,2048]{1,0:T(8,128)(2,1)S(1)}, u32[]{:S(2)}, u32[]{:S(2)}) collective-permute-start(bf16[72,2048]{1,0:T(8,128)(2,1)} %get-tuple-element.36.refs_0_), channel_id=1, source_target_pairs={{0,4},{4,0},{8,12},{12,8},{16,20},{24,28},{1,5},{5,1},{9,13},{13,9... | collective-permute-start | bytes 884744 | tf_op jit(solution)/shard_map/ppermute | solution.py:241
  11.1 4.5 %collective-permute-start.1 = (bf16[72,1024]{1,0:T(8,128)(2,1)}, bf16[72,1024]{1,0:T(8,128)(2,1)S(1)}, u32[]{:S(2)}, u32[]{:S(2)}) collective-permute-start(bf16[72,1024]{1,0:T(8,128)(2,1)} %get-tuple-element.37), channel_id=1, source_target_pairs={{0,8},{4,12},{8,0},{12,4},{16,24},{20,28},{1,9},{5,13},{9,1},{13,5... | collective-permute-start | bytes 442376 | tf_op jit(solution)/shard_map/ppermute | solution.py:241
  15.6 1.3 %copy-done = bf16[72,8192]{1,0:T(8,128)(2,1)S(1)} copy-done((bf16[72,8192]{1,0:T(8,128)(2,1)S(1)}, bf16[72,8192]{1,0:T(8,128)(2,1)}, u32[]{:S(2)}) %copy-start) | copy-done | bytes 1179672
  16.9 1.3 %copy-done.1 = bf16[72,8192]{1,0:T(8,128)(2,1)S(1)} copy-done((bf16[72,8192]{1,0:T(8,128)(2,1)S(1)}, bf16[72,8192]{1,0:T(8,128)(2,1)}, u32[]{:S(2)}) %copy-start.1) | copy-done | bytes 1179672
  18.2 0.8 copy-done.3
  19.7 2.5 %prepare_queries.1 = (bf16[8,576,128]{2,1,0:T(8,128)(2,1)S(1)}, bf16[8,128,576]{2,1,0:T(8,128)(2,1)S(1)}, bf16[8,576,128]{2,1,0:T(8,128)(2,1)S(1)}, bf16[8,128,576]{2,1,0:T(8,128)(2,1)S(1)}, f32[72,128]{1,0:T(8,128)S(1)}) custom-call(bf16[72,8192]{1,0:T(8,128)(2,1)S(1)} %copy-done, bf16[72,8192]{1,0:T(8,128)(2,1)S(1)} %copy-done.1, f32[72,128]{1,0:T(8,128)S(1)} %copy-done.3, ...), custom_call_target="tpu_custom_call" | custom-call | flops 8071000064 | bytes 25830000 | tf_op jit(solution)/shard_map/prepare_queries/pallas_call | solution.py:271
  22.3 3.6 %collective-permute-start.3 = (bf16[72,1024]{1,0:T(8,128)(2,1)S(1)}, bf16[72,1024]{1,0:T(8,128)(2,1)S(1)}, u32[]{:S(2)}, u32[]{:S(2)}) collective-permute-start(bf16[72,1024]{1,0:T(8,128)(2,1)S(1)} %copy-done.8), channel_id=1, source_target_pairs={{0,8},{4,12},{8,0},{12,4},{16,24},{20,28},{1,9},{5,13},{9,1},{13,5... | collective-permute-start | bytes 442376 | tf_op jit(solution)/shard_map/ppermute | solution.py:241
  25.8 1.5 %collective-permute-start.5 = (bf16[72,2048]{1,0:T(8,128)(2,1)S(1)}, bf16[72,2048]{1,0:T(8,128)(2,1)S(1)}, u32[]{:S(2)}, u32[]{:S(2)}) collective-permute-start(bf16[72,2048]{1,0:T(8,128)(2,1)S(1)} %collective-permute-done.refs_1_), channel_id=1, source_target_pairs={{0,16},{4,20},{8,24},{12,28},{1,17},{5,21},{9,25},{13,29},{2,18},{... | collective-permute-start | bytes 884744 | tf_op jit(solution)/shard_map/ppermute | solution.py:249
  27.3 3.3 %collective-permute-start.8 = (bf16[72,1024]{1,0:T(8,128)(2,1)S(1)}, bf16[72,1024]{1,0:T(8,128)(2,1)S(1)}, u32[]{:S(2)}, u32[]{:S(2)}) collective-permute-start(bf16[72,1024]{1,0:T(8,128)(2,1)S(1)} %collective-permute-done.1.refs_2_), channel_id=1, source_target_pairs={{0,4},{4,0},{8,12},{12,8},{24,28},{28,24},{1,5},{5,1},{9,13},{13,9... | collective-permute-start | bytes 442376 | tf_op jit(solution)/shard_map/ppermute | solution.py:241
  30.7 2.4 %collective-permute-done.3.refs_2_ = bf16[72,1024]{1,0:T(8,128)(2,1)S(1)} collective-permute-done((bf16[72,1024]{1,0:T(8,128)(2,1)S(1)}, bf16[72,1024]{1,0:T(8,128)(2,1)S(1)}, u32[]{:S(2)}, u32[]{:S(2)}) %collective-permute-start.3) | collective-permute-done | bytes 147488 | tf_op jit(solution)/shard_map/ppermute | solution.py:241
  33.1 1.9 %collective-permute-start.4 = (bf16[72,1024]{1,0:T(8,128)(2,1)S(1)}, bf16[72,1024]{1,0:T(8,128)(2,1)S(1)}, u32[]{:S(2)}, u32[]{:S(2)}) collective-permute-start(bf16[72,1024]{1,0:T(8,128)(2,1)S(1)} %collective-permute-done.3.refs_2_), channel_id=1, source_target_pairs={{0,4},{4,0},{8,12},{12,8},{24,28},{28,24},{1,5},{5,1},{9,13},{13,9... | collective-permute-start | bytes 442376 | tf_op jit(solution)/shard_map/ppermute | solution.py:241
  35.0 1.3 %collective-permute-start.9 = (bf16[72,1024]{1,0:T(8,128)(2,1)S(1)}, bf16[72,1024]{1,0:T(8,128)(2,1)S(1)}, u32[]{:S(2)}, u32[]{:S(2)}) collective-permute-start(bf16[72,1024]{1,0:T(8,128)(2,1)S(1)} %collective-permute-done.1.refs_2_), channel_id=1, source_target_pairs={{0,16},{4,20},{8,24},{12,28},{1,17},{5,21},{9,25},{13,29},{2,18},{... | collective-permute-start | bytes 442376 | tf_op jit(solution)/shard_map/ppermute | solution.py:249
  36.3 1.3 %collective-permute-start.10 = (bf16[72,1024]{1,0:T(8,128)(2,1)S(1)}, bf16[72,1024]{1,0:T(8,128)(2,1)S(1)}, u32[]{:S(2)}, u32[]{:S(2)}) collective-permute-start(bf16[72,1024]{1,0:T(8,128)(2,1)S(1)} %collective-permute-done.8.refs_3_), channel_id=1, source_target_pairs={{0,16},{4,20},{8,24},{12,28},{1,17},{5,21},{9,25},{13,29},{2,18},{... | collective-permute-start | bytes 442376 | tf_op jit(solution)/shard_map/ppermute | solution.py:249
  37.6 1.3 %collective-permute-start.6 = (bf16[72,1024]{1,0:T(8,128)(2,1)S(1)}, bf16[72,1024]{1,0:T(8,128)(2,1)S(1)}, u32[]{:S(2)}, u32[]{:S(2)}) collective-permute-start(bf16[72,1024]{1,0:T(8,128)(2,1)S(1)} %collective-permute-done.3.refs_2_), channel_id=1, source_target_pairs={{0,16},{4,20},{8,24},{12,28},{1,17},{5,21},{9,25},{13,29},{2,18},{... | collective-permute-start | bytes 442376 | tf_op jit(solution)/shard_map/ppermute | solution.py:249
  38.9 1.2 %collective-permute-done.4.refs_3_ = bf16[72,1024]{1,0:T(8,128)(2,1)S(1)} collective-permute-done((bf16[72,1024]{1,0:T(8,128)(2,1)S(1)}, bf16[72,1024]{1,0:T(8,128)(2,1)S(1)}, u32[]{:S(2)}, u32[]{:S(2)}) %collective-permute-start.4) | collective-permute-done | bytes 147488 | tf_op jit(solution)/shard_map/ppermute | solution.py:241
  40.1 1.3 %collective-permute-start.7 = (bf16[72,1024]{1,0:T(8,128)(2,1)S(1)}, bf16[72,1024]{1,0:T(8,128)(2,1)S(1)}, u32[]{:S(2)}, u32[]{:S(2)}) collective-permute-start(bf16[72,1024]{1,0:T(8,128)(2,1)S(1)} %collective-permute-done.4.refs_3_), channel_id=1, source_target_pairs={{0,16},{4,20},{8,24},{12,28},{1,17},{5,21},{9,25},{13,29},{2,18},{... | collective-permute-start | bytes 442376 | tf_op jit(solution)/shard_map/ppermute | solution.py:249
  41.4 2.3 %collective-permute-done.10.refs_7_ = bf16[72,1024]{1,0:T(8,128)(2,1)S(1)} collective-permute-done((bf16[72,1024]{1,0:T(8,128)(2,1)S(1)}, bf16[72,1024]{1,0:T(8,128)(2,1)S(1)}, u32[]{:S(2)}, u32[]{:S(2)}) %collective-permute-start.10) | collective-permute-done | bytes 147488 | tf_op jit(solution)/shard_map/ppermute | solution.py:249
  43.8 7.9 %attend.2 = (bf16[72,8192]{1,0:T(8,128)(2,1)}, bf16[72,8192]{1,0:T(8,128)(2,1)}, bf16[4,72,1024]{2,1,0:T(8,128)(2,1)S(1)}, bf16[4,72,1024]{2,1,0:T(8,128)(2,1)S(1)}) custom-call(s32[2]{0:T(128)S(1)} %copy-done.7, bf16[72,2048]{1,0:T(8,128)(2,1)S(1)} %copy-done.2, bf16[72,2048]{1,0:T(8,128)(2,1)S(1)} %collective-permute-done.refs_1_, ...), custom_call_target="tpu_custom_call" | custom-call | flops 11530000384 | bytes 36900000 | tf_op jit(solution)/shard_map/attend/pallas_call | solution.py:317
  51.6 1.3 %collective-permute-start.11 = (bf16[4,72,1024]{2,1,0:T(8,128)(2,1)S(1)}, bf16[4,72,1024]{2,1,0:T(8,128)(2,1)S(1)}, u32[]{:S(2)}, u32[]{:S(2)}) collective-permute-start(bf16[4,72,1024]{2,1,0:T(8,128)(2,1)S(1)} %get-tuple-element.55), channel_id=1, source_target_pairs={{16,0},{20,4},{24,8},{28,12},{17,1},{21,5},{25,9},{29,13},{18,2},{... | collective-permute-start | bytes 1769480 | tf_op jit(solution)/shard_map/ppermute | solution.py:249
  52.9 7.9 %attend.3 = (bf16[72,8192]{1,0:T(8,128)(2,1)}, bf16[72,8192]{1,0:T(8,128)(2,1)}, bf16[4,72,1024]{2,1,0:T(8,128)(2,1)S(1)}, bf16[4,72,1024]{2,1,0:T(8,128)(2,1)S(1)}) custom-call(s32[2]{0:T(128)S(1)} %copy-done.7, bf16[72,2048]{1,0:T(8,128)(2,1)S(1)} %copy-done.2, ...), custom_call_target="tpu_custom_call", output_to_operand_aliasing={{0}: (15, {}), {1}: (16, {})} | custom-call | flops 11530000384 | bytes 36900000 | tf_op jit(solution)/shard_map/attend/pallas_call | solution.py:317
  60.8 1.3 %collective-permute-start.15 = (bf16[4,72,1024]{2,1,0:T(8,128)(2,1)S(1)}, bf16[4,72,1024]{2,1,0:T(8,128)(2,1)S(1)}, u32[]{:S(2)}, u32[]{:S(2)}) collective-permute-start(bf16[4,72,1024]{2,1,0:T(8,128)(2,1)S(1)} %get-tuple-element.61), channel_id=1, source_target_pairs={{16,0},{20,4},{24,8},{28,12},{17,1},{21,5},{25,9},{29,13},{18,2},{... | collective-permute-start | bytes 1769480 | tf_op jit(solution)/shard_map/ppermute | solution.py:249
  62.1 6.9 %collective-permute-done.11.refs_1_ = bf16[4,72,1024]{2,1,0:T(8,128)(2,1)S(1)} collective-permute-done((bf16[4,72,1024]{2,1,0:T(8,128)(2,1)S(1)}, bf16[4,72,1024]{2,1,0:T(8,128)(2,1)S(1)}, u32[]{:S(2)}, u32[]{:S(2)}) %collective-permute-start.11) | collective-permute-done | bytes 589856 | tf_op jit(solution)/shard_map/ppermute | solution.py:249
  69.1 3.4 %collective-permute-start.12 = (bf16[72,1024]{1,0:T(8,128)(2,1)S(1)}, bf16[72,1024]{1,0:T(8,128)(2,1)S(1)}, u32[]{:S(2)}, u32[]{:S(2)}) collective-permute-start(bf16[72,1024]{1,0:T(8,128)(2,1)S(1)} %get-tuple-element.57), channel_id=1, source_target_pairs={{0,4},{4,0},{8,12},{12,8},{20,16},{28,24},{1,5},{5,1},{9,13},{13,9... | collective-permute-start | bytes 442376 | tf_op jit(solution)/shard_map/ppermute | solution.py:241
  72.5 1.9 %collective-permute-start.13 = (bf16[72,1024]{1,0:T(8,128)(2,1)S(1)}, bf16[72,1024]{1,0:T(8,128)(2,1)S(1)}, u32[]{:S(2)}, u32[]{:S(2)}) collective-permute-start(bf16[72,1024]{1,0:T(8,128)(2,1)S(1)} %get-tuple-element.58), channel_id=1, source_target_pairs={{0,8},{4,12},{8,0},{12,4},{24,16},{28,20},{1,9},{5,13},{9,1},{13,5... | collective-permute-start | bytes 442376 | tf_op jit(solution)/shard_map/ppermute | solution.py:241
  74.4 4.8 %collective-permute-start.14 = (bf16[72,1024]{1,0:T(8,128)(2,1)S(1)}, bf16[72,1024]{1,0:T(8,128)(2,1)S(1)}, u32[]{:S(2)}, u32[]{:S(2)}) collective-permute-start(bf16[72,1024]{1,0:T(8,128)(2,1)S(1)} %get-tuple-element.59), channel_id=1, source_target_pairs={{0,12},{4,8},{8,4},{12,0},{24,20},{28,16},{1,13},{5,9},{9,5},{13,1... | collective-permute-start | bytes 442376 | tf_op jit(solution)/shard_map/ppermute | solution.py:241
  79.4 2.5 %collective-permute-start.16 = (bf16[72,1024]{1,0:T(8,128)(2,1)S(1)}, bf16[72,1024]{1,0:T(8,128)(2,1)S(1)}, u32[]{:S(2)}, u32[]{:S(2)}) collective-permute-start(bf16[72,1024]{1,0:T(8,128)(2,1)S(1)} %get-tuple-element.63), channel_id=1, source_target_pairs={{0,4},{4,0},{8,12},{12,8},{20,16},{28,24},{1,5},{5,1},{9,13},{13,9... | collective-permute-start | bytes 442376 | tf_op jit(solution)/shard_map/ppermute | solution.py:241
  81.9 2.8 %collective-permute-start.17 = (bf16[72,1024]{1,0:T(8,128)(2,1)S(1)}, bf16[72,1024]{1,0:T(8,128)(2,1)S(1)}, u32[]{:S(2)}, u32[]{:S(2)}) collective-permute-start(bf16[72,1024]{1,0:T(8,128)(2,1)S(1)} %get-tuple-element.64), channel_id=1, source_target_pairs={{0,8},{4,12},{8,0},{12,4},{24,16},{28,20},{1,9},{5,13},{9,1},{13,5... | collective-permute-start | bytes 442376 | tf_op jit(solution)/shard_map/ppermute | solution.py:241
  84.7 4.8 %collective-permute-start.18 = (bf16[72,1024]{1,0:T(8,128)(2,1)S(1)}, bf16[72,1024]{1,0:T(8,128)(2,1)S(1)}, u32[]{:S(2)}, u32[]{:S(2)}) collective-permute-start(bf16[72,1024]{1,0:T(8,128)(2,1)S(1)} %get-tuple-element.65), channel_id=1, source_target_pairs={{0,12},{4,8},{8,4},{12,0},{24,20},{28,16},{1,13},{5,9},{9,5},{13,1... | collective-permute-start | bytes 442376 | tf_op jit(solution)/shard_map/ppermute | solution.py:241
  89.6 6.6 %collective-permute-done.17.refs_8_ = bf16[72,1024]{1,0:T(8,128)(2,1)S(1)} collective-permute-done((bf16[72,1024]{1,0:T(8,128)(2,1)S(1)}, bf16[72,1024]{1,0:T(8,128)(2,1)S(1)}, u32[]{:S(2)}, u32[]{:S(2)}) %collective-permute-start.17) | collective-permute-done | bytes 147488 | tf_op jit(solution)/shard_map/ppermute | solution.py:241
  96.2 0.9 finish.1
  (31 shorter events, 1.1 us)
Async XLA Ops:
  2.7 19.5 %collective-permute-start.2 = (bf16[72,2048]{1,0:T(8,128)(2,1)}, bf16[72,2048]{1,0:T(8,128)(2,1)S(1)}, u32[]{:S(2)}, u32[]{:S(2)}) collective-permute-start(bf16[72,2048]{1,0:T(8,128)(2,1)} %get-tuple-element.36.refs_0_), channel_id=1, source_target_pairs={{0,16},{4,20},{8,24},{12,28},{1,17},{5,21},{9,25},{13,29},{2,18},{... | collective-permute-start | bytes 884744 | tf_op jit(solution)/shard_map/ppermute | solution.py:249
  7.6 18.2 %collective-permute-start = (bf16[72,2048]{1,0:T(8,128)(2,1)}, bf16[72,2048]{1,0:T(8,128)(2,1)S(1)}, u32[]{:S(2)}, u32[]{:S(2)}) collective-permute-start(bf16[72,2048]{1,0:T(8,128)(2,1)} %get-tuple-element.36.refs_0_), channel_id=1, source_target_pairs={{0,4},{4,0},{8,12},{12,8},{16,20},{24,28},{1,5},{5,1},{9,13},{13,9... | collective-permute-start | bytes 884744 | tf_op jit(solution)/shard_map/ppermute | solution.py:241
  11.1 11.1 %collective-permute-start.1 = (bf16[72,1024]{1,0:T(8,128)(2,1)}, bf16[72,1024]{1,0:T(8,128)(2,1)S(1)}, u32[]{:S(2)}, u32[]{:S(2)}) collective-permute-start(bf16[72,1024]{1,0:T(8,128)(2,1)} %get-tuple-element.37), channel_id=1, source_target_pairs={{0,8},{4,12},{8,0},{12,4},{16,24},{20,28},{1,9},{5,13},{9,1},{13,5... | collective-permute-start | bytes 442376 | tf_op jit(solution)/shard_map/ppermute | solution.py:241
  15.6 1.3 %copy-start = (bf16[72,8192]{1,0:T(8,128)(2,1)S(1)}, bf16[72,8192]{1,0:T(8,128)(2,1)}, u32[]{:S(2)}) copy-start(bf16[72,8192]{1,0:T(8,128)(2,1)} %query_ref.1) | copy-start | bytes 3538948
  16.9 1.3 %copy-start.1 = (bf16[72,8192]{1,0:T(8,128)(2,1)S(1)}, bf16[72,8192]{1,0:T(8,128)(2,1)}, u32[]{:S(2)}) copy-start(bf16[72,8192]{1,0:T(8,128)(2,1)} %grad_ref.1) | copy-start | bytes 3538948
  18.2 0.8 copy-start.3
  18.9 0.8 copy-start.5
  19.7 2.6 %copy-start.8 = (bf16[72,1024]{1,0:T(8,128)(2,1)S(1)}, bf16[72,1024]{1,0:T(8,128)(2,1)}, u32[]{:S(2)}) copy-start(bf16[72,1024]{1,0:T(8,128)(2,1)} %get-tuple-element.42) | copy-start | bytes 442372
  19.7 24.1 %copy-start.2 = (bf16[72,2048]{1,0:T(8,128)(2,1)S(1)}, bf16[72,2048]{1,0:T(8,128)(2,1)}, u32[]{:S(2)}) copy-start(bf16[72,2048]{1,0:T(8,128)(2,1)} %get-tuple-element.36.refs_0_) | copy-start | bytes 884740
  19.7 24.1 %copy-start.6 = (f32[72,128]{1,0:T(8,128)S(1)}, f32[72,128]{1,0:T(8,128)}, u32[]{:S(2)}) copy-start(f32[72,128]{1,0:T(8,128)} %get-tuple-element.40.sin_ref.refs_13_.refs_1_) | copy-start | bytes 110596
  19.7 24.1 %copy-start.7 = (s32[2]{0:T(128)S(1)}, s32[2]{0:T(128)}, u32[]{:S(2)}) copy-start(s32[2]{0:T(128)} %counts_ref.3) | copy-start | bytes 28
  22.3 10.8 %collective-permute-start.3 = (bf16[72,1024]{1,0:T(8,128)(2,1)S(1)}, bf16[72,1024]{1,0:T(8,128)(2,1)S(1)}, u32[]{:S(2)}, u32[]{:S(2)}) collective-permute-start(bf16[72,1024]{1,0:T(8,128)(2,1)S(1)} %copy-done.8), channel_id=1, source_target_pairs={{0,8},{4,12},{8,0},{12,4},{16,24},{20,28},{1,9},{5,13},{9,1},{13,5... | collective-permute-start | bytes 442376 | tf_op jit(solution)/shard_map/ppermute | solution.py:241
  25.8 15.6 %collective-permute-start.5 = (bf16[72,2048]{1,0:T(8,128)(2,1)S(1)}, bf16[72,2048]{1,0:T(8,128)(2,1)S(1)}, u32[]{:S(2)}, u32[]{:S(2)}) collective-permute-start(bf16[72,2048]{1,0:T(8,128)(2,1)S(1)} %collective-permute-done.refs_1_), channel_id=1, source_target_pairs={{0,16},{4,20},{8,24},{12,28},{1,17},{5,21},{9,25},{13,29},{2,18},{... | collective-permute-start | bytes 884744 | tf_op jit(solution)/shard_map/ppermute | solution.py:249
  27.3 9.0 %collective-permute-start.8 = (bf16[72,1024]{1,0:T(8,128)(2,1)S(1)}, bf16[72,1024]{1,0:T(8,128)(2,1)S(1)}, u32[]{:S(2)}, u32[]{:S(2)}) collective-permute-start(bf16[72,1024]{1,0:T(8,128)(2,1)S(1)} %collective-permute-done.1.refs_2_), channel_id=1, source_target_pairs={{0,4},{4,0},{8,12},{12,8},{24,28},{28,24},{1,5},{5,1},{9,13},{13,9... | collective-permute-start | bytes 442376 | tf_op jit(solution)/shard_map/ppermute | solution.py:241
  33.1 7.0 %collective-permute-start.4 = (bf16[72,1024]{1,0:T(8,128)(2,1)S(1)}, bf16[72,1024]{1,0:T(8,128)(2,1)S(1)}, u32[]{:S(2)}, u32[]{:S(2)}) collective-permute-start(bf16[72,1024]{1,0:T(8,128)(2,1)S(1)} %collective-permute-done.3.refs_2_), channel_id=1, source_target_pairs={{0,4},{4,0},{8,12},{12,8},{24,28},{28,24},{1,5},{5,1},{9,13},{13,9... | collective-permute-start | bytes 442376 | tf_op jit(solution)/shard_map/ppermute | solution.py:241
  35.0 6.4 %collective-permute-start.9 = (bf16[72,1024]{1,0:T(8,128)(2,1)S(1)}, bf16[72,1024]{1,0:T(8,128)(2,1)S(1)}, u32[]{:S(2)}, u32[]{:S(2)}) collective-permute-start(bf16[72,1024]{1,0:T(8,128)(2,1)S(1)} %collective-permute-done.1.refs_2_), channel_id=1, source_target_pairs={{0,16},{4,20},{8,24},{12,28},{1,17},{5,21},{9,25},{13,29},{2,18},{... | collective-permute-start | bytes 442376 | tf_op jit(solution)/shard_map/ppermute | solution.py:249
  36.3 7.4 %collective-permute-start.10 = (bf16[72,1024]{1,0:T(8,128)(2,1)S(1)}, bf16[72,1024]{1,0:T(8,128)(2,1)S(1)}, u32[]{:S(2)}, u32[]{:S(2)}) collective-permute-start(bf16[72,1024]{1,0:T(8,128)(2,1)S(1)} %collective-permute-done.8.refs_3_), channel_id=1, source_target_pairs={{0,16},{4,20},{8,24},{12,28},{1,17},{5,21},{9,25},{13,29},{2,18},{... | collective-permute-start | bytes 442376 | tf_op jit(solution)/shard_map/ppermute | solution.py:249
  37.6 15.3 %collective-permute-start.6 = (bf16[72,1024]{1,0:T(8,128)(2,1)S(1)}, bf16[72,1024]{1,0:T(8,128)(2,1)S(1)}, u32[]{:S(2)}, u32[]{:S(2)}) collective-permute-start(bf16[72,1024]{1,0:T(8,128)(2,1)S(1)} %collective-permute-done.3.refs_2_), channel_id=1, source_target_pairs={{0,16},{4,20},{8,24},{12,28},{1,17},{5,21},{9,25},{13,29},{2,18},{... | collective-permute-start | bytes 442376 | tf_op jit(solution)/shard_map/ppermute | solution.py:249
  40.1 12.8 %collective-permute-start.7 = (bf16[72,1024]{1,0:T(8,128)(2,1)S(1)}, bf16[72,1024]{1,0:T(8,128)(2,1)S(1)}, u32[]{:S(2)}, u32[]{:S(2)}) collective-permute-start(bf16[72,1024]{1,0:T(8,128)(2,1)S(1)} %collective-permute-done.4.refs_3_), channel_id=1, source_target_pairs={{0,16},{4,20},{8,24},{12,28},{1,17},{5,21},{9,25},{13,29},{2,18},{... | collective-permute-start | bytes 442376 | tf_op jit(solution)/shard_map/ppermute | solution.py:249
  51.6 17.4 %collective-permute-start.11 = (bf16[4,72,1024]{2,1,0:T(8,128)(2,1)S(1)}, bf16[4,72,1024]{2,1,0:T(8,128)(2,1)S(1)}, u32[]{:S(2)}, u32[]{:S(2)}) collective-permute-start(bf16[4,72,1024]{2,1,0:T(8,128)(2,1)S(1)} %get-tuple-element.55), channel_id=1, source_target_pairs={{16,0},{20,4},{24,8},{28,12},{17,1},{21,5},{25,9},{29,13},{18,2},{... | collective-permute-start | bytes 1769480 | tf_op jit(solution)/shard_map/ppermute | solution.py:249
  60.8 18.5 %collective-permute-start.15 = (bf16[4,72,1024]{2,1,0:T(8,128)(2,1)S(1)}, bf16[4,72,1024]{2,1,0:T(8,128)(2,1)S(1)}, u32[]{:S(2)}, u32[]{:S(2)}) collective-permute-start(bf16[4,72,1024]{2,1,0:T(8,128)(2,1)S(1)} %get-tuple-element.61), channel_id=1, source_target_pairs={{16,0},{20,4},{24,8},{28,12},{17,1},{21,5},{25,9},{29,13},{18,2},{... | collective-permute-start | bytes 1769480 | tf_op jit(solution)/shard_map/ppermute | solution.py:249
  69.1 15.6 %collective-permute-start.12 = (bf16[72,1024]{1,0:T(8,128)(2,1)S(1)}, bf16[72,1024]{1,0:T(8,128)(2,1)S(1)}, u32[]{:S(2)}, u32[]{:S(2)}) collective-permute-start(bf16[72,1024]{1,0:T(8,128)(2,1)S(1)} %get-tuple-element.57), channel_id=1, source_target_pairs={{0,4},{4,0},{8,12},{12,8},{20,16},{28,24},{1,5},{5,1},{9,13},{13,9... | collective-permute-start | bytes 442376 | tf_op jit(solution)/shard_map/ppermute | solution.py:241
  72.5 17.1 %collective-permute-start.13 = (bf16[72,1024]{1,0:T(8,128)(2,1)S(1)}, bf16[72,1024]{1,0:T(8,128)(2,1)S(1)}, u32[]{:S(2)}, u32[]{:S(2)}) collective-permute-start(bf16[72,1024]{1,0:T(8,128)(2,1)S(1)} %get-tuple-element.58), channel_id=1, source_target_pairs={{0,8},{4,12},{8,0},{12,4},{24,16},{28,20},{1,9},{5,13},{9,1},{13,5... | collective-permute-start | bytes 442376 | tf_op jit(solution)/shard_map/ppermute | solution.py:241
  74.4 15.2 %collective-permute-start.14 = (bf16[72,1024]{1,0:T(8,128)(2,1)S(1)}, bf16[72,1024]{1,0:T(8,128)(2,1)S(1)}, u32[]{:S(2)}, u32[]{:S(2)}) collective-permute-start(bf16[72,1024]{1,0:T(8,128)(2,1)S(1)} %get-tuple-element.59), channel_id=1, source_target_pairs={{0,12},{4,8},{8,4},{12,0},{24,20},{28,16},{1,13},{5,9},{9,5},{13,1... | collective-permute-start | bytes 442376 | tf_op jit(solution)/shard_map/ppermute | solution.py:241
  79.3 16.9 %copy-start.4 = (f32[72,128]{1,0:T(8,128)S(1)}, f32[72,128]{1,0:T(8,128)}, u32[]{:S(2)}) copy-start(f32[72,128]{1,0:T(8,128)} %get-tuple-element.39.cos_ref.refs_0_) | copy-start | bytes 110596
  79.4 10.2 %collective-permute-start.16 = (bf16[72,1024]{1,0:T(8,128)(2,1)S(1)}, bf16[72,1024]{1,0:T(8,128)(2,1)S(1)}, u32[]{:S(2)}, u32[]{:S(2)}) collective-permute-start(bf16[72,1024]{1,0:T(8,128)(2,1)S(1)} %get-tuple-element.63), channel_id=1, source_target_pairs={{0,4},{4,0},{8,12},{12,8},{20,16},{28,24},{1,5},{5,1},{9,13},{13,9... | collective-permute-start | bytes 442376 | tf_op jit(solution)/shard_map/ppermute | solution.py:241
  81.9 14.3 %collective-permute-start.17 = (bf16[72,1024]{1,0:T(8,128)(2,1)S(1)}, bf16[72,1024]{1,0:T(8,128)(2,1)S(1)}, u32[]{:S(2)}, u32[]{:S(2)}) collective-permute-start(bf16[72,1024]{1,0:T(8,128)(2,1)S(1)} %get-tuple-element.64), channel_id=1, source_target_pairs={{0,8},{4,12},{8,0},{12,4},{24,16},{28,20},{1,9},{5,13},{9,1},{13,5... | collective-permute-start | bytes 442376 | tf_op jit(solution)/shard_map/ppermute | solution.py:241
  84.7 11.5 %collective-permute-start.18 = (bf16[72,1024]{1,0:T(8,128)(2,1)S(1)}, bf16[72,1024]{1,0:T(8,128)(2,1)S(1)}, u32[]{:S(2)}, u32[]{:S(2)}) collective-permute-start(bf16[72,1024]{1,0:T(8,128)(2,1)S(1)} %get-tuple-element.65), channel_id=1, source_target_pairs={{0,12},{4,8},{8,4},{12,0},{24,20},{28,16},{1,13},{5,9},{9,5},{13,1... | collective-permute-start | bytes 442376 | tf_op jit(solution)/shard_map/ppermute | solution.py:241

commit v4 on v3

--- a/solution.py
+++ b/solution.py
@@ -14,7 +14,8 @@
 GROUP = QUERY_HEADS // KEY_VALUE_HEADS
 ROPE_BASE = 500000.0
 SCORE_SCALE = 1.0 / float(np.sqrt(HEAD_WIDTH))
-LOG2_E = 1.4426950408889634
+SCORE_TO_LOG2 = SCORE_SCALE * 1.4426950408889634
+MASK_ROWS = 128
 CHUNKS = 2
 HEADS_PER_CHUNK = KEY_VALUE_HEADS // CHUNKS
 CHUNK_COLS = HEADS_PER_CHUNK * HEAD_WIDTH
@@ -103,7 +104,7 @@
     outs = refs[blocks + 6 + 2 * has_alias :]
     out_ref, grad_ref = outs[:2]
     part_refs = outs[2 : 2 + seq_count]
-    bias_ref, live_ref = outs[2 + seq_count :]
+    key_mask_ref, query_mask_ref, live_ref = outs[2 + seq_count :]
     padded = kv_refs[0].shape[0]
     query_rows = GROUP * padded
     step = pl.program_id(0)
@@ -112,8 +113,9 @@
 
     @pl.when(step == 0)
     def _():
-        key_row = lax.broadcasted_iota(jnp.int32, (padded, query_rows), 0)
-        query_row = lax.rem(lax.broadcasted_iota(jnp.int32, (padded, query_rows), 1), padded)
+        shape = (padded, MASK_ROWS)
+        key_row = lax.broadcasted_iota(jnp.int32, shape, 0)
+        mask_row = lax.broadcasted_iota(jnp.int32, shape, 1)
         for block in range(blocks):
             seq_offset, head_offset = divmod(block, head_count)
             seq_from = jnp.bitwise_xor(seq_index, seq_offset)
@@ -121,11 +123,18 @@
             rank = seq_from * head_count + head_from
             limit = jnp.minimum(counts_ref[seq_from] - head_from * rows, rows)
             limit = jnp.where(rank <= my_rank, limit, 0)
-            allowed = key_row < limit
+            barred = (mask_row == MASK_ROWS - 1) & (key_row >= limit)
             if block == 0:
-                allowed = allowed & (key_row <= query_row)
-                live_ref[...] = (query_row[:8] < limit).astype(jnp.float32)
-            bias_ref[block * padded : (block + 1) * padded, :] = jnp.where(allowed, 0.0, -1e30)
+                barred = barred | ((mask_row < padded) & (key_row > mask_row))
+            piece = slice(block * padded, (block + 1) * padded)
+            key_mask_ref[piece, :] = jnp.where(barred, -1e30, 0.0)
+        shape = (MASK_ROWS, query_rows)
+        query_row = lax.rem(lax.broadcasted_iota(jnp.int32, shape, 1), padded)
+        mask_row = lax.broadcasted_iota(jnp.int32, shape, 0)
+        met = (mask_row == query_row) | (mask_row == MASK_ROWS - 1)
+        query_mask_ref[...] = jnp.where(met, 1.0, 0.0).astype(jnp.bfloat16)
+        limit = jnp.minimum(counts_ref[seq_index] - head_index * rows, rows)
+        live_ref[...] = (query_row[:8] < limit).astype(jnp.float32)
 
     def lanes(first, place):
         start = pl.multiple_of((first + step * STEP_HEADS + place) * HEAD_WIDTH, HEAD_WIDTH)
@@ -138,21 +147,31 @@
 
     heads = range(STEP_HEADS)
     keys, values = [gathered(0, p) for p in heads], [gathered(HEADS_PER_CHUNK, p) for p in heads]
-    bias, live = bias_ref[...], live_ref[0:1, :]
-    scores = [dot(keys[p][0], qt_ref[p]) * (SCORE_SCALE * LOG2_E) + bias for p in heads]
-    dprobs, probs, probs_low = [], [], []
+    key_mask, query_mask = key_mask_ref[...].astype(jnp.bfloat16), query_mask_ref[...]
+    scores = [
+        dot(
+            jnp.concatenate([keys[p][0], key_mask], 1), jnp.concatenate([qt_ref[p], query_mask], 0)
+        )
+        for p in heads
+    ]
+    inverse, weights, dprobs = [], [], []
     for p in heads:
-        weights = jnp.exp2(scores[p] - jnp.max(scores[p], 0, keepdims=True))
-        probs.append(weights * (live / jnp.sum(weights, 0, keepdims=True)))
-        probs_low.append(probs[p].astype(jnp.bfloat16))
+        top = jnp.max(scores[p], 0, keepdims=True) * SCORE_TO_LOG2
+        wide = jnp.exp2(scores[p] * SCORE_TO_LOG2 - top)
+        inverse.append(live_ref[...] / jnp.sum(wide, 0, keepdims=True))
+        weights.append(wide.astype(jnp.bfloat16))
         dprobs.append(dot(values[p][0], gt_ref[p]))
     outs_t, value_parts, dscores = [], [], []
     for p in heads:
-        outs_t.append(dot(values[p][1], probs_low[p]))
-        value_parts.append(dot(probs_low[p], g_ref[p]))
+        factor = inverse[p][0:1]
+        outs_t.append(dot(values[p][1], weights[p]) * factor)
+        scaled = (g_ref[p].astype(jnp.float32) * inverse[p].T[:, 0:1]).astype(jnp.bfloat16)
+        value_parts.append(dot(weights[p], scaled))
         out_low = outs_t[p].astype(jnp.bfloat16).astype(jnp.float32)
-        delta = jnp.sum(gt_ref[p].astype(jnp.float32) * out_low, 0, keepdims=True)
-        dscores.append((probs[p] * (dprobs[p] - delta)).astype(jnp.bfloat16))
+        delta = jnp.sum(gt_ref[p].astype(jnp.float32) * out_low, 0, keepdims=True) * factor
+        dscores.append(
+            (weights[p].astype(jnp.float32) * (dprobs[p] * factor - delta)).astype(jnp.bfloat16)
+        )
     grads_t = [dot(keys[p][1], dscores[p]) * SCORE_SCALE for p in heads]
     key_parts = [dot(dscores[p], q_ref[p]) * SCORE_SCALE for p in heads]
 
@@ -173,30 +192,24 @@
             )
 
 
-def combine(seq_count, head_count, *refs):
-    part_refs, base_ref, send_refs = refs[:seq_count], refs[seq_count], refs[seq_count + 1 :]
-    for offset in range(head_count):
-        total = part_refs[0][offset].astype(jnp.float32)
-        for ref in part_refs[1:]:
-            total = total + ref[offset].astype(jnp.float32)
-        if offset == 0:
-            base_ref[...] = total
-        else:
-            send_refs[offset - 1][...] = total.astype(jnp.bfloat16)
-
-
-def finish(head_count, *refs):
-    cosine, sine = refs[0][...], refs[1][...]
-    key_ref, value_ref = refs[-2:]
+def combine(*refs):
+    *sum_refs, keep_ref, send_ref = refs
+    for place in range(keep_ref.shape[0]):
+        for offset, ref in ((2 * place, keep_ref), (2 * place + 1, send_ref)):
+            total = sum(sum_ref[offset].astype(jnp.float32) for sum_ref in sum_refs)
+            ref[place] = total.astype(ref.dtype)
+
+
+def finish(cos_ref, sin_ref, *refs):
+    cosine, sine = cos_ref[...], sin_ref[...]
+    *sum_refs, key_ref, value_ref = refs
     for chunk in range(CHUNKS):
-        mine = refs[2 + chunk * head_count : 2 + (chunk + 1) * head_count]
+        mine = sum_refs[2 * chunk : 2 * chunk + 2]
         for place in range(HEADS_PER_CHUNK):
+            cols = head_cols(chunk * HEADS_PER_CHUNK + place)
             here, there = head_cols(place), head_cols(HEADS_PER_CHUNK + place)
-            key_total, value_total = mine[0][:, here], mine[0][:, there]
-            for ref in mine[1:]:
-                key_total = key_total + ref[:, here].astype(jnp.float32)
-                value_total = value_total + ref[:, there].astype(jnp.float32)
-            cols = head_cols(chunk * HEADS_PER_CHUNK + place)
+            key_total = sum(ref[0, :, here].astype(jnp.float32) for ref in mine)
+            value_total = sum(ref[0, :, there].astype(jnp.float32) for ref in mine)
             key_ref[:, cols] = rope_back(key_total, cosine, sine).astype(jnp.bfloat16)
             value_ref[:, cols] = value_total.astype(jnp.bfloat16)
 
@@ -232,13 +245,24 @@
     def rank_of(s, z):
         return s * head_count + z
 
-    def along_head(x, offset, upward, held=0):
-        pairs = []
-        for s, z in ranks:
-            other = z ^ offset
-            if s < seq_count - 1 or ((z ^ held) < other) == upward:
-                pairs.append((rank_of(s, z), rank_of(s, other)))
+    def along_head(x, offset, wanted):
+        pairs = [
+            (rank_of(s, z), rank_of(s, z ^ offset))
+            for s, z in ranks
+            if s < seq_count - 1 or wanted(z, z ^ offset)
+        ]
         return lax.ppermute(x, ("seq", "head"), pairs)
+
+    def gather_step(x, offset, held):
+        return along_head(x, offset, lambda z, other: z ^ held < other)
+
+    def halving_step(x, bit):
+        def wanted(z, other):
+            return max(z ^ m for m in range(bit)) >= min(
+                other ^ m for m in range(0, head_count, 2 * bit)
+            )
+
+        return along_head(x, bit, wanted)
 
     def along_seq(x, offset, upward):
         pairs = [
@@ -282,25 +306,32 @@
 
     bits = [1 << b for b in reversed(range((head_count - 1).bit_length()))]
     later = range(1, seq_count)
-    chunked = [{bits[0]: along_head(own[0], bits[0], True)}]
+    chunked = [{bits[0]: gather_step(own[0], bits[0], 0)}]
     far = {(a, 0): along_seq(whole, a, True) for a in later}
-    nearest = along_head(whole, 1, True)
+    nearest = gather_step(whole, 1, 0)
     chunked[0][bits[0]], own[1:], cosine_later, far = lax.optimization_barrier(
         (chunked[0][bits[0]], own[1:], cosine_later, far)
     )
-    chunked += [{bits[0]: along_head(x, bits[0], True)} for x in own[1:]]
+    chunked += [{bits[0]: gather_step(x, bits[0], 0)} for x in own[1:]]
     far.update({(a, 1): along_seq(nearest, a, True) for a in later})
+    top = {}
+    for c, near in enumerate(chunked):
+        near[bits[0]], top = lax.optimization_barrier((near[bits[0]], top))
+        top.update({(a, c): along_seq(near[bits[0]], a, True) for a in later})
     gathered = []
     for c, near in enumerate(chunked):
         near[0] = own[c]
         for bit in bits[1:]:
             near.update(
-                {j ^ bit: along_head(x, bit, True, j) for j, x in near.items() if j ^ bit > 1}
+                {j ^ bit: gather_step(x, bit, j) for j, x in near.items() if j ^ bit > 1}
             )
         blocks_here = [whole, nearest] + [near[j] for j in range(2, head_count)]
         for a in later:
             blocks_here += [far[a, 0], far[a, 1]]
-            blocks_here += [along_seq(near[j], a, True) for j in range(2, head_count)]
+            blocks_here += [
+                top[a, c] if j == bits[0] else along_seq(near[j], a, True)
+                for j in range(2, head_count)
+            ]
         gathered.append(blocks_here)
 
     wide_outs = ()
@@ -325,7 +356,8 @@
             + [pl.BlockSpec(memory_space=pl.ANY)] * (2 * has_alias),
             out_specs=[row_part, row_part] + [part_block] * seq_count,
             scratch_shapes=[
-                pltpu.VMEM((blocks * padded, query_rows), f32),
+                pltpu.VMEM((blocks * padded, MASK_ROWS), f32),
+                pltpu.VMEM((MASK_ROWS, query_rows), bf16),
                 pltpu.VMEM((8, query_rows), f32),
             ],
             input_output_aliases={blocks + 7: 0, blocks + 8: 1} if has_alias else {},
@@ -335,22 +367,32 @@
         )(counts, *gathered[chunk], *stacked, cosine_later, sine, *wide_outs)
         wide_outs = out[:2]
         parts = [out[2]] + [along_seq(out[2 + a], a, False) for a in range(1, seq_count)]
-        base, *sends = pl.pallas_call(
-            functools.partial(combine, seq_count, head_count),
-            out_shape=[shape((padded, 2 * CHUNK_COLS), f32)] + [piece] * (head_count - 1),
-            in_specs=[VMEM] * seq_count,
-            out_specs=[VMEM] * head_count,
-            cost_estimate=cost(2),
-            compiler_params=params(8),
-            name="combine",
-        )(*parts)
-        summed += [base] + [along_head(x, j + 1, False) for j, x in enumerate(sends)]
+        if chunk:
+            parts[-1], send = lax.optimization_barrier((parts[-1], send))
+            summed.append(halving_step(send, head_count // 2))
+        bit = 1
+        while bit < head_count:
+            left = (head_count // (2 * bit), padded, 2 * CHUNK_COLS)
+            keep, send = pl.pallas_call(
+                combine,
+                out_shape=[shape(left, f32), shape(left, bf16)],
+                in_specs=[VMEM] * len(parts),
+                out_specs=[VMEM] * 2,
+                cost_estimate=cost(2),
+                compiler_params=params(8),
+                name="combine",
+            )(*parts)
+            if 2 * bit < head_count:
+                parts = [keep, halving_step(send, bit)]
+            bit *= 2
+        summed.append(keep)
+    summed.append(halving_step(send, head_count // 2))
 
     narrow = shape((padded, KEY_VALUE_HEADS * HEAD_WIDTH), bf16)
     key_grad, value_grad = pl.pallas_call(
-        functools.partial(finish, head_count),
+        finish,
         out_shape=[narrow, narrow],
-        in_specs=[VMEM] * (2 + CHUNKS * head_count),
+        in_specs=[VMEM] * (2 + CHUNKS * 2),
         out_specs=[VMEM, VMEM],
         cost_estimate=cost(2),
         compiler_params=params(8),

time: 97.9 us -> 98.6 us (level)
  waiting for transfers between devices: 19.5 us -> 30.8 us
  starting transfers between devices: 51.1 us -> 40 us
    ppermute x11 -> x9, waiting for transfers between devices: 10.2 us -> 23.3 us  [along_head(): return lax.ppermute(x, ('seq', 'head'), pairs)]
    ppermute x11 -> x9, starting transfers between devices: 37 us -> 26.1 us  [along_head(): return lax.ppermute(x, ('seq', 'head'), pairs)]
    ppermute x8, waiting for transfers between devices: 9.26 us -> 7.46 us  [along_seq(): return lax.ppermute(x, ('seq', 'head'), pairs)]
  transfers between devices with their start and end apart: 19 -> 17, of which waited for: 5 -> 8; matrix products, arithmetic and copies ran while one was open for 0% -> 0% of each run, Pallas kernels for 19% -> 19%
where the time goes in v4:
time: 98.6 us; the launch traced here: 97.9 us
  starting transfers between devices  40 us (41%)
  waiting for transfers between devices  30.8 us (31%)
  Pallas kernels  22.1 us (22%)
  local copies, waits for them, and re-layouts  4.09 us (4%)
    ppermute x9, starting transfers between devices, along_head(): return lax.ppermute(x, ('seq', 'head'), pairs)  26.1 us
    ppermute x9, waiting for transfers between devices, along_head(): return lax.ppermute(x, ('seq', 'head'), pairs)  23.3 us
    pallas_call x2, Pallas kernels, shards(): pl.pallas_call(functools.partial(attend, seq_count, head_count, rows, has...  16.3 us
    ppermute x8, starting transfers between devices, along_seq(): return lax.ppermute(x, ('seq', 'head'), pairs)  13.9 us
    ppermute x8, waiting for transfers between devices, along_seq(): return lax.ppermute(x, ('seq', 'head'), pairs)  7.46 us
    unnamed x18, local copies, waits for them, and re-layouts  4.09 us
    pallas_call x1, Pallas kernels, shards(): pl.pallas_call(prepare_queries, grid=(KEY_VALUE_HEADS,), out_shape=[tall,...  2.53 us
    pallas_call x1, Pallas kernels, shards(): pl.pallas_call(functools.partial(prepare_keys, rows), out_shape=[shape((p...  2.1 us
  transfers between devices with their start and end apart: 17, of which 8 were waited for; matrix products, arithmetic and copies ran while one was open for 0% of the time, Pallas kernels for 19%

profile of v4, /device:TPU:0, one launch (start us, length us, event | category | flops | bytes accessed | tf_op | source)
XLA Modules:
  0.0 97.9 jit_solution(1055140809295520140)
XLA Ops:
  0.6 2.1 %prepare_keys.1 = (bf16[72,2048]{1,0:T(8,128)(2,1)}, bf16[72,1024]{1,0:T(8,128)(2,1)}, bf16[72,1024]{1,0:T(8,128)(2,1)}, f32[72,128]{1,0:T(8,128)}, f32[72,128]{1,0:T(8,128)}) custom-call(s32[576]{0:T(1024)} %pos_ref.1, bf16[72,1024]{1,0:T(8,128)(2,1)} %key_ref.1, bf16[72,1024]{1,0:T(8,128)(2,1)} %value_ref.1), custom_call_target="tpu_custom_call" | custom-call | tf_op jit(solution)/shard_map/prepare_keys/pallas_call | solution.py:277
  2.7 4.9 %collective-permute-start.2 = (bf16[72,2048]{1,0:T(8,128)(2,1)}, bf16[72,2048]{1,0:T(8,128)(2,1)S(1)}, u32[]{:S(2)}, u32[]{:S(2)}) collective-permute-start(bf16[72,2048]{1,0:T(8,128)(2,1)} %get-tuple-element.40.refs_0_), channel_id=1, source_target_pairs={{0,16},{4,20},{8,24},{12,28},{1,17},{5,21},{9,25},{13,29},{2,18},{... | collective-permute-start | bytes 884744 | tf_op jit(solution)/shard_map/ppermute | solution.py:273
  7.6 3.5 %collective-permute-start = (bf16[72,2048]{1,0:T(8,128)(2,1)}, bf16[72,2048]{1,0:T(8,128)(2,1)S(1)}, u32[]{:S(2)}, u32[]{:S(2)}) collective-permute-start(bf16[72,2048]{1,0:T(8,128)(2,1)} %get-tuple-element.40.refs_0_), channel_id=1, source_target_pairs={{0,4},{4,0},{8,12},{12,8},{16,20},{24,28},{1,5},{5,1},{9,13},{13,9... | collective-permute-start | bytes 884744 | tf_op jit(solution)/shard_map/ppermute | solution.py:254
  11.1 4.5 %collective-permute-start.1 = (bf16[72,1024]{1,0:T(8,128)(2,1)}, bf16[72,1024]{1,0:T(8,128)(2,1)S(1)}, u32[]{:S(2)}, u32[]{:S(2)}) collective-permute-start(bf16[72,1024]{1,0:T(8,128)(2,1)} %get-tuple-element.41), channel_id=1, source_target_pairs={{0,8},{4,12},{8,0},{12,4},{16,24},{20,28},{1,9},{5,13},{9,1},{13,5... | collective-permute-start | bytes 442376 | tf_op jit(solution)/shard_map/ppermute | solution.py:254
  15.6 1.3 %copy-done = bf16[72,8192]{1,0:T(8,128)(2,1)S(1)} copy-done((bf16[72,8192]{1,0:T(8,128)(2,1)S(1)}, bf16[72,8192]{1,0:T(8,128)(2,1)}, u32[]{:S(2)}) %copy-start) | copy-done | bytes 1179672
  16.9 1.3 %copy-done.1 = bf16[72,8192]{1,0:T(8,128)(2,1)S(1)} copy-done((bf16[72,8192]{1,0:T(8,128)(2,1)S(1)}, bf16[72,8192]{1,0:T(8,128)(2,1)}, u32[]{:S(2)}) %copy-start.1) | copy-done | bytes 1179672
  18.2 0.8 copy-done.3
  19.7 2.5 %prepare_queries.1 = (bf16[8,576,128]{2,1,0:T(8,128)(2,1)S(1)}, bf16[8,128,576]{2,1,0:T(8,128)(2,1)S(1)}, bf16[8,576,128]{2,1,0:T(8,128)(2,1)S(1)}, bf16[8,128,576]{2,1,0:T(8,128)(2,1)S(1)}, f32[72,128]{1,0:T(8,128)S(1)}) custom-call(bf16[72,8192]{1,0:T(8,128)(2,1)S(1)} %copy-done, bf16[72,8192]{1,0:T(8,128)(2,1)S(1)} %copy-done.1, f32[72,128]{1,0:T(8,128)S(1)} %copy-done.3, ...), custom_call_target="tpu_custom_call" | custom-call | flops 8071000064 | bytes 25830000 | tf_op jit(solution)/shard_map/prepare_queries/pallas_call | solution.py:295
  22.3 1.3 %collective-permute-start.4 = (bf16[72,1024]{1,0:T(8,128)(2,1)S(1)}, bf16[72,1024]{1,0:T(8,128)(2,1)S(1)}, u32[]{:S(2)}, u32[]{:S(2)}) collective-permute-start(bf16[72,1024]{1,0:T(8,128)(2,1)S(1)} %collective-permute-done.1.refs_2_), channel_id=1, source_target_pairs={{0,16},{4,20},{8,24},{12,28},{1,17},{5,21},{9,25},{13,29},{2,18},{... | collective-permute-start | bytes 442376 | tf_op jit(solution)/shard_map/ppermute | solution.py:273
  23.6 3.7 %collective-permute-start.3 = (bf16[72,1024]{1,0:T(8,128)(2,1)S(1)}, bf16[72,1024]{1,0:T(8,128)(2,1)S(1)}, u32[]{:S(2)}, u32[]{:S(2)}) collective-permute-start(bf16[72,1024]{1,0:T(8,128)(2,1)S(1)} %copy-done.8), channel_id=1, source_target_pairs={{0,8},{4,12},{8,0},{12,4},{16,24},{20,28},{1,9},{5,13},{9,1},{13,5... | collective-permute-start | bytes 442376 | tf_op jit(solution)/shard_map/ppermute | solution.py:254
  27.3 3.3 %collective-permute-start.9 = (bf16[72,1024]{1,0:T(8,128)(2,1)S(1)}, bf16[72,1024]{1,0:T(8,128)(2,1)S(1)}, u32[]{:S(2)}, u32[]{:S(2)}) collective-permute-start(bf16[72,1024]{1,0:T(8,128)(2,1)S(1)} %collective-permute-done.1.refs_2_), channel_id=1, source_target_pairs={{0,4},{4,0},{8,12},{12,8},{24,28},{28,24},{1,5},{5,1},{9,13},{13,9... | collective-permute-start | bytes 442376 | tf_op jit(solution)/shard_map/ppermute | solution.py:254
  30.7 1.3 %collective-permute-start.6 = (bf16[72,2048]{1,0:T(8,128)(2,1)S(1)}, bf16[72,2048]{1,0:T(8,128)(2,1)S(1)}, u32[]{:S(2)}, u32[]{:S(2)}) collective-permute-start(bf16[72,2048]{1,0:T(8,128)(2,1)S(1)} %collective-permute-done.refs_1_), channel_id=1, source_target_pairs={{0,16},{4,20},{8,24},{12,28},{1,17},{5,21},{9,25},{13,29},{2,18},{... | collective-permute-start | bytes 884744 | tf_op jit(solution)/shard_map/ppermute | solution.py:273
  32.0 2.3 %collective-permute-done.3.refs_2_ = bf16[72,1024]{1,0:T(8,128)(2,1)S(1)} collective-permute-done((bf16[72,1024]{1,0:T(8,128)(2,1)S(1)}, bf16[72,1024]{1,0:T(8,128)(2,1)S(1)}, u32[]{:S(2)}, u32[]{:S(2)}) %collective-permute-start.3) | collective-permute-done | bytes 147488 | tf_op jit(solution)/shard_map/ppermute | solution.py:254
  34.3 2.3 %collective-permute-start.5 = (bf16[72,1024]{1,0:T(8,128)(2,1)S(1)}, bf16[72,1024]{1,0:T(8,128)(2,1)S(1)}, u32[]{:S(2)}, u32[]{:S(2)}) collective-permute-start(bf16[72,1024]{1,0:T(8,128)(2,1)S(1)} %collective-permute-done.3.refs_2_), channel_id=1, source_target_pairs={{0,4},{4,0},{8,12},{12,8},{24,28},{28,24},{1,5},{5,1},{9,13},{13,9... | collective-permute-start | bytes 442376 | tf_op jit(solution)/shard_map/ppermute | solution.py:254
  36.7 1.3 %collective-permute-start.10 = (bf16[72,1024]{1,0:T(8,128)(2,1)S(1)}, bf16[72,1024]{1,0:T(8,128)(2,1)S(1)}, u32[]{:S(2)}, u32[]{:S(2)}) collective-permute-start(bf16[72,1024]{1,0:T(8,128)(2,1)S(1)} %collective-permute-done.9.refs_3_), channel_id=1, source_target_pairs={{0,16},{4,20},{8,24},{12,28},{1,17},{5,21},{9,25},{13,29},{2,18},{... | collective-permute-start | bytes 442376 | tf_op jit(solution)/shard_map/ppermute | solution.py:273
  38.0 1.3 %collective-permute-start.7 = (bf16[72,1024]{1,0:T(8,128)(2,1)S(1)}, bf16[72,1024]{1,0:T(8,128)(2,1)S(1)}, u32[]{:S(2)}, u32[]{:S(2)}) collective-permute-start(bf16[72,1024]{1,0:T(8,128)(2,1)S(1)} %collective-permute-done.3.refs_2_), channel_id=1, source_target_pairs={{0,16},{4,20},{8,24},{12,28},{1,17},{5,21},{9,25},{13,29},{2,18},{... | collective-permute-start | bytes 442376 | tf_op jit(solution)/shard_map/ppermute | solution.py:273
  39.3 2.1 %collective-permute-done.5.refs_3_ = bf16[72,1024]{1,0:T(8,128)(2,1)S(1)} collective-permute-done((bf16[72,1024]{1,0:T(8,128)(2,1)S(1)}, bf16[72,1024]{1,0:T(8,128)(2,1)S(1)}, u32[]{:S(2)}, u32[]{:S(2)}) %collective-permute-start.5) | collective-permute-done | bytes 147488 | tf_op jit(solution)/shard_map/ppermute | solution.py:254
  41.3 1.3 %collective-permute-start.8 = (bf16[72,1024]{1,0:T(8,128)(2,1)S(1)}, bf16[72,1024]{1,0:T(8,128)(2,1)S(1)}, u32[]{:S(2)}, u32[]{:S(2)}) collective-permute-start(bf16[72,1024]{1,0:T(8,128)(2,1)S(1)} %collective-permute-done.5.refs_3_), channel_id=1, source_target_pairs={{0,16},{4,20},{8,24},{12,28},{1,17},{5,21},{9,25},{13,29},{2,18},{... | collective-permute-start | bytes 442376 | tf_op jit(solution)/shard_map/ppermute | solution.py:273
  42.7 8.1 %attend.2 = (bf16[72,8192]{1,0:T(8,128)(2,1)}, bf16[72,8192]{1,0:T(8,128)(2,1)}, bf16[4,72,1024]{2,1,0:T(8,128)(2,1)S(1)}, bf16[4,72,1024]{2,1,0:T(8,128)(2,1)S(1)}) custom-call(s32[2]{0:T(128)S(1)} %copy-done.7, bf16[72,2048]{1,0:T(8,128)(2,1)S(1)} %copy-done.2, bf16[72,2048]{1,0:T(8,128)(2,1)S(1)} %collective-permute-done.refs_1_, ...), custom_call_target="tpu_custom_call" | custom-call | flops 11530000384 | bytes 36900000 | tf_op jit(solution)/shard_map/attend/pallas_call | solution.py:348
  50.8 1.3 %collective-permute-start.11 = (bf16[4,72,1024]{2,1,0:T(8,128)(2,1)S(1)}, bf16[4,72,1024]{2,1,0:T(8,128)(2,1)S(1)}, u32[]{:S(2)}, u32[]{:S(2)}) collective-permute-start(bf16[4,72,1024]{2,1,0:T(8,128)(2,1)S(1)} %get-tuple-element.61), channel_id=1, source_target_pairs={{16,0},{20,4},{24,8},{28,12},{17,1},{21,5},{25,9},{29,13},{18,2},{... | collective-permute-start | bytes 1769480 | tf_op jit(solution)/shard_map/ppermute | solution.py:273
  52.1 8.1 %attend.3 = (bf16[72,8192]{1,0:T(8,128)(2,1)}, bf16[72,8192]{1,0:T(8,128)(2,1)}, bf16[4,72,1024]{2,1,0:T(8,128)(2,1)S(1)}, bf16[4,72,1024]{2,1,0:T(8,128)(2,1)S(1)}) custom-call(s32[2]{0:T(128)S(1)} %copy-done.7, bf16[72,2048]{1,0:T(8,128)(2,1)S(1)} %copy-done.2, ...), custom_call_target="tpu_custom_call", output_to_operand_aliasing={{0}: (15, {}), {1}: (16, {})} | custom-call | flops 11530000384 | bytes 36900000 | tf_op jit(solution)/shard_map/attend/pallas_call | solution.py:348
  60.3 1.3 %collective-permute-start.13 = (bf16[4,72,1024]{2,1,0:T(8,128)(2,1)S(1)}, bf16[4,72,1024]{2,1,0:T(8,128)(2,1)S(1)}, u32[]{:S(2)}, u32[]{:S(2)}) collective-permute-start(bf16[4,72,1024]{2,1,0:T(8,128)(2,1)S(1)} %get-tuple-element.65), channel_id=1, source_target_pairs={{16,0},{20,4},{24,8},{28,12},{17,1},{21,5},{25,9},{29,13},{18,2},{... | collective-permute-start | bytes 1769480 | tf_op jit(solution)/shard_map/ppermute | solution.py:273
  61.5 6.7 %collective-permute-done.11.refs_1_ = bf16[4,72,1024]{2,1,0:T(8,128)(2,1)S(1)} collective-permute-done((bf16[4,72,1024]{2,1,0:T(8,128)(2,1)S(1)}, bf16[4,72,1024]{2,1,0:T(8,128)(2,1)S(1)}, u32[]{:S(2)}, u32[]{:S(2)}) %collective-permute-start.11) | collective-permute-done | bytes 589856 | tf_op jit(solution)/shard_map/ppermute | solution.py:273
  68.4 2.3 %collective-permute-start.12 = (bf16[2,72,1024]{2,1,0:T(8,128)(2,1)S(1)}, bf16[2,72,1024]{2,1,0:T(8,128)(2,1)S(1)}, u32[]{:S(2)}, u32[]{:S(2)}) collective-permute-start(bf16[2,72,1024]{2,1,0:T(8,128)(2,1)S(1)} %get-tuple-element.63), channel_id=1, source_target_pairs={{0,4},{4,0},{8,12},{12,8},{20,16},{24,28},{28,24},{1,5},{5,1},{9,1... | collective-permute-start | bytes 884744 | tf_op jit(solution)/shard_map/ppermute | solution.py:254
  70.7 6.3 %collective-permute-done.12.refs_1_ = bf16[2,72,1024]{2,1,0:T(8,128)(2,1)S(1)} collective-permute-done((bf16[2,72,1024]{2,1,0:T(8,128)(2,1)S(1)}, bf16[2,72,1024]{2,1,0:T(8,128)(2,1)S(1)}, u32[]{:S(2)}, u32[]{:S(2)}) %collective-permute-start.12) | collective-permute-done | bytes 294944 | tf_op jit(solution)/shard_map/ppermute | solution.py:254
  77.9 2.3 %collective-permute-start.15 = (bf16[2,72,1024]{2,1,0:T(8,128)(2,1)S(1)}, bf16[2,72,1024]{2,1,0:T(8,128)(2,1)S(1)}, u32[]{:S(2)}, u32[]{:S(2)}) collective-permute-start(bf16[2,72,1024]{2,1,0:T(8,128)(2,1)S(1)} %get-tuple-element.71), channel_id=1, source_target_pairs={{0,4},{4,0},{8,12},{12,8},{20,16},{24,28},{28,24},{1,5},{5,1},{9,1... | collective-permute-start | bytes 884744 | tf_op jit(solution)/shard_map/ppermute | solution.py:254
  80.3 2.1 %collective-permute-start.14 = (bf16[1,72,1024]{2,1,0:T(8,128)(2,1)S(1)}, bf16[1,72,1024]{2,1,0:T(8,128)(2,1)S(1)}, u32[]{:S(2)}, u32[]{:S(2)}) collective-permute-start(bf16[1,72,1024]{2,1,0:T(8,128)(2,1)S(1)} %get-tuple-element.67), channel_id=1, source_target_pairs={{0,8},{4,12},{8,0},{12,4},{24,16},{28,20},{1,9},{5,13},{9,1},{13,5... | collective-permute-start | bytes 442376 | tf_op jit(solution)/shard_map/ppermute | solution.py:254
  82.4 6.0 %collective-permute-done.15.refs_1_ = bf16[2,72,1024]{2,1,0:T(8,128)(2,1)S(1)} collective-permute-done((bf16[2,72,1024]{2,1,0:T(8,128)(2,1)S(1)}, bf16[2,72,1024]{2,1,0:T(8,128)(2,1)S(1)}, u32[]{:S(2)}, u32[]{:S(2)}) %collective-permute-start.15) | collective-permute-done | bytes 294944 | tf_op jit(solution)/shard_map/ppermute | solution.py:254
  88.5 1.9 %collective-permute-start.16 = (bf16[1,72,1024]{2,1,0:T(8,128)(2,1)S(1)}, bf16[1,72,1024]{2,1,0:T(8,128)(2,1)S(1)}, u32[]{:S(2)}, u32[]{:S(2)}) collective-permute-start(bf16[1,72,1024]{2,1,0:T(8,128)(2,1)S(1)} %get-tuple-element.73), channel_id=1, source_target_pairs={{0,8},{4,12},{8,0},{12,4},{24,16},{28,20},{1,9},{5,13},{9,1},{13,5... | collective-permute-start | bytes 442376 | tf_op jit(solution)/shard_map/ppermute | solution.py:254
  90.4 1.4 %collective-permute-done.14.refs_1_ = bf16[1,72,1024]{2,1,0:T(8,128)(2,1)S(1)} collective-permute-done((bf16[1,72,1024]{2,1,0:T(8,128)(2,1)S(1)}, bf16[1,72,1024]{2,1,0:T(8,128)(2,1)S(1)}, u32[]{:S(2)}, u32[]{:S(2)}) %collective-permute-start.14) | collective-permute-done | bytes 147488 | tf_op jit(solution)/shard_map/ppermute | solution.py:254
  91.8 5.2 %collective-permute-done.16.refs_3_ = bf16[1,72,1024]{2,1,0:T(8,128)(2,1)S(1)} collective-permute-done((bf16[1,72,1024]{2,1,0:T(8,128)(2,1)S(1)}, bf16[1,72,1024]{2,1,0:T(8,128)(2,1)S(1)}, u32[]{:S(2)}, u32[]{:S(2)}) %collective-permute-start.16) | collective-permute-done | bytes 147488 | tf_op jit(solution)/shard_map/ppermute | solution.py:254
  97.0 0.9 finish.1
  (29 shorter events, 1.9 us)
Async XLA Ops:
  2.7 19.5 %collective-permute-start.2 = (bf16[72,2048]{1,0:T(8,128)(2,1)}, bf16[72,2048]{1,0:T(8,128)(2,1)S(1)}, u32[]{:S(2)}, u32[]{:S(2)}) collective-permute-start(bf16[72,2048]{1,0:T(8,128)(2,1)} %get-tuple-element.40.refs_0_), channel_id=1, source_target_pairs={{0,16},{4,20},{8,24},{12,28},{1,17},{5,21},{9,25},{13,29},{2,18},{... | collective-permute-start | bytes 884744 | tf_op jit(solution)/shard_map/ppermute | solution.py:273
  7.6 23.0 %collective-permute-start = (bf16[72,2048]{1,0:T(8,128)(2,1)}, bf16[72,2048]{1,0:T(8,128)(2,1)S(1)}, u32[]{:S(2)}, u32[]{:S(2)}) collective-permute-start(bf16[72,2048]{1,0:T(8,128)(2,1)} %get-tuple-element.40.refs_0_), channel_id=1, source_target_pairs={{0,4},{4,0},{8,12},{12,8},{16,20},{24,28},{1,5},{5,1},{9,13},{13,9... | collective-permute-start | bytes 884744 | tf_op jit(solution)/shard_map/ppermute | solution.py:254
  11.1 11.1 %collective-permute-start.1 = (bf16[72,1024]{1,0:T(8,128)(2,1)}, bf16[72,1024]{1,0:T(8,128)(2,1)S(1)}, u32[]{:S(2)}, u32[]{:S(2)}) collective-permute-start(bf16[72,1024]{1,0:T(8,128)(2,1)} %get-tuple-element.41), channel_id=1, source_target_pairs={{0,8},{4,12},{8,0},{12,4},{16,24},{20,28},{1,9},{5,13},{9,1},{13,5... | collective-permute-start | bytes 442376 | tf_op jit(solution)/shard_map/ppermute | solution.py:254
  15.6 1.3 %copy-start = (bf16[72,8192]{1,0:T(8,128)(2,1)S(1)}, bf16[72,8192]{1,0:T(8,128)(2,1)}, u32[]{:S(2)}) copy-start(bf16[72,8192]{1,0:T(8,128)(2,1)} %query_ref.1) | copy-start | bytes 3538948
  16.9 1.3 %copy-start.1 = (bf16[72,8192]{1,0:T(8,128)(2,1)S(1)}, bf16[72,8192]{1,0:T(8,128)(2,1)}, u32[]{:S(2)}) copy-start(bf16[72,8192]{1,0:T(8,128)(2,1)} %grad_ref.1) | copy-start | bytes 3538948
  18.2 0.8 copy-start.3
  18.9 0.8 copy-start.5
  19.7 3.9 %copy-start.8 = (bf16[72,1024]{1,0:T(8,128)(2,1)S(1)}, bf16[72,1024]{1,0:T(8,128)(2,1)}, u32[]{:S(2)}) copy-start(bf16[72,1024]{1,0:T(8,128)(2,1)} %get-tuple-element.46) | copy-start | bytes 442372
  19.7 22.9 %copy-start.2 = (bf16[72,2048]{1,0:T(8,128)(2,1)S(1)}, bf16[72,2048]{1,0:T(8,128)(2,1)}, u32[]{:S(2)}) copy-start(bf16[72,2048]{1,0:T(8,128)(2,1)} %get-tuple-element.40.refs_0_) | copy-start | bytes 884740
  19.7 23.0 %copy-start.6 = (f32[72,128]{1,0:T(8,128)S(1)}, f32[72,128]{1,0:T(8,128)}, u32[]{:S(2)}) copy-start(f32[72,128]{1,0:T(8,128)} %get-tuple-element.44.sin_ref.refs_13_) | copy-start | bytes 110596
  19.7 23.0 %copy-start.7 = (s32[2]{0:T(128)S(1)}, s32[2]{0:T(128)}, u32[]{:S(2)}) copy-start(s32[2]{0:T(128)} %counts_ref.3) | copy-start | bytes 28
  22.3 9.7 %collective-permute-start.4 = (bf16[72,1024]{1,0:T(8,128)(2,1)S(1)}, bf16[72,1024]{1,0:T(8,128)(2,1)S(1)}, u32[]{:S(2)}, u32[]{:S(2)}) collective-permute-start(bf16[72,1024]{1,0:T(8,128)(2,1)S(1)} %collective-permute-done.1.refs_2_), channel_id=1, source_target_pairs={{0,16},{4,20},{8,24},{12,28},{1,17},{5,21},{9,25},{13,29},{2,18},{... | collective-permute-start | bytes 442376 | tf_op jit(solution)/shard_map/ppermute | solution.py:273
  23.6 10.7 %collective-permute-start.3 = (bf16[72,1024]{1,0:T(8,128)(2,1)S(1)}, bf16[72,1024]{1,0:T(8,128)(2,1)S(1)}, u32[]{:S(2)}, u32[]{:S(2)}) collective-permute-start(bf16[72,1024]{1,0:T(8,128)(2,1)S(1)} %copy-done.8), channel_id=1, source_target_pairs={{0,8},{4,12},{8,0},{12,4},{16,24},{20,28},{1,9},{5,13},{9,1},{13,5... | collective-permute-start | bytes 442376 | tf_op jit(solution)/shard_map/ppermute | solution.py:254
  27.3 9.3 %collective-permute-start.9 = (bf16[72,1024]{1,0:T(8,128)(2,1)S(1)}, bf16[72,1024]{1,0:T(8,128)(2,1)S(1)}, u32[]{:S(2)}, u32[]{:S(2)}) collective-permute-start(bf16[72,1024]{1,0:T(8,128)(2,1)S(1)} %collective-permute-done.1.refs_2_), channel_id=1, source_target_pairs={{0,4},{4,0},{8,12},{12,8},{24,28},{28,24},{1,5},{5,1},{9,13},{13,9... | collective-permute-start | bytes 442376 | tf_op jit(solution)/shard_map/ppermute | solution.py:254
  30.7 12.0 %collective-permute-start.6 = (bf16[72,2048]{1,0:T(8,128)(2,1)S(1)}, bf16[72,2048]{1,0:T(8,128)(2,1)S(1)}, u32[]{:S(2)}, u32[]{:S(2)}) collective-permute-start(bf16[72,2048]{1,0:T(8,128)(2,1)S(1)} %collective-permute-done.refs_1_), channel_id=1, source_target_pairs={{0,16},{4,20},{8,24},{12,28},{1,17},{5,21},{9,25},{13,29},{2,18},{... | collective-permute-start | bytes 884744 | tf_op jit(solution)/shard_map/ppermute | solution.py:273
  34.3 7.0 %collective-permute-start.5 = (bf16[72,1024]{1,0:T(8,128)(2,1)S(1)}, bf16[72,1024]{1,0:T(8,128)(2,1)S(1)}, u32[]{:S(2)}, u32[]{:S(2)}) collective-permute-start(bf16[72,1024]{1,0:T(8,128)(2,1)S(1)} %collective-permute-done.3.refs_2_), channel_id=1, source_target_pairs={{0,4},{4,0},{8,12},{12,8},{24,28},{28,24},{1,5},{5,1},{9,13},{13,9... | collective-permute-start | bytes 442376 | tf_op jit(solution)/shard_map/ppermute | solution.py:254
  36.7 6.0 %collective-permute-start.10 = (bf16[72,1024]{1,0:T(8,128)(2,1)S(1)}, bf16[72,1024]{1,0:T(8,128)(2,1)S(1)}, u32[]{:S(2)}, u32[]{:S(2)}) collective-permute-start(bf16[72,1024]{1,0:T(8,128)(2,1)S(1)} %collective-permute-done.9.refs_3_), channel_id=1, source_target_pairs={{0,16},{4,20},{8,24},{12,28},{1,17},{5,21},{9,25},{13,29},{2,18},{... | collective-permute-start | bytes 442376 | tf_op jit(solution)/shard_map/ppermute | solution.py:273
  38.0 14.1 %collective-permute-start.7 = (bf16[72,1024]{1,0:T(8,128)(2,1)S(1)}, bf16[72,1024]{1,0:T(8,128)(2,1)S(1)}, u32[]{:S(2)}, u32[]{:S(2)}) collective-permute-start(bf16[72,1024]{1,0:T(8,128)(2,1)S(1)} %collective-permute-done.3.refs_2_), channel_id=1, source_target_pairs={{0,16},{4,20},{8,24},{12,28},{1,17},{5,21},{9,25},{13,29},{2,18},{... | collective-permute-start | bytes 442376 | tf_op jit(solution)/shard_map/ppermute | solution.py:273
  41.3 10.8 %collective-permute-start.8 = (bf16[72,1024]{1,0:T(8,128)(2,1)S(1)}, bf16[72,1024]{1,0:T(8,128)(2,1)S(1)}, u32[]{:S(2)}, u32[]{:S(2)}) collective-permute-start(bf16[72,1024]{1,0:T(8,128)(2,1)S(1)} %collective-permute-done.5.refs_3_), channel_id=1, source_target_pairs={{0,16},{4,20},{8,24},{12,28},{1,17},{5,21},{9,25},{13,29},{2,18},{... | collective-permute-start | bytes 442376 | tf_op jit(solution)/shard_map/ppermute | solution.py:273
  50.8 17.4 %collective-permute-start.11 = (bf16[4,72,1024]{2,1,0:T(8,128)(2,1)S(1)}, bf16[4,72,1024]{2,1,0:T(8,128)(2,1)S(1)}, u32[]{:S(2)}, u32[]{:S(2)}) collective-permute-start(bf16[4,72,1024]{2,1,0:T(8,128)(2,1)S(1)} %get-tuple-element.61), channel_id=1, source_target_pairs={{16,0},{20,4},{24,8},{28,12},{17,1},{21,5},{25,9},{29,13},{18,2},{... | collective-permute-start | bytes 1769480 | tf_op jit(solution)/shard_map/ppermute | solution.py:273
  60.3 17.5 %collective-permute-start.13 = (bf16[4,72,1024]{2,1,0:T(8,128)(2,1)S(1)}, bf16[4,72,1024]{2,1,0:T(8,128)(2,1)S(1)}, u32[]{:S(2)}, u32[]{:S(2)}) collective-permute-start(bf16[4,72,1024]{2,1,0:T(8,128)(2,1)S(1)} %get-tuple-element.65), channel_id=1, source_target_pairs={{16,0},{20,4},{24,8},{28,12},{17,1},{21,5},{25,9},{29,13},{18,2},{... | collective-permute-start | bytes 1769480 | tf_op jit(solution)/shard_map/ppermute | solution.py:273
  68.4 8.6 %collective-permute-start.12 = (bf16[2,72,1024]{2,1,0:T(8,128)(2,1)S(1)}, bf16[2,72,1024]{2,1,0:T(8,128)(2,1)S(1)}, u32[]{:S(2)}, u32[]{:S(2)}) collective-permute-start(bf16[2,72,1024]{2,1,0:T(8,128)(2,1)S(1)} %get-tuple-element.63), channel_id=1, source_target_pairs={{0,4},{4,0},{8,12},{12,8},{20,16},{24,28},{28,24},{1,5},{5,1},{9,1... | collective-permute-start | bytes 884744 | tf_op jit(solution)/shard_map/ppermute | solution.py:254
  77.9 10.5 %collective-permute-start.15 = (bf16[2,72,1024]{2,1,0:T(8,128)(2,1)S(1)}, bf16[2,72,1024]{2,1,0:T(8,128)(2,1)S(1)}, u32[]{:S(2)}, u32[]{:S(2)}) collective-permute-start(bf16[2,72,1024]{2,1,0:T(8,128)(2,1)S(1)} %get-tuple-element.71), channel_id=1, source_target_pairs={{0,4},{4,0},{8,12},{12,8},{20,16},{24,28},{28,24},{1,5},{5,1},{9,1... | collective-permute-start | bytes 884744 | tf_op jit(solution)/shard_map/ppermute | solution.py:254
  80.3 11.6 %collective-permute-start.14 = (bf16[1,72,1024]{2,1,0:T(8,128)(2,1)S(1)}, bf16[1,72,1024]{2,1,0:T(8,128)(2,1)S(1)}, u32[]{:S(2)}, u32[]{:S(2)}) collective-permute-start(bf16[1,72,1024]{2,1,0:T(8,128)(2,1)S(1)} %get-tuple-element.67), channel_id=1, source_target_pairs={{0,8},{4,12},{8,0},{12,4},{24,16},{28,20},{1,9},{5,13},{9,1},{13,5... | collective-permute-start | bytes 442376 | tf_op jit(solution)/shard_map/ppermute | solution.py:254
  88.4 8.6 %copy-start.4 = (f32[72,128]{1,0:T(8,128)S(1)}, f32[72,128]{1,0:T(8,128)}, u32[]{:S(2)}) copy-start(f32[72,128]{1,0:T(8,128)} %get-tuple-element.43.cos_ref) | copy-start | bytes 110596
  88.5 8.5 %collective-permute-start.16 = (bf16[1,72,1024]{2,1,0:T(8,128)(2,1)S(1)}, bf16[1,72,1024]{2,1,0:T(8,128)(2,1)S(1)}, u32[]{:S(2)}, u32[]{:S(2)}) collective-permute-start(bf16[1,72,1024]{2,1,0:T(8,128)(2,1)S(1)} %get-tuple-element.73), channel_id=1, source_target_pairs={{0,8},{4,12},{8,0},{12,4},{24,16},{28,20},{1,9},{5,13},{9,1},{13,5... | collective-permute-start | bytes 442376 | tf_op jit(solution)/shard_map/ppermute | solution.py:254

commit v5 on v3

--- a/solution.py
+++ b/solution.py
@@ -32,21 +32,7 @@
     return row[0:1]
 
 
-def rope(vectors, cosine, sine):
-    return vectors * cosine + pltpu.roll(vectors, HEAD_WIDTH // 2, 1) * sine
-
-
-def rope_back(vectors, cosine, sine):
-    return vectors * cosine - pltpu.roll(vectors, HEAD_WIDTH // 2, 1) * sine
-
-
-def head_cols(index):
-    return slice(index * HEAD_WIDTH, (index + 1) * HEAD_WIDTH)
-
-
-def prepare_keys(rows, pos_ref, key_ref, value_ref, whole_ref, *out_refs):
-    kv_refs, (cos_ref, sin_ref) = out_refs[:CHUNKS], out_refs[CHUNKS:]
-    padded = key_ref.shape[0]
+def angle_tables(rows, padded, pos_ref):
     start = (lax.axis_index("seq") * lax.axis_size("head") + lax.axis_index("head")) * rows
     sublane = lax.broadcasted_iota(jnp.int32, (8, HEAD_WIDTH), 0)
     pieces = []
@@ -57,10 +43,23 @@
         pieces.append(piece)
     angle = jnp.concatenate(pieces, 0).astype(jnp.float32) * inverse_freq_row()
     lane = lax.broadcasted_iota(jnp.int32, angle.shape, 1)
-    cosine = jnp.cos(angle)
-    sine = jnp.sin(angle) * jnp.where(lane < HEAD_WIDTH // 2, -1.0, 1.0)
-    cos_ref[...] = cosine
-    sin_ref[...] = sine
+    return jnp.cos(angle), jnp.sin(angle) * jnp.where(lane < HEAD_WIDTH // 2, -1.0, 1.0)
+
+
+def rope(vectors, cosine, sine):
+    return vectors * cosine + pltpu.roll(vectors, HEAD_WIDTH // 2, 1) * sine
+
+
+def rope_back(vectors, cosine, sine):
+    return vectors * cosine - pltpu.roll(vectors, HEAD_WIDTH // 2, 1) * sine
+
+
+def head_cols(index):
+    return slice(index * HEAD_WIDTH, (index + 1) * HEAD_WIDTH)
+
+
+def prepare_keys(rows, pos_ref, key_ref, value_ref, whole_ref, *kv_refs):
+    cosine, sine = angle_tables(rows, key_ref.shape[0], pos_ref)
     for head in range(KEY_VALUE_HEADS):
         chunk, place = divmod(head, HEADS_PER_CHUNK)
         rotated = rope(key_ref[:, head_cols(head)].astype(jnp.float32), cosine, sine)
@@ -73,7 +72,18 @@
             whole_ref[:, head_cols(2 * chunk * HEADS_PER_CHUNK + column)] = x
 
 
-def prepare_queries(query_ref, grad_ref, cos_ref, sin_ref, q_ref, qt_ref, g_ref, gt_ref, table_ref):
+def prepare_queries(rows, pos_ref, query_ref, grad_ref, *out_refs):
+    q_ref, qt_ref, g_ref, gt_ref, cos_ref, sin_ref, cos_t_ref, sin_t_ref = out_refs
+
+    @pl.when(pl.program_id(0) == 0)
+    def _():
+        cosine, sine = angle_tables(rows, query_ref.shape[0], pos_ref)
+        cos_ref[...] = cosine
+        sin_ref[...] = sine
+        half = HEAD_WIDTH // 2
+        cos_t_ref[...] = jnp.concatenate([cosine] * GROUP, 0).T[half:] * SCORE_SCALE
+        sin_t_ref[...] = jnp.concatenate([sine] * GROUP, 0).T[half:] * SCORE_SCALE
+
     cosine, sine = cos_ref[...], sin_ref[...]
     queries = jnp.concatenate(
         [
@@ -89,7 +99,6 @@
     qt_ref[0] = queries.T.astype(jnp.bfloat16)
     g_ref[0] = grads.astype(jnp.bfloat16)
     gt_ref[0] = grads.T.astype(jnp.bfloat16)
-    table_ref[...] = cosine
 
 
 def dot(left, right):
@@ -134,7 +143,8 @@
     def gathered(first, place):
         cols = lanes(first, place)
         wide = jnp.concatenate([ref[:, cols].astype(jnp.float32) for ref in kv_refs], 0)
-        return wide.astype(jnp.bfloat16), wide.T.astype(jnp.bfloat16)
+        low = wide.astype(jnp.bfloat16)
+        return low, low.T
 
     heads = range(STEP_HEADS)
     keys, values = [gathered(0, p) for p in heads], [gathered(HEADS_PER_CHUNK, p) for p in heads]
@@ -153,16 +163,21 @@
         out_low = outs_t[p].astype(jnp.bfloat16).astype(jnp.float32)
         delta = jnp.sum(gt_ref[p].astype(jnp.float32) * out_low, 0, keepdims=True)
         dscores.append((probs[p] * (dprobs[p] - delta)).astype(jnp.bfloat16))
-    grads_t = [dot(keys[p][1], dscores[p]) * SCORE_SCALE for p in heads]
+    grads_t = [dot(keys[p][1], dscores[p]) for p in heads]
     key_parts = [dot(dscores[p], q_ref[p]) * SCORE_SCALE for p in heads]
 
     cosine, sine = cos_ref[...], sin_ref[...]
+    half = HEAD_WIDTH // 2
     for p in heads:
-        out_heads, grad_heads = outs_t[p].T, grads_t[p].T
+        first, second = grads_t[p][:half], grads_t[p][half:]
+        turned = [first * cosine + second * sine, second * cosine - first * sine]
+        grad_low = jnp.concatenate(turned, 0).astype(jnp.bfloat16)
+        out_heads = outs_t[p].astype(jnp.bfloat16).T.astype(jnp.float32)
+        grad_heads = grad_low.T.astype(jnp.float32)
         for h in range(GROUP):
             piece, cols = slice(h * padded, (h + 1) * padded), head_cols(p * GROUP + h)
             out_ref[:, cols] = out_heads[piece].astype(jnp.bfloat16)
-            grad_ref[:, cols] = rope_back(grad_heads[piece], cosine, sine).astype(jnp.bfloat16)
+            grad_ref[:, cols] = grad_heads[piece].astype(jnp.bfloat16)
         for block in range(blocks):
             seq_offset, head_offset = divmod(block, head_count)
             piece = slice(block * padded, (block + 1) * padded)
@@ -249,14 +264,13 @@
         return lax.ppermute(x, ("seq", "head"), pairs)
 
     table = shape((padded, HEAD_WIDTH), f32)
+    table_t = shape((HEAD_WIDTH // 2, query_rows), f32)
     piece = shape((padded, 2 * CHUNK_COLS), bf16)
-    whole, *own, cosine, sine = pl.pallas_call(
+    whole, *own = pl.pallas_call(
         functools.partial(prepare_keys, rows),
-        out_shape=[shape((padded, CHUNKS * 2 * CHUNK_COLS), bf16)]
-        + [piece] * CHUNKS
-        + [table, table],
+        out_shape=[shape((padded, CHUNKS * 2 * CHUNK_COLS), bf16)] + [piece] * CHUNKS,
         in_specs=[SMEM, VMEM, VMEM],
-        out_specs=[VMEM] * (CHUNKS + 3),
+        out_specs=[VMEM] * (CHUNKS + 1),
         compiler_params=params(56),
         name="prepare_keys",
     )(positions, routed_keys, routed_values)
@@ -268,49 +282,58 @@
     flat_block = pl.BlockSpec((1, HEAD_WIDTH, query_rows), lambda g: (g, 0, 0))
     tall = shape((KEY_VALUE_HEADS, query_rows, HEAD_WIDTH), bf16)
     flat = shape((KEY_VALUE_HEADS, HEAD_WIDTH, query_rows), bf16)
-    *stacked, cosine_later = pl.pallas_call(
-        prepare_queries,
+    table_t_block = pl.BlockSpec(table_t.shape, lambda g: (0, 0))
+    *stacked, cosine, sine, cosine_t, sine_t = pl.pallas_call(
+        functools.partial(prepare_queries, rows),
         grid=(KEY_VALUE_HEADS,),
-        out_shape=[tall, flat, tall, flat, table],
-        in_specs=[row_block, row_block, table_block, table_block],
+        out_shape=[tall, flat, tall, flat, table, table, table_t, table_t],
+        in_specs=[SMEM, row_block, row_block],
         out_specs=[tall_block, flat_block, tall_block, flat_block]
-        + [table_block],
+        + [table_block, table_block, table_t_block, table_t_block],
         cost_estimate=cost(7),
         compiler_params=params(16),
         name="prepare_queries",
-    )(queries, output_gradient, cosine, sine)
+    )(positions, queries, output_gradient)
 
     bits = [1 << b for b in reversed(range((head_count - 1).bit_length()))]
     later = range(1, seq_count)
-    chunked = [{bits[0]: along_head(own[0], bits[0], True)}]
-    far = {(a, 0): along_seq(whole, a, True) for a in later}
-    nearest = along_head(whole, 1, True)
-    chunked[0][bits[0]], own[1:], cosine_later, far = lax.optimization_barrier(
-        (chunked[0][bits[0]], own[1:], cosine_later, far)
-    )
-    chunked += [{bits[0]: along_head(x, bits[0], True)} for x in own[1:]]
-    far.update({(a, 1): along_seq(nearest, a, True) for a in later})
-    gathered = []
-    for c, near in enumerate(chunked):
-        near[0] = own[c]
+    firsts = sorted({bits[0], 1})
+    far = {a: along_seq(whole, a, True) for a in later}
+    near = {0: own[0], **{j: along_head(own[0], j, True) for j in firsts}}
+    near, cosine_t, far = lax.optimization_barrier((near, cosine_t, far))
+
+    def gather(near):
         for bit in bits[1:]:
             near.update(
-                {j ^ bit: along_head(x, bit, True, j) for j, x in near.items() if j ^ bit > 1}
+                {j ^ bit: along_head(x, bit, True, j) for j, x in near.items() if j ^ bit not in near}
             )
-        blocks_here = [whole, nearest] + [near[j] for j in range(2, head_count)]
+        crossed = {
+            (a, j): along_seq(near[j], a, True) for j in range(1, head_count) for a in later
+        }
+        blocks_here = [near[j] for j in range(head_count)]
         for a in later:
-            blocks_here += [far[a, 0], far[a, 1]]
-            blocks_here += [along_seq(near[j], a, True) for j in range(2, head_count)]
-        gathered.append(blocks_here)
+            blocks_here += [far[a]] + [crossed[a, j] for j in range(1, head_count)]
+        return blocks_here
 
     wide_outs = ()
-    summed = []
+    parts = []
     for chunk in range(CHUNKS):
         first = chunk * HEADS_PER_CHUNK // STEP_HEADS
         has_alias = int(chunk > 0)
-        tall_part = pl.BlockSpec((STEP_HEADS, query_rows, HEAD_WIDTH), lambda g, f=first: (f + g, 0, 0))
-        flat_part = pl.BlockSpec((STEP_HEADS, HEAD_WIDTH, query_rows), lambda g, f=first: (f + g, 0, 0))
+        tall_part, flat_part = (
+            pl.BlockSpec((STEP_HEADS, *x.shape[1:]), lambda g, f=first: (f + g, 0, 0))
+            for x in (tall, flat)
+        )
         row_part = pl.BlockSpec((padded, STEP_HEADS * wide), lambda g, f=first: (0, f + g))
+        if chunk:
+            near = {0: own[chunk], **{j: along_head(own[chunk], j, True) for j in firsts}}
+            near, parts[-1][0] = lax.optimization_barrier((near, parts[-1][0]))
+        gathered = gather(near)
+        if chunk + 1 < CHUNKS:
+            last = head_count - 1
+            own[chunk + 1], gathered[last] = lax.optimization_barrier(
+                (own[chunk + 1], gathered[last])
+            )
         kv_whole = pl.BlockSpec((padded, 2 * CHUNK_COLS), lambda g, c=chunk: (0, c))
         kv_chunk = pl.BlockSpec((padded, 2 * CHUNK_COLS), lambda g: (0, 0))
         part_block = pl.BlockSpec((head_count, padded, 2 * CHUNK_COLS), lambda g: (0, 0, 0))
@@ -320,8 +343,9 @@
             out_shape=[shape((padded, QUERY_HEADS * HEAD_WIDTH), bf16)] * 2
             + [shape((head_count, padded, 2 * CHUNK_COLS), bf16)] * seq_count,
             in_specs=[SMEM]
-            + ([kv_whole] * 2 + [kv_chunk] * (head_count - 2)) * seq_count
-            + [tall_part, flat_part, tall_part, flat_part, table_block, table_block]
+            + [kv_chunk] * head_count
+            + ([kv_whole] + [kv_chunk] * (head_count - 1)) * (seq_count - 1)
+            + [tall_part, flat_part, tall_part, flat_part, table_t_block, table_t_block]
             + [pl.BlockSpec(memory_space=pl.ANY)] * (2 * has_alias),
             out_specs=[row_part, row_part] + [part_block] * seq_count,
             scratch_shapes=[
@@ -332,9 +356,16 @@
             cost_estimate=cost(10),
             compiler_params=params(32),
             name="attend",
-        )(counts, *gathered[chunk], *stacked, cosine_later, sine, *wide_outs)
+        )(counts, *gathered, *stacked, cosine_t, sine_t, *wide_outs)
         wide_outs = out[:2]
-        parts = [out[2]] + [along_seq(out[2 + a], a, False) for a in range(1, seq_count)]
+        parts.append([out[2]] + [along_seq(out[2 + a], a, False) for a in later])
+
+    summed = []
+    for mine in parts:
+        if summed:
+            mine[-1], summed[-head_count] = lax.optimization_barrier(
+                (mine[-1], summed[-head_count])
+            )
         base, *sends = pl.pallas_call(
             functools.partial(combine, seq_count, head_count),
             out_shape=[shape((padded, 2 * CHUNK_COLS), f32)] + [piece] * (head_count - 1),
@@ -343,7 +374,7 @@
             cost_estimate=cost(2),
             compiler_params=params(8),
             name="combine",
-        )(*parts)
+        )(*mine)
         summed += [base] + [along_head(x, j + 1, False) for j, x in enumerate(sends)]
 
     narrow = shape((padded, KEY_VALUE_HEADS * HEAD_WIDTH), bf16)

time: 97.9 us -> 97.4 us (level)
  waiting for transfers between devices: 19.5 us -> 14.5 us
  starting transfers between devices: 51.1 us -> 55.6 us
  Pallas kernels: 21.5 us -> 22.5 us
    ppermute x8 -> x9, waiting for transfers between devices: 9.26 us -> 5.06 us  [along_seq(): return lax.ppermute(x, ('seq', 'head'), pairs)]
    ppermute x11 -> x12, starting transfers between devices: 37 us -> 41 us  [along_head(): return lax.ppermute(x, ('seq', 'head'), pairs)]
    pallas_call x1, Pallas kernels: 2.53 us -> 3.65 us  [shards(): pl.pallas_call(functools.partial(prepare_queries, rows), grid=(KEY_VALUE_...]
    unnamed x18 -> x12, local copies, waits for them, and re-layouts: 4.09 us -> 3.23 us
    ppermute x11 -> x12, waiting for transfers between devices: 10.2 us -> 9.41 us  [along_head(): return lax.ppermute(x, ('seq', 'head'), pairs)]
    ppermute x8 -> x9, starting transfers between devices: 14.1 us -> 14.6 us  [along_seq(): return lax.ppermute(x, ('seq', 'head'), pairs)]
  transfers between devices with their start and end apart: 19 -> 21, of which waited for: 5 -> 7; matrix products, arithmetic and copies ran while one was open for 0% -> 0% of each run, Pallas kernels for 19% -> 20%
where the time goes in v5:
time: 97.4 us; the launch traced here: 96.7 us
  starting transfers between devices  55.6 us (57%)
  Pallas kernels  22.5 us (23%)
  waiting for transfers between devices  14.5 us (15%)
  local copies, waits for them, and re-layouts  3.23 us (3%)
    ppermute x12, starting transfers between devices, along_head(): return lax.ppermute(x, ('seq', 'head'), pairs)  41 us
    pallas_call x2, Pallas kernels, shards(): pl.pallas_call(functools.partial(attend, seq_count, head_count, rows, has...  15.6 us
    ppermute x9, starting transfers between devices, along_seq(): return lax.ppermute(x, ('seq', 'head'), pairs)  14.6 us
    ppermute x12, waiting for transfers between devices, along_head(): return lax.ppermute(x, ('seq', 'head'), pairs)  9.41 us
    ppermute x9, waiting for transfers between devices, along_seq(): return lax.ppermute(x, ('seq', 'head'), pairs)  5.06 us
    pallas_call x1, Pallas kernels, shards(): pl.pallas_call(functools.partial(prepare_queries, rows), grid=(KEY_VALUE_...  3.65 us
    unnamed x12, local copies, waits for them, and re-layouts  3.23 us
    pallas_call x1, Pallas kernels, shards(): pl.pallas_call(functools.partial(prepare_keys, rows), out_shape=[shape((p...  2.09 us
  transfers between devices with their start and end apart: 21, of which 7 were waited for; matrix products, arithmetic and copies ran while one was open for 0% of the time, Pallas kernels for 20%

profile of v5, /device:TPU:0, one launch (start us, length us, event | category | flops | bytes accessed | tf_op | source)
XLA Modules:
  0.0 96.7 jit_solution(1083461769309943160)
XLA Ops:
  0.6 2.1 %prepare_keys.1 = (bf16[72,2048]{1,0:T(8,128)(2,1)}, bf16[72,1024]{1,0:T(8,128)(2,1)}, bf16[72,1024]{1,0:T(8,128)(2,1)}) custom-call(s32[576]{0:T(1024)} %pos_ref.3, bf16[72,1024]{1,0:T(8,128)(2,1)} %key_ref.1, bf16[72,1024]{1,0:T(8,128)(2,1)} %value_ref.1), custom_call_target="tpu_custom_call" | custom-call | tf_op jit(solution)/shard_map/prepare_keys/pallas_call | solution.py:269
  2.7 4.9 %collective-permute-start = (bf16[72,1024]{1,0:T(8,128)(2,1)}, bf16[72,1024]{1,0:T(8,128)(2,1)S(1)}, u32[]{:S(2)}, u32[]{:S(2)}) collective-permute-start(bf16[72,1024]{1,0:T(8,128)(2,1)} %get-tuple-element.52.refs_0_), channel_id=1, source_target_pairs={{0,4},{4,0},{8,12},{12,8},{16,20},{24,28},{1,5},{5,1},{9,13},{13,9... | collective-permute-start | bytes 442376 | tf_op jit(solution)/shard_map/ppermute | solution.py:256
  7.6 4.5 %collective-permute-start.1 = (bf16[72,1024]{1,0:T(8,128)(2,1)}, bf16[72,1024]{1,0:T(8,128)(2,1)S(1)}, u32[]{:S(2)}, u32[]{:S(2)}) collective-permute-start(bf16[72,1024]{1,0:T(8,128)(2,1)} %get-tuple-element.52.refs_0_), channel_id=1, source_target_pairs={{0,8},{4,12},{8,0},{12,4},{16,24},{20,28},{1,9},{5,13},{9,1},{13,5... | collective-permute-start | bytes 442376 | tf_op jit(solution)/shard_map/ppermute | solution.py:256
  12.2 3.4 %collective-permute-start.2 = (bf16[72,2048]{1,0:T(8,128)(2,1)}, bf16[72,2048]{1,0:T(8,128)(2,1)S(1)}, u32[]{:S(2)}, u32[]{:S(2)}) collective-permute-start(bf16[72,2048]{1,0:T(8,128)(2,1)} %get-tuple-element.49), channel_id=1, source_target_pairs={{0,16},{4,20},{8,24},{12,28},{1,17},{5,21},{9,25},{13,29},{2,18},{... | collective-permute-start | bytes 884744 | tf_op jit(solution)/shard_map/ppermute | solution.py:264
  16.3 1.3 %copy-done.1 = bf16[72,8192]{1,0:T(8,128)(2,1)S(1)} copy-done((bf16[72,8192]{1,0:T(8,128)(2,1)S(1)}, bf16[72,8192]{1,0:T(8,128)(2,1)}, u32[]{:S(2)}) %copy-start.1) | copy-done | bytes 1179672
  17.6 1.3 %copy-done.2 = bf16[72,8192]{1,0:T(8,128)(2,1)S(1)} copy-done((bf16[72,8192]{1,0:T(8,128)(2,1)S(1)}, bf16[72,8192]{1,0:T(8,128)(2,1)}, u32[]{:S(2)}) %copy-start.2) | copy-done | bytes 1179672
  18.8 3.6 %prepare_queries.1 = (bf16[8,576,128]{2,1,0:T(8,128)(2,1)S(1)}, bf16[8,128,576]{2,1,0:T(8,128)(2,1)S(1)}, bf16[8,576,128]{2,1,0:T(8,128)(2,1)S(1)}, bf16[8,128,5...) custom-call(s32[576]{0:T(1024)S(1)} %copy-done, ...), custom_call_target="tpu_custom_call" | custom-call | flops 8071000064 | bytes 25830000 | tf_op jit(solution)/shard_map/prepare_queries/pallas_call | solution.py:286
  22.5 1.9 %collective-permute-start.3 = (bf16[72,1024]{1,0:T(8,128)(2,1)S(1)}, bf16[72,1024]{1,0:T(8,128)(2,1)S(1)}, u32[]{:S(2)}, u32[]{:S(2)}) collective-permute-start(bf16[72,1024]{1,0:T(8,128)(2,1)S(1)} %collective-permute-done.1.refs_2_), channel_id=1, source_target_pairs={{0,4},{4,0},{8,12},{12,8},{24,28},{28,24},{1,5},{5,1},{9,13},{13,9... | collective-permute-start | bytes 442376 | tf_op jit(solution)/shard_map/ppermute | solution.py:256
  24.5 2.1 %collective-permute-start.7 = (bf16[72,1024]{1,0:T(8,128)(2,1)S(1)}, bf16[72,1024]{1,0:T(8,128)(2,1)S(1)}, u32[]{:S(2)}, u32[]{:S(2)}) collective-permute-start(bf16[72,1024]{1,0:T(8,128)(2,1)S(1)} %collective-permute-done.1.refs_2_), channel_id=1, source_target_pairs={{0,16},{4,20},{8,24},{12,28},{1,17},{5,21},{9,25},{13,29},{2,18},{... | collective-permute-start | bytes 442376 | tf_op jit(solution)/shard_map/ppermute | solution.py:264
  26.6 1.3 %collective-permute-start.6 = (bf16[72,1024]{1,0:T(8,128)(2,1)S(1)}, bf16[72,1024]{1,0:T(8,128)(2,1)S(1)}, u32[]{:S(2)}, u32[]{:S(2)}) collective-permute-start(bf16[72,1024]{1,0:T(8,128)(2,1)S(1)} %collective-permute-done.refs_1_), channel_id=1, source_target_pairs={{0,16},{4,20},{8,24},{12,28},{1,17},{5,21},{9,25},{13,29},{2,18},{... | collective-permute-start | bytes 442376 | tf_op jit(solution)/shard_map/ppermute | solution.py:264
  27.9 1.7 %collective-permute-done.3.refs_3_ = bf16[72,1024]{1,0:T(8,128)(2,1)S(1)} collective-permute-done((bf16[72,1024]{1,0:T(8,128)(2,1)S(1)}, bf16[72,1024]{1,0:T(8,128)(2,1)S(1)}, u32[]{:S(2)}, u32[]{:S(2)}) %collective-permute-start.3) | collective-permute-done | bytes 147488 | tf_op jit(solution)/shard_map/ppermute | solution.py:256
  29.6 1.3 %collective-permute-start.8 = (bf16[72,1024]{1,0:T(8,128)(2,1)S(1)}, bf16[72,1024]{1,0:T(8,128)(2,1)S(1)}, u32[]{:S(2)}, u32[]{:S(2)}) collective-permute-start(bf16[72,1024]{1,0:T(8,128)(2,1)S(1)} %collective-permute-done.3.refs_3_), channel_id=1, source_target_pairs={{0,16},{4,20},{8,24},{12,28},{1,17},{5,21},{9,25},{13,29},{2,18},{... | collective-permute-start | bytes 442376 | tf_op jit(solution)/shard_map/ppermute | solution.py:264
  30.9 1.9 %collective-permute-start.4 = (bf16[72,1024]{1,0:T(8,128)(2,1)S(1)}, bf16[72,1024]{1,0:T(8,128)(2,1)S(1)}, u32[]{:S(2)}, u32[]{:S(2)}) collective-permute-start(bf16[72,1024]{1,0:T(8,128)(2,1)S(1)} %copy-done.3), channel_id=1, source_target_pairs={{0,4},{4,0},{8,12},{12,8},{16,20},{24,28},{1,5},{5,1},{9,13},{13,9... | collective-permute-start | bytes 442376 | tf_op jit(solution)/shard_map/ppermute | solution.py:256
  32.8 3.6 %collective-permute-start.5 = (bf16[72,1024]{1,0:T(8,128)(2,1)S(1)}, bf16[72,1024]{1,0:T(8,128)(2,1)S(1)}, u32[]{:S(2)}, u32[]{:S(2)}) collective-permute-start(bf16[72,1024]{1,0:T(8,128)(2,1)S(1)} %copy-done.3), channel_id=1, source_target_pairs={{0,8},{4,12},{8,0},{12,4},{16,24},{20,28},{1,9},{5,13},{9,1},{13,5... | collective-permute-start | bytes 442376 | tf_op jit(solution)/shard_map/ppermute | solution.py:256
  36.5 7.8 %attend.2 = (bf16[72,8192]{1,0:T(8,128)(2,1)}, bf16[72,8192]{1,0:T(8,128)(2,1)}, bf16[4,72,1024]{2,1,0:T(8,128)(2,1)S(1)}, bf16[4,72,1024]{2,1,0:T(8,128)(2,1)S(1)}) custom-call(s32[2]{0:T(128)S(1)} %copy-done.5, bf16[72,1024]{1,0:T(8,128)(2,1)S(1)} %copy-done.4, bf16[72,1024]{1,0:T(8,128)(2,1)S(1)} %collective-permute-done.refs_1_, ...), custom_call_target="tpu_custom_call" | custom-call | flops 11530000384 | bytes 36900000 | tf_op jit(solution)/shard_map/attend/pallas_call | solution.py:340
  44.3 3.9 %collective-permute-start.9 = (bf16[72,1024]{1,0:T(8,128)(2,1)S(1)}, bf16[72,1024]{1,0:T(8,128)(2,1)S(1)}, u32[]{:S(2)}, u32[]{:S(2)}) collective-permute-start(bf16[72,1024]{1,0:T(8,128)(2,1)S(1)} %collective-permute-done.5.refs_2_), channel_id=1, source_target_pairs={{0,4},{4,0},{8,12},{12,8},{24,28},{28,24},{1,5},{5,1},{9,13},{13,9... | collective-permute-start | bytes 442376 | tf_op jit(solution)/shard_map/ppermute | solution.py:256
  48.2 1.3 %collective-permute-start.11 = (bf16[72,1024]{1,0:T(8,128)(2,1)S(1)}, bf16[72,1024]{1,0:T(8,128)(2,1)S(1)}, u32[]{:S(2)}, u32[]{:S(2)}) collective-permute-start(bf16[72,1024]{1,0:T(8,128)(2,1)S(1)} %collective-permute-done.5.refs_2_), channel_id=1, source_target_pairs={{0,16},{4,20},{8,24},{12,28},{1,17},{5,21},{9,25},{13,29},{2,18},{... | collective-permute-start | bytes 442376 | tf_op jit(solution)/shard_map/ppermute | solution.py:264
  49.5 1.3 %collective-permute-start.10 = (bf16[72,1024]{1,0:T(8,128)(2,1)S(1)}, bf16[72,1024]{1,0:T(8,128)(2,1)S(1)}, u32[]{:S(2)}, u32[]{:S(2)}) collective-permute-start(bf16[72,1024]{1,0:T(8,128)(2,1)S(1)} %collective-permute-done.4.refs_1_), channel_id=1, source_target_pairs={{0,16},{4,20},{8,24},{12,28},{1,17},{5,21},{9,25},{13,29},{2,18},{... | collective-permute-start | bytes 442376 | tf_op jit(solution)/shard_map/ppermute | solution.py:264
  51.3 1.3 %collective-permute-start.12 = (bf16[72,1024]{1,0:T(8,128)(2,1)S(1)}, bf16[72,1024]{1,0:T(8,128)(2,1)S(1)}, u32[]{:S(2)}, u32[]{:S(2)}) collective-permute-start(bf16[72,1024]{1,0:T(8,128)(2,1)S(1)} %collective-permute-done.9.refs_3_), channel_id=1, source_target_pairs={{0,16},{4,20},{8,24},{12,28},{1,17},{5,21},{9,25},{13,29},{2,18},{... | collective-permute-start | bytes 442376 | tf_op jit(solution)/shard_map/ppermute | solution.py:264
  52.6 1.3 %collective-permute-start.14 = (bf16[4,72,1024]{2,1,0:T(8,128)(2,1)S(1)}, bf16[4,72,1024]{2,1,0:T(8,128)(2,1)S(1)}, u32[]{:S(2)}, u32[]{:S(2)}) collective-permute-start(bf16[4,72,1024]{2,1,0:T(8,128)(2,1)S(1)} %get-tuple-element.74), channel_id=1, source_target_pairs={{16,0},{20,4},{24,8},{28,12},{17,1},{21,5},{25,9},{29,13},{18,2},{... | collective-permute-start | bytes 1769480 | tf_op jit(solution)/shard_map/ppermute | solution.py:264
  54.2 1.6 %collective-permute-done.12.refs_7_ = bf16[72,1024]{1,0:T(8,128)(2,1)S(1)} collective-permute-done((bf16[72,1024]{1,0:T(8,128)(2,1)S(1)}, bf16[72,1024]{1,0:T(8,128)(2,1)S(1)}, u32[]{:S(2)}, u32[]{:S(2)}) %collective-permute-start.12) | collective-permute-done | bytes 147488 | tf_op jit(solution)/shard_map/ppermute | solution.py:264
  55.8 7.8 %attend.3 = (bf16[72,8192]{1,0:T(8,128)(2,1)}, bf16[72,8192]{1,0:T(8,128)(2,1)}, bf16[4,72,1024]{2,1,0:T(8,128)(2,1)S(1)}, bf16[4,72,1024]{2,1,0:T(8,128)(2,1)S(1)}) custom-call(s32[2]{0:T(128)S(1)} %copy-done.5, bf16[72,1024]{1,0:T(8,128)(2,1)S(1)} %copy-done.3, ...), custom_call_target="tpu_custom_call", output_to_operand_aliasing={{0}: (15, {}), {1}: (16, {})} | custom-call | flops 11530000384 | bytes 36900000 | tf_op jit(solution)/shard_map/attend/pallas_call | solution.py:340
  63.5 1.3 %collective-permute-start.13 = (bf16[4,72,1024]{2,1,0:T(8,128)(2,1)S(1)}, bf16[4,72,1024]{2,1,0:T(8,128)(2,1)S(1)}, u32[]{:S(2)}, u32[]{:S(2)}) collective-permute-start(bf16[4,72,1024]{2,1,0:T(8,128)(2,1)S(1)} %get-tuple-element.72), channel_id=1, source_target_pairs={{16,0},{20,4},{24,8},{28,12},{17,1},{21,5},{25,9},{29,13},{18,2},{... | collective-permute-start | bytes 1769480 | tf_op jit(solution)/shard_map/ppermute | solution.py:264
  64.8 2.6 %collective-permute-done.14.refs_1_ = bf16[4,72,1024]{2,1,0:T(8,128)(2,1)S(1)} collective-permute-done((bf16[4,72,1024]{2,1,0:T(8,128)(2,1)S(1)}, bf16[4,72,1024]{2,1,0:T(8,128)(2,1)S(1)}, u32[]{:S(2)}, u32[]{:S(2)}) %collective-permute-start.14) | collective-permute-done | bytes 589856 | tf_op jit(solution)/shard_map/ppermute | solution.py:264
  67.5 2.9 %collective-permute-start.15 = (bf16[72,1024]{1,0:T(8,128)(2,1)S(1)}, bf16[72,1024]{1,0:T(8,128)(2,1)S(1)}, u32[]{:S(2)}, u32[]{:S(2)}) collective-permute-start(bf16[72,1024]{1,0:T(8,128)(2,1)S(1)} %get-tuple-element.77), channel_id=1, source_target_pairs={{0,4},{4,0},{8,12},{12,8},{20,16},{28,24},{1,5},{5,1},{9,13},{13,9... | collective-permute-start | bytes 442376 | tf_op jit(solution)/shard_map/ppermute | solution.py:256
  70.5 4.3 %collective-permute-start.16 = (bf16[72,1024]{1,0:T(8,128)(2,1)S(1)}, bf16[72,1024]{1,0:T(8,128)(2,1)S(1)}, u32[]{:S(2)}, u32[]{:S(2)}) collective-permute-start(bf16[72,1024]{1,0:T(8,128)(2,1)S(1)} %get-tuple-element.78), channel_id=1, source_target_pairs={{0,8},{4,12},{8,0},{12,4},{24,16},{28,20},{1,9},{5,13},{9,1},{13,5... | collective-permute-start | bytes 442376 | tf_op jit(solution)/shard_map/ppermute | solution.py:256
  74.8 2.8 %collective-permute-start.17 = (bf16[72,1024]{1,0:T(8,128)(2,1)S(1)}, bf16[72,1024]{1,0:T(8,128)(2,1)S(1)}, u32[]{:S(2)}, u32[]{:S(2)}) collective-permute-start(bf16[72,1024]{1,0:T(8,128)(2,1)S(1)} %get-tuple-element.79), channel_id=1, source_target_pairs={{0,12},{4,8},{8,4},{12,0},{24,20},{28,16},{1,13},{5,9},{9,5},{13,1... | collective-permute-start | bytes 442376 | tf_op jit(solution)/shard_map/ppermute | solution.py:256
  78.4 3.5 %collective-permute-start.18 = (bf16[72,1024]{1,0:T(8,128)(2,1)S(1)}, bf16[72,1024]{1,0:T(8,128)(2,1)S(1)}, u32[]{:S(2)}, u32[]{:S(2)}) collective-permute-start(bf16[72,1024]{1,0:T(8,128)(2,1)S(1)} %get-tuple-element.83), channel_id=1, source_target_pairs={{0,4},{4,0},{8,12},{12,8},{20,16},{28,24},{1,5},{5,1},{9,13},{13,9... | collective-permute-start | bytes 442376 | tf_op jit(solution)/shard_map/ppermute | solution.py:256
  82.0 4.4 %collective-permute-start.19 = (bf16[72,1024]{1,0:T(8,128)(2,1)S(1)}, bf16[72,1024]{1,0:T(8,128)(2,1)S(1)}, u32[]{:S(2)}, u32[]{:S(2)}) collective-permute-start(bf16[72,1024]{1,0:T(8,128)(2,1)S(1)} %get-tuple-element.84), channel_id=1, source_target_pairs={{0,8},{4,12},{8,0},{12,4},{24,16},{28,20},{1,9},{5,13},{9,1},{13,5... | collective-permute-start | bytes 442376 | tf_op jit(solution)/shard_map/ppermute | solution.py:256
  86.4 2.2 %collective-permute-start.20 = (bf16[72,1024]{1,0:T(8,128)(2,1)S(1)}, bf16[72,1024]{1,0:T(8,128)(2,1)S(1)}, u32[]{:S(2)}, u32[]{:S(2)}) collective-permute-start(bf16[72,1024]{1,0:T(8,128)(2,1)S(1)} %get-tuple-element.85), channel_id=1, source_target_pairs={{0,12},{4,8},{8,4},{12,0},{24,20},{28,16},{1,13},{5,9},{9,5},{13,1... | collective-permute-start | bytes 442376 | tf_op jit(solution)/shard_map/ppermute | solution.py:256
  88.6 7.2 %collective-permute-done.19.refs_8_ = bf16[72,1024]{1,0:T(8,128)(2,1)S(1)} collective-permute-done((bf16[72,1024]{1,0:T(8,128)(2,1)S(1)}, bf16[72,1024]{1,0:T(8,128)(2,1)S(1)}, u32[]{:S(2)}, u32[]{:S(2)}) %collective-permute-start.19) | collective-permute-done | bytes 147488 | tf_op jit(solution)/shard_map/ppermute | solution.py:256
  95.8 0.9 finish.1
  (29 shorter events, 2.4 us)
Async XLA Ops:
  2.7 19.8 %collective-permute-start = (bf16[72,1024]{1,0:T(8,128)(2,1)}, bf16[72,1024]{1,0:T(8,128)(2,1)S(1)}, u32[]{:S(2)}, u32[]{:S(2)}) collective-permute-start(bf16[72,1024]{1,0:T(8,128)(2,1)} %get-tuple-element.52.refs_0_), channel_id=1, source_target_pairs={{0,4},{4,0},{8,12},{12,8},{16,20},{24,28},{1,5},{5,1},{9,13},{13,9... | collective-permute-start | bytes 442376 | tf_op jit(solution)/shard_map/ppermute | solution.py:256
  7.6 14.9 %collective-permute-start.1 = (bf16[72,1024]{1,0:T(8,128)(2,1)}, bf16[72,1024]{1,0:T(8,128)(2,1)S(1)}, u32[]{:S(2)}, u32[]{:S(2)}) collective-permute-start(bf16[72,1024]{1,0:T(8,128)(2,1)} %get-tuple-element.52.refs_0_), channel_id=1, source_target_pairs={{0,8},{4,12},{8,0},{12,4},{16,24},{20,28},{1,9},{5,13},{9,1},{13,5... | collective-permute-start | bytes 442376 | tf_op jit(solution)/shard_map/ppermute | solution.py:256
  12.2 10.4 %collective-permute-start.2 = (bf16[72,2048]{1,0:T(8,128)(2,1)}, bf16[72,2048]{1,0:T(8,128)(2,1)S(1)}, u32[]{:S(2)}, u32[]{:S(2)}) collective-permute-start(bf16[72,2048]{1,0:T(8,128)(2,1)} %get-tuple-element.49), channel_id=1, source_target_pairs={{0,16},{4,20},{8,24},{12,28},{1,17},{5,21},{9,25},{13,29},{2,18},{... | collective-permute-start | bytes 884744 | tf_op jit(solution)/shard_map/ppermute | solution.py:264
  15.6 0.7 copy-start
  16.3 1.3 %copy-start.1 = (bf16[72,8192]{1,0:T(8,128)(2,1)S(1)}, bf16[72,8192]{1,0:T(8,128)(2,1)}, u32[]{:S(2)}) copy-start(bf16[72,8192]{1,0:T(8,128)(2,1)} %query_ref.1) | copy-start | bytes 3538948
  17.6 1.3 %copy-start.2 = (bf16[72,8192]{1,0:T(8,128)(2,1)S(1)}, bf16[72,8192]{1,0:T(8,128)(2,1)}, u32[]{:S(2)}) copy-start(bf16[72,8192]{1,0:T(8,128)(2,1)} %grad_ref.1) | copy-start | bytes 3538948
  18.8 12.0 %copy-start.3 = (bf16[72,1024]{1,0:T(8,128)(2,1)S(1)}, bf16[72,1024]{1,0:T(8,128)(2,1)}, u32[]{:S(2)}) copy-start(bf16[72,1024]{1,0:T(8,128)(2,1)} %get-tuple-element.63.refs_0_) | copy-start | bytes 442372
  18.8 17.6 %copy-start.4 = (bf16[72,1024]{1,0:T(8,128)(2,1)S(1)}, bf16[72,1024]{1,0:T(8,128)(2,1)}, u32[]{:S(2)}) copy-start(bf16[72,1024]{1,0:T(8,128)(2,1)} %get-tuple-element.52.refs_0_) | copy-start | bytes 442372
  18.8 17.6 %copy-start.5 = (s32[2]{0:T(128)S(1)}, s32[2]{0:T(128)}, u32[]{:S(2)}) copy-start(s32[2]{0:T(128)} %counts_ref.3) | copy-start | bytes 28
  22.5 7.0 %collective-permute-start.3 = (bf16[72,1024]{1,0:T(8,128)(2,1)S(1)}, bf16[72,1024]{1,0:T(8,128)(2,1)S(1)}, u32[]{:S(2)}, u32[]{:S(2)}) collective-permute-start(bf16[72,1024]{1,0:T(8,128)(2,1)S(1)} %collective-permute-done.1.refs_2_), channel_id=1, source_target_pairs={{0,4},{4,0},{8,12},{12,8},{24,28},{28,24},{1,5},{5,1},{9,13},{13,9... | collective-permute-start | bytes 442376 | tf_op jit(solution)/shard_map/ppermute | solution.py:256
  24.5 12.0 %collective-permute-start.7 = (bf16[72,1024]{1,0:T(8,128)(2,1)S(1)}, bf16[72,1024]{1,0:T(8,128)(2,1)S(1)}, u32[]{:S(2)}, u32[]{:S(2)}) collective-permute-start(bf16[72,1024]{1,0:T(8,128)(2,1)S(1)} %collective-permute-done.1.refs_2_), channel_id=1, source_target_pairs={{0,16},{4,20},{8,24},{12,28},{1,17},{5,21},{9,25},{13,29},{2,18},{... | collective-permute-start | bytes 442376 | tf_op jit(solution)/shard_map/ppermute | solution.py:264
  26.6 9.9 %collective-permute-start.6 = (bf16[72,1024]{1,0:T(8,128)(2,1)S(1)}, bf16[72,1024]{1,0:T(8,128)(2,1)S(1)}, u32[]{:S(2)}, u32[]{:S(2)}) collective-permute-start(bf16[72,1024]{1,0:T(8,128)(2,1)S(1)} %collective-permute-done.refs_1_), channel_id=1, source_target_pairs={{0,16},{4,20},{8,24},{12,28},{1,17},{5,21},{9,25},{13,29},{2,18},{... | collective-permute-start | bytes 442376 | tf_op jit(solution)/shard_map/ppermute | solution.py:264
  29.6 6.9 %collective-permute-start.8 = (bf16[72,1024]{1,0:T(8,128)(2,1)S(1)}, bf16[72,1024]{1,0:T(8,128)(2,1)S(1)}, u32[]{:S(2)}, u32[]{:S(2)}) collective-permute-start(bf16[72,1024]{1,0:T(8,128)(2,1)S(1)} %collective-permute-done.3.refs_3_), channel_id=1, source_target_pairs={{0,16},{4,20},{8,24},{12,28},{1,17},{5,21},{9,25},{13,29},{2,18},{... | collective-permute-start | bytes 442376 | tf_op jit(solution)/shard_map/ppermute | solution.py:264
  30.9 13.4 %collective-permute-start.4 = (bf16[72,1024]{1,0:T(8,128)(2,1)S(1)}, bf16[72,1024]{1,0:T(8,128)(2,1)S(1)}, u32[]{:S(2)}, u32[]{:S(2)}) collective-permute-start(bf16[72,1024]{1,0:T(8,128)(2,1)S(1)} %copy-done.3), channel_id=1, source_target_pairs={{0,4},{4,0},{8,12},{12,8},{16,20},{24,28},{1,5},{5,1},{9,13},{13,9... | collective-permute-start | bytes 442376 | tf_op jit(solution)/shard_map/ppermute | solution.py:256
  32.8 11.5 %collective-permute-start.5 = (bf16[72,1024]{1,0:T(8,128)(2,1)S(1)}, bf16[72,1024]{1,0:T(8,128)(2,1)S(1)}, u32[]{:S(2)}, u32[]{:S(2)}) collective-permute-start(bf16[72,1024]{1,0:T(8,128)(2,1)S(1)} %copy-done.3), channel_id=1, source_target_pairs={{0,8},{4,12},{8,0},{12,4},{16,24},{20,28},{1,9},{5,13},{9,1},{13,5... | collective-permute-start | bytes 442376 | tf_op jit(solution)/shard_map/ppermute | solution.py:256
  44.3 7.0 %collective-permute-start.9 = (bf16[72,1024]{1,0:T(8,128)(2,1)S(1)}, bf16[72,1024]{1,0:T(8,128)(2,1)S(1)}, u32[]{:S(2)}, u32[]{:S(2)}) collective-permute-start(bf16[72,1024]{1,0:T(8,128)(2,1)S(1)} %collective-permute-done.5.refs_2_), channel_id=1, source_target_pairs={{0,4},{4,0},{8,12},{12,8},{24,28},{28,24},{1,5},{5,1},{9,13},{13,9... | collective-permute-start | bytes 442376 | tf_op jit(solution)/shard_map/ppermute | solution.py:256
  48.2 5.9 %collective-permute-start.11 = (bf16[72,1024]{1,0:T(8,128)(2,1)S(1)}, bf16[72,1024]{1,0:T(8,128)(2,1)S(1)}, u32[]{:S(2)}, u32[]{:S(2)}) collective-permute-start(bf16[72,1024]{1,0:T(8,128)(2,1)S(1)} %collective-permute-done.5.refs_2_), channel_id=1, source_target_pairs={{0,16},{4,20},{8,24},{12,28},{1,17},{5,21},{9,25},{13,29},{2,18},{... | collective-permute-start | bytes 442376 | tf_op jit(solution)/shard_map/ppermute | solution.py:264
  49.5 4.6 %collective-permute-start.10 = (bf16[72,1024]{1,0:T(8,128)(2,1)S(1)}, bf16[72,1024]{1,0:T(8,128)(2,1)S(1)}, u32[]{:S(2)}, u32[]{:S(2)}) collective-permute-start(bf16[72,1024]{1,0:T(8,128)(2,1)S(1)} %collective-permute-done.4.refs_1_), channel_id=1, source_target_pairs={{0,16},{4,20},{8,24},{12,28},{1,17},{5,21},{9,25},{13,29},{2,18},{... | collective-permute-start | bytes 442376 | tf_op jit(solution)/shard_map/ppermute | solution.py:264
  51.3 4.4 %collective-permute-start.12 = (bf16[72,1024]{1,0:T(8,128)(2,1)S(1)}, bf16[72,1024]{1,0:T(8,128)(2,1)S(1)}, u32[]{:S(2)}, u32[]{:S(2)}) collective-permute-start(bf16[72,1024]{1,0:T(8,128)(2,1)S(1)} %collective-permute-done.9.refs_3_), channel_id=1, source_target_pairs={{0,16},{4,20},{8,24},{12,28},{1,17},{5,21},{9,25},{13,29},{2,18},{... | collective-permute-start | bytes 442376 | tf_op jit(solution)/shard_map/ppermute | solution.py:264
  52.6 14.8 %collective-permute-start.14 = (bf16[4,72,1024]{2,1,0:T(8,128)(2,1)S(1)}, bf16[4,72,1024]{2,1,0:T(8,128)(2,1)S(1)}, u32[]{:S(2)}, u32[]{:S(2)}) collective-permute-start(bf16[4,72,1024]{2,1,0:T(8,128)(2,1)S(1)} %get-tuple-element.74), channel_id=1, source_target_pairs={{16,0},{20,4},{24,8},{28,12},{17,1},{21,5},{25,9},{29,13},{18,2},{... | collective-permute-start | bytes 1769480 | tf_op jit(solution)/shard_map/ppermute | solution.py:264
  63.5 14.8 %collective-permute-start.13 = (bf16[4,72,1024]{2,1,0:T(8,128)(2,1)S(1)}, bf16[4,72,1024]{2,1,0:T(8,128)(2,1)S(1)}, u32[]{:S(2)}, u32[]{:S(2)}) collective-permute-start(bf16[4,72,1024]{2,1,0:T(8,128)(2,1)S(1)} %get-tuple-element.72), channel_id=1, source_target_pairs={{16,0},{20,4},{24,8},{28,12},{17,1},{21,5},{25,9},{29,13},{18,2},{... | collective-permute-start | bytes 1769480 | tf_op jit(solution)/shard_map/ppermute | solution.py:264
  67.5 18.9 %collective-permute-start.15 = (bf16[72,1024]{1,0:T(8,128)(2,1)S(1)}, bf16[72,1024]{1,0:T(8,128)(2,1)S(1)}, u32[]{:S(2)}, u32[]{:S(2)}) collective-permute-start(bf16[72,1024]{1,0:T(8,128)(2,1)S(1)} %get-tuple-element.77), channel_id=1, source_target_pairs={{0,4},{4,0},{8,12},{12,8},{20,16},{28,24},{1,5},{5,1},{9,13},{13,9... | collective-permute-start | bytes 442376 | tf_op jit(solution)/shard_map/ppermute | solution.py:256
  70.5 18.1 %collective-permute-start.16 = (bf16[72,1024]{1,0:T(8,128)(2,1)S(1)}, bf16[72,1024]{1,0:T(8,128)(2,1)S(1)}, u32[]{:S(2)}, u32[]{:S(2)}) collective-permute-start(bf16[72,1024]{1,0:T(8,128)(2,1)S(1)} %get-tuple-element.78), channel_id=1, source_target_pairs={{0,8},{4,12},{8,0},{12,4},{24,16},{28,20},{1,9},{5,13},{9,1},{13,5... | collective-permute-start | bytes 442376 | tf_op jit(solution)/shard_map/ppermute | solution.py:256
  74.8 13.8 %collective-permute-start.17 = (bf16[72,1024]{1,0:T(8,128)(2,1)S(1)}, bf16[72,1024]{1,0:T(8,128)(2,1)S(1)}, u32[]{:S(2)}, u32[]{:S(2)}) collective-permute-start(bf16[72,1024]{1,0:T(8,128)(2,1)S(1)} %get-tuple-element.79), channel_id=1, source_target_pairs={{0,12},{4,8},{8,4},{12,0},{24,20},{28,16},{1,13},{5,9},{9,5},{13,1... | collective-permute-start | bytes 442376 | tf_op jit(solution)/shard_map/ppermute | solution.py:256
  78.4 10.2 %collective-permute-start.18 = (bf16[72,1024]{1,0:T(8,128)(2,1)S(1)}, bf16[72,1024]{1,0:T(8,128)(2,1)S(1)}, u32[]{:S(2)}, u32[]{:S(2)}) collective-permute-start(bf16[72,1024]{1,0:T(8,128)(2,1)S(1)} %get-tuple-element.83), channel_id=1, source_target_pairs={{0,4},{4,0},{8,12},{12,8},{20,16},{28,24},{1,5},{5,1},{9,13},{13,9... | collective-permute-start | bytes 442376 | tf_op jit(solution)/shard_map/ppermute | solution.py:256
  82.0 13.8 %collective-permute-start.19 = (bf16[72,1024]{1,0:T(8,128)(2,1)S(1)}, bf16[72,1024]{1,0:T(8,128)(2,1)S(1)}, u32[]{:S(2)}, u32[]{:S(2)}) collective-permute-start(bf16[72,1024]{1,0:T(8,128)(2,1)S(1)} %get-tuple-element.84), channel_id=1, source_target_pairs={{0,8},{4,12},{8,0},{12,4},{24,16},{28,20},{1,9},{5,13},{9,1},{13,5... | collective-permute-start | bytes 442376 | tf_op jit(solution)/shard_map/ppermute | solution.py:256
  86.4 9.4 %collective-permute-start.20 = (bf16[72,1024]{1,0:T(8,128)(2,1)S(1)}, bf16[72,1024]{1,0:T(8,128)(2,1)S(1)}, u32[]{:S(2)}, u32[]{:S(2)}) collective-permute-start(bf16[72,1024]{1,0:T(8,128)(2,1)S(1)} %get-tuple-element.85), channel_id=1, source_target_pairs={{0,12},{4,8},{8,4},{12,0},{24,20},{28,16},{1,13},{5,9},{9,5},{13,1... | collective-permute-start | bytes 442376 | tf_op jit(solution)/shard_map/ppermute | solution.py:256

commit v6 on v5

--- a/solution.py
+++ b/solution.py
@@ -73,16 +73,13 @@
 
 
 def prepare_queries(rows, pos_ref, query_ref, grad_ref, *out_refs):
-    q_ref, qt_ref, g_ref, gt_ref, cos_ref, sin_ref, cos_t_ref, sin_t_ref = out_refs
+    q_ref, qt_ref, g_ref, gt_ref, cos_ref, sin_ref = out_refs
 
     @pl.when(pl.program_id(0) == 0)
     def _():
         cosine, sine = angle_tables(rows, query_ref.shape[0], pos_ref)
         cos_ref[...] = cosine
         sin_ref[...] = sine
-        half = HEAD_WIDTH // 2
-        cos_t_ref[...] = jnp.concatenate([cosine] * GROUP, 0).T[half:] * SCORE_SCALE
-        sin_t_ref[...] = jnp.concatenate([sine] * GROUP, 0).T[half:] * SCORE_SCALE
 
     cosine, sine = cos_ref[...], sin_ref[...]
     queries = jnp.concatenate(
@@ -143,41 +140,32 @@
     def gathered(first, place):
         cols = lanes(first, place)
         wide = jnp.concatenate([ref[:, cols].astype(jnp.float32) for ref in kv_refs], 0)
-        low = wide.astype(jnp.bfloat16)
-        return low, low.T
+        return wide.astype(jnp.bfloat16)
 
     heads = range(STEP_HEADS)
     keys, values = [gathered(0, p) for p in heads], [gathered(HEADS_PER_CHUNK, p) for p in heads]
     bias, live = bias_ref[...], live_ref[0:1, :]
-    scores = [dot(keys[p][0], qt_ref[p]) * (SCORE_SCALE * LOG2_E) + bias for p in heads]
-    dprobs, probs, probs_low = [], [], []
+    scores = [dot(keys[p], qt_ref[p]) * (SCORE_SCALE * LOG2_E) + bias for p in heads]
+    probs, probs_low, dscores = [], [], []
     for p in heads:
         weights = jnp.exp2(scores[p] - jnp.max(scores[p], 0, keepdims=True))
         probs.append(weights * (live / jnp.sum(weights, 0, keepdims=True)))
         probs_low.append(probs[p].astype(jnp.bfloat16))
-        dprobs.append(dot(values[p][0], gt_ref[p]))
-    outs_t, value_parts, dscores = [], [], []
     for p in heads:
-        outs_t.append(dot(values[p][1], probs_low[p]))
-        value_parts.append(dot(probs_low[p], g_ref[p]))
-        out_low = outs_t[p].astype(jnp.bfloat16).astype(jnp.float32)
-        delta = jnp.sum(gt_ref[p].astype(jnp.float32) * out_low, 0, keepdims=True)
-        dscores.append((probs[p] * (dprobs[p] - delta)).astype(jnp.bfloat16))
-    grads_t = [dot(keys[p][1], dscores[p]) for p in heads]
+        weighted = probs[p] * dot(values[p], gt_ref[p])
+        delta = jnp.sum(weighted, 0, keepdims=True)
+        dscores.append((weighted - probs[p] * delta).astype(jnp.bfloat16))
+    outs = [dot(probs_low[p].T, values[p]) for p in heads]
+    value_parts = [dot(probs_low[p], g_ref[p]) for p in heads]
+    grads = [dot(dscores[p].T, keys[p]) * SCORE_SCALE for p in heads]
     key_parts = [dot(dscores[p], q_ref[p]) * SCORE_SCALE for p in heads]
 
     cosine, sine = cos_ref[...], sin_ref[...]
-    half = HEAD_WIDTH // 2
     for p in heads:
-        first, second = grads_t[p][:half], grads_t[p][half:]
-        turned = [first * cosine + second * sine, second * cosine - first * sine]
-        grad_low = jnp.concatenate(turned, 0).astype(jnp.bfloat16)
-        out_heads = outs_t[p].astype(jnp.bfloat16).T.astype(jnp.float32)
-        grad_heads = grad_low.T.astype(jnp.float32)
         for h in range(GROUP):
             piece, cols = slice(h * padded, (h + 1) * padded), head_cols(p * GROUP + h)
-            out_ref[:, cols] = out_heads[piece].astype(jnp.bfloat16)
-            grad_ref[:, cols] = grad_heads[piece].astype(jnp.bfloat16)
+            out_ref[:, cols] = outs[p][piece].astype(jnp.bfloat16)
+            grad_ref[:, cols] = rope_back(grads[p][piece], cosine, sine).astype(jnp.bfloat16)
         for block in range(blocks):
             seq_offset, head_offset = divmod(block, head_count)
             piece = slice(block * padded, (block + 1) * padded)
@@ -264,7 +252,6 @@
         return lax.ppermute(x, ("seq", "head"), pairs)
 
     table = shape((padded, HEAD_WIDTH), f32)
-    table_t = shape((HEAD_WIDTH // 2, query_rows), f32)
     piece = shape((padded, 2 * CHUNK_COLS), bf16)
     whole, *own = pl.pallas_call(
         functools.partial(prepare_keys, rows),
@@ -282,14 +269,13 @@
     flat_block = pl.BlockSpec((1, HEAD_WIDTH, query_rows), lambda g: (g, 0, 0))
     tall = shape((KEY_VALUE_HEADS, query_rows, HEAD_WIDTH), bf16)
     flat = shape((KEY_VALUE_HEADS, HEAD_WIDTH, query_rows), bf16)
-    table_t_block = pl.BlockSpec(table_t.shape, lambda g: (0, 0))
-    *stacked, cosine, sine, cosine_t, sine_t = pl.pallas_call(
+    *stacked, cosine, sine = pl.pallas_call(
         functools.partial(prepare_queries, rows),
         grid=(KEY_VALUE_HEADS,),
-        out_shape=[tall, flat, tall, flat, table, table, table_t, table_t],
+        out_shape=[tall, flat, tall, flat, table, table],
         in_specs=[SMEM, row_block, row_block],
         out_specs=[tall_block, flat_block, tall_block, flat_block]
-        + [table_block, table_block, table_t_block, table_t_block],
+        + [table_block, table_block],
         cost_estimate=cost(7),
         compiler_params=params(16),
         name="prepare_queries",
@@ -300,20 +286,30 @@
     firsts = sorted({bits[0], 1})
     far = {a: along_seq(whole, a, True) for a in later}
     near = {0: own[0], **{j: along_head(own[0], j, True) for j in firsts}}
-    near, cosine_t, far = lax.optimization_barrier((near, cosine_t, far))
-
-    def gather(near):
+    near, own[1:], cosine, far = lax.optimization_barrier((near, own[1:], cosine, far))
+
+    def exchange(near):
         for bit in bits[1:]:
             near.update(
                 {j ^ bit: along_head(x, bit, True, j) for j, x in near.items() if j ^ bit not in near}
             )
-        crossed = {
-            (a, j): along_seq(near[j], a, True) for j in range(1, head_count) for a in later
-        }
-        blocks_here = [near[j] for j in range(head_count)]
-        for a in later:
-            blocks_here += [far[a]] + [crossed[a, j] for j in range(1, head_count)]
-        return blocks_here
+
+    def cross(near, offsets):
+        return {(a, j): along_seq(near[j], a, True) for j in offsets for a in later}
+
+    gathered = []
+    for chunk in range(CHUNKS):
+        if chunk:
+            near = {0: own[chunk], **{j: along_head(own[chunk], j, True) for j in firsts}}
+            near, crossed = lax.optimization_barrier((near, crossed))
+            gathered[-1].update(crossed)
+        crossed = cross(near, firsts)
+        exchange(near)
+        gathered.append(
+            near | crossed | cross(near, [j for j in near if j not in (0, *firsts)])
+        )
+    far_own = [(a, 0) for a in later]
+    order = list(range(head_count)) + [(a, j) for a in later for j in range(head_count)]
 
     wide_outs = ()
     parts = []
@@ -325,15 +321,6 @@
             for x in (tall, flat)
         )
         row_part = pl.BlockSpec((padded, STEP_HEADS * wide), lambda g, f=first: (0, f + g))
-        if chunk:
-            near = {0: own[chunk], **{j: along_head(own[chunk], j, True) for j in firsts}}
-            near, parts[-1][0] = lax.optimization_barrier((near, parts[-1][0]))
-        gathered = gather(near)
-        if chunk + 1 < CHUNKS:
-            last = head_count - 1
-            own[chunk + 1], gathered[last] = lax.optimization_barrier(
-                (own[chunk + 1], gathered[last])
-            )
         kv_whole = pl.BlockSpec((padded, 2 * CHUNK_COLS), lambda g, c=chunk: (0, c))
         kv_chunk = pl.BlockSpec((padded, 2 * CHUNK_COLS), lambda g: (0, 0))
         part_block = pl.BlockSpec((head_count, padded, 2 * CHUNK_COLS), lambda g: (0, 0, 0))
@@ -345,7 +332,7 @@
             in_specs=[SMEM]
             + [kv_chunk] * head_count
             + ([kv_whole] + [kv_chunk] * (head_count - 1)) * (seq_count - 1)
-            + [tall_part, flat_part, tall_part, flat_part, table_t_block, table_t_block]
+            + [tall_part, flat_part, tall_part, flat_part, table_block, table_block]
             + [pl.BlockSpec(memory_space=pl.ANY)] * (2 * has_alias),
             out_specs=[row_part, row_part] + [part_block] * seq_count,
             scratch_shapes=[
@@ -356,7 +343,14 @@
             cost_estimate=cost(10),
             compiler_params=params(32),
             name="attend",
-        )(counts, *gathered, *stacked, cosine_t, sine_t, *wide_outs)
+        )(
+            counts,
+            *(far[k[0]] if k in far_own else gathered[chunk][k] for k in order),
+            *stacked,
+            cosine,
+            sine,
+            *wide_outs,
+        )
         wide_outs = out[:2]
         parts.append([out[2]] + [along_seq(out[2 + a], a, False) for a in later])
 

time: 97.4 us -> 99.3 us (1.020)
  waiting for transfers between devices: 14.5 us -> 17.1 us
  starting transfers between devices: 55.6 us -> 54.3 us
    ppermute x12, starting transfers between devices: 41 us -> 39 us  [along_head(): return lax.ppermute(x, ('seq', 'head'), pairs)]
    ppermute x9, waiting for transfers between devices: 5.06 us -> 6.92 us  [along_seq(): return lax.ppermute(x, ('seq', 'head'), pairs)]
  transfers between devices with their start and end apart: 21 -> 21, of which waited for: 7 -> 6; matrix products, arithmetic and copies ran while one was open for 0% -> 0% of each run, Pallas kernels for 20% -> 20%
where the time goes in v6:
time: 99.3 us; the launch traced here: 98.6 us
  starting transfers between devices  54.3 us (55%)
  Pallas kernels  23 us (23%)
  waiting for transfers between devices  17.1 us (17%)
  local copies, waits for them, and re-layouts  3.23 us (3%)
    ppermute x12, starting transfers between devices, along_head(): return lax.ppermute(x, ('seq', 'head'), pairs)  39 us
    pallas_call x2, Pallas kernels, shards(): pl.pallas_call(functools.partial(attend, seq_count, head_count, rows, has...  16.3 us
    ppermute x9, starting transfers between devices, along_seq(): return lax.ppermute(x, ('seq', 'head'), pairs)  15.4 us
    ppermute x12, waiting for transfers between devices, along_head(): return lax.ppermute(x, ('seq', 'head'), pairs)  10.2 us
    ppermute x9, waiting for transfers between devices, along_seq(): return lax.ppermute(x, ('seq', 'head'), pairs)  6.92 us
    pallas_call x1, Pallas kernels, shards(): pl.pallas_call(functools.partial(prepare_queries, rows), grid=(KEY_VALUE_...  3.41 us
    unnamed x12, local copies, waits for them, and re-layouts  3.23 us
    pallas_call x1, Pallas kernels, shards(): pl.pallas_call(functools.partial(prepare_keys, rows), out_shape=[shape((p...  2.09 us
  transfers between devices with their start and end apart: 21, of which 6 were waited for; matrix products, arithmetic and copies ran while one was open for 0% of the time, Pallas kernels for 20%

profile of v6, /device:TPU:0, one launch (start us, length us, event | category | flops | bytes accessed | tf_op | source)
XLA Modules:
  0.0 98.6 jit_solution(12845225640993233793)
XLA Ops:
  0.6 2.1 %prepare_keys.1 = (bf16[72,2048]{1,0:T(8,128)(2,1)}, bf16[72,1024]{1,0:T(8,128)(2,1)}, bf16[72,1024]{1,0:T(8,128)(2,1)}) custom-call(s32[576]{0:T(1024)} %pos_ref.3, bf16[72,1024]{1,0:T(8,128)(2,1)} %key_ref.1, bf16[72,1024]{1,0:T(8,128)(2,1)} %value_ref.1), custom_call_target="tpu_custom_call" | custom-call | tf_op jit(solution)/shard_map/prepare_keys/pallas_call | solution.py:256
  2.7 4.9 %collective-permute-start = (bf16[72,1024]{1,0:T(8,128)(2,1)}, bf16[72,1024]{1,0:T(8,128)(2,1)S(1)}, u32[]{:S(2)}, u32[]{:S(2)}) collective-permute-start(bf16[72,1024]{1,0:T(8,128)(2,1)} %get-tuple-element.61.refs_0_), channel_id=1, source_target_pairs={{0,4},{4,0},{8,12},{12,8},{16,20},{24,28},{1,5},{5,1},{9,13},{13,9... | collective-permute-start | bytes 442376 | tf_op jit(solution)/shard_map/ppermute | solution.py:244
  7.6 4.5 %collective-permute-start.1 = (bf16[72,1024]{1,0:T(8,128)(2,1)}, bf16[72,1024]{1,0:T(8,128)(2,1)S(1)}, u32[]{:S(2)}, u32[]{:S(2)}) collective-permute-start(bf16[72,1024]{1,0:T(8,128)(2,1)} %get-tuple-element.61.refs_0_), channel_id=1, source_target_pairs={{0,8},{4,12},{8,0},{12,4},{16,24},{20,28},{1,9},{5,13},{9,1},{13,5... | collective-permute-start | bytes 442376 | tf_op jit(solution)/shard_map/ppermute | solution.py:244
  12.2 3.4 %collective-permute-start.2 = (bf16[72,2048]{1,0:T(8,128)(2,1)}, bf16[72,2048]{1,0:T(8,128)(2,1)S(1)}, u32[]{:S(2)}, u32[]{:S(2)}) collective-permute-start(bf16[72,2048]{1,0:T(8,128)(2,1)} %get-tuple-element.47), channel_id=1, source_target_pairs={{0,16},{4,20},{8,24},{12,28},{1,17},{5,21},{9,25},{13,29},{2,18},{... | collective-permute-start | bytes 884744 | tf_op jit(solution)/shard_map/ppermute | solution.py:252
  16.3 1.3 %copy-done.1 = bf16[72,8192]{1,0:T(8,128)(2,1)S(1)} copy-done((bf16[72,8192]{1,0:T(8,128)(2,1)S(1)}, bf16[72,8192]{1,0:T(8,128)(2,1)}, u32[]{:S(2)}) %copy-start.1) | copy-done | bytes 1179672
  17.6 1.3 %copy-done.2 = bf16[72,8192]{1,0:T(8,128)(2,1)S(1)} copy-done((bf16[72,8192]{1,0:T(8,128)(2,1)S(1)}, bf16[72,8192]{1,0:T(8,128)(2,1)}, u32[]{:S(2)}) %copy-start.2) | copy-done | bytes 1179672
  18.8 3.4 %prepare_queries.1 = (bf16[8,576,128]{2,1,0:T(8,128)(2,1)S(1)}, bf16[8,128,576]{2,1,0:T(8,128)(2,1)S(1)}, bf16[8,576,128]{2,1,0:T(8,128)(2,1)S(1)}, bf16[8,128,5...) custom-call(s32[576]{0:T(1024)S(1)} %copy-done, bf16[72,8192]{1,0:T(8,128)(2,1)S(1)} %copy-done.1, ...), custom_call_target="tpu_custom_call" | custom-call | flops 8071000064 | bytes 25830000 | tf_op jit(solution)/shard_map/prepare_queries/pallas_call | solution.py:272
  22.3 1.9 %collective-permute-start.3 = (bf16[72,1024]{1,0:T(8,128)(2,1)S(1)}, bf16[72,1024]{1,0:T(8,128)(2,1)S(1)}, u32[]{:S(2)}, u32[]{:S(2)}) collective-permute-start(bf16[72,1024]{1,0:T(8,128)(2,1)S(1)} %copy-done.3), channel_id=1, source_target_pairs={{0,4},{4,0},{8,12},{12,8},{16,20},{24,28},{1,5},{5,1},{9,13},{13,9... | collective-permute-start | bytes 442376 | tf_op jit(solution)/shard_map/ppermute | solution.py:244
  24.2 1.9 %collective-permute-start.4 = (bf16[72,1024]{1,0:T(8,128)(2,1)S(1)}, bf16[72,1024]{1,0:T(8,128)(2,1)S(1)}, u32[]{:S(2)}, u32[]{:S(2)}) collective-permute-start(bf16[72,1024]{1,0:T(8,128)(2,1)S(1)} %copy-done.3), channel_id=1, source_target_pairs={{0,8},{4,12},{8,0},{12,4},{16,24},{20,28},{1,9},{5,13},{9,1},{13,5... | collective-permute-start | bytes 442376 | tf_op jit(solution)/shard_map/ppermute | solution.py:244
  26.2 2.9 %collective-permute-start.6 = (bf16[72,1024]{1,0:T(8,128)(2,1)S(1)}, bf16[72,1024]{1,0:T(8,128)(2,1)S(1)}, u32[]{:S(2)}, u32[]{:S(2)}) collective-permute-start(bf16[72,1024]{1,0:T(8,128)(2,1)S(1)} %collective-permute-done.1.refs_2_), channel_id=1, source_target_pairs={{0,16},{4,20},{8,24},{12,28},{1,17},{5,21},{9,25},{13,29},{2,18},{... | collective-permute-start | bytes 442376 | tf_op jit(solution)/shard_map/ppermute | solution.py:252
  29.0 1.3 %collective-permute-start.5 = (bf16[72,1024]{1,0:T(8,128)(2,1)S(1)}, bf16[72,1024]{1,0:T(8,128)(2,1)S(1)}, u32[]{:S(2)}, u32[]{:S(2)}) collective-permute-start(bf16[72,1024]{1,0:T(8,128)(2,1)S(1)} %collective-permute-done.refs_1_), channel_id=1, source_target_pairs={{0,16},{4,20},{8,24},{12,28},{1,17},{5,21},{9,25},{13,29},{2,18},{... | collective-permute-start | bytes 442376 | tf_op jit(solution)/shard_map/ppermute | solution.py:252
  30.4 2.3 %collective-permute-start.11 = (bf16[72,1024]{1,0:T(8,128)(2,1)S(1)}, bf16[72,1024]{1,0:T(8,128)(2,1)S(1)}, u32[]{:S(2)}, u32[]{:S(2)}) collective-permute-start(bf16[72,1024]{1,0:T(8,128)(2,1)S(1)} %collective-permute-done.1.refs_2_), channel_id=1, source_target_pairs={{0,4},{4,0},{8,12},{12,8},{24,28},{28,24},{1,5},{5,1},{9,13},{13,9... | collective-permute-start | bytes 442376 | tf_op jit(solution)/shard_map/ppermute | solution.py:244
  32.7 2.4 %collective-permute-done.4.refs_2_ = bf16[72,1024]{1,0:T(8,128)(2,1)S(1)} collective-permute-done((bf16[72,1024]{1,0:T(8,128)(2,1)S(1)}, bf16[72,1024]{1,0:T(8,128)(2,1)S(1)}, u32[]{:S(2)}, u32[]{:S(2)}) %collective-permute-start.4) | collective-permute-done | bytes 147488 | tf_op jit(solution)/shard_map/ppermute | solution.py:244
  35.1 1.9 %collective-permute-start.7 = (bf16[72,1024]{1,0:T(8,128)(2,1)S(1)}, bf16[72,1024]{1,0:T(8,128)(2,1)S(1)}, u32[]{:S(2)}, u32[]{:S(2)}) collective-permute-start(bf16[72,1024]{1,0:T(8,128)(2,1)S(1)} %collective-permute-done.4.refs_2_), channel_id=1, source_target_pairs={{0,4},{4,0},{8,12},{12,8},{24,28},{28,24},{1,5},{5,1},{9,13},{13,9... | collective-permute-start | bytes 442376 | tf_op jit(solution)/shard_map/ppermute | solution.py:244
  37.0 1.1 %collective-permute-done.11.refs_3_ = bf16[72,1024]{1,0:T(8,128)(2,1)S(1)} collective-permute-done((bf16[72,1024]{1,0:T(8,128)(2,1)S(1)}, bf16[72,1024]{1,0:T(8,128)(2,1)S(1)}, u32[]{:S(2)}, u32[]{:S(2)}) %collective-permute-start.11) | collective-permute-done | bytes 147488 | tf_op jit(solution)/shard_map/ppermute | solution.py:244
  38.1 1.3 %collective-permute-start.12 = (bf16[72,1024]{1,0:T(8,128)(2,1)S(1)}, bf16[72,1024]{1,0:T(8,128)(2,1)S(1)}, u32[]{:S(2)}, u32[]{:S(2)}) collective-permute-start(bf16[72,1024]{1,0:T(8,128)(2,1)S(1)} %collective-permute-done.11.refs_3_), channel_id=1, source_target_pairs={{0,16},{4,20},{8,24},{12,28},{1,17},{5,21},{9,25},{13,29},{2,18},{... | collective-permute-start | bytes 442376 | tf_op jit(solution)/shard_map/ppermute | solution.py:252
  39.4 1.3 %collective-permute-start.9 = (bf16[72,1024]{1,0:T(8,128)(2,1)S(1)}, bf16[72,1024]{1,0:T(8,128)(2,1)S(1)}, u32[]{:S(2)}, u32[]{:S(2)}) collective-permute-start(bf16[72,1024]{1,0:T(8,128)(2,1)S(1)} %collective-permute-done.4.refs_2_), channel_id=1, source_target_pairs={{0,16},{4,20},{8,24},{12,28},{1,17},{5,21},{9,25},{13,29},{2,18},{... | collective-permute-start | bytes 442376 | tf_op jit(solution)/shard_map/ppermute | solution.py:252
  40.7 1.3 %collective-permute-start.8 = (bf16[72,1024]{1,0:T(8,128)(2,1)S(1)}, bf16[72,1024]{1,0:T(8,128)(2,1)S(1)}, u32[]{:S(2)}, u32[]{:S(2)}) collective-permute-start(bf16[72,1024]{1,0:T(8,128)(2,1)S(1)} %collective-permute-done.3.refs_1_), channel_id=1, source_target_pairs={{0,16},{4,20},{8,24},{12,28},{1,17},{5,21},{9,25},{13,29},{2,18},{... | collective-permute-start | bytes 442376 | tf_op jit(solution)/shard_map/ppermute | solution.py:252
  42.1 1.3 %collective-permute-start.10 = (bf16[72,1024]{1,0:T(8,128)(2,1)S(1)}, bf16[72,1024]{1,0:T(8,128)(2,1)S(1)}, u32[]{:S(2)}, u32[]{:S(2)}) collective-permute-start(bf16[72,1024]{1,0:T(8,128)(2,1)S(1)} %collective-permute-done.7.refs_3_), channel_id=1, source_target_pairs={{0,16},{4,20},{8,24},{12,28},{1,17},{5,21},{9,25},{13,29},{2,18},{... | collective-permute-start | bytes 442376 | tf_op jit(solution)/shard_map/ppermute | solution.py:252
  43.6 8.1 %attend.2 = (bf16[72,8192]{1,0:T(8,128)(2,1)}, bf16[72,8192]{1,0:T(8,128)(2,1)}, bf16[4,72,1024]{2,1,0:T(8,128)(2,1)S(1)}, bf16[4,72,1024]{2,1,0:T(8,128)(2,1)S(1)}) custom-call(s32[2]{0:T(128)S(1)} %copy-done.5, bf16[72,1024]{1,0:T(8,128)(2,1)S(1)} %copy-done.4, bf16[72,1024]{1,0:T(8,128)(2,1)S(1)} %collective-permute-done.refs_1_, ...), custom_call_target="tpu_custom_call" | custom-call | flops 11530000384 | bytes 36900000 | tf_op jit(solution)/shard_map/attend/pallas_call | solution.py:327
  51.8 1.3 %collective-permute-start.14 = (bf16[4,72,1024]{2,1,0:T(8,128)(2,1)S(1)}, bf16[4,72,1024]{2,1,0:T(8,128)(2,1)S(1)}, u32[]{:S(2)}, u32[]{:S(2)}) collective-permute-start(bf16[4,72,1024]{2,1,0:T(8,128)(2,1)S(1)} %get-tuple-element.70), channel_id=1, source_target_pairs={{16,0},{20,4},{24,8},{28,12},{17,1},{21,5},{25,9},{29,13},{18,2},{... | collective-permute-start | bytes 1769480 | tf_op jit(solution)/shard_map/ppermute | solution.py:252
  53.1 8.2 %attend.3 = (bf16[72,8192]{1,0:T(8,128)(2,1)}, bf16[72,8192]{1,0:T(8,128)(2,1)}, bf16[4,72,1024]{2,1,0:T(8,128)(2,1)S(1)}, bf16[4,72,1024]{2,1,0:T(8,128)(2,1)S(1)}) custom-call(s32[2]{0:T(128)S(1)} %copy-done.5, bf16[72,1024]{1,0:T(8,128)(2,1)S(1)} %copy-done.3, ...), custom_call_target="tpu_custom_call", output_to_operand_aliasing={{0}: (15, {}), {1}: (16, {})} | custom-call | flops 11530000384 | bytes 36900000 | tf_op jit(solution)/shard_map/attend/pallas_call | solution.py:327
  61.3 1.3 %collective-permute-start.13 = (bf16[4,72,1024]{2,1,0:T(8,128)(2,1)S(1)}, bf16[4,72,1024]{2,1,0:T(8,128)(2,1)S(1)}, u32[]{:S(2)}, u32[]{:S(2)}) collective-permute-start(bf16[4,72,1024]{2,1,0:T(8,128)(2,1)S(1)} %get-tuple-element.68), channel_id=1, source_target_pairs={{16,0},{20,4},{24,8},{28,12},{17,1},{21,5},{25,9},{29,13},{18,2},{... | collective-permute-start | bytes 1769480 | tf_op jit(solution)/shard_map/ppermute | solution.py:252
  62.6 6.7 %collective-permute-done.14.refs_1_ = bf16[4,72,1024]{2,1,0:T(8,128)(2,1)S(1)} collective-permute-done((bf16[4,72,1024]{2,1,0:T(8,128)(2,1)S(1)}, bf16[4,72,1024]{2,1,0:T(8,128)(2,1)S(1)}, u32[]{:S(2)}, u32[]{:S(2)}) %collective-permute-start.14) | collective-permute-done | bytes 589856 | tf_op jit(solution)/shard_map/ppermute | solution.py:252
  69.4 2.7 %collective-permute-start.15 = (bf16[72,1024]{1,0:T(8,128)(2,1)S(1)}, bf16[72,1024]{1,0:T(8,128)(2,1)S(1)}, u32[]{:S(2)}, u32[]{:S(2)}) collective-permute-start(bf16[72,1024]{1,0:T(8,128)(2,1)S(1)} %get-tuple-element.73), channel_id=1, source_target_pairs={{0,4},{4,0},{8,12},{12,8},{20,16},{28,24},{1,5},{5,1},{9,13},{13,9... | collective-permute-start | bytes 442376 | tf_op jit(solution)/shard_map/ppermute | solution.py:244
  72.1 5.8 %collective-permute-start.16 = (bf16[72,1024]{1,0:T(8,128)(2,1)S(1)}, bf16[72,1024]{1,0:T(8,128)(2,1)S(1)}, u32[]{:S(2)}, u32[]{:S(2)}) collective-permute-start(bf16[72,1024]{1,0:T(8,128)(2,1)S(1)} %get-tuple-element.74), channel_id=1, source_target_pairs={{0,8},{4,12},{8,0},{12,4},{24,16},{28,20},{1,9},{5,13},{9,1},{13,5... | collective-permute-start | bytes 442376 | tf_op jit(solution)/shard_map/ppermute | solution.py:244
  77.9 2.8 %collective-permute-start.17 = (bf16[72,1024]{1,0:T(8,128)(2,1)S(1)}, bf16[72,1024]{1,0:T(8,128)(2,1)S(1)}, u32[]{:S(2)}, u32[]{:S(2)}) collective-permute-start(bf16[72,1024]{1,0:T(8,128)(2,1)S(1)} %get-tuple-element.75), channel_id=1, source_target_pairs={{0,12},{4,8},{8,4},{12,0},{24,20},{28,16},{1,13},{5,9},{9,5},{13,1... | collective-permute-start | bytes 442376 | tf_op jit(solution)/shard_map/ppermute | solution.py:244
  80.9 2.5 %collective-permute-start.18 = (bf16[72,1024]{1,0:T(8,128)(2,1)S(1)}, bf16[72,1024]{1,0:T(8,128)(2,1)S(1)}, u32[]{:S(2)}, u32[]{:S(2)}) collective-permute-start(bf16[72,1024]{1,0:T(8,128)(2,1)S(1)} %get-tuple-element.79), channel_id=1, source_target_pairs={{0,4},{4,0},{8,12},{12,8},{20,16},{28,24},{1,5},{5,1},{9,13},{13,9... | collective-permute-start | bytes 442376 | tf_op jit(solution)/shard_map/ppermute | solution.py:244
  83.4 4.8 %collective-permute-start.19 = (bf16[72,1024]{1,0:T(8,128)(2,1)S(1)}, bf16[72,1024]{1,0:T(8,128)(2,1)S(1)}, u32[]{:S(2)}, u32[]{:S(2)}) collective-permute-start(bf16[72,1024]{1,0:T(8,128)(2,1)S(1)} %get-tuple-element.80), channel_id=1, source_target_pairs={{0,8},{4,12},{8,0},{12,4},{24,16},{28,20},{1,9},{5,13},{9,1},{13,5... | collective-permute-start | bytes 442376 | tf_op jit(solution)/shard_map/ppermute | solution.py:244
  88.2 2.8 %collective-permute-start.20 = (bf16[72,1024]{1,0:T(8,128)(2,1)S(1)}, bf16[72,1024]{1,0:T(8,128)(2,1)S(1)}, u32[]{:S(2)}, u32[]{:S(2)}) collective-permute-start(bf16[72,1024]{1,0:T(8,128)(2,1)S(1)} %get-tuple-element.81), channel_id=1, source_target_pairs={{0,12},{4,8},{8,4},{12,0},{24,20},{28,16},{1,13},{5,9},{9,5},{13,1... | collective-permute-start | bytes 442376 | tf_op jit(solution)/shard_map/ppermute | solution.py:244
  91.1 6.6 %collective-permute-done.19.refs_8_ = bf16[72,1024]{1,0:T(8,128)(2,1)S(1)} collective-permute-done((bf16[72,1024]{1,0:T(8,128)(2,1)S(1)}, bf16[72,1024]{1,0:T(8,128)(2,1)S(1)}, u32[]{:S(2)}, u32[]{:S(2)}) %collective-permute-start.19) | collective-permute-done | bytes 147488 | tf_op jit(solution)/shard_map/ppermute | solution.py:244
  97.7 0.9 finish.1
  (29 shorter events, 1.4 us)
Async XLA Ops:
  2.7 19.5 %collective-permute-start = (bf16[72,1024]{1,0:T(8,128)(2,1)}, bf16[72,1024]{1,0:T(8,128)(2,1)S(1)}, u32[]{:S(2)}, u32[]{:S(2)}) collective-permute-start(bf16[72,1024]{1,0:T(8,128)(2,1)} %get-tuple-element.61.refs_0_), channel_id=1, source_target_pairs={{0,4},{4,0},{8,12},{12,8},{16,20},{24,28},{1,5},{5,1},{9,13},{13,9... | collective-permute-start | bytes 442376 | tf_op jit(solution)/shard_map/ppermute | solution.py:244
  7.6 14.6 %collective-permute-start.1 = (bf16[72,1024]{1,0:T(8,128)(2,1)}, bf16[72,1024]{1,0:T(8,128)(2,1)S(1)}, u32[]{:S(2)}, u32[]{:S(2)}) collective-permute-start(bf16[72,1024]{1,0:T(8,128)(2,1)} %get-tuple-element.61.refs_0_), channel_id=1, source_target_pairs={{0,8},{4,12},{8,0},{12,4},{16,24},{20,28},{1,9},{5,13},{9,1},{13,5... | collective-permute-start | bytes 442376 | tf_op jit(solution)/shard_map/ppermute | solution.py:244
  12.2 10.1 %collective-permute-start.2 = (bf16[72,2048]{1,0:T(8,128)(2,1)}, bf16[72,2048]{1,0:T(8,128)(2,1)S(1)}, u32[]{:S(2)}, u32[]{:S(2)}) collective-permute-start(bf16[72,2048]{1,0:T(8,128)(2,1)} %get-tuple-element.47), channel_id=1, source_target_pairs={{0,16},{4,20},{8,24},{12,28},{1,17},{5,21},{9,25},{13,29},{2,18},{... | collective-permute-start | bytes 884744 | tf_op jit(solution)/shard_map/ppermute | solution.py:252
  15.6 0.7 copy-start
  16.3 1.3 %copy-start.1 = (bf16[72,8192]{1,0:T(8,128)(2,1)S(1)}, bf16[72,8192]{1,0:T(8,128)(2,1)}, u32[]{:S(2)}) copy-start(bf16[72,8192]{1,0:T(8,128)(2,1)} %query_ref.1) | copy-start | bytes 3538948
  17.6 1.3 %copy-start.2 = (bf16[72,8192]{1,0:T(8,128)(2,1)S(1)}, bf16[72,8192]{1,0:T(8,128)(2,1)}, u32[]{:S(2)}) copy-start(bf16[72,8192]{1,0:T(8,128)(2,1)} %grad_ref.1) | copy-start | bytes 3538948
  18.8 3.5 %copy-start.3 = (bf16[72,1024]{1,0:T(8,128)(2,1)S(1)}, bf16[72,1024]{1,0:T(8,128)(2,1)}, u32[]{:S(2)}) copy-start(bf16[72,1024]{1,0:T(8,128)(2,1)} %get-tuple-element.51.refs_0_) | copy-start | bytes 442372
  18.8 24.8 %copy-start.4 = (bf16[72,1024]{1,0:T(8,128)(2,1)S(1)}, bf16[72,1024]{1,0:T(8,128)(2,1)}, u32[]{:S(2)}) copy-start(bf16[72,1024]{1,0:T(8,128)(2,1)} %get-tuple-element.61.refs_0_) | copy-start | bytes 442372
  18.8 24.8 %copy-start.5 = (s32[2]{0:T(128)S(1)}, s32[2]{0:T(128)}, u32[]{:S(2)}) copy-start(s32[2]{0:T(128)} %counts_ref.3) | copy-start | bytes 28
  22.3 10.4 %collective-permute-start.3 = (bf16[72,1024]{1,0:T(8,128)(2,1)S(1)}, bf16[72,1024]{1,0:T(8,128)(2,1)S(1)}, u32[]{:S(2)}, u32[]{:S(2)}) collective-permute-start(bf16[72,1024]{1,0:T(8,128)(2,1)S(1)} %copy-done.3), channel_id=1, source_target_pairs={{0,4},{4,0},{8,12},{12,8},{16,20},{24,28},{1,5},{5,1},{9,13},{13,9... | collective-permute-start | bytes 442376 | tf_op jit(solution)/shard_map/ppermute | solution.py:244
  24.2 10.9 %collective-permute-start.4 = (bf16[72,1024]{1,0:T(8,128)(2,1)S(1)}, bf16[72,1024]{1,0:T(8,128)(2,1)S(1)}, u32[]{:S(2)}, u32[]{:S(2)}) collective-permute-start(bf16[72,1024]{1,0:T(8,128)(2,1)S(1)} %copy-done.3), channel_id=1, source_target_pairs={{0,8},{4,12},{8,0},{12,4},{16,24},{20,28},{1,9},{5,13},{9,1},{13,5... | collective-permute-start | bytes 442376 | tf_op jit(solution)/shard_map/ppermute | solution.py:244
  26.2 8.9 %collective-permute-start.6 = (bf16[72,1024]{1,0:T(8,128)(2,1)S(1)}, bf16[72,1024]{1,0:T(8,128)(2,1)S(1)}, u32[]{:S(2)}, u32[]{:S(2)}) collective-permute-start(bf16[72,1024]{1,0:T(8,128)(2,1)S(1)} %collective-permute-done.1.refs_2_), channel_id=1, source_target_pairs={{0,16},{4,20},{8,24},{12,28},{1,17},{5,21},{9,25},{13,29},{2,18},{... | collective-permute-start | bytes 442376 | tf_op jit(solution)/shard_map/ppermute | solution.py:252
  29.0 6.0 %collective-permute-start.5 = (bf16[72,1024]{1,0:T(8,128)(2,1)S(1)}, bf16[72,1024]{1,0:T(8,128)(2,1)S(1)}, u32[]{:S(2)}, u32[]{:S(2)}) collective-permute-start(bf16[72,1024]{1,0:T(8,128)(2,1)S(1)} %collective-permute-done.refs_1_), channel_id=1, source_target_pairs={{0,16},{4,20},{8,24},{12,28},{1,17},{5,21},{9,25},{13,29},{2,18},{... | collective-permute-start | bytes 442376 | tf_op jit(solution)/shard_map/ppermute | solution.py:252
  30.4 7.7 %collective-permute-start.11 = (bf16[72,1024]{1,0:T(8,128)(2,1)S(1)}, bf16[72,1024]{1,0:T(8,128)(2,1)S(1)}, u32[]{:S(2)}, u32[]{:S(2)}) collective-permute-start(bf16[72,1024]{1,0:T(8,128)(2,1)S(1)} %collective-permute-done.1.refs_2_), channel_id=1, source_target_pairs={{0,4},{4,0},{8,12},{12,8},{24,28},{28,24},{1,5},{5,1},{9,13},{13,9... | collective-permute-start | bytes 442376 | tf_op jit(solution)/shard_map/ppermute | solution.py:244
  35.1 7.0 %collective-permute-start.7 = (bf16[72,1024]{1,0:T(8,128)(2,1)S(1)}, bf16[72,1024]{1,0:T(8,128)(2,1)S(1)}, u32[]{:S(2)}, u32[]{:S(2)}) collective-permute-start(bf16[72,1024]{1,0:T(8,128)(2,1)S(1)} %collective-permute-done.4.refs_2_), channel_id=1, source_target_pairs={{0,4},{4,0},{8,12},{12,8},{24,28},{28,24},{1,5},{5,1},{9,13},{13,9... | collective-permute-start | bytes 442376 | tf_op jit(solution)/shard_map/ppermute | solution.py:244
  38.1 5.6 %collective-permute-start.12 = (bf16[72,1024]{1,0:T(8,128)(2,1)S(1)}, bf16[72,1024]{1,0:T(8,128)(2,1)S(1)}, u32[]{:S(2)}, u32[]{:S(2)}) collective-permute-start(bf16[72,1024]{1,0:T(8,128)(2,1)S(1)} %collective-permute-done.11.refs_3_), channel_id=1, source_target_pairs={{0,16},{4,20},{8,24},{12,28},{1,17},{5,21},{9,25},{13,29},{2,18},{... | collective-permute-start | bytes 442376 | tf_op jit(solution)/shard_map/ppermute | solution.py:252
  39.4 13.7 %collective-permute-start.9 = (bf16[72,1024]{1,0:T(8,128)(2,1)S(1)}, bf16[72,1024]{1,0:T(8,128)(2,1)S(1)}, u32[]{:S(2)}, u32[]{:S(2)}) collective-permute-start(bf16[72,1024]{1,0:T(8,128)(2,1)S(1)} %collective-permute-done.4.refs_2_), channel_id=1, source_target_pairs={{0,16},{4,20},{8,24},{12,28},{1,17},{5,21},{9,25},{13,29},{2,18},{... | collective-permute-start | bytes 442376 | tf_op jit(solution)/shard_map/ppermute | solution.py:252
  40.7 12.4 %collective-permute-start.8 = (bf16[72,1024]{1,0:T(8,128)(2,1)S(1)}, bf16[72,1024]{1,0:T(8,128)(2,1)S(1)}, u32[]{:S(2)}, u32[]{:S(2)}) collective-permute-start(bf16[72,1024]{1,0:T(8,128)(2,1)S(1)} %collective-permute-done.3.refs_1_), channel_id=1, source_target_pairs={{0,16},{4,20},{8,24},{12,28},{1,17},{5,21},{9,25},{13,29},{2,18},{... | collective-permute-start | bytes 442376 | tf_op jit(solution)/shard_map/ppermute | solution.py:252
  42.1 11.0 %collective-permute-start.10 = (bf16[72,1024]{1,0:T(8,128)(2,1)S(1)}, bf16[72,1024]{1,0:T(8,128)(2,1)S(1)}, u32[]{:S(2)}, u32[]{:S(2)}) collective-permute-start(bf16[72,1024]{1,0:T(8,128)(2,1)S(1)} %collective-permute-done.7.refs_3_), channel_id=1, source_target_pairs={{0,16},{4,20},{8,24},{12,28},{1,17},{5,21},{9,25},{13,29},{2,18},{... | collective-permute-start | bytes 442376 | tf_op jit(solution)/shard_map/ppermute | solution.py:252
  51.8 17.4 %collective-permute-start.14 = (bf16[4,72,1024]{2,1,0:T(8,128)(2,1)S(1)}, bf16[4,72,1024]{2,1,0:T(8,128)(2,1)S(1)}, u32[]{:S(2)}, u32[]{:S(2)}) collective-permute-start(bf16[4,72,1024]{2,1,0:T(8,128)(2,1)S(1)} %get-tuple-element.70), channel_id=1, source_target_pairs={{16,0},{20,4},{24,8},{28,12},{17,1},{21,5},{25,9},{29,13},{18,2},{... | collective-permute-start | bytes 1769480 | tf_op jit(solution)/shard_map/ppermute | solution.py:252
  61.3 19.5 %collective-permute-start.13 = (bf16[4,72,1024]{2,1,0:T(8,128)(2,1)S(1)}, bf16[4,72,1024]{2,1,0:T(8,128)(2,1)S(1)}, u32[]{:S(2)}, u32[]{:S(2)}) collective-permute-start(bf16[4,72,1024]{2,1,0:T(8,128)(2,1)S(1)} %get-tuple-element.68), channel_id=1, source_target_pairs={{16,0},{20,4},{24,8},{28,12},{17,1},{21,5},{25,9},{29,13},{18,2},{... | collective-permute-start | bytes 1769480 | tf_op jit(solution)/shard_map/ppermute | solution.py:252
  69.4 18.9 %collective-permute-start.15 = (bf16[72,1024]{1,0:T(8,128)(2,1)S(1)}, bf16[72,1024]{1,0:T(8,128)(2,1)S(1)}, u32[]{:S(2)}, u32[]{:S(2)}) collective-permute-start(bf16[72,1024]{1,0:T(8,128)(2,1)S(1)} %get-tuple-element.73), channel_id=1, source_target_pairs={{0,4},{4,0},{8,12},{12,8},{20,16},{28,24},{1,5},{5,1},{9,13},{13,9... | collective-permute-start | bytes 442376 | tf_op jit(solution)/shard_map/ppermute | solution.py:244
  72.1 18.9 %collective-permute-start.16 = (bf16[72,1024]{1,0:T(8,128)(2,1)S(1)}, bf16[72,1024]{1,0:T(8,128)(2,1)S(1)}, u32[]{:S(2)}, u32[]{:S(2)}) collective-permute-start(bf16[72,1024]{1,0:T(8,128)(2,1)S(1)} %get-tuple-element.74), channel_id=1, source_target_pairs={{0,8},{4,12},{8,0},{12,4},{24,16},{28,20},{1,9},{5,13},{9,1},{13,5... | collective-permute-start | bytes 442376 | tf_op jit(solution)/shard_map/ppermute | solution.py:244
  77.9 13.1 %collective-permute-start.17 = (bf16[72,1024]{1,0:T(8,128)(2,1)S(1)}, bf16[72,1024]{1,0:T(8,128)(2,1)S(1)}, u32[]{:S(2)}, u32[]{:S(2)}) collective-permute-start(bf16[72,1024]{1,0:T(8,128)(2,1)S(1)} %get-tuple-element.75), channel_id=1, source_target_pairs={{0,12},{4,8},{8,4},{12,0},{24,20},{28,16},{1,13},{5,9},{9,5},{13,1... | collective-permute-start | bytes 442376 | tf_op jit(solution)/shard_map/ppermute | solution.py:244
  80.9 10.2 %collective-permute-start.18 = (bf16[72,1024]{1,0:T(8,128)(2,1)S(1)}, bf16[72,1024]{1,0:T(8,128)(2,1)S(1)}, u32[]{:S(2)}, u32[]{:S(2)}) collective-permute-start(bf16[72,1024]{1,0:T(8,128)(2,1)S(1)} %get-tuple-element.79), channel_id=1, source_target_pairs={{0,4},{4,0},{8,12},{12,8},{20,16},{28,24},{1,5},{5,1},{9,13},{13,9... | collective-permute-start | bytes 442376 | tf_op jit(solution)/shard_map/ppermute | solution.py:244
  83.4 14.3 %collective-permute-start.19 = (bf16[72,1024]{1,0:T(8,128)(2,1)S(1)}, bf16[72,1024]{1,0:T(8,128)(2,1)S(1)}, u32[]{:S(2)}, u32[]{:S(2)}) collective-permute-start(bf16[72,1024]{1,0:T(8,128)(2,1)S(1)} %get-tuple-element.80), channel_id=1, source_target_pairs={{0,8},{4,12},{8,0},{12,4},{24,16},{28,20},{1,9},{5,13},{9,1},{13,5... | collective-permute-start | bytes 442376 | tf_op jit(solution)/shard_map/ppermute | solution.py:244
  88.2 9.5 %collective-permute-start.20 = (bf16[72,1024]{1,0:T(8,128)(2,1)S(1)}, bf16[72,1024]{1,0:T(8,128)(2,1)S(1)}, u32[]{:S(2)}, u32[]{:S(2)}) collective-permute-start(bf16[72,1024]{1,0:T(8,128)(2,1)S(1)} %get-tuple-element.81), channel_id=1, source_target_pairs={{0,12},{4,8},{8,4},{12,0},{24,20},{28,16},{1,13},{5,9},{9,5},{13,1... | collective-permute-start | bytes 442376 | tf_op jit(solution)/shard_map/ppermute | solution.py:244

commit v7 on v5

--- a/solution.py
+++ b/solution.py
@@ -14,7 +14,6 @@
 GROUP = QUERY_HEADS // KEY_VALUE_HEADS
 ROPE_BASE = 500000.0
 SCORE_SCALE = 1.0 / float(np.sqrt(HEAD_WIDTH))
-LOG2_E = 1.4426950408889634
 CHUNKS = 2
 HEADS_PER_CHUNK = KEY_VALUE_HEADS // CHUNKS
 CHUNK_COLS = HEADS_PER_CHUNK * HEAD_WIDTH
@@ -58,18 +57,20 @@
     return slice(index * HEAD_WIDTH, (index + 1) * HEAD_WIDTH)
 
 
-def prepare_keys(rows, pos_ref, key_ref, value_ref, whole_ref, *kv_refs):
+def prepare_keys(rows, pos_ref, key_ref, value_ref, kv_ref):
     cosine, sine = angle_tables(rows, key_ref.shape[0], pos_ref)
     for head in range(KEY_VALUE_HEADS):
         chunk, place = divmod(head, HEADS_PER_CHUNK)
+        place += 2 * chunk * HEADS_PER_CHUNK
         rotated = rope(key_ref[:, head_cols(head)].astype(jnp.float32), cosine, sine)
-        columns = {
-            place: rotated.astype(jnp.bfloat16),
-            HEADS_PER_CHUNK + place: value_ref[:, head_cols(head)],
-        }
-        for column, x in columns.items():
-            kv_refs[chunk][:, head_cols(column)] = x
-            whole_ref[:, head_cols(2 * chunk * HEADS_PER_CHUNK + column)] = x
+        kv_ref[:, head_cols(place)] = rotated.astype(jnp.bfloat16)
+        kv_ref[:, head_cols(HEADS_PER_CHUNK + place)] = value_ref[:, head_cols(head)]
+
+
+def stack(chunk, *refs):
+    *block_refs, stack_ref = refs
+    for place, ref in enumerate(block_refs):
+        stack_ref[place] = ref[:, 2 * chunk * CHUNK_COLS : 2 * (chunk + 1) * CHUNK_COLS]
 
 
 def prepare_queries(rows, pos_ref, query_ref, grad_ref, *out_refs):
@@ -105,11 +106,13 @@
     return jnp.dot(left, right, preferred_element_type=jnp.float32)
 
 
-def attend(seq_count, head_count, rows, has_alias, counts_ref, *refs):
+def attend(seq_count, head_count, rows, pieces, has_alias, counts_ref, *refs):
     blocks = seq_count * head_count
-    kv_refs = refs[:blocks]
-    q_ref, qt_ref, g_ref, gt_ref, cos_ref, sin_ref = refs[blocks : blocks + 6]
-    outs = refs[blocks + 6 + 2 * has_alias :]
+    kv_refs = []
+    for ref in refs[:pieces]:
+        kv_refs += [ref] if len(ref.shape) == 2 else [ref.at[i] for i in range(ref.shape[0])]
+    q_ref, qt_ref, g_ref, gt_ref, cos_ref, sin_ref = refs[pieces : pieces + 6]
+    outs = refs[pieces + 6 + 2 * has_alias :]
     out_ref, grad_ref = outs[:2]
     part_refs = outs[2 : 2 + seq_count]
     bias_ref, live_ref = outs[2 + seq_count :]
@@ -149,10 +152,10 @@
     heads = range(STEP_HEADS)
     keys, values = [gathered(0, p) for p in heads], [gathered(HEADS_PER_CHUNK, p) for p in heads]
     bias, live = bias_ref[...], live_ref[0:1, :]
-    scores = [dot(keys[p][0], qt_ref[p]) * (SCORE_SCALE * LOG2_E) + bias for p in heads]
+    scores = [dot(keys[p][0], qt_ref[p]) * SCORE_SCALE + bias for p in heads]
     dprobs, probs, probs_low = [], [], []
     for p in heads:
-        weights = jnp.exp2(scores[p] - jnp.max(scores[p], 0, keepdims=True))
+        weights = jnp.exp(scores[p] - jnp.max(scores[p], 0, keepdims=True))
         probs.append(weights * (live / jnp.sum(weights, 0, keepdims=True)))
         probs_low.append(probs[p].astype(jnp.bfloat16))
         dprobs.append(dot(values[p][0], gt_ref[p]))
@@ -266,11 +269,11 @@
     table = shape((padded, HEAD_WIDTH), f32)
     table_t = shape((HEAD_WIDTH // 2, query_rows), f32)
     piece = shape((padded, 2 * CHUNK_COLS), bf16)
-    whole, *own = pl.pallas_call(
+    own = pl.pallas_call(
         functools.partial(prepare_keys, rows),
-        out_shape=[shape((padded, CHUNKS * 2 * CHUNK_COLS), bf16)] + [piece] * CHUNKS,
+        out_shape=shape((padded, CHUNKS * 2 * CHUNK_COLS), bf16),
         in_specs=[SMEM, VMEM, VMEM],
-        out_specs=[VMEM] * (CHUNKS + 1),
+        out_specs=VMEM,
         compiler_params=params(56),
         name="prepare_keys",
     )(positions, routed_keys, routed_values)
@@ -297,23 +300,29 @@
 
     bits = [1 << b for b in reversed(range((head_count - 1).bit_length()))]
     later = range(1, seq_count)
-    firsts = sorted({bits[0], 1})
-    far = {a: along_seq(whole, a, True) for a in later}
-    near = {0: own[0], **{j: along_head(own[0], j, True) for j in firsts}}
+    last = head_count - 1
+    near = {0: own, **{j: along_head(own, j, True) for j in sorted({bits[0], 1}, reverse=True)}}
+    far = {a: along_seq(own, a, True) for a in later}
     near, cosine_t, far = lax.optimization_barrier((near, cosine_t, far))
-
-    def gather(near):
-        for bit in bits[1:]:
-            near.update(
-                {j ^ bit: along_head(x, bit, True, j) for j, x in near.items() if j ^ bit not in near}
-            )
-        crossed = {
-            (a, j): along_seq(near[j], a, True) for j in range(1, head_count) for a in later
-        }
-        blocks_here = [near[j] for j in range(head_count)]
-        for a in later:
-            blocks_here += [far[a]] + [crossed[a, j] for j in range(1, head_count)]
-        return blocks_here
+    for bit in bits[1:]:
+        near.update(
+            {j ^ bit: along_head(x, bit, True, j) for j, x in near.items() if j ^ bit not in near}
+        )
+
+    def cross(chunk, offsets):
+        held = pl.pallas_call(
+            functools.partial(stack, chunk),
+            out_shape=shape((len(offsets), padded, 2 * CHUNK_COLS), bf16),
+            in_specs=[VMEM] * len(offsets),
+            out_specs=VMEM,
+            compiler_params=params(8),
+            name="stack",
+        )(*(near[j] for j in offsets))
+        return {a: along_seq(held, a, True) for a in later}
+
+    crossed = [[cross(0, range(1, last)), cross(0, [last])]]
+    near[last], crossed[0][0] = lax.optimization_barrier((near[last], crossed[0][0]))
+    crossed += [[cross(chunk, range(1, head_count))] for chunk in range(1, CHUNKS)]
 
     wide_outs = ()
     parts = []
@@ -325,26 +334,23 @@
             for x in (tall, flat)
         )
         row_part = pl.BlockSpec((padded, STEP_HEADS * wide), lambda g, f=first: (0, f + g))
-        if chunk:
-            near = {0: own[chunk], **{j: along_head(own[chunk], j, True) for j in firsts}}
-            near, parts[-1][0] = lax.optimization_barrier((near, parts[-1][0]))
-        gathered = gather(near)
-        if chunk + 1 < CHUNKS:
-            last = head_count - 1
-            own[chunk + 1], gathered[last] = lax.optimization_barrier(
-                (own[chunk + 1], gathered[last])
-            )
+        gathered = [near[j] for j in range(head_count)]
+        for a in later:
+            gathered += [far[a]] + [part[a] for part in crossed[chunk]]
+        inputs = len(gathered)
         kv_whole = pl.BlockSpec((padded, 2 * CHUNK_COLS), lambda g, c=chunk: (0, c))
-        kv_chunk = pl.BlockSpec((padded, 2 * CHUNK_COLS), lambda g: (0, 0))
+        kv_specs = [
+            kv_whole if len(x.shape) == 2 else pl.BlockSpec(x.shape, lambda g: (0, 0, 0))
+            for x in gathered
+        ]
         part_block = pl.BlockSpec((head_count, padded, 2 * CHUNK_COLS), lambda g: (0, 0, 0))
         out = pl.pallas_call(
-            functools.partial(attend, seq_count, head_count, rows, has_alias),
+            functools.partial(attend, seq_count, head_count, rows, inputs, has_alias),
             grid=(HEADS_PER_CHUNK // STEP_HEADS,),
             out_shape=[shape((padded, QUERY_HEADS * HEAD_WIDTH), bf16)] * 2
             + [shape((head_count, padded, 2 * CHUNK_COLS), bf16)] * seq_count,
             in_specs=[SMEM]
-            + [kv_chunk] * head_count
-            + ([kv_whole] + [kv_chunk] * (head_count - 1)) * (seq_count - 1)
+            + kv_specs
             + [tall_part, flat_part, tall_part, flat_part, table_t_block, table_t_block]
             + [pl.BlockSpec(memory_space=pl.ANY)] * (2 * has_alias),
             out_specs=[row_part, row_part] + [part_block] * seq_count,
@@ -352,7 +358,7 @@
                 pltpu.VMEM((blocks * padded, query_rows), f32),
                 pltpu.VMEM((8, query_rows), f32),
             ],
-            input_output_aliases={blocks + 7: 0, blocks + 8: 1} if has_alias else {},
+            input_output_aliases={inputs + 7: 0, inputs + 8: 1} if has_alias else {},
             cost_estimate=cost(10),
             compiler_params=params(32),
             name="attend",

time: 97.4 us -> 93.8 us (0.963)
  starting transfers between devices: 55.6 us -> 43.5 us
  waiting for transfers between devices: 14.5 us -> 22.7 us
    ppermute x12 -> x9, starting transfers between devices: 41 us -> 32.7 us  [along_head(): return lax.ppermute(x, ('seq', 'head'), pairs)]
    ppermute x12 -> x9, waiting for transfers between devices: 9.41 us -> 15.2 us  [along_head(): return lax.ppermute(x, ('seq', 'head'), pairs)]
    ppermute x9 -> x6, starting transfers between devices: 14.6 us -> 10.9 us  [along_seq(): return lax.ppermute(x, ('seq', 'head'), pairs)]
    ppermute x9 -> x6, waiting for transfers between devices: 5.06 us -> 7.5 us  [along_seq(): return lax.ppermute(x, ('seq', 'head'), pairs)]
    pallas_call x3 -> x6, Pallas kernels: 17.7 us -> 18 us  [the longest x2 16 us: shards(): pl.pallas_call(functools.partial(attend, seq_count, head_count, rows, inp...]
    unnamed x12 -> x10, local copies, waits for them, and re-layouts: 3.23 us -> 3.23 us
  transfers between devices with their start and end apart: 21 -> 15, of which waited for: 7 -> 5; matrix products, arithmetic and copies ran while one was open for 0% -> 0% of each run, Pallas kernels for 20% -> 21%
where the time goes in v7:
time: 93.8 us; the launch traced here: 93.2 us
  starting transfers between devices  43.5 us (46%)
  Pallas kernels  22.8 us (24%)
  waiting for transfers between devices  22.7 us (24%)
  local copies, waits for them, and re-layouts  3.23 us (3%)
    ppermute x9, starting transfers between devices, along_head(): return lax.ppermute(x, ('seq', 'head'), pairs)  32.7 us
    pallas_call x2, Pallas kernels, shards(): pl.pallas_call(functools.partial(attend, seq_count, head_count, rows, inp...  16 us
    ppermute x9, waiting for transfers between devices, along_head(): return lax.ppermute(x, ('seq', 'head'), pairs)  15.2 us
    ppermute x6, starting transfers between devices, along_seq(): return lax.ppermute(x, ('seq', 'head'), pairs)  10.9 us
    ppermute x6, waiting for transfers between devices, along_seq(): return lax.ppermute(x, ('seq', 'head'), pairs)  7.5 us
    pallas_call x1, Pallas kernels, shards(): pl.pallas_call(functools.partial(prepare_queries, rows), grid=(KEY_VALUE_...  3.65 us
    unnamed x10, local copies, waits for them, and re-layouts  3.23 us
    pallas_call x1, Pallas kernels, shards(): pl.pallas_call(functools.partial(prepare_keys, rows), out_shape=shape((pa...  1.96 us
  transfers between devices with their start and end apart: 15, of which 5 were waited for; matrix products, arithmetic and copies ran while one was open for 0% of the time, Pallas kernels for 21%

profile of v7, /device:TPU:0, one launch (start us, length us, event | category | flops | bytes accessed | tf_op | source)
XLA Modules:
  0.0 93.2 jit_solution(4277501295540305920)
XLA Ops:
  0.6 2.0 %prepare_keys.1.refs_0_ = bf16[72,2048]{1,0:T(8,128)(2,1)} custom-call(s32[576]{0:T(1024)} %pos_ref.3, bf16[72,1024]{1,0:T(8,128)(2,1)} %key_ref.1, bf16[72,1024]{1,0:T(8,128)(2,1)} %value_ref.1), custom_call_target="tpu_custom_call" | custom-call | tf_op jit(solution)/shard_map/prepare_keys/pallas_call | solution.py:272
  2.6 4.9 %collective-permute-start = (bf16[72,2048]{1,0:T(8,128)(2,1)}, bf16[72,2048]{1,0:T(8,128)(2,1)S(1)}, u32[]{:S(2)}, u32[]{:S(2)}) collective-permute-start(bf16[72,2048]{1,0:T(8,128)(2,1)} %prepare_keys.1.refs_0_), channel_id=1, source_target_pairs={{0,4},{4,0},{8,12},{12,8},{16,20},{24,28},{1,5},{5,1},{9,13},{13,9... | collective-permute-start | bytes 884744 | tf_op jit(solution)/shard_map/ppermute | solution.py:259
  7.5 4.5 %collective-permute-start.1 = (bf16[72,2048]{1,0:T(8,128)(2,1)}, bf16[72,2048]{1,0:T(8,128)(2,1)S(1)}, u32[]{:S(2)}, u32[]{:S(2)}) collective-permute-start(bf16[72,2048]{1,0:T(8,128)(2,1)} %prepare_keys.1.refs_0_), channel_id=1, source_target_pairs={{0,8},{4,12},{8,0},{12,4},{16,24},{20,28},{1,9},{5,13},{9,1},{13,5... | collective-permute-start | bytes 884744 | tf_op jit(solution)/shard_map/ppermute | solution.py:259
  12.0 3.5 %collective-permute-start.2 = (bf16[72,2048]{1,0:T(8,128)(2,1)}, bf16[72,2048]{1,0:T(8,128)(2,1)S(1)}, u32[]{:S(2)}, u32[]{:S(2)}) collective-permute-start(bf16[72,2048]{1,0:T(8,128)(2,1)} %prepare_keys.1.refs_0_), channel_id=1, source_target_pairs={{0,16},{4,20},{8,24},{12,28},{1,17},{5,21},{9,25},{13,29},{2,18},{... | collective-permute-start | bytes 884744 | tf_op jit(solution)/shard_map/ppermute | solution.py:267
  15.5 0.0 copy-start.1
  15.5 0.7 copy-done.1
  16.2 1.3 %copy-done.2 = bf16[72,8192]{1,0:T(8,128)(2,1)S(1)} copy-done((bf16[72,8192]{1,0:T(8,128)(2,1)S(1)}, bf16[72,8192]{1,0:T(8,128)(2,1)}, u32[]{:S(2)}) %copy-start.2) | copy-done | bytes 1179672
  17.5 1.3 %copy-done.3 = bf16[72,8192]{1,0:T(8,128)(2,1)S(1)} copy-done((bf16[72,8192]{1,0:T(8,128)(2,1)S(1)}, bf16[72,8192]{1,0:T(8,128)(2,1)}, u32[]{:S(2)}) %copy-start.3) | copy-done | bytes 1179672
  18.7 3.7 %prepare_queries.1 = (bf16[8,576,128]{2,1,0:T(8,128)(2,1)S(1)}, bf16[8,128,576]{2,1,0:T(8,128)(2,1)S(1)}, bf16[8,576,128]{2,1,0:T(8,128)(2,1)S(1)}, bf16[8,128,5...) custom-call(s32[576]{0:T(1024)S(1)} %copy-done.1, ...), custom_call_target="tpu_custom_call" | custom-call | flops 8071000064 | bytes 25830000 | tf_op jit(solution)/shard_map/prepare_queries/pallas_call | solution.py:289
  22.4 0.0 collective-permute-done.refs_0_.refs_1_
  22.4 3.0 %collective-permute-done.1.refs_1_.refs_2_ = bf16[72,2048]{1,0:T(8,128)(2,1)S(1)} collective-permute-done((bf16[72,2048]{1,0:T(8,128)(2,1)}, bf16[72,2048]{1,0:T(8,128)(2,1)S(1)}, u32[]{:S(2)}, u32[]{:S(2)}) %collective-permute-start.1) | collective-permute-done | bytes 294944 | tf_op jit(solution)/shard_map/ppermute | solution.py:259
  25.4 2.0 %collective-permute-start.3 = (bf16[72,2048]{1,0:T(8,128)(2,1)S(1)}, bf16[72,2048]{1,0:T(8,128)(2,1)S(1)}, u32[]{:S(2)}, u32[]{:S(2)}) collective-permute-start(bf16[72,2048]{1,0:T(8,128)(2,1)S(1)} %collective-permute-done.1.refs_1_.refs_2_), channel_id=1, source_target_pairs={{0,4},{4,0},{8,12},{12,8},{24,28},{28,24},{1,5},{5,1},{9,13},{13,9... | collective-permute-start | bytes 884744 | tf_op jit(solution)/shard_map/ppermute | solution.py:259
  27.4 1.3 %collective-permute-start.4 = (bf16[2,72,1024]{2,1,0:T(8,128)(2,1)S(1)}, bf16[2,72,1024]{2,1,0:T(8,128)(2,1)S(1)}, u32[]{:S(2)}, u32[]{:S(2)}) collective-permute-start(bf16[2,72,1024]{2,1,0:T(8,128)(2,1)S(1)} %stack.3), channel_id=1, source_target_pairs={{0,16},{4,20},{8,24},{12,28},{1,17},{5,21},{9,25},{13,29},{2,18},{... | collective-permute-start | bytes 884744 | tf_op jit(solution)/shard_map/ppermute | solution.py:267
  28.8 6.2 %collective-permute-done.3.refs_2_.refs_0_.refs_3_ = bf16[72,2048]{1,0:T(8,128)(2,1)S(1)} collective-permute-done((bf16[72,2048]{1,0:T(8,128)(2,1)S(1)}, bf16[72,2048]{1,0:T(8,128)(2,1)S(1)}, u32[]{:S(2)}, u32[]{:S(2)}) %collective-permute-start.3) | collective-permute-done | bytes 294944 | tf_op jit(solution)/shard_map/ppermute | solution.py:259
  35.0 1.3 %collective-permute-start.6 = (bf16[1,72,1024]{2,1,0:T(8,128)(2,1)S(1)}, bf16[1,72,1024]{2,1,0:T(8,128)(2,1)S(1)}, u32[]{:S(2)}, u32[]{:S(2)}) collective-permute-start(bf16[1,72,1024]{2,1,0:T(8,128)(2,1)S(1)} %stack.5), channel_id=1, source_target_pairs={{0,16},{4,20},{8,24},{12,28},{1,17},{5,21},{9,25},{13,29},{2,18},{... | collective-permute-start | bytes 442376 | tf_op jit(solution)/shard_map/ppermute | solution.py:267
  36.4 2.2 %collective-permute-start.5 = (bf16[3,72,1024]{2,1,0:T(8,128)(2,1)S(1)}, bf16[3,72,1024]{2,1,0:T(8,128)(2,1)S(1)}, u32[]{:S(2)}, u32[]{:S(2)}) collective-permute-start(bf16[3,72,1024]{2,1,0:T(8,128)(2,1)S(1)} %stack.4), channel_id=1, source_target_pairs={{0,16},{4,20},{8,24},{12,28},{1,17},{5,21},{9,25},{13,29},{2,18},{... | collective-permute-start | bytes 1327112 | tf_op jit(solution)/shard_map/ppermute | solution.py:267
  38.6 1.9 %collective-permute-done.6.refs_6_ = bf16[1,72,1024]{2,1,0:T(8,128)(2,1)S(1)} collective-permute-done((bf16[1,72,1024]{2,1,0:T(8,128)(2,1)S(1)}, bf16[1,72,1024]{2,1,0:T(8,128)(2,1)S(1)}, u32[]{:S(2)}, u32[]{:S(2)}) %collective-permute-start.6) | collective-permute-done | bytes 147488 | tf_op jit(solution)/shard_map/ppermute | solution.py:267
  40.5 8.0 %attend.2 = (bf16[72,8192]{1,0:T(8,128)(2,1)}, bf16[72,8192]{1,0:T(8,128)(2,1)}, bf16[4,72,1024]{2,1,0:T(8,128)(2,1)S(1)}, bf16[4,72,1024]{2,1,0:T(8,128)(2,1)S(1)}) custom-call(s32[2]{0:T(128)S(1)} %copy-done.4, bf16[72,2048]{1,0:T(8,128)(2,1)S(1)} %copy-done, bf16[72,2048]{1,0:T(8,128)(2,1)S(1)} %collective-permute-done.refs_0_.refs_1_, ...), custom_call_target="tpu_custom_call" | custom-call | flops 11530000384 | bytes 36900000 | tf_op jit(solution)/shard_map/attend/pallas_call | solution.py:347
  48.4 1.3 %collective-permute-start.8 = (bf16[4,72,1024]{2,1,0:T(8,128)(2,1)S(1)}, bf16[4,72,1024]{2,1,0:T(8,128)(2,1)S(1)}, u32[]{:S(2)}, u32[]{:S(2)}) collective-permute-start(bf16[4,72,1024]{2,1,0:T(8,128)(2,1)S(1)} %get-tuple-element.60), channel_id=1, source_target_pairs={{16,0},{20,4},{24,8},{28,12},{17,1},{21,5},{25,9},{29,13},{18,2},{... | collective-permute-start | bytes 1769480 | tf_op jit(solution)/shard_map/ppermute | solution.py:267
  49.7 8.0 %attend.3 = (bf16[72,8192]{1,0:T(8,128)(2,1)}, bf16[72,8192]{1,0:T(8,128)(2,1)}, bf16[4,72,1024]{2,1,0:T(8,128)(2,1)S(1)}, bf16[4,72,1024]{2,1,0:T(8,128)(2,1)S(1)}) custom-call(s32[2]{0:T(128)S(1)} %copy-done.4, bf16[72,2048]{1,0:T(8,128)(2,1)S(1)} %copy-done, ...), custom_call_target="tpu_custom_call", output_to_operand_aliasing={{0}: (13, {}), {1}: (14, {})} | custom-call | flops 11530000384 | bytes 36900000 | tf_op jit(solution)/shard_map/attend/pallas_call | solution.py:347
  57.8 1.3 %collective-permute-start.7 = (bf16[4,72,1024]{2,1,0:T(8,128)(2,1)S(1)}, bf16[4,72,1024]{2,1,0:T(8,128)(2,1)S(1)}, u32[]{:S(2)}, u32[]{:S(2)}) collective-permute-start(bf16[4,72,1024]{2,1,0:T(8,128)(2,1)S(1)} %get-tuple-element.58), channel_id=1, source_target_pairs={{16,0},{20,4},{24,8},{28,12},{17,1},{21,5},{25,9},{29,13},{18,2},{... | collective-permute-start | bytes 1769480 | tf_op jit(solution)/shard_map/ppermute | solution.py:267
  59.1 5.6 %collective-permute-done.8.refs_1_ = bf16[4,72,1024]{2,1,0:T(8,128)(2,1)S(1)} collective-permute-done((bf16[4,72,1024]{2,1,0:T(8,128)(2,1)S(1)}, bf16[4,72,1024]{2,1,0:T(8,128)(2,1)S(1)}, u32[]{:S(2)}, u32[]{:S(2)}) %collective-permute-start.8) | collective-permute-done | bytes 589856 | tf_op jit(solution)/shard_map/ppermute | solution.py:267
  64.7 0.1 combine.2
  64.8 5.8 %collective-permute-start.10 = (bf16[72,1024]{1,0:T(8,128)(2,1)S(1)}, bf16[72,1024]{1,0:T(8,128)(2,1)S(1)}, u32[]{:S(2)}, u32[]{:S(2)}) collective-permute-start(bf16[72,1024]{1,0:T(8,128)(2,1)S(1)} %get-tuple-element.64), channel_id=1, source_target_pairs={{0,8},{4,12},{8,0},{12,4},{24,16},{28,20},{1,9},{5,13},{9,1},{13,5... | collective-permute-start | bytes 442376 | tf_op jit(solution)/shard_map/ppermute | solution.py:259
  70.6 2.0 %collective-permute-start.11 = (bf16[72,1024]{1,0:T(8,128)(2,1)S(1)}, bf16[72,1024]{1,0:T(8,128)(2,1)S(1)}, u32[]{:S(2)}, u32[]{:S(2)}) collective-permute-start(bf16[72,1024]{1,0:T(8,128)(2,1)S(1)} %get-tuple-element.65), channel_id=1, source_target_pairs={{0,12},{4,8},{8,4},{12,0},{24,20},{28,16},{1,13},{5,9},{9,5},{13,1... | collective-permute-start | bytes 442376 | tf_op jit(solution)/shard_map/ppermute | solution.py:259
  72.6 2.5 %collective-permute-start.9 = (bf16[72,1024]{1,0:T(8,128)(2,1)S(1)}, bf16[72,1024]{1,0:T(8,128)(2,1)S(1)}, u32[]{:S(2)}, u32[]{:S(2)}) collective-permute-start(bf16[72,1024]{1,0:T(8,128)(2,1)S(1)} %get-tuple-element.63), channel_id=1, source_target_pairs={{0,4},{4,0},{8,12},{12,8},{20,16},{28,24},{1,5},{5,1},{9,13},{13,9... | collective-permute-start | bytes 442376 | tf_op jit(solution)/shard_map/ppermute | solution.py:259
  75.1 0.1 combine.3
  75.2 3.4 %collective-permute-start.12 = (bf16[72,1024]{1,0:T(8,128)(2,1)S(1)}, bf16[72,1024]{1,0:T(8,128)(2,1)S(1)}, u32[]{:S(2)}, u32[]{:S(2)}) collective-permute-start(bf16[72,1024]{1,0:T(8,128)(2,1)S(1)} %get-tuple-element.69), channel_id=1, source_target_pairs={{0,4},{4,0},{8,12},{12,8},{20,16},{28,24},{1,5},{5,1},{9,13},{13,9... | collective-permute-start | bytes 442376 | tf_op jit(solution)/shard_map/ppermute | solution.py:259
  78.6 4.2 %collective-permute-start.13 = (bf16[72,1024]{1,0:T(8,128)(2,1)S(1)}, bf16[72,1024]{1,0:T(8,128)(2,1)S(1)}, u32[]{:S(2)}, u32[]{:S(2)}) collective-permute-start(bf16[72,1024]{1,0:T(8,128)(2,1)S(1)} %get-tuple-element.70), channel_id=1, source_target_pairs={{0,8},{4,12},{8,0},{12,4},{24,16},{28,20},{1,9},{5,13},{9,1},{13,5... | collective-permute-start | bytes 442376 | tf_op jit(solution)/shard_map/ppermute | solution.py:259
  82.8 3.4 %collective-permute-start.14 = (bf16[72,1024]{1,0:T(8,128)(2,1)S(1)}, bf16[72,1024]{1,0:T(8,128)(2,1)S(1)}, u32[]{:S(2)}, u32[]{:S(2)}) collective-permute-start(bf16[72,1024]{1,0:T(8,128)(2,1)S(1)} %get-tuple-element.71), channel_id=1, source_target_pairs={{0,12},{4,8},{8,4},{12,0},{24,20},{28,16},{1,13},{5,9},{9,5},{13,1... | collective-permute-start | bytes 442376 | tf_op jit(solution)/shard_map/ppermute | solution.py:259
  86.3 6.0 %collective-permute-done.13.refs_8_ = bf16[72,1024]{1,0:T(8,128)(2,1)S(1)} collective-permute-done((bf16[72,1024]{1,0:T(8,128)(2,1)S(1)}, bf16[72,1024]{1,0:T(8,128)(2,1)S(1)}, u32[]{:S(2)}, u32[]{:S(2)}) %collective-permute-start.13) | collective-permute-done | bytes 147488 | tf_op jit(solution)/shard_map/ppermute | solution.py:259
  92.3 0.9 finish.1
  (18 shorter events, 0.1 us)
Async XLA Ops:
  2.6 19.8 %collective-permute-start = (bf16[72,2048]{1,0:T(8,128)(2,1)}, bf16[72,2048]{1,0:T(8,128)(2,1)S(1)}, u32[]{:S(2)}, u32[]{:S(2)}) collective-permute-start(bf16[72,2048]{1,0:T(8,128)(2,1)} %prepare_keys.1.refs_0_), channel_id=1, source_target_pairs={{0,4},{4,0},{8,12},{12,8},{16,20},{24,28},{1,5},{5,1},{9,13},{13,9... | collective-permute-start | bytes 884744 | tf_op jit(solution)/shard_map/ppermute | solution.py:259
  7.5 17.8 %collective-permute-start.1 = (bf16[72,2048]{1,0:T(8,128)(2,1)}, bf16[72,2048]{1,0:T(8,128)(2,1)S(1)}, u32[]{:S(2)}, u32[]{:S(2)}) collective-permute-start(bf16[72,2048]{1,0:T(8,128)(2,1)} %prepare_keys.1.refs_0_), channel_id=1, source_target_pairs={{0,8},{4,12},{8,0},{12,4},{16,24},{20,28},{1,9},{5,13},{9,1},{13,5... | collective-permute-start | bytes 884744 | tf_op jit(solution)/shard_map/ppermute | solution.py:259
  12.0 13.3 %collective-permute-start.2 = (bf16[72,2048]{1,0:T(8,128)(2,1)}, bf16[72,2048]{1,0:T(8,128)(2,1)S(1)}, u32[]{:S(2)}, u32[]{:S(2)}) collective-permute-start(bf16[72,2048]{1,0:T(8,128)(2,1)} %prepare_keys.1.refs_0_), channel_id=1, source_target_pairs={{0,16},{4,20},{8,24},{12,28},{1,17},{5,21},{9,25},{13,29},{2,18},{... | collective-permute-start | bytes 884744 | tf_op jit(solution)/shard_map/ppermute | solution.py:267
  15.5 0.7 copy-start.1
  16.2 1.3 %copy-start.2 = (bf16[72,8192]{1,0:T(8,128)(2,1)S(1)}, bf16[72,8192]{1,0:T(8,128)(2,1)}, u32[]{:S(2)}) copy-start(bf16[72,8192]{1,0:T(8,128)(2,1)} %query_ref.1) | copy-start | bytes 3538948
  17.5 1.3 %copy-start.3 = (bf16[72,8192]{1,0:T(8,128)(2,1)S(1)}, bf16[72,8192]{1,0:T(8,128)(2,1)}, u32[]{:S(2)}) copy-start(bf16[72,8192]{1,0:T(8,128)(2,1)} %grad_ref.1) | copy-start | bytes 3538948
  25.4 15.1 %copy-start = (bf16[72,2048]{1,0:T(8,128)(2,1)S(1)}, bf16[72,2048]{1,0:T(8,128)(2,1)}, u32[]{:S(2)}) copy-start(bf16[72,2048]{1,0:T(8,128)(2,1)} %prepare_keys.1.refs_0_) | copy-start | bytes 884740
  25.4 15.1 %copy-start.4 = (s32[2]{0:T(128)S(1)}, s32[2]{0:T(128)}, u32[]{:S(2)}) copy-start(s32[2]{0:T(128)} %counts_ref.3) | copy-start | bytes 28
  25.4 9.6 %collective-permute-start.3 = (bf16[72,2048]{1,0:T(8,128)(2,1)S(1)}, bf16[72,2048]{1,0:T(8,128)(2,1)S(1)}, u32[]{:S(2)}, u32[]{:S(2)}) collective-permute-start(bf16[72,2048]{1,0:T(8,128)(2,1)S(1)} %collective-permute-done.1.refs_1_.refs_2_), channel_id=1, source_target_pairs={{0,4},{4,0},{8,12},{12,8},{24,28},{28,24},{1,5},{5,1},{9,13},{13,9... | collective-permute-start | bytes 884744 | tf_op jit(solution)/shard_map/ppermute | solution.py:259
  27.4 8.9 %collective-permute-start.4 = (bf16[2,72,1024]{2,1,0:T(8,128)(2,1)S(1)}, bf16[2,72,1024]{2,1,0:T(8,128)(2,1)S(1)}, u32[]{:S(2)}, u32[]{:S(2)}) collective-permute-start(bf16[2,72,1024]{2,1,0:T(8,128)(2,1)S(1)} %stack.3), channel_id=1, source_target_pairs={{0,16},{4,20},{8,24},{12,28},{1,17},{5,21},{9,25},{13,29},{2,18},{... | collective-permute-start | bytes 884744 | tf_op jit(solution)/shard_map/ppermute | solution.py:267
  35.0 5.5 %collective-permute-start.6 = (bf16[1,72,1024]{2,1,0:T(8,128)(2,1)S(1)}, bf16[1,72,1024]{2,1,0:T(8,128)(2,1)S(1)}, u32[]{:S(2)}, u32[]{:S(2)}) collective-permute-start(bf16[1,72,1024]{2,1,0:T(8,128)(2,1)S(1)} %stack.5), channel_id=1, source_target_pairs={{0,16},{4,20},{8,24},{12,28},{1,17},{5,21},{9,25},{13,29},{2,18},{... | collective-permute-start | bytes 442376 | tf_op jit(solution)/shard_map/ppermute | solution.py:267
  36.4 13.4 %collective-permute-start.5 = (bf16[3,72,1024]{2,1,0:T(8,128)(2,1)S(1)}, bf16[3,72,1024]{2,1,0:T(8,128)(2,1)S(1)}, u32[]{:S(2)}, u32[]{:S(2)}) collective-permute-start(bf16[3,72,1024]{2,1,0:T(8,128)(2,1)S(1)} %stack.4), channel_id=1, source_target_pairs={{0,16},{4,20},{8,24},{12,28},{1,17},{5,21},{9,25},{13,29},{2,18},{... | collective-permute-start | bytes 1327112 | tf_op jit(solution)/shard_map/ppermute | solution.py:267
  48.4 16.2 %collective-permute-start.8 = (bf16[4,72,1024]{2,1,0:T(8,128)(2,1)S(1)}, bf16[4,72,1024]{2,1,0:T(8,128)(2,1)S(1)}, u32[]{:S(2)}, u32[]{:S(2)}) collective-permute-start(bf16[4,72,1024]{2,1,0:T(8,128)(2,1)S(1)} %get-tuple-element.60), channel_id=1, source_target_pairs={{16,0},{20,4},{24,8},{28,12},{17,1},{21,5},{25,9},{29,13},{18,2},{... | collective-permute-start | bytes 1769480 | tf_op jit(solution)/shard_map/ppermute | solution.py:267
  57.8 17.3 %collective-permute-start.7 = (bf16[4,72,1024]{2,1,0:T(8,128)(2,1)S(1)}, bf16[4,72,1024]{2,1,0:T(8,128)(2,1)S(1)}, u32[]{:S(2)}, u32[]{:S(2)}) collective-permute-start(bf16[4,72,1024]{2,1,0:T(8,128)(2,1)S(1)} %get-tuple-element.58), channel_id=1, source_target_pairs={{16,0},{20,4},{24,8},{28,12},{17,1},{21,5},{25,9},{29,13},{18,2},{... | collective-permute-start | bytes 1769480 | tf_op jit(solution)/shard_map/ppermute | solution.py:267
  64.8 18.0 %collective-permute-start.10 = (bf16[72,1024]{1,0:T(8,128)(2,1)S(1)}, bf16[72,1024]{1,0:T(8,128)(2,1)S(1)}, u32[]{:S(2)}, u32[]{:S(2)}) collective-permute-start(bf16[72,1024]{1,0:T(8,128)(2,1)S(1)} %get-tuple-element.64), channel_id=1, source_target_pairs={{0,8},{4,12},{8,0},{12,4},{24,16},{28,20},{1,9},{5,13},{9,1},{13,5... | collective-permute-start | bytes 442376 | tf_op jit(solution)/shard_map/ppermute | solution.py:259
  70.6 15.6 %collective-permute-start.11 = (bf16[72,1024]{1,0:T(8,128)(2,1)S(1)}, bf16[72,1024]{1,0:T(8,128)(2,1)S(1)}, u32[]{:S(2)}, u32[]{:S(2)}) collective-permute-start(bf16[72,1024]{1,0:T(8,128)(2,1)S(1)} %get-tuple-element.65), channel_id=1, source_target_pairs={{0,12},{4,8},{8,4},{12,0},{24,20},{28,16},{1,13},{5,9},{9,5},{13,1... | collective-permute-start | bytes 442376 | tf_op jit(solution)/shard_map/ppermute | solution.py:259
  72.6 13.7 %collective-permute-start.9 = (bf16[72,1024]{1,0:T(8,128)(2,1)S(1)}, bf16[72,1024]{1,0:T(8,128)(2,1)S(1)}, u32[]{:S(2)}, u32[]{:S(2)}) collective-permute-start(bf16[72,1024]{1,0:T(8,128)(2,1)S(1)} %get-tuple-element.63), channel_id=1, source_target_pairs={{0,4},{4,0},{8,12},{12,8},{20,16},{28,24},{1,5},{5,1},{9,13},{13,9... | collective-permute-start | bytes 442376 | tf_op jit(solution)/shard_map/ppermute | solution.py:259
  75.2 11.0 %collective-permute-start.12 = (bf16[72,1024]{1,0:T(8,128)(2,1)S(1)}, bf16[72,1024]{1,0:T(8,128)(2,1)S(1)}, u32[]{:S(2)}, u32[]{:S(2)}) collective-permute-start(bf16[72,1024]{1,0:T(8,128)(2,1)S(1)} %get-tuple-element.69), channel_id=1, source_target_pairs={{0,4},{4,0},{8,12},{12,8},{20,16},{28,24},{1,5},{5,1},{9,13},{13,9... | collective-permute-start | bytes 442376 | tf_op jit(solution)/shard_map/ppermute | solution.py:259
  78.6 13.7 %collective-permute-start.13 = (bf16[72,1024]{1,0:T(8,128)(2,1)S(1)}, bf16[72,1024]{1,0:T(8,128)(2,1)S(1)}, u32[]{:S(2)}, u32[]{:S(2)}) collective-permute-start(bf16[72,1024]{1,0:T(8,128)(2,1)S(1)} %get-tuple-element.70), channel_id=1, source_target_pairs={{0,8},{4,12},{8,0},{12,4},{24,16},{28,20},{1,9},{5,13},{9,1},{13,5... | collective-permute-start | bytes 442376 | tf_op jit(solution)/shard_map/ppermute | solution.py:259
  82.8 9.4 %collective-permute-start.14 = (bf16[72,1024]{1,0:T(8,128)(2,1)S(1)}, bf16[72,1024]{1,0:T(8,128)(2,1)S(1)}, u32[]{:S(2)}, u32[]{:S(2)}) collective-permute-start(bf16[72,1024]{1,0:T(8,128)(2,1)S(1)} %get-tuple-element.71), channel_id=1, source_target_pairs={{0,12},{4,8},{8,4},{12,0},{24,20},{28,16},{1,13},{5,9},{9,5},{13,1... | collective-permute-start | bytes 442376 | tf_op jit(solution)/shard_map/ppermute | solution.py:259

commit v8 on v7

--- a/solution.py
+++ b/solution.py
@@ -57,20 +57,27 @@
     return slice(index * HEAD_WIDTH, (index + 1) * HEAD_WIDTH)
 
 
-def prepare_keys(rows, pos_ref, key_ref, value_ref, kv_ref):
+def prepare_keys(rows, pos_ref, key_ref, value_ref, whole_ref, *kv_refs):
     cosine, sine = angle_tables(rows, key_ref.shape[0], pos_ref)
     for head in range(KEY_VALUE_HEADS):
         chunk, place = divmod(head, HEADS_PER_CHUNK)
-        place += 2 * chunk * HEADS_PER_CHUNK
         rotated = rope(key_ref[:, head_cols(head)].astype(jnp.float32), cosine, sine)
-        kv_ref[:, head_cols(place)] = rotated.astype(jnp.bfloat16)
-        kv_ref[:, head_cols(HEADS_PER_CHUNK + place)] = value_ref[:, head_cols(head)]
-
-
-def stack(chunk, *refs):
+        columns = {
+            place: rotated.astype(jnp.bfloat16),
+            HEADS_PER_CHUNK + place: value_ref[:, head_cols(head)],
+        }
+        for column, x in columns.items():
+            kv_refs[chunk][0, :, head_cols(column)] = x
+            whole_ref[:, head_cols(2 * chunk * HEADS_PER_CHUNK + column)] = x
+
+
+def stack(*refs):
     *block_refs, stack_ref = refs
-    for place, ref in enumerate(block_refs):
-        stack_ref[place] = ref[:, 2 * chunk * CHUNK_COLS : 2 * (chunk + 1) * CHUNK_COLS]
+    place = 0
+    for ref in block_refs:
+        for i in range(ref.shape[0]):
+            stack_ref[place] = ref[i]
+            place += 1
 
 
 def prepare_queries(rows, pos_ref, query_ref, grad_ref, *out_refs):
@@ -106,11 +113,17 @@
     return jnp.dot(left, right, preferred_element_type=jnp.float32)
 
 
-def attend(seq_count, head_count, rows, pieces, has_alias, counts_ref, *refs):
+def blocks_of(refs):
+    return [
+        block
+        for ref in refs
+        for block in ([ref] if len(ref.shape) == 2 else [ref.at[i] for i in range(ref.shape[0])])
+    ]
+
+
+def attend(seq_count, head_count, rows, pieces, order, has_alias, counts_ref, *refs):
     blocks = seq_count * head_count
-    kv_refs = []
-    for ref in refs[:pieces]:
-        kv_refs += [ref] if len(ref.shape) == 2 else [ref.at[i] for i in range(ref.shape[0])]
+    kv_refs = [ref for _, ref in sorted(zip(order, blocks_of(refs[:pieces])), key=lambda x: x[0])]
     q_ref, qt_ref, g_ref, gt_ref, cos_ref, sin_ref = refs[pieces : pieces + 6]
     outs = refs[pieces + 6 + 2 * has_alias :]
     out_ref, grad_ref = outs[:2]
@@ -191,29 +204,32 @@
             )
 
 
-def combine(seq_count, head_count, *refs):
+def combine_near(seq_count, *refs):
     part_refs, base_ref, send_refs = refs[:seq_count], refs[seq_count], refs[seq_count + 1 :]
-    for offset in range(head_count):
-        total = part_refs[0][offset].astype(jnp.float32)
-        for ref in part_refs[1:]:
-            total = total + ref[offset].astype(jnp.float32)
+    for offset in range(len(send_refs) + 1):
+        total = sum(ref[offset].astype(jnp.float32) for ref in part_refs)
         if offset == 0:
             base_ref[...] = total
         else:
             send_refs[offset - 1][...] = total.astype(jnp.bfloat16)
 
 
-def finish(head_count, *refs):
-    cosine, sine = refs[0][...], refs[1][...]
+def combine_ranks(*refs):
+    *part_refs, send_ref = refs
+    for offset in range(send_ref.shape[0]):
+        total = sum(ref[offset].astype(jnp.float32) for ref in part_refs)
+        send_ref[jnp.bitwise_xor(lax.axis_index("head"), offset)] = total.astype(jnp.bfloat16)
+
+
+def finish(inputs, cos_ref, sin_ref, *refs):
+    cosine, sine = cos_ref[...], sin_ref[...]
     key_ref, value_ref = refs[-2:]
     for chunk in range(CHUNKS):
-        mine = refs[2 + chunk * head_count : 2 + (chunk + 1) * head_count]
+        mine = blocks_of(refs[sum(inputs[:chunk]) : sum(inputs[: chunk + 1])])
         for place in range(HEADS_PER_CHUNK):
             here, there = head_cols(place), head_cols(HEADS_PER_CHUNK + place)
-            key_total, value_total = mine[0][:, here], mine[0][:, there]
-            for ref in mine[1:]:
-                key_total = key_total + ref[:, here].astype(jnp.float32)
-                value_total = value_total + ref[:, there].astype(jnp.float32)
+            key_total = sum(ref[:, here].astype(jnp.float32) for ref in mine)
+            value_total = sum(ref[:, there].astype(jnp.float32) for ref in mine)
             cols = head_cols(chunk * HEADS_PER_CHUNK + place)
             key_ref[:, cols] = rope_back(key_total, cosine, sine).astype(jnp.bfloat16)
             value_ref[:, cols] = value_total.astype(jnp.bfloat16)
@@ -250,11 +266,11 @@
     def rank_of(s, z):
         return s * head_count + z
 
-    def along_head(x, offset, upward, held=0):
+    def along_head(x, offset, upward, held=(0,)):
         pairs = []
         for s, z in ranks:
             other = z ^ offset
-            if s < seq_count - 1 or ((z ^ held) < other) == upward:
+            if s < seq_count - 1 or any(((z ^ h) < other) == upward for h in held):
                 pairs.append((rank_of(s, z), rank_of(s, other)))
         return lax.ppermute(x, ("seq", "head"), pairs)
 
@@ -269,11 +285,12 @@
     table = shape((padded, HEAD_WIDTH), f32)
     table_t = shape((HEAD_WIDTH // 2, query_rows), f32)
     piece = shape((padded, 2 * CHUNK_COLS), bf16)
-    own = pl.pallas_call(
+    whole, *own = pl.pallas_call(
         functools.partial(prepare_keys, rows),
-        out_shape=shape((padded, CHUNKS * 2 * CHUNK_COLS), bf16),
+        out_shape=[shape((padded, CHUNKS * 2 * CHUNK_COLS), bf16)]
+        + [shape((1, padded, 2 * CHUNK_COLS), bf16)] * CHUNKS,
         in_specs=[SMEM, VMEM, VMEM],
-        out_specs=VMEM,
+        out_specs=[VMEM] * (CHUNKS + 1),
         compiler_params=params(56),
         name="prepare_keys",
     )(positions, routed_keys, routed_values)
@@ -298,31 +315,44 @@
         name="prepare_queries",
     )(positions, queries, output_gradient)
 
+    later = range(1, seq_count)
     bits = [1 << b for b in reversed(range((head_count - 1).bit_length()))]
-    later = range(1, seq_count)
-    last = head_count - 1
-    near = {0: own, **{j: along_head(own, j, True) for j in sorted({bits[0], 1}, reverse=True)}}
-    far = {a: along_seq(own, a, True) for a in later}
-    near, cosine_t, far = lax.optimization_barrier((near, cosine_t, far))
-    for bit in bits[1:]:
-        near.update(
-            {j ^ bit: along_head(x, bit, True, j) for j, x in near.items() if j ^ bit not in near}
-        )
-
-    def cross(chunk, offsets):
-        held = pl.pallas_call(
-            functools.partial(stack, chunk),
-            out_shape=shape((len(offsets), padded, 2 * CHUNK_COLS), bf16),
-            in_specs=[VMEM] * len(offsets),
+
+    def stacked_blocks(xs):
+        if len(xs) == 1:
+            return xs[0]
+        return pl.pallas_call(
+            stack,
+            out_shape=shape((sum(x.shape[0] for x in xs), *xs[0].shape[1:]), bf16),
+            in_specs=[VMEM] * len(xs),
             out_specs=VMEM,
             compiler_params=params(8),
             name="stack",
-        )(*(near[j] for j in offsets))
-        return {a: along_seq(held, a, True) for a in later}
-
-    crossed = [[cross(0, range(1, last)), cross(0, [last])]]
-    near[last], crossed[0][0] = lax.optimization_barrier((near[last], crossed[0][0]))
-    crossed += [[cross(chunk, range(1, head_count))] for chunk in range(1, CHUNKS)]
+        )(*xs)
+
+    far = {a: along_seq(whole, a, True) for a in later}
+    near, crossed = [], []
+    for chunk in range(CHUNKS):
+        held, received, passed = [0], [], []
+        for bit in bits:
+            x = along_head(stacked_blocks([own[chunk], *received]), bit, True, held)
+            if chunk == 0 and bit == bits[0]:
+                x, own[1:], cosine_t, far = lax.optimization_barrier(
+                    (x, own[1:], cosine_t, far)
+                )
+            if chunk == 0:
+                if bit == bits[-1]:
+                    x, passed = lax.optimization_barrier((x, passed))
+                passed.append({a: along_seq(x, a, True) for a in later})
+            elif bit == bits[0]:
+                x, near[-1][-1] = lax.optimization_barrier((x, near[-1][-1]))
+            received.append(x)
+            held += [h ^ bit for h in held]
+        near.append(received)
+        if chunk:
+            passed = [{a: along_seq(stacked_blocks(received), a, True) for a in later}]
+        crossed.append(passed)
+    order = [a * head_count + h for a in range(seq_count) for h in held]
 
     wide_outs = ()
     parts = []
@@ -334,7 +364,7 @@
             for x in (tall, flat)
         )
         row_part = pl.BlockSpec((padded, STEP_HEADS * wide), lambda g, f=first: (0, f + g))
-        gathered = [near[j] for j in range(head_count)]
+        gathered = [whole, *near[chunk]]
         for a in later:
             gathered += [far[a]] + [part[a] for part in crossed[chunk]]
         inputs = len(gathered)
@@ -345,7 +375,7 @@
         ]
         part_block = pl.BlockSpec((head_count, padded, 2 * CHUNK_COLS), lambda g: (0, 0, 0))
         out = pl.pallas_call(
-            functools.partial(attend, seq_count, head_count, rows, inputs, has_alias),
+            functools.partial(attend, seq_count, head_count, rows, inputs, order, has_alias),
             grid=(HEADS_PER_CHUNK // STEP_HEADS,),
             out_shape=[shape((padded, QUERY_HEADS * HEAD_WIDTH), bf16)] * 2
             + [shape((head_count, padded, 2 * CHUNK_COLS), bf16)] * seq_count,
@@ -367,32 +397,39 @@
         parts.append([out[2]] + [along_seq(out[2 + a], a, False) for a in later])
 
     summed = []
-    for mine in parts:
-        if summed:
-            mine[-1], summed[-head_count] = lax.optimization_barrier(
-                (mine[-1], summed[-head_count])
-            )
+    for mine in parts[:-1]:
         base, *sends = pl.pallas_call(
-            functools.partial(combine, seq_count, head_count),
+            functools.partial(combine_near, seq_count),
             out_shape=[shape((padded, 2 * CHUNK_COLS), f32)] + [piece] * (head_count - 1),
             in_specs=[VMEM] * seq_count,
             out_specs=[VMEM] * head_count,
             cost_estimate=cost(2),
             compiler_params=params(8),
-            name="combine",
+            name="combine_near",
         )(*mine)
-        summed += [base] + [along_head(x, j + 1, False) for j, x in enumerate(sends)]
+        parts[-1][-1], base = lax.optimization_barrier((parts[-1][-1], base))
+        summed.append([base] + [along_head(x, j + 1, False) for j, x in enumerate(sends)])
+    sums = pl.pallas_call(
+        combine_ranks,
+        out_shape=shape((head_count, padded, 2 * CHUNK_COLS), bf16),
+        in_specs=[VMEM] * seq_count,
+        out_specs=VMEM,
+        cost_estimate=cost(2),
+        compiler_params=params(8),
+        name="combine_ranks",
+    )(*parts[-1])
+    summed.append([lax.all_to_all(sums, "head", split_axis=0, concat_axis=0, tiled=True)])
 
     narrow = shape((padded, KEY_VALUE_HEADS * HEAD_WIDTH), bf16)
     key_grad, value_grad = pl.pallas_call(
-        functools.partial(finish, head_count),
+        functools.partial(finish, [len(xs) for xs in summed]),
         out_shape=[narrow, narrow],
-        in_specs=[VMEM] * (2 + CHUNKS * head_count),
+        in_specs=[VMEM] * (2 + sum(len(xs) for xs in summed)),
         out_specs=[VMEM, VMEM],
         cost_estimate=cost(2),
         compiler_params=params(8),
         name="finish",
-    )(cosine, sine, *summed)
+    )(cosine, sine, *(x for xs in summed for x in xs))
     results = (*wide_outs, key_grad, value_grad)
     if padded != rows:
         results = tuple(x[:rows] for x in results)

time: 93.8 us -> 113 us (1.20)
  waiting for transfers between devices: 22.7 us -> 42.9 us
  starting transfers between devices: 43.5 us -> 41.7 us
    ppermute x9 -> x7, waiting for transfers between devices: 15.2 us -> 26 us  [along_head(): return lax.ppermute(x, ('seq', 'head'), pairs)]
    ppermute x6, waiting for transfers between devices: 7.5 us -> 16.9 us  [along_seq(): return lax.ppermute(x, ('seq', 'head'), pairs)]
    ppermute x9 -> x7, starting transfers between devices: 32.7 us -> 25 us  [along_head(): return lax.ppermute(x, ('seq', 'head'), pairs)]
    all_to_all x0 -> x1, starting transfers between devices: none -> 5.28 us  [shards(): lax.all_to_all(sums, 'head', split_axis=0, concat_axis=0, tiled=True)]
    unnamed x10 -> x14, local copies, waits for them, and re-layouts: 3.23 us -> 3.25 us
  transfers between devices with their start and end apart: 15 -> 14, of which waited for: 5 -> 9; matrix products, arithmetic and copies ran while one was open for 0% -> 0% of each run, Pallas kernels for 21% -> 18%
where the time goes in v8:
time: 113 us
  waiting for transfers between devices  42.9 us (38%)
  starting transfers between devices  41.7 us (37%)
  Pallas kernels  23.9 us (21%)
  local copies, waits for them, and re-layouts  3.25 us (3%)
    ppermute x7, waiting for transfers between devices, along_head(): return lax.ppermute(x, ('seq', 'head'), pairs)  26 us
    ppermute x7, starting transfers between devices, along_head(): return lax.ppermute(x, ('seq', 'head'), pairs)  25 us
    ppermute x6, waiting for transfers between devices, along_seq(): return lax.ppermute(x, ('seq', 'head'), pairs)  16.9 us
    pallas_call x2, Pallas kernels, shards(): pl.pallas_call(functools.partial(attend, seq_count, head_count, rows, inp...  16.1 us
    ppermute x6, starting transfers between devices, along_seq(): return lax.ppermute(x, ('seq', 'head'), pairs)  11.4 us
    all_to_all x1, starting transfers between devices, shards(): lax.all_to_all(sums, 'head', split_axis=0, concat_axis=0, tiled=True)  5.28 us
    pallas_call x1, Pallas kernels, shards(): pl.pallas_call(functools.partial(prepare_queries, rows), grid=(KEY_VALUE_...  3.65 us
    unnamed x14, local copies, waits for them, and re-layouts  3.25 us
  transfers between devices with their start and end apart: 14, of which 9 were waited for; matrix products, arithmetic and copies ran while one was open for 0% of the time, Pallas kernels for 18%

profile of v8, /device:TPU:0, one launch (start us, length us, event | category | flops | bytes accessed | tf_op | source)
XLA Modules:
  0.0 112.5 jit_solution(10029590230280991762)
XLA Ops:
  0.6 2.1 %prepare_keys.1 = (bf16[72,2048]{1,0:T(8,128)(2,1)}, bf16[1,72,1024]{2,1,0:T(8,128)(2,1)}, bf16[1,72,1024]{2,1,0:T(8,128)(2,1)}) custom-call(s32[576]{0:T(1024)} %pos_ref.3, bf16[72,1024]{1,0:T(8,128)(2,1)} %key_ref.1, bf16[72,1024]{1,0:T(8,128)(2,1)} %value_ref.1), custom_call_target="tpu_custom_call" | custom-call | tf_op jit(solution)/shard_map/prepare_keys/pallas_call | solution.py:288
  2.7 4.9 %collective-permute-start.1 = (bf16[72,2048]{1,0:T(8,128)(2,1)}, bf16[72,2048]{1,0:T(8,128)(2,1)S(1)}, u32[]{:S(2)}, u32[]{:S(2)}) collective-permute-start(bf16[72,2048]{1,0:T(8,128)(2,1)} %get-tuple-element.39.refs_0_), channel_id=1, source_target_pairs={{0,16},{4,20},{8,24},{12,28},{1,17},{5,21},{9,25},{13,29},{2,18},{... | collective-permute-start | bytes 884744 | tf_op jit(solution)/shard_map/ppermute | solution.py:283
  7.6 4.6 %collective-permute-start = (bf16[1,72,1024]{2,1,0:T(8,128)(2,1)}, bf16[1,72,1024]{2,1,0:T(8,128)(2,1)S(1)}, u32[]{:S(2)}, u32[]{:S(2)}) collective-permute-start(bf16[1,72,1024]{2,1,0:T(8,128)(2,1)} %get-tuple-element.40.refs_0_), channel_id=1, source_target_pairs={{0,8},{4,12},{8,0},{12,4},{16,24},{20,28},{1,9},{5,13},{9,1},{13,5... | collective-permute-start | bytes 442376 | tf_op jit(solution)/shard_map/ppermute | solution.py:275
  12.3 0.7 copy-done.2
  13.0 1.3 %copy-done.3 = bf16[72,8192]{1,0:T(8,128)(2,1)S(1)} copy-done((bf16[72,8192]{1,0:T(8,128)(2,1)S(1)}, bf16[72,8192]{1,0:T(8,128)(2,1)}, u32[]{:S(2)}) %copy-start.3) | copy-done | bytes 1179672
  14.2 1.3 %copy-done.4 = bf16[72,8192]{1,0:T(8,128)(2,1)S(1)} copy-done((bf16[72,8192]{1,0:T(8,128)(2,1)S(1)}, bf16[72,8192]{1,0:T(8,128)(2,1)}, u32[]{:S(2)}) %copy-start.4) | copy-done | bytes 1179672
  15.5 3.6 %prepare_queries.1 = (bf16[8,576,128]{2,1,0:T(8,128)(2,1)S(1)}, bf16[8,128,576]{2,1,0:T(8,128)(2,1)S(1)}, bf16[8,576,128]{2,1,0:T(8,128)(2,1)S(1)}, bf16[8,128,5...) custom-call(s32[576]{0:T(1024)S(1)} %copy-done.2, ...), custom_call_target="tpu_custom_call" | custom-call | flops 8071000064 | bytes 25830000 | tf_op jit(solution)/shard_map/prepare_queries/pallas_call | solution.py:306
  19.3 3.6 %collective-permute-start.3 = (bf16[2,72,1024]{2,1,0:T(8,128)(2,1)S(1)}, bf16[2,72,1024]{2,1,0:T(8,128)(2,1)S(1)}, u32[]{:S(2)}, u32[]{:S(2)}) collective-permute-start(bf16[2,72,1024]{2,1,0:T(8,128)(2,1)S(1)} %stack.3), channel_id=1, source_target_pairs={{0,4},{4,0},{8,12},{12,8},{16,20},{24,28},{28,24},{1,5},{5,1},{9,1... | collective-permute-start | bytes 884744 | tf_op jit(solution)/shard_map/ppermute | solution.py:275
  22.9 1.3 %collective-permute-start.4 = (bf16[1,72,1024]{2,1,0:T(8,128)(2,1)S(1)}, bf16[1,72,1024]{2,1,0:T(8,128)(2,1)S(1)}, u32[]{:S(2)}, u32[]{:S(2)}) collective-permute-start(bf16[1,72,1024]{2,1,0:T(8,128)(2,1)S(1)} %collective-permute-done.refs_1_), channel_id=1, source_target_pairs={{0,16},{4,20},{8,24},{12,28},{1,17},{5,21},{9,25},{13,29},{2,18},{... | collective-permute-start | bytes 442376 | tf_op jit(solution)/shard_map/ppermute | solution.py:283
  24.2 4.5 %collective-permute-start.2 = (bf16[1,72,1024]{2,1,0:T(8,128)(2,1)S(1)}, bf16[1,72,1024]{2,1,0:T(8,128)(2,1)S(1)}, u32[]{:S(2)}, u32[]{:S(2)}) collective-permute-start(bf16[1,72,1024]{2,1,0:T(8,128)(2,1)S(1)} %copy-done), channel_id=1, source_target_pairs={{0,8},{4,12},{8,0},{12,4},{16,24},{20,28},{1,9},{5,13},{9,1},{13,5... | collective-permute-start | bytes 442376 | tf_op jit(solution)/shard_map/ppermute | solution.py:275
  28.7 3.2 %collective-permute-done.3.refs_2_ = bf16[2,72,1024]{2,1,0:T(8,128)(2,1)S(1)} collective-permute-done((bf16[2,72,1024]{2,1,0:T(8,128)(2,1)S(1)}, bf16[2,72,1024]{2,1,0:T(8,128)(2,1)S(1)}, u32[]{:S(2)}, u32[]{:S(2)}) %collective-permute-start.3) | collective-permute-done | bytes 294944 | tf_op jit(solution)/shard_map/ppermute | solution.py:275
  31.9 3.4 %collective-permute-done.2.refs_1_.refs_0_ = bf16[1,72,1024]{2,1,0:T(8,128)(2,1)S(1)} collective-permute-done((bf16[1,72,1024]{2,1,0:T(8,128)(2,1)S(1)}, bf16[1,72,1024]{2,1,0:T(8,128)(2,1)S(1)}, u32[]{:S(2)}, u32[]{:S(2)}) %collective-permute-start.2) | collective-permute-done | bytes 147488 | tf_op jit(solution)/shard_map/ppermute | solution.py:275
  35.4 2.2 %collective-permute-start.5 = (bf16[2,72,1024]{2,1,0:T(8,128)(2,1)S(1)}, bf16[2,72,1024]{2,1,0:T(8,128)(2,1)S(1)}, u32[]{:S(2)}, u32[]{:S(2)}) collective-permute-start(bf16[2,72,1024]{2,1,0:T(8,128)(2,1)S(1)} %stack.4), channel_id=1, source_target_pairs={{0,4},{4,0},{8,12},{12,8},{16,20},{24,28},{28,24},{1,5},{5,1},{9,1... | collective-permute-start | bytes 884744 | tf_op jit(solution)/shard_map/ppermute | solution.py:275
  37.6 1.3 %collective-permute-start.7 = (bf16[2,72,1024]{2,1,0:T(8,128)(2,1)S(1)}, bf16[2,72,1024]{2,1,0:T(8,128)(2,1)S(1)}, u32[]{:S(2)}, u32[]{:S(2)}) collective-permute-start(bf16[2,72,1024]{2,1,0:T(8,128)(2,1)S(1)} %collective-permute-done.3.refs_2_), channel_id=1, source_target_pairs={{0,16},{4,20},{8,24},{12,28},{1,17},{5,21},{9,25},{13,29},{2,18},{... | collective-permute-start | bytes 884744 | tf_op jit(solution)/shard_map/ppermute | solution.py:283
  38.9 5.3 %collective-permute-done.5.refs_1_.refs_2_ = bf16[2,72,1024]{2,1,0:T(8,128)(2,1)S(1)} collective-permute-done((bf16[2,72,1024]{2,1,0:T(8,128)(2,1)S(1)}, bf16[2,72,1024]{2,1,0:T(8,128)(2,1)S(1)}, u32[]{:S(2)}, u32[]{:S(2)}) %collective-permute-start.5) | collective-permute-done | bytes 294944 | tf_op jit(solution)/shard_map/ppermute | solution.py:275
  44.2 1.3 %collective-permute-start.6 = (bf16[3,72,1024]{2,1,0:T(8,128)(2,1)S(1)}, bf16[3,72,1024]{2,1,0:T(8,128)(2,1)S(1)}, u32[]{:S(2)}, u32[]{:S(2)}) collective-permute-start(bf16[3,72,1024]{2,1,0:T(8,128)(2,1)S(1)} %stack.5), channel_id=1, source_target_pairs={{0,16},{4,20},{8,24},{12,28},{1,17},{5,21},{9,25},{13,29},{2,18},{... | collective-permute-start | bytes 1327112 | tf_op jit(solution)/shard_map/ppermute | solution.py:283
  45.6 0.2 collective-permute-done.7.refs_5_
  45.8 8.0 %attend.2 = (bf16[72,8192]{1,0:T(8,128)(2,1)}, bf16[72,8192]{1,0:T(8,128)(2,1)}, bf16[4,72,1024]{2,1,0:T(8,128)(2,1)S(1)}, bf16[4,72,1024]{2,1,0:T(8,128)(2,1)S(1)}) custom-call(s32[2]{0:T(128)S(1)} %copy-done.6, bf16[72,2048]{1,0:T(8,128)(2,1)S(1)} %copy-done.5, bf16[1,72,1024]{2,1,0:T(8,128)(2,1)S(1)} %collective-permute-done.refs_1_, ...), custom_call_target="tpu_custom_call" | custom-call | flops 11530000384 | bytes 36900000 | tf_op jit(solution)/shard_map/attend/pallas_call | solution.py:377
  53.8 1.3 %collective-permute-start.9 = (bf16[4,72,1024]{2,1,0:T(8,128)(2,1)S(1)}, bf16[4,72,1024]{2,1,0:T(8,128)(2,1)S(1)}, u32[]{:S(2)}, u32[]{:S(2)}) collective-permute-start(bf16[4,72,1024]{2,1,0:T(8,128)(2,1)S(1)} %get-tuple-element.64), channel_id=1, source_target_pairs={{16,0},{20,4},{24,8},{28,12},{17,1},{21,5},{25,9},{29,13},{18,2},{... | collective-permute-start | bytes 1769480 | tf_op jit(solution)/shard_map/ppermute | solution.py:283
  55.1 8.0 %attend.3 = (bf16[72,8192]{1,0:T(8,128)(2,1)}, bf16[72,8192]{1,0:T(8,128)(2,1)}, bf16[4,72,1024]{2,1,0:T(8,128)(2,1)S(1)}, bf16[4,72,1024]{2,1,0:T(8,128)(2,1)S(1)}) custom-call(s32[2]{0:T(128)S(1)} %copy-done.6, bf16[72,2048]{1,0:T(8,128)(2,1)S(1)} %copy-done.5, ...), custom_call_target="tpu_custom_call", output_to_operand_aliasing={{0}: (12, {}), {1}: (13, {})} | custom-call | flops 11530000384 | bytes 36900000 | tf_op jit(solution)/shard_map/attend/pallas_call | solution.py:377
  63.1 1.3 %collective-permute-start.8 = (bf16[4,72,1024]{2,1,0:T(8,128)(2,1)S(1)}, bf16[4,72,1024]{2,1,0:T(8,128)(2,1)S(1)}, u32[]{:S(2)}, u32[]{:S(2)}) collective-permute-start(bf16[4,72,1024]{2,1,0:T(8,128)(2,1)S(1)} %get-tuple-element.62), channel_id=1, source_target_pairs={{16,0},{20,4},{24,8},{28,12},{17,1},{21,5},{25,9},{29,13},{18,2},{... | collective-permute-start | bytes 1769480 | tf_op jit(solution)/shard_map/ppermute | solution.py:283
  64.4 7.3 %collective-permute-done.9.refs_1_ = bf16[4,72,1024]{2,1,0:T(8,128)(2,1)S(1)} collective-permute-done((bf16[4,72,1024]{2,1,0:T(8,128)(2,1)S(1)}, bf16[4,72,1024]{2,1,0:T(8,128)(2,1)S(1)}, u32[]{:S(2)}, u32[]{:S(2)}) %collective-permute-start.9) | collective-permute-done | bytes 589856 | tf_op jit(solution)/shard_map/ppermute | solution.py:283
  71.7 0.1 combine_near.1
  71.9 9.3 %collective-permute-done.8.refs_1_ = bf16[4,72,1024]{2,1,0:T(8,128)(2,1)S(1)} collective-permute-done((bf16[4,72,1024]{2,1,0:T(8,128)(2,1)S(1)}, bf16[4,72,1024]{2,1,0:T(8,128)(2,1)S(1)}, u32[]{:S(2)}, u32[]{:S(2)}) %collective-permute-start.8) | collective-permute-done | bytes 589856 | tf_op jit(solution)/shard_map/ppermute | solution.py:283
  81.2 1.0 combine_ranks.1
  82.2 5.3 %all-to-all-start = ((bf16[4,72,1024]{2,1,0:T(8,128)(2,1)}), bf16[4,72,1024]{2,1,0:T(8,128)(2,1)S(1)}, u32[]{:S(2)}, u32[]{:S(2)}) async-start(bf16[4,72,1024]{2,1,0:T(8,128)(2,1)} %combine_ranks.1), calls=%async_computation | async-start | bytes 1179648 | tf_op jit(solution)/shard_map/all_to_all | solution.py:421
  87.5 3.9 %collective-permute-start.10 = (bf16[72,1024]{1,0:T(8,128)(2,1)S(1)}, bf16[72,1024]{1,0:T(8,128)(2,1)S(1)}, u32[]{:S(2)}, u32[]{:S(2)}) collective-permute-start(bf16[72,1024]{1,0:T(8,128)(2,1)S(1)} %get-tuple-element.67), channel_id=1, source_target_pairs={{0,4},{4,0},{8,12},{12,8},{20,16},{28,24},{1,5},{5,1},{9,13},{13,9... | collective-permute-start | bytes 442376 | tf_op jit(solution)/shard_map/ppermute | solution.py:275
  91.4 4.3 %collective-permute-start.11 = (bf16[72,1024]{1,0:T(8,128)(2,1)S(1)}, bf16[72,1024]{1,0:T(8,128)(2,1)S(1)}, u32[]{:S(2)}, u32[]{:S(2)}) collective-permute-start(bf16[72,1024]{1,0:T(8,128)(2,1)S(1)} %get-tuple-element.68), channel_id=1, source_target_pairs={{0,8},{4,12},{8,0},{12,4},{24,16},{28,20},{1,9},{5,13},{9,1},{13,5... | collective-permute-start | bytes 442376 | tf_op jit(solution)/shard_map/ppermute | solution.py:275
  95.7 1.9 %collective-permute-start.12 = (bf16[72,1024]{1,0:T(8,128)(2,1)S(1)}, bf16[72,1024]{1,0:T(8,128)(2,1)S(1)}, u32[]{:S(2)}, u32[]{:S(2)}) collective-permute-start(bf16[72,1024]{1,0:T(8,128)(2,1)S(1)} %get-tuple-element.69), channel_id=1, source_target_pairs={{0,12},{4,8},{8,4},{12,0},{24,20},{28,16},{1,13},{5,9},{9,5},{13,1... | collective-permute-start | bytes 442376 | tf_op jit(solution)/shard_map/ppermute | solution.py:275
  97.6 3.1 %collective-permute-done.10.refs_1_ = bf16[72,1024]{1,0:T(8,128)(2,1)S(1)} collective-permute-done((bf16[72,1024]{1,0:T(8,128)(2,1)S(1)}, bf16[72,1024]{1,0:T(8,128)(2,1)S(1)}, u32[]{:S(2)}, u32[]{:S(2)}) %collective-permute-start.10) | collective-permute-done | bytes 147488 | tf_op jit(solution)/shard_map/ppermute | solution.py:275
  100.7 10.9 %collective-permute-done.11.refs_2_ = bf16[72,1024]{1,0:T(8,128)(2,1)S(1)} collective-permute-done((bf16[72,1024]{1,0:T(8,128)(2,1)S(1)}, bf16[72,1024]{1,0:T(8,128)(2,1)S(1)}, u32[]{:S(2)}, u32[]{:S(2)}) %collective-permute-start.11) | collective-permute-done | bytes 147488 | tf_op jit(solution)/shard_map/ppermute | solution.py:275
  111.6 0.9 finish.1
  (20 shorter events, 0.2 us)
Async XLA Ops:
  2.7 16.5 %collective-permute-start.1 = (bf16[72,2048]{1,0:T(8,128)(2,1)}, bf16[72,2048]{1,0:T(8,128)(2,1)S(1)}, u32[]{:S(2)}, u32[]{:S(2)}) collective-permute-start(bf16[72,2048]{1,0:T(8,128)(2,1)} %get-tuple-element.39.refs_0_), channel_id=1, source_target_pairs={{0,16},{4,20},{8,24},{12,28},{1,17},{5,21},{9,25},{13,29},{2,18},{... | collective-permute-start | bytes 884744 | tf_op jit(solution)/shard_map/ppermute | solution.py:283
  7.6 11.6 %copy-start.1 = (bf16[1,72,1024]{2,1,0:T(8,128)(2,1)S(1)}, bf16[1,72,1024]{2,1,0:T(8,128)(2,1)}, u32[]{:S(2)}) copy-start(bf16[1,72,1024]{2,1,0:T(8,128)(2,1)} %get-tuple-element.40.refs_0_) | copy-start | bytes 442372
  7.6 16.6 %copy-start = (bf16[1,72,1024]{2,1,0:T(8,128)(2,1)S(1)}, bf16[1,72,1024]{2,1,0:T(8,128)(2,1)}, u32[]{:S(2)}) copy-start(bf16[1,72,1024]{2,1,0:T(8,128)(2,1)} %get-tuple-element.43.refs_0_) | copy-start | bytes 442372
  7.6 11.6 %collective-permute-start = (bf16[1,72,1024]{2,1,0:T(8,128)(2,1)}, bf16[1,72,1024]{2,1,0:T(8,128)(2,1)S(1)}, u32[]{:S(2)}, u32[]{:S(2)}) collective-permute-start(bf16[1,72,1024]{2,1,0:T(8,128)(2,1)} %get-tuple-element.40.refs_0_), channel_id=1, source_target_pairs={{0,8},{4,12},{8,0},{12,4},{16,24},{20,28},{1,9},{5,13},{9,1},{13,5... | collective-permute-start | bytes 442376 | tf_op jit(solution)/shard_map/ppermute | solution.py:275
  12.3 0.7 copy-start.2
  13.0 1.3 %copy-start.3 = (bf16[72,8192]{1,0:T(8,128)(2,1)S(1)}, bf16[72,8192]{1,0:T(8,128)(2,1)}, u32[]{:S(2)}) copy-start(bf16[72,8192]{1,0:T(8,128)(2,1)} %query_ref.1) | copy-start | bytes 3538948
  14.2 1.3 %copy-start.4 = (bf16[72,8192]{1,0:T(8,128)(2,1)S(1)}, bf16[72,8192]{1,0:T(8,128)(2,1)}, u32[]{:S(2)}) copy-start(bf16[72,8192]{1,0:T(8,128)(2,1)} %grad_ref.1) | copy-start | bytes 3538948
  19.1 26.6 %copy-start.5 = (bf16[72,2048]{1,0:T(8,128)(2,1)S(1)}, bf16[72,2048]{1,0:T(8,128)(2,1)}, u32[]{:S(2)}) copy-start(bf16[72,2048]{1,0:T(8,128)(2,1)} %get-tuple-element.39.refs_0_) | copy-start | bytes 884740
  19.2 26.6 %copy-start.6 = (s32[2]{0:T(128)S(1)}, s32[2]{0:T(128)}, u32[]{:S(2)}) copy-start(s32[2]{0:T(128)} %counts_ref.3) | copy-start | bytes 28
  19.3 12.7 %collective-permute-start.3 = (bf16[2,72,1024]{2,1,0:T(8,128)(2,1)S(1)}, bf16[2,72,1024]{2,1,0:T(8,128)(2,1)S(1)}, u32[]{:S(2)}, u32[]{:S(2)}) collective-permute-start(bf16[2,72,1024]{2,1,0:T(8,128)(2,1)S(1)} %stack.3), channel_id=1, source_target_pairs={{0,4},{4,0},{8,12},{12,8},{16,20},{24,28},{28,24},{1,5},{5,1},{9,1... | collective-permute-start | bytes 884744 | tf_op jit(solution)/shard_map/ppermute | solution.py:275
  22.9 5.9 %collective-permute-start.4 = (bf16[1,72,1024]{2,1,0:T(8,128)(2,1)S(1)}, bf16[1,72,1024]{2,1,0:T(8,128)(2,1)S(1)}, u32[]{:S(2)}, u32[]{:S(2)}) collective-permute-start(bf16[1,72,1024]{2,1,0:T(8,128)(2,1)S(1)} %collective-permute-done.refs_1_), channel_id=1, source_target_pairs={{0,16},{4,20},{8,24},{12,28},{1,17},{5,21},{9,25},{13,29},{2,18},{... | collective-permute-start | bytes 442376 | tf_op jit(solution)/shard_map/ppermute | solution.py:283
  24.2 11.2 %collective-permute-start.2 = (bf16[1,72,1024]{2,1,0:T(8,128)(2,1)S(1)}, bf16[1,72,1024]{2,1,0:T(8,128)(2,1)S(1)}, u32[]{:S(2)}, u32[]{:S(2)}) collective-permute-start(bf16[1,72,1024]{2,1,0:T(8,128)(2,1)S(1)} %copy-done), channel_id=1, source_target_pairs={{0,8},{4,12},{8,0},{12,4},{16,24},{20,28},{1,9},{5,13},{9,1},{13,5... | collective-permute-start | bytes 442376 | tf_op jit(solution)/shard_map/ppermute | solution.py:275
  35.4 8.8 %collective-permute-start.5 = (bf16[2,72,1024]{2,1,0:T(8,128)(2,1)S(1)}, bf16[2,72,1024]{2,1,0:T(8,128)(2,1)S(1)}, u32[]{:S(2)}, u32[]{:S(2)}) collective-permute-start(bf16[2,72,1024]{2,1,0:T(8,128)(2,1)S(1)} %stack.4), channel_id=1, source_target_pairs={{0,4},{4,0},{8,12},{12,8},{16,20},{24,28},{28,24},{1,5},{5,1},{9,1... | collective-permute-start | bytes 884744 | tf_op jit(solution)/shard_map/ppermute | solution.py:275
  37.6 8.2 %collective-permute-start.7 = (bf16[2,72,1024]{2,1,0:T(8,128)(2,1)S(1)}, bf16[2,72,1024]{2,1,0:T(8,128)(2,1)S(1)}, u32[]{:S(2)}, u32[]{:S(2)}) collective-permute-start(bf16[2,72,1024]{2,1,0:T(8,128)(2,1)S(1)} %collective-permute-done.3.refs_2_), channel_id=1, source_target_pairs={{0,16},{4,20},{8,24},{12,28},{1,17},{5,21},{9,25},{13,29},{2,18},{... | collective-permute-start | bytes 884744 | tf_op jit(solution)/shard_map/ppermute | solution.py:283
  44.2 10.8 %collective-permute-start.6 = (bf16[3,72,1024]{2,1,0:T(8,128)(2,1)S(1)}, bf16[3,72,1024]{2,1,0:T(8,128)(2,1)S(1)}, u32[]{:S(2)}, u32[]{:S(2)}) collective-permute-start(bf16[3,72,1024]{2,1,0:T(8,128)(2,1)S(1)} %stack.5), channel_id=1, source_target_pairs={{0,16},{4,20},{8,24},{12,28},{1,17},{5,21},{9,25},{13,29},{2,18},{... | collective-permute-start | bytes 1327112 | tf_op jit(solution)/shard_map/ppermute | solution.py:283
  53.8 18.0 %collective-permute-start.9 = (bf16[4,72,1024]{2,1,0:T(8,128)(2,1)S(1)}, bf16[4,72,1024]{2,1,0:T(8,128)(2,1)S(1)}, u32[]{:S(2)}, u32[]{:S(2)}) collective-permute-start(bf16[4,72,1024]{2,1,0:T(8,128)(2,1)S(1)} %get-tuple-element.64), channel_id=1, source_target_pairs={{16,0},{20,4},{24,8},{28,12},{17,1},{21,5},{25,9},{29,13},{18,2},{... | collective-permute-start | bytes 1769480 | tf_op jit(solution)/shard_map/ppermute | solution.py:283
  63.1 18.1 %collective-permute-start.8 = (bf16[4,72,1024]{2,1,0:T(8,128)(2,1)S(1)}, bf16[4,72,1024]{2,1,0:T(8,128)(2,1)S(1)}, u32[]{:S(2)}, u32[]{:S(2)}) collective-permute-start(bf16[4,72,1024]{2,1,0:T(8,128)(2,1)S(1)} %get-tuple-element.62), channel_id=1, source_target_pairs={{16,0},{20,4},{24,8},{28,12},{17,1},{21,5},{25,9},{29,13},{18,2},{... | collective-permute-start | bytes 1769480 | tf_op jit(solution)/shard_map/ppermute | solution.py:283
  82.2 29.4 %all-to-all-start = ((bf16[4,72,1024]{2,1,0:T(8,128)(2,1)}), bf16[4,72,1024]{2,1,0:T(8,128)(2,1)S(1)}, u32[]{:S(2)}, u32[]{:S(2)}) async-start(bf16[4,72,1024]{2,1,0:T(8,128)(2,1)} %combine_ranks.1), calls=%async_computation | async-start | bytes 1179648 | tf_op jit(solution)/shard_map/all_to_all | solution.py:421
  87.5 13.3 %collective-permute-start.10 = (bf16[72,1024]{1,0:T(8,128)(2,1)S(1)}, bf16[72,1024]{1,0:T(8,128)(2,1)S(1)}, u32[]{:S(2)}, u32[]{:S(2)}) collective-permute-start(bf16[72,1024]{1,0:T(8,128)(2,1)S(1)} %get-tuple-element.67), channel_id=1, source_target_pairs={{0,4},{4,0},{8,12},{12,8},{20,16},{28,24},{1,5},{5,1},{9,13},{13,9... | collective-permute-start | bytes 442376 | tf_op jit(solution)/shard_map/ppermute | solution.py:275
  91.4 20.2 %collective-permute-start.11 = (bf16[72,1024]{1,0:T(8,128)(2,1)S(1)}, bf16[72,1024]{1,0:T(8,128)(2,1)S(1)}, u32[]{:S(2)}, u32[]{:S(2)}) collective-permute-start(bf16[72,1024]{1,0:T(8,128)(2,1)S(1)} %get-tuple-element.68), channel_id=1, source_target_pairs={{0,8},{4,12},{8,0},{12,4},{24,16},{28,20},{1,9},{5,13},{9,1},{13,5... | collective-permute-start | bytes 442376 | tf_op jit(solution)/shard_map/ppermute | solution.py:275
  95.7 16.0 %collective-permute-start.12 = (bf16[72,1024]{1,0:T(8,128)(2,1)S(1)}, bf16[72,1024]{1,0:T(8,128)(2,1)S(1)}, u32[]{:S(2)}, u32[]{:S(2)}) collective-permute-start(bf16[72,1024]{1,0:T(8,128)(2,1)S(1)} %get-tuple-element.69), channel_id=1, source_target_pairs={{0,12},{4,8},{8,4},{12,0},{24,20},{28,16},{1,13},{5,9},{9,5},{13,1... | collective-permute-start | bytes 442376 | tf_op jit(solution)/shard_map/ppermute | solution.py:275

commit v9 on v7

--- a/solution.py
+++ b/solution.py
@@ -14,6 +14,7 @@
 GROUP = QUERY_HEADS // KEY_VALUE_HEADS
 ROPE_BASE = 500000.0
 SCORE_SCALE = 1.0 / float(np.sqrt(HEAD_WIDTH))
+SCORE_TO_LOG2 = SCORE_SCALE * 1.4426950408889634
 CHUNKS = 2
 HEADS_PER_CHUNK = KEY_VALUE_HEADS // CHUNKS
 CHUNK_COLS = HEADS_PER_CHUNK * HEAD_WIDTH
@@ -69,8 +70,15 @@
 
 def stack(chunk, *refs):
     *block_refs, stack_ref = refs
-    for place, ref in enumerate(block_refs):
-        stack_ref[place] = ref[:, 2 * chunk * CHUNK_COLS : 2 * (chunk + 1) * CHUNK_COLS]
+    place = 0
+    for ref in block_refs:
+        if len(ref.shape) == 2:
+            stack_ref[place] = ref[:, 2 * chunk * CHUNK_COLS : 2 * (chunk + 1) * CHUNK_COLS]
+            place += 1
+        else:
+            for i in range(ref.shape[0]):
+                stack_ref[place + i] = ref[i]
+            place += ref.shape[0]
 
 
 def prepare_queries(rows, pos_ref, query_ref, grad_ref, *out_refs):
@@ -106,11 +114,13 @@
     return jnp.dot(left, right, preferred_element_type=jnp.float32)
 
 
-def attend(seq_count, head_count, rows, pieces, has_alias, counts_ref, *refs):
+def attend(seq_count, head_count, rows, pieces, order, has_alias, counts_ref, *refs):
     blocks = seq_count * head_count
-    kv_refs = []
+    kv_refs = [None] * blocks
+    places = iter(order)
     for ref in refs[:pieces]:
-        kv_refs += [ref] if len(ref.shape) == 2 else [ref.at[i] for i in range(ref.shape[0])]
+        for block in [ref] if len(ref.shape) == 2 else [ref.at[i] for i in range(ref.shape[0])]:
+            kv_refs[next(places)] = block
     q_ref, qt_ref, g_ref, gt_ref, cos_ref, sin_ref = refs[pieces : pieces + 6]
     outs = refs[pieces + 6 + 2 * has_alias :]
     out_ref, grad_ref = outs[:2]
@@ -152,10 +162,10 @@
     heads = range(STEP_HEADS)
     keys, values = [gathered(0, p) for p in heads], [gathered(HEADS_PER_CHUNK, p) for p in heads]
     bias, live = bias_ref[...], live_ref[0:1, :]
-    scores = [dot(keys[p][0], qt_ref[p]) * SCORE_SCALE + bias for p in heads]
+    scores = [dot(keys[p][0], qt_ref[p]) * SCORE_TO_LOG2 + bias for p in heads]
     dprobs, probs, probs_low = [], [], []
     for p in heads:
-        weights = jnp.exp(scores[p] - jnp.max(scores[p], 0, keepdims=True))
+        weights = jnp.exp2(scores[p] - jnp.max(scores[p], 0, keepdims=True))
         probs.append(weights * (live / jnp.sum(weights, 0, keepdims=True)))
         probs_low.append(probs[p].astype(jnp.bfloat16))
         dprobs.append(dot(values[p][0], gt_ref[p]))
@@ -300,29 +310,45 @@
 
     bits = [1 << b for b in reversed(range((head_count - 1).bit_length()))]
     later = range(1, seq_count)
-    last = head_count - 1
-    near = {0: own, **{j: along_head(own, j, True) for j in sorted({bits[0], 1}, reverse=True)}}
+    whole = {0: own, **{j: along_head(own, j, True) for j in sorted({bits[0], 1})}}
     far = {a: along_seq(own, a, True) for a in later}
-    near, cosine_t, far = lax.optimization_barrier((near, cosine_t, far))
-    for bit in bits[1:]:
-        near.update(
-            {j ^ bit: along_head(x, bit, True, j) for j, x in near.items() if j ^ bit not in near}
-        )
-
-    def cross(chunk, offsets):
-        held = pl.pallas_call(
+    whole, cosine_t, far = lax.optimization_barrier((whole, cosine_t, far))
+
+    def stacked_blocks(chunk, xs):
+        if len(xs) == 1 and len(xs[0].shape) == 3:
+            return xs[0]
+        count = sum(1 if len(x.shape) == 2 else x.shape[0] for x in xs)
+        return pl.pallas_call(
             functools.partial(stack, chunk),
-            out_shape=shape((len(offsets), padded, 2 * CHUNK_COLS), bf16),
-            in_specs=[VMEM] * len(offsets),
+            out_shape=shape((count, padded, 2 * CHUNK_COLS), bf16),
+            in_specs=[VMEM] * len(xs),
             out_specs=VMEM,
             compiler_params=params(8),
             name="stack",
-        )(*(near[j] for j in offsets))
+        )(*xs)
+
+    def cross(chunk, xs):
+        held = stacked_blocks(chunk, xs)
         return {a: along_seq(held, a, True) for a in later}
 
-    crossed = [[cross(0, range(1, last)), cross(0, [last])]]
-    near[last], crossed[0][0] = lax.optimization_barrier((near[last], crossed[0][0]))
-    crossed += [[cross(chunk, range(1, head_count))] for chunk in range(1, CHUNKS)]
+    near, crossed = [], []
+    for chunk in range(CHUNKS):
+        blocks_here = dict(whole)
+        for bit in bits[1:]:
+            for j, x in list(blocks_here.items()):
+                if j ^ bit not in blocks_here:
+                    held = stacked_blocks(chunk, [x])
+                    blocks_here[j ^ bit] = along_head(held, bit, True, j)
+        direct = [x for j, x in blocks_here.items() if j in whole and j]
+        derived = [x for j, x in blocks_here.items() if j not in whole]
+        if chunk == 0:
+            crossed.append([cross(chunk, direct), cross(chunk, derived)])
+        else:
+            derived, crossed[0][0] = lax.optimization_barrier((derived, crossed[0][0]))
+            crossed.append([cross(chunk, direct + derived)])
+        near.append([*whole.values(), *derived])
+    offsets = list(blocks_here)
+    order = [a * head_count + j for a in range(seq_count) for j in offsets]
 
     wide_outs = ()
     parts = []
@@ -334,7 +360,7 @@
             for x in (tall, flat)
         )
         row_part = pl.BlockSpec((padded, STEP_HEADS * wide), lambda g, f=first: (0, f + g))
-        gathered = [near[j] for j in range(head_count)]
+        gathered = list(near[chunk])
         for a in later:
             gathered += [far[a]] + [part[a] for part in crossed[chunk]]
         inputs = len(gathered)
@@ -345,7 +371,7 @@
         ]
         part_block = pl.BlockSpec((head_count, padded, 2 * CHUNK_COLS), lambda g: (0, 0, 0))
         out = pl.pallas_call(
-            functools.partial(attend, seq_count, head_count, rows, inputs, has_alias),
+            functools.partial(attend, seq_count, head_count, rows, inputs, order, has_alias),
             grid=(HEADS_PER_CHUNK // STEP_HEADS,),
             out_shape=[shape((padded, QUERY_HEADS * HEAD_WIDTH), bf16)] * 2
             + [shape((head_count, padded, 2 * CHUNK_COLS), bf16)] * seq_count,

time: 93.8 us -> 94.6 us (level)
  starting transfers between devices: 43.5 us -> 45.9 us
  waiting for transfers between devices: 22.7 us -> 21.5 us
    ppermute x9 -> x10, starting transfers between devices: 32.7 us -> 35.9 us  [along_head(): return lax.ppermute(x, ('seq', 'head'), pairs)]
    ppermute x9 -> x10, waiting for transfers between devices: 15.2 us -> 13.5 us  [along_head(): return lax.ppermute(x, ('seq', 'head'), pairs)]
  transfers between devices with their start and end apart: 15 -> 16, of which waited for: 5 -> 6; matrix products, arithmetic and copies ran while one was open for 0% -> 0% of each run, Pallas kernels for 21% -> 21%
where the time goes in v9:
time: 94.6 us; the launch traced here: 94 us
  starting transfers between devices  45.9 us (49%)
  Pallas kernels  22.4 us (24%)
  waiting for transfers between devices  21.5 us (23%)
  local copies, waits for them, and re-layouts  3.23 us (3%)
    ppermute x10, starting transfers between devices, along_head(): return lax.ppermute(x, ('seq', 'head'), pairs)  35.9 us
    pallas_call x2, Pallas kernels, shards(): pl.pallas_call(functools.partial(attend, seq_count, head_count, rows, inp...  15.6 us
    ppermute x10, waiting for transfers between devices, along_head(): return lax.ppermute(x, ('seq', 'head'), pairs)  13.5 us
    ppermute x6, starting transfers between devices, along_seq(): return lax.ppermute(x, ('seq', 'head'), pairs)  10.1 us
    ppermute x6, waiting for transfers between devices, along_seq(): return lax.ppermute(x, ('seq', 'head'), pairs)  7.98 us
    pallas_call x1, Pallas kernels, shards(): pl.pallas_call(functools.partial(prepare_queries, rows), grid=(KEY_VALUE_...  3.65 us
    unnamed x10, local copies, waits for them, and re-layouts  3.23 us
    pallas_call x1, Pallas kernels, shards(): pl.pallas_call(functools.partial(prepare_keys, rows), out_shape=shape((pa...  1.96 us
  transfers between devices with their start and end apart: 16, of which 6 were waited for; matrix products, arithmetic and copies ran while one was open for 0% of the time, Pallas kernels for 21%

profile of v9, /device:TPU:0, one launch (start us, length us, event | category | flops | bytes accessed | tf_op | source)
XLA Modules:
  0.0 94.0 jit_solution(7713469592449854540)
XLA Ops:
  0.6 2.0 %prepare_keys.1.refs_0_ = bf16[72,2048]{1,0:T(8,128)(2,1)} custom-call(s32[576]{0:T(1024)} %pos_ref.3, bf16[72,1024]{1,0:T(8,128)(2,1)} %key_ref.1, bf16[72,1024]{1,0:T(8,128)(2,1)} %value_ref.1), custom_call_target="tpu_custom_call" | custom-call | tf_op jit(solution)/shard_map/prepare_keys/pallas_call | solution.py:282
  2.6 4.9 %collective-permute-start = (bf16[72,2048]{1,0:T(8,128)(2,1)}, bf16[72,2048]{1,0:T(8,128)(2,1)S(1)}, u32[]{:S(2)}, u32[]{:S(2)}) collective-permute-start(bf16[72,2048]{1,0:T(8,128)(2,1)} %prepare_keys.1.refs_0_), channel_id=1, source_target_pairs={{0,4},{4,0},{8,12},{12,8},{16,20},{24,28},{1,5},{5,1},{9,13},{13,9... | collective-permute-start | bytes 884744 | tf_op jit(solution)/shard_map/ppermute | solution.py:269
  7.5 4.5 %collective-permute-start.1 = (bf16[72,2048]{1,0:T(8,128)(2,1)}, bf16[72,2048]{1,0:T(8,128)(2,1)S(1)}, u32[]{:S(2)}, u32[]{:S(2)}) collective-permute-start(bf16[72,2048]{1,0:T(8,128)(2,1)} %prepare_keys.1.refs_0_), channel_id=1, source_target_pairs={{0,8},{4,12},{8,0},{12,4},{16,24},{20,28},{1,9},{5,13},{9,1},{13,5... | collective-permute-start | bytes 884744 | tf_op jit(solution)/shard_map/ppermute | solution.py:269
  12.0 3.5 %collective-permute-start.2 = (bf16[72,2048]{1,0:T(8,128)(2,1)}, bf16[72,2048]{1,0:T(8,128)(2,1)S(1)}, u32[]{:S(2)}, u32[]{:S(2)}) collective-permute-start(bf16[72,2048]{1,0:T(8,128)(2,1)} %prepare_keys.1.refs_0_), channel_id=1, source_target_pairs={{0,16},{4,20},{8,24},{12,28},{1,17},{5,21},{9,25},{13,29},{2,18},{... | collective-permute-start | bytes 884744 | tf_op jit(solution)/shard_map/ppermute | solution.py:277
  15.5 0.7 copy-done.1
  16.2 1.3 %copy-done.2 = bf16[72,8192]{1,0:T(8,128)(2,1)S(1)} copy-done((bf16[72,8192]{1,0:T(8,128)(2,1)S(1)}, bf16[72,8192]{1,0:T(8,128)(2,1)}, u32[]{:S(2)}) %copy-start.2) | copy-done | bytes 1179672
  17.5 1.3 %copy-done.3 = bf16[72,8192]{1,0:T(8,128)(2,1)S(1)} copy-done((bf16[72,8192]{1,0:T(8,128)(2,1)S(1)}, bf16[72,8192]{1,0:T(8,128)(2,1)}, u32[]{:S(2)}) %copy-start.3) | copy-done | bytes 1179672
  18.7 3.7 %prepare_queries.1 = (bf16[8,576,128]{2,1,0:T(8,128)(2,1)S(1)}, bf16[8,128,576]{2,1,0:T(8,128)(2,1)S(1)}, bf16[8,576,128]{2,1,0:T(8,128)(2,1)S(1)}, bf16[8,128,5...) custom-call(s32[576]{0:T(1024)S(1)} %copy-done.1, ...), custom_call_target="tpu_custom_call" | custom-call | flops 8071000064 | bytes 25830000 | tf_op jit(solution)/shard_map/prepare_queries/pallas_call | solution.py:299
  22.4 3.0 %collective-permute-done.1.refs_0_.refs_1_.refs_2_ = bf16[72,2048]{1,0:T(8,128)(2,1)S(1)} collective-permute-done((bf16[72,2048]{1,0:T(8,128)(2,1)}, bf16[72,2048]{1,0:T(8,128)(2,1)S(1)}, u32[]{:S(2)}, u32[]{:S(2)}) %collective-permute-start.1) | collective-permute-done | bytes 294944 | tf_op jit(solution)/shard_map/ppermute | solution.py:269
  25.4 1.4 %collective-permute-start.4 = (bf16[2,72,1024]{2,1,0:T(8,128)(2,1)S(1)}, bf16[2,72,1024]{2,1,0:T(8,128)(2,1)S(1)}, u32[]{:S(2)}, u32[]{:S(2)}) collective-permute-start(bf16[2,72,1024]{2,1,0:T(8,128)(2,1)S(1)} %stack.5), channel_id=1, source_target_pairs={{0,16},{4,20},{8,24},{12,28},{1,17},{5,21},{9,25},{13,29},{2,18},{... | collective-permute-start | bytes 884744 | tf_op jit(solution)/shard_map/ppermute | solution.py:277
  26.9 3.0 %collective-permute-start.6 = (bf16[1,72,1024]{2,1,0:T(8,128)(2,1)S(1)}, bf16[1,72,1024]{2,1,0:T(8,128)(2,1)S(1)}, u32[]{:S(2)}, u32[]{:S(2)}) collective-permute-start(bf16[1,72,1024]{2,1,0:T(8,128)(2,1)S(1)} %stack.7), channel_id=1, source_target_pairs={{0,4},{4,0},{8,12},{12,8},{24,28},{28,24},{1,5},{5,1},{9,13},{13,9... | collective-permute-start | bytes 442376 | tf_op jit(solution)/shard_map/ppermute | solution.py:269
  29.9 2.8 %collective-permute-start.3 = (bf16[1,72,1024]{2,1,0:T(8,128)(2,1)S(1)}, bf16[1,72,1024]{2,1,0:T(8,128)(2,1)S(1)}, u32[]{:S(2)}, u32[]{:S(2)}) collective-permute-start(bf16[1,72,1024]{2,1,0:T(8,128)(2,1)S(1)} %stack.4), channel_id=1, source_target_pairs={{0,4},{4,0},{8,12},{12,8},{24,28},{28,24},{1,5},{5,1},{9,13},{13,9... | collective-permute-start | bytes 442376 | tf_op jit(solution)/shard_map/ppermute | solution.py:269
  32.8 2.3 %collective-permute-done.6.refs_3_ = bf16[1,72,1024]{2,1,0:T(8,128)(2,1)S(1)} collective-permute-done((bf16[1,72,1024]{2,1,0:T(8,128)(2,1)S(1)}, bf16[1,72,1024]{2,1,0:T(8,128)(2,1)S(1)}, u32[]{:S(2)}, u32[]{:S(2)}) %collective-permute-start.6) | collective-permute-done | bytes 147488 | tf_op jit(solution)/shard_map/ppermute | solution.py:269
  35.0 1.3 %collective-permute-start.7 = (bf16[1,72,1024]{2,1,0:T(8,128)(2,1)S(1)}, bf16[1,72,1024]{2,1,0:T(8,128)(2,1)S(1)}, u32[]{:S(2)}, u32[]{:S(2)}) collective-permute-start(bf16[1,72,1024]{2,1,0:T(8,128)(2,1)S(1)} %collective-permute-done.6.refs_3_), channel_id=1, source_target_pairs={{0,16},{4,20},{8,24},{12,28},{1,17},{5,21},{9,25},{13,29},{2,18},{... | collective-permute-start | bytes 442376 | tf_op jit(solution)/shard_map/ppermute | solution.py:277
  36.3 0.7 collective-permute-done.3.refs_2_.refs_3_
  37.1 1.3 %collective-permute-start.5 = (bf16[3,72,1024]{2,1,0:T(8,128)(2,1)S(1)}, bf16[3,72,1024]{2,1,0:T(8,128)(2,1)S(1)}, u32[]{:S(2)}, u32[]{:S(2)}) collective-permute-start(bf16[3,72,1024]{2,1,0:T(8,128)(2,1)S(1)} %stack.6), channel_id=1, source_target_pairs={{0,16},{4,20},{8,24},{12,28},{1,17},{5,21},{9,25},{13,29},{2,18},{... | collective-permute-start | bytes 1327112 | tf_op jit(solution)/shard_map/ppermute | solution.py:277
  38.4 2.1 %collective-permute-done.7.refs_6_ = bf16[1,72,1024]{2,1,0:T(8,128)(2,1)S(1)} collective-permute-done((bf16[1,72,1024]{2,1,0:T(8,128)(2,1)S(1)}, bf16[1,72,1024]{2,1,0:T(8,128)(2,1)S(1)}, u32[]{:S(2)}, u32[]{:S(2)}) %collective-permute-start.7) | collective-permute-done | bytes 147488 | tf_op jit(solution)/shard_map/ppermute | solution.py:277
  40.6 7.8 %attend.2 = (bf16[72,8192]{1,0:T(8,128)(2,1)}, bf16[72,8192]{1,0:T(8,128)(2,1)}, bf16[4,72,1024]{2,1,0:T(8,128)(2,1)S(1)}, bf16[4,72,1024]{2,1,0:T(8,128)(2,1)S(1)}) custom-call(s32[2]{0:T(128)S(1)} %copy-done.4, bf16[72,2048]{1,0:T(8,128)(2,1)S(1)} %copy-done, bf16[72,2048]{1,0:T(8,128)(2,1)S(1)} %collective-permute-done.refs_0_.refs_1_, ...), custom_call_target="tpu_custom_call" | custom-call | flops 11530000384 | bytes 36900000 | tf_op jit(solution)/shard_map/attend/pallas_call | solution.py:373
  48.3 1.3 %collective-permute-start.9 = (bf16[4,72,1024]{2,1,0:T(8,128)(2,1)S(1)}, bf16[4,72,1024]{2,1,0:T(8,128)(2,1)S(1)}, u32[]{:S(2)}, u32[]{:S(2)}) collective-permute-start(bf16[4,72,1024]{2,1,0:T(8,128)(2,1)S(1)} %get-tuple-element.60), channel_id=1, source_target_pairs={{16,0},{20,4},{24,8},{28,12},{17,1},{21,5},{25,9},{29,13},{18,2},{... | collective-permute-start | bytes 1769480 | tf_op jit(solution)/shard_map/ppermute | solution.py:277
  49.6 7.8 %attend.3 = (bf16[72,8192]{1,0:T(8,128)(2,1)}, bf16[72,8192]{1,0:T(8,128)(2,1)}, bf16[4,72,1024]{2,1,0:T(8,128)(2,1)S(1)}, bf16[4,72,1024]{2,1,0:T(8,128)(2,1)S(1)}) custom-call(s32[2]{0:T(128)S(1)} %copy-done.4, bf16[72,2048]{1,0:T(8,128)(2,1)S(1)} %copy-done, ...), custom_call_target="tpu_custom_call", output_to_operand_aliasing={{0}: (13, {}), {1}: (14, {})} | custom-call | flops 11530000384 | bytes 36900000 | tf_op jit(solution)/shard_map/attend/pallas_call | solution.py:373
  57.5 1.3 %collective-permute-start.8 = (bf16[4,72,1024]{2,1,0:T(8,128)(2,1)S(1)}, bf16[4,72,1024]{2,1,0:T(8,128)(2,1)S(1)}, u32[]{:S(2)}, u32[]{:S(2)}) collective-permute-start(bf16[4,72,1024]{2,1,0:T(8,128)(2,1)S(1)} %get-tuple-element.58), channel_id=1, source_target_pairs={{16,0},{20,4},{24,8},{28,12},{17,1},{21,5},{25,9},{29,13},{18,2},{... | collective-permute-start | bytes 1769480 | tf_op jit(solution)/shard_map/ppermute | solution.py:277
  58.7 5.9 %collective-permute-done.9.refs_1_ = bf16[4,72,1024]{2,1,0:T(8,128)(2,1)S(1)} collective-permute-done((bf16[4,72,1024]{2,1,0:T(8,128)(2,1)S(1)}, bf16[4,72,1024]{2,1,0:T(8,128)(2,1)S(1)}, u32[]{:S(2)}, u32[]{:S(2)}) %collective-permute-start.9) | collective-permute-done | bytes 589856 | tf_op jit(solution)/shard_map/ppermute | solution.py:277
  64.6 0.1 combine.2
  64.7 3.2 %collective-permute-start.10 = (bf16[72,1024]{1,0:T(8,128)(2,1)S(1)}, bf16[72,1024]{1,0:T(8,128)(2,1)S(1)}, u32[]{:S(2)}, u32[]{:S(2)}) collective-permute-start(bf16[72,1024]{1,0:T(8,128)(2,1)S(1)} %get-tuple-element.63), channel_id=1, source_target_pairs={{0,4},{4,0},{8,12},{12,8},{20,16},{28,24},{1,5},{5,1},{9,13},{13,9... | collective-permute-start | bytes 442376 | tf_op jit(solution)/shard_map/ppermute | solution.py:269
  68.0 5.3 %collective-permute-start.11 = (bf16[72,1024]{1,0:T(8,128)(2,1)S(1)}, bf16[72,1024]{1,0:T(8,128)(2,1)S(1)}, u32[]{:S(2)}, u32[]{:S(2)}) collective-permute-start(bf16[72,1024]{1,0:T(8,128)(2,1)S(1)} %get-tuple-element.64), channel_id=1, source_target_pairs={{0,8},{4,12},{8,0},{12,4},{24,16},{28,20},{1,9},{5,13},{9,1},{13,5... | collective-permute-start | bytes 442376 | tf_op jit(solution)/shard_map/ppermute | solution.py:269
  73.3 1.9 %collective-permute-start.12 = (bf16[72,1024]{1,0:T(8,128)(2,1)S(1)}, bf16[72,1024]{1,0:T(8,128)(2,1)S(1)}, u32[]{:S(2)}, u32[]{:S(2)}) collective-permute-start(bf16[72,1024]{1,0:T(8,128)(2,1)S(1)} %get-tuple-element.65), channel_id=1, source_target_pairs={{0,12},{4,8},{8,4},{12,0},{24,20},{28,16},{1,13},{5,9},{9,5},{13,1... | collective-permute-start | bytes 442376 | tf_op jit(solution)/shard_map/ppermute | solution.py:269
  75.3 0.1 combine.3
  75.4 2.6 %collective-permute-start.13 = (bf16[72,1024]{1,0:T(8,128)(2,1)S(1)}, bf16[72,1024]{1,0:T(8,128)(2,1)S(1)}, u32[]{:S(2)}, u32[]{:S(2)}) collective-permute-start(bf16[72,1024]{1,0:T(8,128)(2,1)S(1)} %get-tuple-element.69), channel_id=1, source_target_pairs={{0,4},{4,0},{8,12},{12,8},{20,16},{28,24},{1,5},{5,1},{9,13},{13,9... | collective-permute-start | bytes 442376 | tf_op jit(solution)/shard_map/ppermute | solution.py:269
  78.0 5.6 %collective-permute-start.14 = (bf16[72,1024]{1,0:T(8,128)(2,1)S(1)}, bf16[72,1024]{1,0:T(8,128)(2,1)S(1)}, u32[]{:S(2)}, u32[]{:S(2)}) collective-permute-start(bf16[72,1024]{1,0:T(8,128)(2,1)S(1)} %get-tuple-element.70), channel_id=1, source_target_pairs={{0,8},{4,12},{8,0},{12,4},{24,16},{28,20},{1,9},{5,13},{9,1},{13,5... | collective-permute-start | bytes 442376 | tf_op jit(solution)/shard_map/ppermute | solution.py:269
  83.6 1.9 %collective-permute-start.15 = (bf16[72,1024]{1,0:T(8,128)(2,1)S(1)}, bf16[72,1024]{1,0:T(8,128)(2,1)S(1)}, u32[]{:S(2)}, u32[]{:S(2)}) collective-permute-start(bf16[72,1024]{1,0:T(8,128)(2,1)S(1)} %get-tuple-element.71), channel_id=1, source_target_pairs={{0,12},{4,8},{8,4},{12,0},{24,20},{28,16},{1,13},{5,9},{9,5},{13,1... | collective-permute-start | bytes 442376 | tf_op jit(solution)/shard_map/ppermute | solution.py:269
  85.6 7.5 %collective-permute-done.14.refs_8_ = bf16[72,1024]{1,0:T(8,128)(2,1)S(1)} collective-permute-done((bf16[72,1024]{1,0:T(8,128)(2,1)S(1)}, bf16[72,1024]{1,0:T(8,128)(2,1)S(1)}, u32[]{:S(2)}, u32[]{:S(2)}) %collective-permute-start.14) | collective-permute-done | bytes 147488 | tf_op jit(solution)/shard_map/ppermute | solution.py:269
  93.1 0.9 finish.1
  (21 shorter events, 0.1 us)
Async XLA Ops:
  2.6 19.8 %collective-permute-start = (bf16[72,2048]{1,0:T(8,128)(2,1)}, bf16[72,2048]{1,0:T(8,128)(2,1)S(1)}, u32[]{:S(2)}, u32[]{:S(2)}) collective-permute-start(bf16[72,2048]{1,0:T(8,128)(2,1)} %prepare_keys.1.refs_0_), channel_id=1, source_target_pairs={{0,4},{4,0},{8,12},{12,8},{16,20},{24,28},{1,5},{5,1},{9,13},{13,9... | collective-permute-start | bytes 884744 | tf_op jit(solution)/shard_map/ppermute | solution.py:269
  7.5 17.8 %collective-permute-start.1 = (bf16[72,2048]{1,0:T(8,128)(2,1)}, bf16[72,2048]{1,0:T(8,128)(2,1)S(1)}, u32[]{:S(2)}, u32[]{:S(2)}) collective-permute-start(bf16[72,2048]{1,0:T(8,128)(2,1)} %prepare_keys.1.refs_0_), channel_id=1, source_target_pairs={{0,8},{4,12},{8,0},{12,4},{16,24},{20,28},{1,9},{5,13},{9,1},{13,5... | collective-permute-start | bytes 884744 | tf_op jit(solution)/shard_map/ppermute | solution.py:269
  12.0 13.3 %collective-permute-start.2 = (bf16[72,2048]{1,0:T(8,128)(2,1)}, bf16[72,2048]{1,0:T(8,128)(2,1)S(1)}, u32[]{:S(2)}, u32[]{:S(2)}) collective-permute-start(bf16[72,2048]{1,0:T(8,128)(2,1)} %prepare_keys.1.refs_0_), channel_id=1, source_target_pairs={{0,16},{4,20},{8,24},{12,28},{1,17},{5,21},{9,25},{13,29},{2,18},{... | collective-permute-start | bytes 884744 | tf_op jit(solution)/shard_map/ppermute | solution.py:277
  15.5 0.7 copy-start.1
  16.2 1.3 %copy-start.2 = (bf16[72,8192]{1,0:T(8,128)(2,1)S(1)}, bf16[72,8192]{1,0:T(8,128)(2,1)}, u32[]{:S(2)}) copy-start(bf16[72,8192]{1,0:T(8,128)(2,1)} %query_ref.1) | copy-start | bytes 3538948
  17.5 1.3 %copy-start.3 = (bf16[72,8192]{1,0:T(8,128)(2,1)S(1)}, bf16[72,8192]{1,0:T(8,128)(2,1)}, u32[]{:S(2)}) copy-start(bf16[72,8192]{1,0:T(8,128)(2,1)} %grad_ref.1) | copy-start | bytes 3538948
  25.4 15.2 %copy-start = (bf16[72,2048]{1,0:T(8,128)(2,1)S(1)}, bf16[72,2048]{1,0:T(8,128)(2,1)}, u32[]{:S(2)}) copy-start(bf16[72,2048]{1,0:T(8,128)(2,1)} %prepare_keys.1.refs_0_) | copy-start | bytes 884740
  25.4 15.2 %copy-start.4 = (s32[2]{0:T(128)S(1)}, s32[2]{0:T(128)}, u32[]{:S(2)}) copy-start(s32[2]{0:T(128)} %counts_ref.3) | copy-start | bytes 28
  25.4 11.7 %collective-permute-start.4 = (bf16[2,72,1024]{2,1,0:T(8,128)(2,1)S(1)}, bf16[2,72,1024]{2,1,0:T(8,128)(2,1)S(1)}, u32[]{:S(2)}, u32[]{:S(2)}) collective-permute-start(bf16[2,72,1024]{2,1,0:T(8,128)(2,1)S(1)} %stack.5), channel_id=1, source_target_pairs={{0,16},{4,20},{8,24},{12,28},{1,17},{5,21},{9,25},{13,29},{2,18},{... | collective-permute-start | bytes 884744 | tf_op jit(solution)/shard_map/ppermute | solution.py:277
  26.9 8.2 %collective-permute-start.6 = (bf16[1,72,1024]{2,1,0:T(8,128)(2,1)S(1)}, bf16[1,72,1024]{2,1,0:T(8,128)(2,1)S(1)}, u32[]{:S(2)}, u32[]{:S(2)}) collective-permute-start(bf16[1,72,1024]{2,1,0:T(8,128)(2,1)S(1)} %stack.7), channel_id=1, source_target_pairs={{0,4},{4,0},{8,12},{12,8},{24,28},{28,24},{1,5},{5,1},{9,13},{13,9... | collective-permute-start | bytes 442376 | tf_op jit(solution)/shard_map/ppermute | solution.py:269
  29.9 7.2 %collective-permute-start.3 = (bf16[1,72,1024]{2,1,0:T(8,128)(2,1)S(1)}, bf16[1,72,1024]{2,1,0:T(8,128)(2,1)S(1)}, u32[]{:S(2)}, u32[]{:S(2)}) collective-permute-start(bf16[1,72,1024]{2,1,0:T(8,128)(2,1)S(1)} %stack.4), channel_id=1, source_target_pairs={{0,4},{4,0},{8,12},{12,8},{24,28},{28,24},{1,5},{5,1},{9,13},{13,9... | collective-permute-start | bytes 442376 | tf_op jit(solution)/shard_map/ppermute | solution.py:269
  35.0 5.5 %collective-permute-start.7 = (bf16[1,72,1024]{2,1,0:T(8,128)(2,1)S(1)}, bf16[1,72,1024]{2,1,0:T(8,128)(2,1)S(1)}, u32[]{:S(2)}, u32[]{:S(2)}) collective-permute-start(bf16[1,72,1024]{2,1,0:T(8,128)(2,1)S(1)} %collective-permute-done.6.refs_3_), channel_id=1, source_target_pairs={{0,16},{4,20},{8,24},{12,28},{1,17},{5,21},{9,25},{13,29},{2,18},{... | collective-permute-start | bytes 442376 | tf_op jit(solution)/shard_map/ppermute | solution.py:277
  37.1 12.5 %collective-permute-start.5 = (bf16[3,72,1024]{2,1,0:T(8,128)(2,1)S(1)}, bf16[3,72,1024]{2,1,0:T(8,128)(2,1)S(1)}, u32[]{:S(2)}, u32[]{:S(2)}) collective-permute-start(bf16[3,72,1024]{2,1,0:T(8,128)(2,1)S(1)} %stack.6), channel_id=1, source_target_pairs={{0,16},{4,20},{8,24},{12,28},{1,17},{5,21},{9,25},{13,29},{2,18},{... | collective-permute-start | bytes 1327112 | tf_op jit(solution)/shard_map/ppermute | solution.py:277
  48.3 16.3 %collective-permute-start.9 = (bf16[4,72,1024]{2,1,0:T(8,128)(2,1)S(1)}, bf16[4,72,1024]{2,1,0:T(8,128)(2,1)S(1)}, u32[]{:S(2)}, u32[]{:S(2)}) collective-permute-start(bf16[4,72,1024]{2,1,0:T(8,128)(2,1)S(1)} %get-tuple-element.60), channel_id=1, source_target_pairs={{16,0},{20,4},{24,8},{28,12},{17,1},{21,5},{25,9},{29,13},{18,2},{... | collective-permute-start | bytes 1769480 | tf_op jit(solution)/shard_map/ppermute | solution.py:277
  57.5 17.8 %collective-permute-start.8 = (bf16[4,72,1024]{2,1,0:T(8,128)(2,1)S(1)}, bf16[4,72,1024]{2,1,0:T(8,128)(2,1)S(1)}, u32[]{:S(2)}, u32[]{:S(2)}) collective-permute-start(bf16[4,72,1024]{2,1,0:T(8,128)(2,1)S(1)} %get-tuple-element.58), channel_id=1, source_target_pairs={{16,0},{20,4},{24,8},{28,12},{17,1},{21,5},{25,9},{29,13},{18,2},{... | collective-permute-start | bytes 1769480 | tf_op jit(solution)/shard_map/ppermute | solution.py:277
  64.7 18.9 %collective-permute-start.10 = (bf16[72,1024]{1,0:T(8,128)(2,1)S(1)}, bf16[72,1024]{1,0:T(8,128)(2,1)S(1)}, u32[]{:S(2)}, u32[]{:S(2)}) collective-permute-start(bf16[72,1024]{1,0:T(8,128)(2,1)S(1)} %get-tuple-element.63), channel_id=1, source_target_pairs={{0,4},{4,0},{8,12},{12,8},{20,16},{28,24},{1,5},{5,1},{9,13},{13,9... | collective-permute-start | bytes 442376 | tf_op jit(solution)/shard_map/ppermute | solution.py:269
  68.0 17.6 %collective-permute-start.11 = (bf16[72,1024]{1,0:T(8,128)(2,1)S(1)}, bf16[72,1024]{1,0:T(8,128)(2,1)S(1)}, u32[]{:S(2)}, u32[]{:S(2)}) collective-permute-start(bf16[72,1024]{1,0:T(8,128)(2,1)S(1)} %get-tuple-element.64), channel_id=1, source_target_pairs={{0,8},{4,12},{8,0},{12,4},{24,16},{28,20},{1,9},{5,13},{9,1},{13,5... | collective-permute-start | bytes 442376 | tf_op jit(solution)/shard_map/ppermute | solution.py:269
  73.3 12.2 %collective-permute-start.12 = (bf16[72,1024]{1,0:T(8,128)(2,1)S(1)}, bf16[72,1024]{1,0:T(8,128)(2,1)S(1)}, u32[]{:S(2)}, u32[]{:S(2)}) collective-permute-start(bf16[72,1024]{1,0:T(8,128)(2,1)S(1)} %get-tuple-element.65), channel_id=1, source_target_pairs={{0,12},{4,8},{8,4},{12,0},{24,20},{28,16},{1,13},{5,9},{9,5},{13,1... | collective-permute-start | bytes 442376 | tf_op jit(solution)/shard_map/ppermute | solution.py:269
  75.4 10.2 %collective-permute-start.13 = (bf16[72,1024]{1,0:T(8,128)(2,1)S(1)}, bf16[72,1024]{1,0:T(8,128)(2,1)S(1)}, u32[]{:S(2)}, u32[]{:S(2)}) collective-permute-start(bf16[72,1024]{1,0:T(8,128)(2,1)S(1)} %get-tuple-element.69), channel_id=1, source_target_pairs={{0,4},{4,0},{8,12},{12,8},{20,16},{28,24},{1,5},{5,1},{9,13},{13,9... | collective-permute-start | bytes 442376 | tf_op jit(solution)/shard_map/ppermute | solution.py:269
  78.0 15.1 %collective-permute-start.14 = (bf16[72,1024]{1,0:T(8,128)(2,1)S(1)}, bf16[72,1024]{1,0:T(8,128)(2,1)S(1)}, u32[]{:S(2)}, u32[]{:S(2)}) collective-permute-start(bf16[72,1024]{1,0:T(8,128)(2,1)S(1)} %get-tuple-element.70), channel_id=1, source_target_pairs={{0,8},{4,12},{8,0},{12,4},{24,16},{28,20},{1,9},{5,13},{9,1},{13,5... | collective-permute-start | bytes 442376 | tf_op jit(solution)/shard_map/ppermute | solution.py:269
  83.6 9.5 %collective-permute-start.15 = (bf16[72,1024]{1,0:T(8,128)(2,1)S(1)}, bf16[72,1024]{1,0:T(8,128)(2,1)S(1)}, u32[]{:S(2)}, u32[]{:S(2)}) collective-permute-start(bf16[72,1024]{1,0:T(8,128)(2,1)S(1)} %get-tuple-element.71), channel_id=1, source_target_pairs={{0,12},{4,8},{8,4},{12,0},{24,20},{28,16},{1,13},{5,9},{9,5},{13,1... | collective-permute-start | bytes 442376 | tf_op jit(solution)/shard_map/ppermute | solution.py:269

commit v10 on v7

--- a/solution.py
+++ b/solution.py
@@ -14,6 +14,7 @@
 GROUP = QUERY_HEADS // KEY_VALUE_HEADS
 ROPE_BASE = 500000.0
 SCORE_SCALE = 1.0 / float(np.sqrt(HEAD_WIDTH))
+SCORE_TO_LOG2 = SCORE_SCALE * 1.4426950408889634
 CHUNKS = 2
 HEADS_PER_CHUNK = KEY_VALUE_HEADS // CHUNKS
 CHUNK_COLS = HEADS_PER_CHUNK * HEAD_WIDTH
@@ -67,9 +68,9 @@
         kv_ref[:, head_cols(HEADS_PER_CHUNK + place)] = value_ref[:, head_cols(head)]
 
 
-def stack(chunk, *refs):
+def stack(chunks, *refs):
     *block_refs, stack_ref = refs
-    for place, ref in enumerate(block_refs):
+    for place, (chunk, ref) in enumerate(zip(chunks, block_refs)):
         stack_ref[place] = ref[:, 2 * chunk * CHUNK_COLS : 2 * (chunk + 1) * CHUNK_COLS]
 
 
@@ -106,13 +107,11 @@
     return jnp.dot(left, right, preferred_element_type=jnp.float32)
 
 
-def attend(seq_count, head_count, rows, pieces, has_alias, counts_ref, *refs):
+def attend(seq_count, head_count, rows, has_alias, counts_ref, *refs):
     blocks = seq_count * head_count
-    kv_refs = []
-    for ref in refs[:pieces]:
-        kv_refs += [ref] if len(ref.shape) == 2 else [ref.at[i] for i in range(ref.shape[0])]
-    q_ref, qt_ref, g_ref, gt_ref, cos_ref, sin_ref = refs[pieces : pieces + 6]
-    outs = refs[pieces + 6 + 2 * has_alias :]
+    kv_refs = [ref if len(ref.shape) == 2 else ref.at[0] for ref in refs[:blocks]]
+    q_ref, qt_ref, g_ref, gt_ref, cos_ref, sin_ref = refs[blocks : blocks + 6]
+    outs = refs[blocks + 6 + 2 * has_alias :]
     out_ref, grad_ref = outs[:2]
     part_refs = outs[2 : 2 + seq_count]
     bias_ref, live_ref = outs[2 + seq_count :]
@@ -152,10 +151,10 @@
     heads = range(STEP_HEADS)
     keys, values = [gathered(0, p) for p in heads], [gathered(HEADS_PER_CHUNK, p) for p in heads]
     bias, live = bias_ref[...], live_ref[0:1, :]
-    scores = [dot(keys[p][0], qt_ref[p]) * SCORE_SCALE + bias for p in heads]
+    scores = [dot(keys[p][0], qt_ref[p]) * SCORE_TO_LOG2 + bias for p in heads]
     dprobs, probs, probs_low = [], [], []
     for p in heads:
-        weights = jnp.exp(scores[p] - jnp.max(scores[p], 0, keepdims=True))
+        weights = jnp.exp2(scores[p] - jnp.max(scores[p], 0, keepdims=True))
         probs.append(weights * (live / jnp.sum(weights, 0, keepdims=True)))
         probs_low.append(probs[p].astype(jnp.bfloat16))
         dprobs.append(dot(values[p][0], gt_ref[p]))
@@ -300,29 +299,40 @@
 
     bits = [1 << b for b in reversed(range((head_count - 1).bit_length()))]
     later = range(1, seq_count)
-    last = head_count - 1
-    near = {0: own, **{j: along_head(own, j, True) for j in sorted({bits[0], 1}, reverse=True)}}
+    near = {0: own, **{j: along_head(own, j, True) for j in sorted({bits[0], 1})}}
     far = {a: along_seq(own, a, True) for a in later}
-    near, cosine_t, far = lax.optimization_barrier((near, cosine_t, far))
+    near[1], cosine_t, far = lax.optimization_barrier((near[1], cosine_t, far))
+
+    def cross(*pieces):
+        held = pl.pallas_call(
+            functools.partial(stack, [chunk for _, chunk in pieces]),
+            out_shape=shape((len(pieces), padded, 2 * CHUNK_COLS), bf16),
+            in_specs=[VMEM] * len(pieces),
+            out_specs=VMEM,
+            compiler_params=params(8),
+            name="stack",
+        )(*(near[j] for j, _ in pieces))
+        for a in later:
+            moved = along_seq(held, a, True)
+            crossed.update({(a, *piece): (moved, i) for i, piece in enumerate(pieces)})
+
+    crossed = {}
+    cross((1, 0))
+    if bits[0] > 1:
+        first = {a: crossed[a, 1, 0][0] for a in later}
+        near[bits[0]], first = lax.optimization_barrier((near[bits[0]], first))
+        crossed = {(a, 1, 0): (first[a], 0) for a in later}
     for bit in bits[1:]:
         near.update(
             {j ^ bit: along_head(x, bit, True, j) for j, x in near.items() if j ^ bit not in near}
         )
-
-    def cross(chunk, offsets):
-        held = pl.pallas_call(
-            functools.partial(stack, chunk),
-            out_shape=shape((len(offsets), padded, 2 * CHUNK_COLS), bf16),
-            in_specs=[VMEM] * len(offsets),
-            out_specs=VMEM,
-            compiler_params=params(8),
-            name="stack",
-        )(*(near[j] for j in offsets))
-        return {a: along_seq(held, a, True) for a in later}
-
-    crossed = [[cross(0, range(1, last)), cross(0, [last])]]
-    near[last], crossed[0][0] = lax.optimization_barrier((near[last], crossed[0][0]))
-    crossed += [[cross(chunk, range(1, head_count))] for chunk in range(1, CHUNKS)]
+    rest = range(2, head_count)
+    for j in rest[:1]:
+        cross((j, 0), *((1, chunk) for chunk in range(1, CHUNKS)))
+    for j in rest[1:]:
+        cross((j, 0))
+    for chunk in range(1, CHUNKS):
+        cross(*((j, chunk) for j in (rest or [1])))
 
     wide_outs = ()
     parts = []
@@ -334,18 +344,21 @@
             for x in (tall, flat)
         )
         row_part = pl.BlockSpec((padded, STEP_HEADS * wide), lambda g, f=first: (0, f + g))
-        gathered = [near[j] for j in range(head_count)]
+        gathered = [(near[j], None) for j in range(head_count)]
         for a in later:
-            gathered += [far[a]] + [part[a] for part in crossed[chunk]]
+            gathered.append((far[a], None))
+            gathered += [crossed[a, j, chunk] for j in range(1, head_count)]
         inputs = len(gathered)
         kv_whole = pl.BlockSpec((padded, 2 * CHUNK_COLS), lambda g, c=chunk: (0, c))
         kv_specs = [
-            kv_whole if len(x.shape) == 2 else pl.BlockSpec(x.shape, lambda g: (0, 0, 0))
-            for x in gathered
+            kv_whole
+            if place is None
+            else pl.BlockSpec((1, padded, 2 * CHUNK_COLS), lambda g, i=place: (i, 0, 0))
+            for _, place in gathered
         ]
         part_block = pl.BlockSpec((head_count, padded, 2 * CHUNK_COLS), lambda g: (0, 0, 0))
         out = pl.pallas_call(
-            functools.partial(attend, seq_count, head_count, rows, inputs, has_alias),
+            functools.partial(attend, seq_count, head_count, rows, has_alias),
             grid=(HEADS_PER_CHUNK // STEP_HEADS,),
             out_shape=[shape((padded, QUERY_HEADS * HEAD_WIDTH), bf16)] * 2
             + [shape((head_count, padded, 2 * CHUNK_COLS), bf16)] * seq_count,
@@ -362,7 +375,7 @@
             cost_estimate=cost(10),
             compiler_params=params(32),
             name="attend",
-        )(counts, *gathered, *stacked, cosine_t, sine_t, *wide_outs)
+        )(counts, *(x for x, _ in gathered), *stacked, cosine_t, sine_t, *wide_outs)
         wide_outs = out[:2]
         parts.append([out[2]] + [along_seq(out[2 + a], a, False) for a in later])
 

time: 93.8 us -> 95.8 us (1.021)
  waiting for transfers between devices: 22.7 us -> 25.7 us
    ppermute x6 -> x7, waiting for transfers between devices: 7.5 us -> 9.08 us  [along_seq(): return lax.ppermute(x, ('seq', 'head'), pairs)]
    ppermute x9, waiting for transfers between devices: 15.2 us -> 16.6 us  [along_head(): return lax.ppermute(x, ('seq', 'head'), pairs)]
    ppermute x9, starting transfers between devices: 32.7 us -> 31.6 us  [along_head(): return lax.ppermute(x, ('seq', 'head'), pairs)]
    ppermute x6 -> x7, starting transfers between devices: 10.9 us -> 11.4 us  [along_seq(): return lax.ppermute(x, ('seq', 'head'), pairs)]
    pallas_call x5 -> x6, Pallas kernels: 16.1 us -> 15.7 us  [the longest x2 15.6 us: shards(): pl.pallas_call(functools.partial(attend, seq_count, head_count, rows, has...]
  transfers between devices with their start and end apart: 15 -> 16, of which waited for: 5 -> 5; matrix products, arithmetic and copies ran while one was open for 0% -> 0% of each run, Pallas kernels for 21% -> 21%
where the time goes in v10:
time: 95.8 us; the launch traced here: 95.2 us
  starting transfers between devices  42.9 us (45%)
  waiting for transfers between devices  25.7 us (27%)
  Pallas kernels  22.5 us (23%)
  local copies, waits for them, and re-layouts  3.23 us (3%)
    ppermute x9, starting transfers between devices, along_head(): return lax.ppermute(x, ('seq', 'head'), pairs)  31.6 us
    ppermute x9, waiting for transfers between devices, along_head(): return lax.ppermute(x, ('seq', 'head'), pairs)  16.6 us
    pallas_call x2, Pallas kernels, shards(): pl.pallas_call(functools.partial(attend, seq_count, head_count, rows, has...  15.6 us
    ppermute x7, starting transfers between devices, along_seq(): return lax.ppermute(x, ('seq', 'head'), pairs)  11.4 us
    ppermute x7, waiting for transfers between devices, along_seq(): return lax.ppermute(x, ('seq', 'head'), pairs)  9.08 us
    pallas_call x1, Pallas kernels, shards(): pl.pallas_call(functools.partial(prepare_queries, rows), grid=(KEY_VALUE_...  3.65 us
    unnamed x10, local copies, waits for them, and re-layouts  3.23 us
    pallas_call x1, Pallas kernels, shards(): pl.pallas_call(functools.partial(prepare_keys, rows), out_shape=shape((pa...  1.96 us
  transfers between devices with their start and end apart: 16, of which 5 were waited for; matrix products, arithmetic and copies ran while one was open for 0% of the time, Pallas kernels for 21%

profile of v10, /device:TPU:0, one launch (start us, length us, event | category | flops | bytes accessed | tf_op | source)
XLA Modules:
  0.0 95.2 jit_solution(7394499205080689858)
XLA Ops:
  0.6 2.0 %prepare_keys.1.refs_0_ = bf16[72,2048]{1,0:T(8,128)(2,1)} custom-call(s32[576]{0:T(1024)} %pos_ref.3, bf16[72,1024]{1,0:T(8,128)(2,1)} %key_ref.1, bf16[72,1024]{1,0:T(8,128)(2,1)} %value_ref.1), custom_call_target="tpu_custom_call" | custom-call | tf_op jit(solution)/shard_map/prepare_keys/pallas_call | solution.py:271
  2.6 4.9 %collective-permute-start = (bf16[72,2048]{1,0:T(8,128)(2,1)}, bf16[72,2048]{1,0:T(8,128)(2,1)S(1)}, u32[]{:S(2)}, u32[]{:S(2)}) collective-permute-start(bf16[72,2048]{1,0:T(8,128)(2,1)} %prepare_keys.1.refs_0_), channel_id=1, source_target_pairs={{0,4},{4,0},{8,12},{12,8},{16,20},{24,28},{1,5},{5,1},{9,13},{13,9... | collective-permute-start | bytes 884744 | tf_op jit(solution)/shard_map/ppermute | solution.py:258
  7.5 3.5 %collective-permute-start.1 = (bf16[72,2048]{1,0:T(8,128)(2,1)}, bf16[72,2048]{1,0:T(8,128)(2,1)S(1)}, u32[]{:S(2)}, u32[]{:S(2)}) collective-permute-start(bf16[72,2048]{1,0:T(8,128)(2,1)} %prepare_keys.1.refs_0_), channel_id=1, source_target_pairs={{0,16},{4,20},{8,24},{12,28},{1,17},{5,21},{9,25},{13,29},{2,18},{... | collective-permute-start | bytes 884744 | tf_op jit(solution)/shard_map/ppermute | solution.py:266
  11.0 4.5 %collective-permute-start.2 = (bf16[72,2048]{1,0:T(8,128)(2,1)}, bf16[72,2048]{1,0:T(8,128)(2,1)S(1)}, u32[]{:S(2)}, u32[]{:S(2)}) collective-permute-start(bf16[72,2048]{1,0:T(8,128)(2,1)} %prepare_keys.1.refs_0_), channel_id=1, source_target_pairs={{0,8},{4,12},{8,0},{12,4},{16,24},{20,28},{1,9},{5,13},{9,1},{13,5... | collective-permute-start | bytes 884744 | tf_op jit(solution)/shard_map/ppermute | solution.py:258
  15.5 0.0 copy-start.1
  15.5 0.7 copy-done.1
  16.2 1.3 %copy-done.2 = bf16[72,8192]{1,0:T(8,128)(2,1)S(1)} copy-done((bf16[72,8192]{1,0:T(8,128)(2,1)S(1)}, bf16[72,8192]{1,0:T(8,128)(2,1)}, u32[]{:S(2)}) %copy-start.2) | copy-done | bytes 1179672
  17.4 1.3 %copy-done.3 = bf16[72,8192]{1,0:T(8,128)(2,1)S(1)} copy-done((bf16[72,8192]{1,0:T(8,128)(2,1)S(1)}, bf16[72,8192]{1,0:T(8,128)(2,1)}, u32[]{:S(2)}) %copy-start.3) | copy-done | bytes 1179672
  18.7 3.6 %prepare_queries.1 = (bf16[8,576,128]{2,1,0:T(8,128)(2,1)S(1)}, bf16[8,128,576]{2,1,0:T(8,128)(2,1)S(1)}, bf16[8,576,128]{2,1,0:T(8,128)(2,1)S(1)}, bf16[8,128,5...) custom-call(s32[576]{0:T(1024)S(1)} %copy-done.1, ...), custom_call_target="tpu_custom_call" | custom-call | flops 8071000064 | bytes 25830000 | tf_op jit(solution)/shard_map/prepare_queries/pallas_call | solution.py:288
  22.4 1.4 %collective-permute-start.3 = (bf16[1,72,1024]{2,1,0:T(8,128)(2,1)S(1)}, bf16[1,72,1024]{2,1,0:T(8,128)(2,1)S(1)}, u32[]{:S(2)}, u32[]{:S(2)}) collective-permute-start(bf16[1,72,1024]{2,1,0:T(8,128)(2,1)S(1)} %stack.4), channel_id=1, source_target_pairs={{0,16},{4,20},{8,24},{12,28},{1,17},{5,21},{9,25},{13,29},{2,18},{... | collective-permute-start | bytes 442376 | tf_op jit(solution)/shard_map/ppermute | solution.py:266
  23.9 4.6 %collective-permute-done.2.refs_0_.refs_2_ = bf16[72,2048]{1,0:T(8,128)(2,1)S(1)} collective-permute-done((bf16[72,2048]{1,0:T(8,128)(2,1)}, bf16[72,2048]{1,0:T(8,128)(2,1)S(1)}, u32[]{:S(2)}, u32[]{:S(2)}) %collective-permute-start.2) | collective-permute-done | bytes 294944 | tf_op jit(solution)/shard_map/ppermute | solution.py:258
  28.4 1.9 %collective-permute-start.4 = (bf16[72,2048]{1,0:T(8,128)(2,1)S(1)}, bf16[72,2048]{1,0:T(8,128)(2,1)S(1)}, u32[]{:S(2)}, u32[]{:S(2)}) collective-permute-start(bf16[72,2048]{1,0:T(8,128)(2,1)S(1)} %collective-permute-done.2.refs_0_.refs_2_), channel_id=1, source_target_pairs={{0,4},{4,0},{8,12},{12,8},{24,28},{28,24},{1,5},{5,1},{9,13},{13,9... | collective-permute-start | bytes 884744 | tf_op jit(solution)/shard_map/ppermute | solution.py:258
  30.4 1.3 %collective-permute-start.5 = (bf16[2,72,1024]{2,1,0:T(8,128)(2,1)S(1)}, bf16[2,72,1024]{2,1,0:T(8,128)(2,1)S(1)}, u32[]{:S(2)}, u32[]{:S(2)}) collective-permute-start(bf16[2,72,1024]{2,1,0:T(8,128)(2,1)S(1)} %stack.5), channel_id=1, source_target_pairs={{0,16},{4,20},{8,24},{12,28},{1,17},{5,21},{9,25},{13,29},{2,18},{... | collective-permute-start | bytes 884744 | tf_op jit(solution)/shard_map/ppermute | solution.py:266
  31.7 6.7 %collective-permute-done.4.refs_1_.refs_0_.refs_3_ = bf16[72,2048]{1,0:T(8,128)(2,1)S(1)} collective-permute-done((bf16[72,2048]{1,0:T(8,128)(2,1)S(1)}, bf16[72,2048]{1,0:T(8,128)(2,1)S(1)}, u32[]{:S(2)}, u32[]{:S(2)}) %collective-permute-start.4) | collective-permute-done | bytes 294944 | tf_op jit(solution)/shard_map/ppermute | solution.py:258
  38.5 1.3 %collective-permute-start.7 = (bf16[1,72,1024]{2,1,0:T(8,128)(2,1)S(1)}, bf16[1,72,1024]{2,1,0:T(8,128)(2,1)S(1)}, u32[]{:S(2)}, u32[]{:S(2)}) collective-permute-start(bf16[1,72,1024]{2,1,0:T(8,128)(2,1)S(1)} %stack.7), channel_id=1, source_target_pairs={{0,16},{4,20},{8,24},{12,28},{1,17},{5,21},{9,25},{13,29},{2,18},{... | collective-permute-start | bytes 442376 | tf_op jit(solution)/shard_map/ppermute | solution.py:266
  39.8 1.3 %collective-permute-start.6 = (bf16[2,72,1024]{2,1,0:T(8,128)(2,1)S(1)}, bf16[2,72,1024]{2,1,0:T(8,128)(2,1)S(1)}, u32[]{:S(2)}, u32[]{:S(2)}) collective-permute-start(bf16[2,72,1024]{2,1,0:T(8,128)(2,1)S(1)} %stack.6), channel_id=1, source_target_pairs={{0,16},{4,20},{8,24},{12,28},{1,17},{5,21},{9,25},{13,29},{2,18},{... | collective-permute-start | bytes 884744 | tf_op jit(solution)/shard_map/ppermute | solution.py:266
  41.1 2.9 %collective-permute-done.7.refs_7_ = bf16[1,72,1024]{2,1,0:T(8,128)(2,1)S(1)} collective-permute-done((bf16[1,72,1024]{2,1,0:T(8,128)(2,1)S(1)}, bf16[1,72,1024]{2,1,0:T(8,128)(2,1)S(1)}, u32[]{:S(2)}, u32[]{:S(2)}) %collective-permute-start.7) | collective-permute-done | bytes 147488 | tf_op jit(solution)/shard_map/ppermute | solution.py:266
  44.0 7.8 %attend.2 = (bf16[72,8192]{1,0:T(8,128)(2,1)}, bf16[72,8192]{1,0:T(8,128)(2,1)}, bf16[4,72,1024]{2,1,0:T(8,128)(2,1)S(1)}, bf16[4,72,1024]{2,1,0:T(8,128)(2,1)S(1)}) custom-call(s32[2]{0:T(128)S(1)} %copy-done.4, bf16[72,2048]{1,0:T(8,128)(2,1)S(1)} %copy-done, bf16[72,2048]{1,0:T(8,128)(2,1)S(1)} %collective-permute-done.refs_0_.refs_1_, ...), custom_call_target="tpu_custom_call" | custom-call | flops 11530000384 | bytes 36900000 | tf_op jit(solution)/shard_map/attend/pallas_call | solution.py:360
  51.8 1.3 %collective-permute-start.9 = (bf16[4,72,1024]{2,1,0:T(8,128)(2,1)S(1)}, bf16[4,72,1024]{2,1,0:T(8,128)(2,1)S(1)}, u32[]{:S(2)}, u32[]{:S(2)}) collective-permute-start(bf16[4,72,1024]{2,1,0:T(8,128)(2,1)S(1)} %get-tuple-element.56), channel_id=1, source_target_pairs={{16,0},{20,4},{24,8},{28,12},{17,1},{21,5},{25,9},{29,13},{18,2},{... | collective-permute-start | bytes 1769480 | tf_op jit(solution)/shard_map/ppermute | solution.py:266
  53.1 7.8 %attend.3 = (bf16[72,8192]{1,0:T(8,128)(2,1)}, bf16[72,8192]{1,0:T(8,128)(2,1)}, bf16[4,72,1024]{2,1,0:T(8,128)(2,1)S(1)}, bf16[4,72,1024]{2,1,0:T(8,128)(2,1)S(1)}) custom-call(s32[2]{0:T(128)S(1)} %copy-done.4, bf16[72,2048]{1,0:T(8,128)(2,1)S(1)} %copy-done, ...), custom_call_target="tpu_custom_call", output_to_operand_aliasing={{0}: (15, {}), {1}: (16, {})} | custom-call | flops 11530000384 | bytes 36900000 | tf_op jit(solution)/shard_map/attend/pallas_call | solution.py:360
  61.0 1.3 %collective-permute-start.8 = (bf16[4,72,1024]{2,1,0:T(8,128)(2,1)S(1)}, bf16[4,72,1024]{2,1,0:T(8,128)(2,1)S(1)}, u32[]{:S(2)}, u32[]{:S(2)}) collective-permute-start(bf16[4,72,1024]{2,1,0:T(8,128)(2,1)S(1)} %get-tuple-element.54), channel_id=1, source_target_pairs={{16,0},{20,4},{24,8},{28,12},{17,1},{21,5},{25,9},{29,13},{18,2},{... | collective-permute-start | bytes 1769480 | tf_op jit(solution)/shard_map/ppermute | solution.py:266
  62.3 6.1 %collective-permute-done.9.refs_1_ = bf16[4,72,1024]{2,1,0:T(8,128)(2,1)S(1)} collective-permute-done((bf16[4,72,1024]{2,1,0:T(8,128)(2,1)S(1)}, bf16[4,72,1024]{2,1,0:T(8,128)(2,1)S(1)}, u32[]{:S(2)}, u32[]{:S(2)}) %collective-permute-start.9) | collective-permute-done | bytes 589856 | tf_op jit(solution)/shard_map/ppermute | solution.py:266
  68.4 0.1 combine.2
  68.5 2.8 %collective-permute-start.10 = (bf16[72,1024]{1,0:T(8,128)(2,1)S(1)}, bf16[72,1024]{1,0:T(8,128)(2,1)S(1)}, u32[]{:S(2)}, u32[]{:S(2)}) collective-permute-start(bf16[72,1024]{1,0:T(8,128)(2,1)S(1)} %get-tuple-element.59), channel_id=1, source_target_pairs={{0,4},{4,0},{8,12},{12,8},{20,16},{28,24},{1,5},{5,1},{9,13},{13,9... | collective-permute-start | bytes 442376 | tf_op jit(solution)/shard_map/ppermute | solution.py:258
  71.4 2.9 %collective-permute-start.11 = (bf16[72,1024]{1,0:T(8,128)(2,1)S(1)}, bf16[72,1024]{1,0:T(8,128)(2,1)S(1)}, u32[]{:S(2)}, u32[]{:S(2)}) collective-permute-start(bf16[72,1024]{1,0:T(8,128)(2,1)S(1)} %get-tuple-element.60), channel_id=1, source_target_pairs={{0,8},{4,12},{8,0},{12,4},{24,16},{28,20},{1,9},{5,13},{9,1},{13,5... | collective-permute-start | bytes 442376 | tf_op jit(solution)/shard_map/ppermute | solution.py:258
  74.3 4.4 %collective-permute-start.12 = (bf16[72,1024]{1,0:T(8,128)(2,1)S(1)}, bf16[72,1024]{1,0:T(8,128)(2,1)S(1)}, u32[]{:S(2)}, u32[]{:S(2)}) collective-permute-start(bf16[72,1024]{1,0:T(8,128)(2,1)S(1)} %get-tuple-element.61), channel_id=1, source_target_pairs={{0,12},{4,8},{8,4},{12,0},{24,20},{28,16},{1,13},{5,9},{9,5},{13,1... | collective-permute-start | bytes 442376 | tf_op jit(solution)/shard_map/ppermute | solution.py:258
  78.7 0.1 combine.3
  78.8 1.9 %collective-permute-start.13 = (bf16[72,1024]{1,0:T(8,128)(2,1)S(1)}, bf16[72,1024]{1,0:T(8,128)(2,1)S(1)}, u32[]{:S(2)}, u32[]{:S(2)}) collective-permute-start(bf16[72,1024]{1,0:T(8,128)(2,1)S(1)} %get-tuple-element.65), channel_id=1, source_target_pairs={{0,4},{4,0},{8,12},{12,8},{20,16},{28,24},{1,5},{5,1},{9,13},{13,9... | collective-permute-start | bytes 442376 | tf_op jit(solution)/shard_map/ppermute | solution.py:258
  80.8 3.8 %collective-permute-start.14 = (bf16[72,1024]{1,0:T(8,128)(2,1)S(1)}, bf16[72,1024]{1,0:T(8,128)(2,1)S(1)}, u32[]{:S(2)}, u32[]{:S(2)}) collective-permute-start(bf16[72,1024]{1,0:T(8,128)(2,1)S(1)} %get-tuple-element.66), channel_id=1, source_target_pairs={{0,8},{4,12},{8,0},{12,4},{24,16},{28,20},{1,9},{5,13},{9,1},{13,5... | collective-permute-start | bytes 442376 | tf_op jit(solution)/shard_map/ppermute | solution.py:258
  84.6 4.4 %collective-permute-start.15 = (bf16[72,1024]{1,0:T(8,128)(2,1)S(1)}, bf16[72,1024]{1,0:T(8,128)(2,1)S(1)}, u32[]{:S(2)}, u32[]{:S(2)}) collective-permute-start(bf16[72,1024]{1,0:T(8,128)(2,1)S(1)} %get-tuple-element.67), channel_id=1, source_target_pairs={{0,12},{4,8},{8,4},{12,0},{24,20},{28,16},{1,13},{5,9},{9,5},{13,1... | collective-permute-start | bytes 442376 | tf_op jit(solution)/shard_map/ppermute | solution.py:258
  89.0 5.3 %collective-permute-done.14.refs_8_ = bf16[72,1024]{1,0:T(8,128)(2,1)S(1)} collective-permute-done((bf16[72,1024]{1,0:T(8,128)(2,1)S(1)}, bf16[72,1024]{1,0:T(8,128)(2,1)S(1)}, u32[]{:S(2)}, u32[]{:S(2)}) %collective-permute-start.14) | collective-permute-done | bytes 147488 | tf_op jit(solution)/shard_map/ppermute | solution.py:258
  94.3 0.9 finish.1
  (21 shorter events, 0.1 us)
Async XLA Ops:
  2.6 19.8 %collective-permute-start = (bf16[72,2048]{1,0:T(8,128)(2,1)}, bf16[72,2048]{1,0:T(8,128)(2,1)S(1)}, u32[]{:S(2)}, u32[]{:S(2)}) collective-permute-start(bf16[72,2048]{1,0:T(8,128)(2,1)} %prepare_keys.1.refs_0_), channel_id=1, source_target_pairs={{0,4},{4,0},{8,12},{12,8},{16,20},{24,28},{1,5},{5,1},{9,13},{13,9... | collective-permute-start | bytes 884744 | tf_op jit(solution)/shard_map/ppermute | solution.py:258
  7.5 14.9 %collective-permute-start.1 = (bf16[72,2048]{1,0:T(8,128)(2,1)}, bf16[72,2048]{1,0:T(8,128)(2,1)S(1)}, u32[]{:S(2)}, u32[]{:S(2)}) collective-permute-start(bf16[72,2048]{1,0:T(8,128)(2,1)} %prepare_keys.1.refs_0_), channel_id=1, source_target_pairs={{0,16},{4,20},{8,24},{12,28},{1,17},{5,21},{9,25},{13,29},{2,18},{... | collective-permute-start | bytes 884744 | tf_op jit(solution)/shard_map/ppermute | solution.py:266
  11.0 17.5 %collective-permute-start.2 = (bf16[72,2048]{1,0:T(8,128)(2,1)}, bf16[72,2048]{1,0:T(8,128)(2,1)S(1)}, u32[]{:S(2)}, u32[]{:S(2)}) collective-permute-start(bf16[72,2048]{1,0:T(8,128)(2,1)} %prepare_keys.1.refs_0_), channel_id=1, source_target_pairs={{0,8},{4,12},{8,0},{12,4},{16,24},{20,28},{1,9},{5,13},{9,1},{13,5... | collective-permute-start | bytes 884744 | tf_op jit(solution)/shard_map/ppermute | solution.py:258
  15.5 0.7 copy-start.1
  16.2 1.3 %copy-start.2 = (bf16[72,8192]{1,0:T(8,128)(2,1)S(1)}, bf16[72,8192]{1,0:T(8,128)(2,1)}, u32[]{:S(2)}) copy-start(bf16[72,8192]{1,0:T(8,128)(2,1)} %query_ref.1) | copy-start | bytes 3538948
  17.4 1.3 %copy-start.3 = (bf16[72,8192]{1,0:T(8,128)(2,1)S(1)}, bf16[72,8192]{1,0:T(8,128)(2,1)}, u32[]{:S(2)}) copy-start(bf16[72,8192]{1,0:T(8,128)(2,1)} %grad_ref.1) | copy-start | bytes 3538948
  22.4 21.6 %copy-start = (bf16[72,2048]{1,0:T(8,128)(2,1)S(1)}, bf16[72,2048]{1,0:T(8,128)(2,1)}, u32[]{:S(2)}) copy-start(bf16[72,2048]{1,0:T(8,128)(2,1)} %prepare_keys.1.refs_0_) | copy-start | bytes 884740
  22.4 21.6 %copy-start.4 = (s32[2]{0:T(128)S(1)}, s32[2]{0:T(128)}, u32[]{:S(2)}) copy-start(s32[2]{0:T(128)} %counts_ref.3) | copy-start | bytes 28
  22.4 6.0 %collective-permute-start.3 = (bf16[1,72,1024]{2,1,0:T(8,128)(2,1)S(1)}, bf16[1,72,1024]{2,1,0:T(8,128)(2,1)S(1)}, u32[]{:S(2)}, u32[]{:S(2)}) collective-permute-start(bf16[1,72,1024]{2,1,0:T(8,128)(2,1)S(1)} %stack.4), channel_id=1, source_target_pairs={{0,16},{4,20},{8,24},{12,28},{1,17},{5,21},{9,25},{13,29},{2,18},{... | collective-permute-start | bytes 442376 | tf_op jit(solution)/shard_map/ppermute | solution.py:266
  28.4 10.0 %collective-permute-start.4 = (bf16[72,2048]{1,0:T(8,128)(2,1)S(1)}, bf16[72,2048]{1,0:T(8,128)(2,1)S(1)}, u32[]{:S(2)}, u32[]{:S(2)}) collective-permute-start(bf16[72,2048]{1,0:T(8,128)(2,1)S(1)} %collective-permute-done.2.refs_0_.refs_2_), channel_id=1, source_target_pairs={{0,4},{4,0},{8,12},{12,8},{24,28},{28,24},{1,5},{5,1},{9,13},{13,9... | collective-permute-start | bytes 884744 | tf_op jit(solution)/shard_map/ppermute | solution.py:258
  30.4 10.7 %collective-permute-start.5 = (bf16[2,72,1024]{2,1,0:T(8,128)(2,1)S(1)}, bf16[2,72,1024]{2,1,0:T(8,128)(2,1)S(1)}, u32[]{:S(2)}, u32[]{:S(2)}) collective-permute-start(bf16[2,72,1024]{2,1,0:T(8,128)(2,1)S(1)} %stack.5), channel_id=1, source_target_pairs={{0,16},{4,20},{8,24},{12,28},{1,17},{5,21},{9,25},{13,29},{2,18},{... | collective-permute-start | bytes 884744 | tf_op jit(solution)/shard_map/ppermute | solution.py:266
  38.5 5.6 %collective-permute-start.7 = (bf16[1,72,1024]{2,1,0:T(8,128)(2,1)S(1)}, bf16[1,72,1024]{2,1,0:T(8,128)(2,1)S(1)}, u32[]{:S(2)}, u32[]{:S(2)}) collective-permute-start(bf16[1,72,1024]{2,1,0:T(8,128)(2,1)S(1)} %stack.7), channel_id=1, source_target_pairs={{0,16},{4,20},{8,24},{12,28},{1,17},{5,21},{9,25},{13,29},{2,18},{... | collective-permute-start | bytes 442376 | tf_op jit(solution)/shard_map/ppermute | solution.py:266
  39.8 13.3 %collective-permute-start.6 = (bf16[2,72,1024]{2,1,0:T(8,128)(2,1)S(1)}, bf16[2,72,1024]{2,1,0:T(8,128)(2,1)S(1)}, u32[]{:S(2)}, u32[]{:S(2)}) collective-permute-start(bf16[2,72,1024]{2,1,0:T(8,128)(2,1)S(1)} %stack.6), channel_id=1, source_target_pairs={{0,16},{4,20},{8,24},{12,28},{1,17},{5,21},{9,25},{13,29},{2,18},{... | collective-permute-start | bytes 884744 | tf_op jit(solution)/shard_map/ppermute | solution.py:266
  51.8 16.6 %collective-permute-start.9 = (bf16[4,72,1024]{2,1,0:T(8,128)(2,1)S(1)}, bf16[4,72,1024]{2,1,0:T(8,128)(2,1)S(1)}, u32[]{:S(2)}, u32[]{:S(2)}) collective-permute-start(bf16[4,72,1024]{2,1,0:T(8,128)(2,1)S(1)} %get-tuple-element.56), channel_id=1, source_target_pairs={{16,0},{20,4},{24,8},{28,12},{17,1},{21,5},{25,9},{29,13},{18,2},{... | collective-permute-start | bytes 1769480 | tf_op jit(solution)/shard_map/ppermute | solution.py:266
  61.0 17.7 %collective-permute-start.8 = (bf16[4,72,1024]{2,1,0:T(8,128)(2,1)S(1)}, bf16[4,72,1024]{2,1,0:T(8,128)(2,1)S(1)}, u32[]{:S(2)}, u32[]{:S(2)}) collective-permute-start(bf16[4,72,1024]{2,1,0:T(8,128)(2,1)S(1)} %get-tuple-element.54), channel_id=1, source_target_pairs={{16,0},{20,4},{24,8},{28,12},{17,1},{21,5},{25,9},{29,13},{18,2},{... | collective-permute-start | bytes 1769480 | tf_op jit(solution)/shard_map/ppermute | solution.py:266
  68.5 16.1 %collective-permute-start.10 = (bf16[72,1024]{1,0:T(8,128)(2,1)S(1)}, bf16[72,1024]{1,0:T(8,128)(2,1)S(1)}, u32[]{:S(2)}, u32[]{:S(2)}) collective-permute-start(bf16[72,1024]{1,0:T(8,128)(2,1)S(1)} %get-tuple-element.59), channel_id=1, source_target_pairs={{0,4},{4,0},{8,12},{12,8},{20,16},{28,24},{1,5},{5,1},{9,13},{13,9... | collective-permute-start | bytes 442376 | tf_op jit(solution)/shard_map/ppermute | solution.py:258
  71.4 17.6 %collective-permute-start.11 = (bf16[72,1024]{1,0:T(8,128)(2,1)S(1)}, bf16[72,1024]{1,0:T(8,128)(2,1)S(1)}, u32[]{:S(2)}, u32[]{:S(2)}) collective-permute-start(bf16[72,1024]{1,0:T(8,128)(2,1)S(1)} %get-tuple-element.60), channel_id=1, source_target_pairs={{0,8},{4,12},{8,0},{12,4},{24,16},{28,20},{1,9},{5,13},{9,1},{13,5... | collective-permute-start | bytes 442376 | tf_op jit(solution)/shard_map/ppermute | solution.py:258
  74.3 14.7 %collective-permute-start.12 = (bf16[72,1024]{1,0:T(8,128)(2,1)S(1)}, bf16[72,1024]{1,0:T(8,128)(2,1)S(1)}, u32[]{:S(2)}, u32[]{:S(2)}) collective-permute-start(bf16[72,1024]{1,0:T(8,128)(2,1)S(1)} %get-tuple-element.61), channel_id=1, source_target_pairs={{0,12},{4,8},{8,4},{12,0},{24,20},{28,16},{1,13},{5,9},{9,5},{13,1... | collective-permute-start | bytes 442376 | tf_op jit(solution)/shard_map/ppermute | solution.py:258
  78.8 10.2 %collective-permute-start.13 = (bf16[72,1024]{1,0:T(8,128)(2,1)S(1)}, bf16[72,1024]{1,0:T(8,128)(2,1)S(1)}, u32[]{:S(2)}, u32[]{:S(2)}) collective-permute-start(bf16[72,1024]{1,0:T(8,128)(2,1)S(1)} %get-tuple-element.65), channel_id=1, source_target_pairs={{0,4},{4,0},{8,12},{12,8},{20,16},{28,24},{1,5},{5,1},{9,13},{13,9... | collective-permute-start | bytes 442376 | tf_op jit(solution)/shard_map/ppermute | solution.py:258
  80.8 13.6 %collective-permute-start.14 = (bf16[72,1024]{1,0:T(8,128)(2,1)S(1)}, bf16[72,1024]{1,0:T(8,128)(2,1)S(1)}, u32[]{:S(2)}, u32[]{:S(2)}) collective-permute-start(bf16[72,1024]{1,0:T(8,128)(2,1)S(1)} %get-tuple-element.66), channel_id=1, source_target_pairs={{0,8},{4,12},{8,0},{12,4},{24,16},{28,20},{1,9},{5,13},{9,1},{13,5... | collective-permute-start | bytes 442376 | tf_op jit(solution)/shard_map/ppermute | solution.py:258
  84.6 9.7 %collective-permute-start.15 = (bf16[72,1024]{1,0:T(8,128)(2,1)S(1)}, bf16[72,1024]{1,0:T(8,128)(2,1)S(1)}, u32[]{:S(2)}, u32[]{:S(2)}) collective-permute-start(bf16[72,1024]{1,0:T(8,128)(2,1)S(1)} %get-tuple-element.67), channel_id=1, source_target_pairs={{0,12},{4,8},{8,4},{12,0},{24,20},{28,16},{1,13},{5,9},{9,5},{13,1... | collective-permute-start | bytes 442376 | tf_op jit(solution)/shard_map/ppermute | solution.py:258

commit v11 on v7

--- a/solution.py
+++ b/solution.py
@@ -14,6 +14,7 @@
 GROUP = QUERY_HEADS // KEY_VALUE_HEADS
 ROPE_BASE = 500000.0
 SCORE_SCALE = 1.0 / float(np.sqrt(HEAD_WIDTH))
+SCORE_TO_LOG2 = SCORE_SCALE * 1.4426950408889634
 CHUNKS = 2
 HEADS_PER_CHUNK = KEY_VALUE_HEADS // CHUNKS
 CHUNK_COLS = HEADS_PER_CHUNK * HEAD_WIDTH
@@ -106,89 +107,98 @@
     return jnp.dot(left, right, preferred_element_type=jnp.float32)
 
 
-def attend(seq_count, head_count, rows, pieces, has_alias, counts_ref, *refs):
+def attend(seq_count, head_count, rows, chunk, pieces, counts_ref, *refs):
     blocks = seq_count * head_count
     kv_refs = []
     for ref in refs[:pieces]:
-        kv_refs += [ref] if len(ref.shape) == 2 else [ref.at[i] for i in range(ref.shape[0])]
+        if len(ref.shape) == 2:
+            kv_refs.append(ref.at[:, 2 * chunk * CHUNK_COLS : 2 * (chunk + 1) * CHUNK_COLS])
+        else:
+            kv_refs += [ref.at[i] for i in range(ref.shape[0])]
     q_ref, qt_ref, g_ref, gt_ref, cos_ref, sin_ref = refs[pieces : pieces + 6]
-    outs = refs[pieces + 6 + 2 * has_alias :]
+    outs = refs[pieces + 6 + 2 * int(chunk > 0) :]
     out_ref, grad_ref = outs[:2]
     part_refs = outs[2 : 2 + seq_count]
     bias_ref, live_ref = outs[2 + seq_count :]
     padded = kv_refs[0].shape[0]
     query_rows = GROUP * padded
-    step = pl.program_id(0)
     seq_index, head_index = lax.axis_index("seq"), lax.axis_index("head")
     my_rank = seq_index * head_count + head_index
 
-    @pl.when(step == 0)
-    def _():
-        key_row = lax.broadcasted_iota(jnp.int32, (padded, query_rows), 0)
-        query_row = lax.rem(lax.broadcasted_iota(jnp.int32, (padded, query_rows), 1), padded)
-        for block in range(blocks):
-            seq_offset, head_offset = divmod(block, head_count)
-            seq_from = jnp.bitwise_xor(seq_index, seq_offset)
-            head_from = jnp.bitwise_xor(head_index, head_offset)
-            rank = seq_from * head_count + head_from
-            limit = jnp.minimum(counts_ref[seq_from] - head_from * rows, rows)
-            limit = jnp.where(rank <= my_rank, limit, 0)
-            allowed = key_row < limit
-            if block == 0:
-                allowed = allowed & (key_row <= query_row)
-                live_ref[...] = (query_row[:8] < limit).astype(jnp.float32)
-            bias_ref[block * padded : (block + 1) * padded, :] = jnp.where(allowed, 0.0, -1e30)
-
-    def lanes(first, place):
-        start = pl.multiple_of((first + step * STEP_HEADS + place) * HEAD_WIDTH, HEAD_WIDTH)
-        return pl.ds(start, HEAD_WIDTH)
-
-    def gathered(first, place):
-        cols = lanes(first, place)
-        wide = jnp.concatenate([ref[:, cols].astype(jnp.float32) for ref in kv_refs], 0)
-        low = wide.astype(jnp.bfloat16)
-        return low, low.T
-
-    heads = range(STEP_HEADS)
-    keys, values = [gathered(0, p) for p in heads], [gathered(HEADS_PER_CHUNK, p) for p in heads]
-    bias, live = bias_ref[...], live_ref[0:1, :]
-    scores = [dot(keys[p][0], qt_ref[p]) * SCORE_SCALE + bias for p in heads]
-    dprobs, probs, probs_low = [], [], []
-    for p in heads:
-        weights = jnp.exp(scores[p] - jnp.max(scores[p], 0, keepdims=True))
-        probs.append(weights * (live / jnp.sum(weights, 0, keepdims=True)))
-        probs_low.append(probs[p].astype(jnp.bfloat16))
-        dprobs.append(dot(values[p][0], gt_ref[p]))
-    outs_t, value_parts, dscores = [], [], []
-    for p in heads:
-        outs_t.append(dot(values[p][1], probs_low[p]))
-        value_parts.append(dot(probs_low[p], g_ref[p]))
-        out_low = outs_t[p].astype(jnp.bfloat16).astype(jnp.float32)
-        delta = jnp.sum(gt_ref[p].astype(jnp.float32) * out_low, 0, keepdims=True)
-        dscores.append((probs[p] * (dprobs[p] - delta)).astype(jnp.bfloat16))
-    grads_t = [dot(keys[p][1], dscores[p]) for p in heads]
-    key_parts = [dot(dscores[p], q_ref[p]) * SCORE_SCALE for p in heads]
-
-    cosine, sine = cos_ref[...], sin_ref[...]
-    half = HEAD_WIDTH // 2
-    for p in heads:
-        first, second = grads_t[p][:half], grads_t[p][half:]
-        turned = [first * cosine + second * sine, second * cosine - first * sine]
-        grad_low = jnp.concatenate(turned, 0).astype(jnp.bfloat16)
-        out_heads = outs_t[p].astype(jnp.bfloat16).T.astype(jnp.float32)
-        grad_heads = grad_low.T.astype(jnp.float32)
-        for h in range(GROUP):
-            piece, cols = slice(h * padded, (h + 1) * padded), head_cols(p * GROUP + h)
-            out_ref[:, cols] = out_heads[piece].astype(jnp.bfloat16)
-            grad_ref[:, cols] = grad_heads[piece].astype(jnp.bfloat16)
-        for block in range(blocks):
-            seq_offset, head_offset = divmod(block, head_count)
-            piece = slice(block * padded, (block + 1) * padded)
-            part_ref = part_refs[seq_offset]
-            part_ref[head_offset, :, lanes(0, p)] = key_parts[p][piece].astype(jnp.bfloat16)
-            part_ref[head_offset, :, lanes(HEADS_PER_CHUNK, p)] = value_parts[p][piece].astype(
-                jnp.bfloat16
-            )
+    key_row = lax.broadcasted_iota(jnp.int32, (padded, query_rows), 0)
+    query_row = lax.rem(lax.broadcasted_iota(jnp.int32, (padded, query_rows), 1), padded)
+    for block in range(blocks):
+        seq_offset, head_offset = divmod(block, head_count)
+        seq_from = jnp.bitwise_xor(seq_index, seq_offset)
+        head_from = jnp.bitwise_xor(head_index, head_offset)
+        rank = seq_from * head_count + head_from
+        limit = jnp.minimum(counts_ref[seq_from] - head_from * rows, rows)
+        limit = jnp.where(rank <= my_rank, limit, 0)
+        allowed = key_row < limit
+        if block == 0:
+            allowed = allowed & (key_row <= query_row)
+            live_ref[...] = (query_row[:8] < limit).astype(jnp.float32)
+        bias_ref[block * padded : (block + 1) * padded, :] = jnp.where(allowed, 0.0, -1e30)
+
+    @pl.loop(0, HEADS_PER_CHUNK // STEP_HEADS)
+    def _(step):
+        first_head = chunk * HEADS_PER_CHUNK + step * STEP_HEADS
+
+        def lanes(first, place):
+            start = pl.multiple_of((first + step * STEP_HEADS + place) * HEAD_WIDTH, HEAD_WIDTH)
+            return pl.ds(start, HEAD_WIDTH)
+
+        def query_lanes(place, head):
+            start = (step * STEP_HEADS + place) * GROUP * HEAD_WIDTH + head * HEAD_WIDTH
+            start = pl.multiple_of(start, HEAD_WIDTH)
+            return pl.ds(start, HEAD_WIDTH)
+
+        def gathered(first, place):
+            cols = lanes(first, place)
+            wide = jnp.concatenate([ref[:, cols].astype(jnp.float32) for ref in kv_refs], 0)
+            low = wide.astype(jnp.bfloat16)
+            return low, low.T
+
+        heads = range(STEP_HEADS)
+        keys, values = [gathered(0, p) for p in heads], [gathered(HEADS_PER_CHUNK, p) for p in heads]
+        bias, live = bias_ref[...], live_ref[0:1, :]
+        scores = [dot(keys[p][0], qt_ref[first_head + p]) * SCORE_TO_LOG2 + bias for p in heads]
+        dprobs, probs, probs_low = [], [], []
+        for p in heads:
+            weights = jnp.exp2(scores[p] - jnp.max(scores[p], 0, keepdims=True))
+            probs.append(weights * (live / jnp.sum(weights, 0, keepdims=True)))
+            probs_low.append(probs[p].astype(jnp.bfloat16))
+            dprobs.append(dot(values[p][0], gt_ref[first_head + p]))
+        outs_t, value_parts, dscores = [], [], []
+        for p in heads:
+            outs_t.append(dot(values[p][1], probs_low[p]))
+            value_parts.append(dot(probs_low[p], g_ref[first_head + p]))
+            out_low = outs_t[p].astype(jnp.bfloat16).astype(jnp.float32)
+            delta = jnp.sum(gt_ref[first_head + p].astype(jnp.float32) * out_low, 0, keepdims=True)
+            dscores.append((probs[p] * (dprobs[p] - delta)).astype(jnp.bfloat16))
+        grads_t = [dot(keys[p][1], dscores[p]) for p in heads]
+        key_parts = [dot(dscores[p], q_ref[first_head + p]) * SCORE_SCALE for p in heads]
+
+        cosine, sine = cos_ref[...], sin_ref[...]
+        half = HEAD_WIDTH // 2
+        for p in heads:
+            first, second = grads_t[p][:half], grads_t[p][half:]
+            turned = [first * cosine + second * sine, second * cosine - first * sine]
+            grad_low = jnp.concatenate(turned, 0).astype(jnp.bfloat16)
+            out_heads = outs_t[p].astype(jnp.bfloat16).T.astype(jnp.float32)
+            grad_heads = grad_low.T.astype(jnp.float32)
+            for h in range(GROUP):
+                piece, cols = slice(h * padded, (h + 1) * padded), query_lanes(p, h)
+                out_ref[:, cols] = out_heads[piece].astype(jnp.bfloat16)
+                grad_ref[:, cols] = grad_heads[piece].astype(jnp.bfloat16)
+            for block in range(blocks):
+                seq_offset, head_offset = divmod(block, head_count)
+                piece = slice(block * padded, (block + 1) * padded)
+                part_ref = part_refs[seq_offset]
+                part_ref[head_offset, :, lanes(0, p)] = key_parts[p][piece].astype(jnp.bfloat16)
+                part_ref[head_offset, :, lanes(HEADS_PER_CHUNK, p)] = value_parts[p][piece].astype(
+                    jnp.bfloat16
+                )
 
 
 def combine(seq_count, head_count, *refs):
@@ -327,33 +337,21 @@
     wide_outs = ()
     parts = []
     for chunk in range(CHUNKS):
-        first = chunk * HEADS_PER_CHUNK // STEP_HEADS
         has_alias = int(chunk > 0)
-        tall_part, flat_part = (
-            pl.BlockSpec((STEP_HEADS, *x.shape[1:]), lambda g, f=first: (f + g, 0, 0))
-            for x in (tall, flat)
-        )
-        row_part = pl.BlockSpec((padded, STEP_HEADS * wide), lambda g, f=first: (0, f + g))
         gathered = [near[j] for j in range(head_count)]
         for a in later:
             gathered += [far[a]] + [part[a] for part in crossed[chunk]]
         inputs = len(gathered)
-        kv_whole = pl.BlockSpec((padded, 2 * CHUNK_COLS), lambda g, c=chunk: (0, c))
-        kv_specs = [
-            kv_whole if len(x.shape) == 2 else pl.BlockSpec(x.shape, lambda g: (0, 0, 0))
-            for x in gathered
-        ]
-        part_block = pl.BlockSpec((head_count, padded, 2 * CHUNK_COLS), lambda g: (0, 0, 0))
         out = pl.pallas_call(
-            functools.partial(attend, seq_count, head_count, rows, inputs, has_alias),
-            grid=(HEADS_PER_CHUNK // STEP_HEADS,),
+            functools.partial(attend, seq_count, head_count, rows, chunk, inputs),
             out_shape=[shape((padded, QUERY_HEADS * HEAD_WIDTH), bf16)] * 2
             + [shape((head_count, padded, 2 * CHUNK_COLS), bf16)] * seq_count,
             in_specs=[SMEM]
-            + kv_specs
-            + [tall_part, flat_part, tall_part, flat_part, table_t_block, table_t_block]
+            + [VMEM] * (inputs + 6)
             + [pl.BlockSpec(memory_space=pl.ANY)] * (2 * has_alias),
-            out_specs=[row_part, row_part] + [part_block] * seq_count,
+            out_specs=[pl.BlockSpec((padded, HEADS_PER_CHUNK * wide), lambda i, c=chunk: (0, c))] * 2
+            + [VMEM] * seq_count,
+            grid=(1,),
             scratch_shapes=[
                 pltpu.VMEM((blocks * padded, query_rows), f32),
                 pltpu.VMEM((8, query_rows), f32),

time: 93.8 us -> 93.7 us (level)
  no operation moved by 1% of the time
where the time goes in v11:
time: 93.7 us; the launch traced here: 93.1 us
  starting transfers between devices  43.6 us (47%)
  Pallas kernels  22.7 us (24%)
  waiting for transfers between devices  22.7 us (24%)
  local copies, waits for them, and re-layouts  3.23 us (3%)
    ppermute x9, starting transfers between devices, along_head(): return lax.ppermute(x, ('seq', 'head'), pairs)  32.8 us
    pallas_call x2, Pallas kernels, shards(): pl.pallas_call(functools.partial(attend, seq_count, head_count, rows, chu...  15.9 us
    ppermute x9, waiting for transfers between devices, along_head(): return lax.ppermute(x, ('seq', 'head'), pairs)  15.1 us
    ppermute x6, starting transfers between devices, along_seq(): return lax.ppermute(x, ('seq', 'head'), pairs)  10.9 us
    ppermute x6, waiting for transfers between devices, along_seq(): return lax.ppermute(x, ('seq', 'head'), pairs)  7.58 us
    pallas_call x1, Pallas kernels, shards(): pl.pallas_call(functools.partial(prepare_queries, rows), grid=(KEY_VALUE_...  3.65 us
    unnamed x10, local copies, waits for them, and re-layouts  3.23 us
    pallas_call x1, Pallas kernels, shards(): pl.pallas_call(functools.partial(prepare_keys, rows), out_shape=shape((pa...  1.96 us
  transfers between devices with their start and end apart: 15, of which 5 were waited for; matrix products, arithmetic and copies ran while one was open for 0% of the time, Pallas kernels for 21%

profile of v11, /device:TPU:0, one launch (start us, length us, event | category | flops | bytes accessed | tf_op | source)
XLA Modules:
  0.0 93.1 jit_solution(11341578414292449946)
XLA Ops:
  0.6 2.0 %prepare_keys.1.refs_0_ = bf16[72,2048]{1,0:T(8,128)(2,1)} custom-call(s32[576]{0:T(1024)} %pos_ref.3, bf16[72,1024]{1,0:T(8,128)(2,1)} %key_ref.1, bf16[72,1024]{1,0:T(8,128)(2,1)} %value_ref.1), custom_call_target="tpu_custom_call" | custom-call | tf_op jit(solution)/shard_map/prepare_keys/pallas_call | solution.py:282
  2.6 4.9 %collective-permute-start = (bf16[72,2048]{1,0:T(8,128)(2,1)}, bf16[72,2048]{1,0:T(8,128)(2,1)S(1)}, u32[]{:S(2)}, u32[]{:S(2)}) collective-permute-start(bf16[72,2048]{1,0:T(8,128)(2,1)} %prepare_keys.1.refs_0_), channel_id=1, source_target_pairs={{0,4},{4,0},{8,12},{12,8},{16,20},{24,28},{1,5},{5,1},{9,13},{13,9... | collective-permute-start | bytes 884744 | tf_op jit(solution)/shard_map/ppermute | solution.py:269
  7.5 4.5 %collective-permute-start.1 = (bf16[72,2048]{1,0:T(8,128)(2,1)}, bf16[72,2048]{1,0:T(8,128)(2,1)S(1)}, u32[]{:S(2)}, u32[]{:S(2)}) collective-permute-start(bf16[72,2048]{1,0:T(8,128)(2,1)} %prepare_keys.1.refs_0_), channel_id=1, source_target_pairs={{0,8},{4,12},{8,0},{12,4},{16,24},{20,28},{1,9},{5,13},{9,1},{13,5... | collective-permute-start | bytes 884744 | tf_op jit(solution)/shard_map/ppermute | solution.py:269
  12.0 3.5 %collective-permute-start.2 = (bf16[72,2048]{1,0:T(8,128)(2,1)}, bf16[72,2048]{1,0:T(8,128)(2,1)S(1)}, u32[]{:S(2)}, u32[]{:S(2)}) collective-permute-start(bf16[72,2048]{1,0:T(8,128)(2,1)} %prepare_keys.1.refs_0_), channel_id=1, source_target_pairs={{0,16},{4,20},{8,24},{12,28},{1,17},{5,21},{9,25},{13,29},{2,18},{... | collective-permute-start | bytes 884744 | tf_op jit(solution)/shard_map/ppermute | solution.py:277
  15.5 0.0 copy-start.1
  15.5 0.7 copy-done.1
  16.2 1.3 %copy-done.2 = bf16[72,8192]{1,0:T(8,128)(2,1)S(1)} copy-done((bf16[72,8192]{1,0:T(8,128)(2,1)S(1)}, bf16[72,8192]{1,0:T(8,128)(2,1)}, u32[]{:S(2)}) %copy-start.2) | copy-done | bytes 1179672
  17.5 1.3 %copy-done.3 = bf16[72,8192]{1,0:T(8,128)(2,1)S(1)} copy-done((bf16[72,8192]{1,0:T(8,128)(2,1)S(1)}, bf16[72,8192]{1,0:T(8,128)(2,1)}, u32[]{:S(2)}) %copy-start.3) | copy-done | bytes 1179672
  18.7 3.7 %prepare_queries.1 = (bf16[8,576,128]{2,1,0:T(8,128)(2,1)S(1)}, bf16[8,128,576]{2,1,0:T(8,128)(2,1)S(1)}, bf16[8,576,128]{2,1,0:T(8,128)(2,1)S(1)}, bf16[8,128,5...) custom-call(s32[576]{0:T(1024)S(1)} %copy-done.1, ...), custom_call_target="tpu_custom_call" | custom-call | flops 8071000064 | bytes 25830000 | tf_op jit(solution)/shard_map/prepare_queries/pallas_call | solution.py:299
  22.4 3.0 %collective-permute-done.1.refs_1_.refs_2_ = bf16[72,2048]{1,0:T(8,128)(2,1)S(1)} collective-permute-done((bf16[72,2048]{1,0:T(8,128)(2,1)}, bf16[72,2048]{1,0:T(8,128)(2,1)S(1)}, u32[]{:S(2)}, u32[]{:S(2)}) %collective-permute-start.1) | collective-permute-done | bytes 294944 | tf_op jit(solution)/shard_map/ppermute | solution.py:269
  25.4 2.0 %collective-permute-start.3 = (bf16[72,2048]{1,0:T(8,128)(2,1)S(1)}, bf16[72,2048]{1,0:T(8,128)(2,1)S(1)}, u32[]{:S(2)}, u32[]{:S(2)}) collective-permute-start(bf16[72,2048]{1,0:T(8,128)(2,1)S(1)} %collective-permute-done.1.refs_1_.refs_2_), channel_id=1, source_target_pairs={{0,4},{4,0},{8,12},{12,8},{24,28},{28,24},{1,5},{5,1},{9,13},{13,9... | collective-permute-start | bytes 884744 | tf_op jit(solution)/shard_map/ppermute | solution.py:269
  27.4 1.3 %collective-permute-start.4 = (bf16[2,72,1024]{2,1,0:T(8,128)(2,1)S(1)}, bf16[2,72,1024]{2,1,0:T(8,128)(2,1)S(1)}, u32[]{:S(2)}, u32[]{:S(2)}) collective-permute-start(bf16[2,72,1024]{2,1,0:T(8,128)(2,1)S(1)} %stack.3), channel_id=1, source_target_pairs={{0,16},{4,20},{8,24},{12,28},{1,17},{5,21},{9,25},{13,29},{2,18},{... | collective-permute-start | bytes 884744 | tf_op jit(solution)/shard_map/ppermute | solution.py:277
  28.8 6.2 %collective-permute-done.3.refs_2_.refs_0_.refs_3_ = bf16[72,2048]{1,0:T(8,128)(2,1)S(1)} collective-permute-done((bf16[72,2048]{1,0:T(8,128)(2,1)S(1)}, bf16[72,2048]{1,0:T(8,128)(2,1)S(1)}, u32[]{:S(2)}, u32[]{:S(2)}) %collective-permute-start.3) | collective-permute-done | bytes 294944 | tf_op jit(solution)/shard_map/ppermute | solution.py:269
  35.0 1.3 %collective-permute-start.6 = (bf16[1,72,1024]{2,1,0:T(8,128)(2,1)S(1)}, bf16[1,72,1024]{2,1,0:T(8,128)(2,1)S(1)}, u32[]{:S(2)}, u32[]{:S(2)}) collective-permute-start(bf16[1,72,1024]{2,1,0:T(8,128)(2,1)S(1)} %stack.5), channel_id=1, source_target_pairs={{0,16},{4,20},{8,24},{12,28},{1,17},{5,21},{9,25},{13,29},{2,18},{... | collective-permute-start | bytes 442376 | tf_op jit(solution)/shard_map/ppermute | solution.py:277
  36.3 0.0 collective-permute-done.4.refs_5_
  36.4 2.2 %collective-permute-start.5 = (bf16[3,72,1024]{2,1,0:T(8,128)(2,1)S(1)}, bf16[3,72,1024]{2,1,0:T(8,128)(2,1)S(1)}, u32[]{:S(2)}, u32[]{:S(2)}) collective-permute-start(bf16[3,72,1024]{2,1,0:T(8,128)(2,1)S(1)} %stack.4), channel_id=1, source_target_pairs={{0,16},{4,20},{8,24},{12,28},{1,17},{5,21},{9,25},{13,29},{2,18},{... | collective-permute-start | bytes 1327112 | tf_op jit(solution)/shard_map/ppermute | solution.py:277
  38.6 1.9 %collective-permute-done.6.refs_6_ = bf16[1,72,1024]{2,1,0:T(8,128)(2,1)S(1)} collective-permute-done((bf16[1,72,1024]{2,1,0:T(8,128)(2,1)S(1)}, bf16[1,72,1024]{2,1,0:T(8,128)(2,1)S(1)}, u32[]{:S(2)}, u32[]{:S(2)}) %collective-permute-start.6) | collective-permute-done | bytes 147488 | tf_op jit(solution)/shard_map/ppermute | solution.py:277
  40.5 7.9 %attend.2 = (bf16[72,8192]{1,0:T(8,128)(2,1)}, bf16[72,8192]{1,0:T(8,128)(2,1)}, bf16[4,72,1024]{2,1,0:T(8,128)(2,1)S(1)}, bf16[4,72,1024]{2,1,0:T(8,128)(2,1)S(1)}) custom-call(s32[2]{0:T(128)S(1)} %copy-done.4, bf16[72,2048]{1,0:T(8,128)(2,1)S(1)} %copy-done, bf16[72,2048]{1,0:T(8,128)(2,1)S(1)} %collective-permute-done.refs_0_.refs_1_, ...), custom_call_target="tpu_custom_call" | custom-call | flops 11530000384 | bytes 36900000 | tf_op jit(solution)/shard_map/attend/pallas_call | solution.py:345
  48.4 1.3 %collective-permute-start.8 = (bf16[4,72,1024]{2,1,0:T(8,128)(2,1)S(1)}, bf16[4,72,1024]{2,1,0:T(8,128)(2,1)S(1)}, u32[]{:S(2)}, u32[]{:S(2)}) collective-permute-start(bf16[4,72,1024]{2,1,0:T(8,128)(2,1)S(1)} %get-tuple-element.60), channel_id=1, source_target_pairs={{16,0},{20,4},{24,8},{28,12},{17,1},{21,5},{25,9},{29,13},{18,2},{... | collective-permute-start | bytes 1769480 | tf_op jit(solution)/shard_map/ppermute | solution.py:277
  49.7 7.9 %attend.3 = (bf16[72,8192]{1,0:T(8,128)(2,1)}, bf16[72,8192]{1,0:T(8,128)(2,1)}, bf16[4,72,1024]{2,1,0:T(8,128)(2,1)S(1)}, bf16[4,72,1024]{2,1,0:T(8,128)(2,1)S(1)}) custom-call(s32[2]{0:T(128)S(1)} %copy-done.4, bf16[72,2048]{1,0:T(8,128)(2,1)S(1)} %copy-done, ...), custom_call_target="tpu_custom_call", output_to_operand_aliasing={{0}: (13, {}), {1}: (14, {})} | custom-call | flops 11530000384 | bytes 36900000 | tf_op jit(solution)/shard_map/attend/pallas_call | solution.py:345
  57.6 1.3 %collective-permute-start.7 = (bf16[4,72,1024]{2,1,0:T(8,128)(2,1)S(1)}, bf16[4,72,1024]{2,1,0:T(8,128)(2,1)S(1)}, u32[]{:S(2)}, u32[]{:S(2)}) collective-permute-start(bf16[4,72,1024]{2,1,0:T(8,128)(2,1)S(1)} %get-tuple-element.58), channel_id=1, source_target_pairs={{16,0},{20,4},{24,8},{28,12},{17,1},{21,5},{25,9},{29,13},{18,2},{... | collective-permute-start | bytes 1769480 | tf_op jit(solution)/shard_map/ppermute | solution.py:277
  58.9 5.7 %collective-permute-done.8.refs_1_ = bf16[4,72,1024]{2,1,0:T(8,128)(2,1)S(1)} collective-permute-done((bf16[4,72,1024]{2,1,0:T(8,128)(2,1)S(1)}, bf16[4,72,1024]{2,1,0:T(8,128)(2,1)S(1)}, u32[]{:S(2)}, u32[]{:S(2)}) %collective-permute-start.8) | collective-permute-done | bytes 589856 | tf_op jit(solution)/shard_map/ppermute | solution.py:277
  64.6 0.1 combine.2
  64.7 5.9 %collective-permute-start.10 = (bf16[72,1024]{1,0:T(8,128)(2,1)S(1)}, bf16[72,1024]{1,0:T(8,128)(2,1)S(1)}, u32[]{:S(2)}, u32[]{:S(2)}) collective-permute-start(bf16[72,1024]{1,0:T(8,128)(2,1)S(1)} %get-tuple-element.64), channel_id=1, source_target_pairs={{0,8},{4,12},{8,0},{12,4},{24,16},{28,20},{1,9},{5,13},{9,1},{13,5... | collective-permute-start | bytes 442376 | tf_op jit(solution)/shard_map/ppermute | solution.py:269
  70.7 2.0 %collective-permute-start.11 = (bf16[72,1024]{1,0:T(8,128)(2,1)S(1)}, bf16[72,1024]{1,0:T(8,128)(2,1)S(1)}, u32[]{:S(2)}, u32[]{:S(2)}) collective-permute-start(bf16[72,1024]{1,0:T(8,128)(2,1)S(1)} %get-tuple-element.65), channel_id=1, source_target_pairs={{0,12},{4,8},{8,4},{12,0},{24,20},{28,16},{1,13},{5,9},{9,5},{13,1... | collective-permute-start | bytes 442376 | tf_op jit(solution)/shard_map/ppermute | solution.py:269
  72.6 2.5 %collective-permute-start.9 = (bf16[72,1024]{1,0:T(8,128)(2,1)S(1)}, bf16[72,1024]{1,0:T(8,128)(2,1)S(1)}, u32[]{:S(2)}, u32[]{:S(2)}) collective-permute-start(bf16[72,1024]{1,0:T(8,128)(2,1)S(1)} %get-tuple-element.63), channel_id=1, source_target_pairs={{0,4},{4,0},{8,12},{12,8},{20,16},{28,24},{1,5},{5,1},{9,13},{13,9... | collective-permute-start | bytes 442376 | tf_op jit(solution)/shard_map/ppermute | solution.py:269
  75.1 0.1 combine.3
  75.3 3.4 %collective-permute-start.12 = (bf16[72,1024]{1,0:T(8,128)(2,1)S(1)}, bf16[72,1024]{1,0:T(8,128)(2,1)S(1)}, u32[]{:S(2)}, u32[]{:S(2)}) collective-permute-start(bf16[72,1024]{1,0:T(8,128)(2,1)S(1)} %get-tuple-element.69), channel_id=1, source_target_pairs={{0,4},{4,0},{8,12},{12,8},{20,16},{28,24},{1,5},{5,1},{9,13},{13,9... | collective-permute-start | bytes 442376 | tf_op jit(solution)/shard_map/ppermute | solution.py:269
  78.6 4.2 %collective-permute-start.13 = (bf16[72,1024]{1,0:T(8,128)(2,1)S(1)}, bf16[72,1024]{1,0:T(8,128)(2,1)S(1)}, u32[]{:S(2)}, u32[]{:S(2)}) collective-permute-start(bf16[72,1024]{1,0:T(8,128)(2,1)S(1)} %get-tuple-element.70), channel_id=1, source_target_pairs={{0,8},{4,12},{8,0},{12,4},{24,16},{28,20},{1,9},{5,13},{9,1},{13,5... | collective-permute-start | bytes 442376 | tf_op jit(solution)/shard_map/ppermute | solution.py:269
  82.9 3.4 %collective-permute-start.14 = (bf16[72,1024]{1,0:T(8,128)(2,1)S(1)}, bf16[72,1024]{1,0:T(8,128)(2,1)S(1)}, u32[]{:S(2)}, u32[]{:S(2)}) collective-permute-start(bf16[72,1024]{1,0:T(8,128)(2,1)S(1)} %get-tuple-element.71), channel_id=1, source_target_pairs={{0,12},{4,8},{8,4},{12,0},{24,20},{28,16},{1,13},{5,9},{9,5},{13,1... | collective-permute-start | bytes 442376 | tf_op jit(solution)/shard_map/ppermute | solution.py:269
  86.3 5.9 %collective-permute-done.13.refs_8_ = bf16[72,1024]{1,0:T(8,128)(2,1)S(1)} collective-permute-done((bf16[72,1024]{1,0:T(8,128)(2,1)S(1)}, bf16[72,1024]{1,0:T(8,128)(2,1)S(1)}, u32[]{:S(2)}, u32[]{:S(2)}) %collective-permute-start.13) | collective-permute-done | bytes 147488 | tf_op jit(solution)/shard_map/ppermute | solution.py:269
  92.2 0.9 finish.1
  (18 shorter events, 0.1 us)
Async XLA Ops:
  2.6 19.8 %collective-permute-start = (bf16[72,2048]{1,0:T(8,128)(2,1)}, bf16[72,2048]{1,0:T(8,128)(2,1)S(1)}, u32[]{:S(2)}, u32[]{:S(2)}) collective-permute-start(bf16[72,2048]{1,0:T(8,128)(2,1)} %prepare_keys.1.refs_0_), channel_id=1, source_target_pairs={{0,4},{4,0},{8,12},{12,8},{16,20},{24,28},{1,5},{5,1},{9,13},{13,9... | collective-permute-start | bytes 884744 | tf_op jit(solution)/shard_map/ppermute | solution.py:269
  7.5 17.8 %collective-permute-start.1 = (bf16[72,2048]{1,0:T(8,128)(2,1)}, bf16[72,2048]{1,0:T(8,128)(2,1)S(1)}, u32[]{:S(2)}, u32[]{:S(2)}) collective-permute-start(bf16[72,2048]{1,0:T(8,128)(2,1)} %prepare_keys.1.refs_0_), channel_id=1, source_target_pairs={{0,8},{4,12},{8,0},{12,4},{16,24},{20,28},{1,9},{5,13},{9,1},{13,5... | collective-permute-start | bytes 884744 | tf_op jit(solution)/shard_map/ppermute | solution.py:269
  12.0 13.3 %collective-permute-start.2 = (bf16[72,2048]{1,0:T(8,128)(2,1)}, bf16[72,2048]{1,0:T(8,128)(2,1)S(1)}, u32[]{:S(2)}, u32[]{:S(2)}) collective-permute-start(bf16[72,2048]{1,0:T(8,128)(2,1)} %prepare_keys.1.refs_0_), channel_id=1, source_target_pairs={{0,16},{4,20},{8,24},{12,28},{1,17},{5,21},{9,25},{13,29},{2,18},{... | collective-permute-start | bytes 884744 | tf_op jit(solution)/shard_map/ppermute | solution.py:277
  15.5 0.7 copy-start.1
  16.2 1.3 %copy-start.2 = (bf16[72,8192]{1,0:T(8,128)(2,1)S(1)}, bf16[72,8192]{1,0:T(8,128)(2,1)}, u32[]{:S(2)}) copy-start(bf16[72,8192]{1,0:T(8,128)(2,1)} %query_ref.1) | copy-start | bytes 3538948
  17.5 1.3 %copy-start.3 = (bf16[72,8192]{1,0:T(8,128)(2,1)S(1)}, bf16[72,8192]{1,0:T(8,128)(2,1)}, u32[]{:S(2)}) copy-start(bf16[72,8192]{1,0:T(8,128)(2,1)} %grad_ref.1) | copy-start | bytes 3538948
  25.4 15.1 %copy-start = (bf16[72,2048]{1,0:T(8,128)(2,1)S(1)}, bf16[72,2048]{1,0:T(8,128)(2,1)}, u32[]{:S(2)}) copy-start(bf16[72,2048]{1,0:T(8,128)(2,1)} %prepare_keys.1.refs_0_) | copy-start | bytes 884740
  25.4 15.1 %copy-start.4 = (s32[2]{0:T(128)S(1)}, s32[2]{0:T(128)}, u32[]{:S(2)}) copy-start(s32[2]{0:T(128)} %counts_ref.3) | copy-start | bytes 28
  25.4 9.6 %collective-permute-start.3 = (bf16[72,2048]{1,0:T(8,128)(2,1)S(1)}, bf16[72,2048]{1,0:T(8,128)(2,1)S(1)}, u32[]{:S(2)}, u32[]{:S(2)}) collective-permute-start(bf16[72,2048]{1,0:T(8,128)(2,1)S(1)} %collective-permute-done.1.refs_1_.refs_2_), channel_id=1, source_target_pairs={{0,4},{4,0},{8,12},{12,8},{24,28},{28,24},{1,5},{5,1},{9,13},{13,9... | collective-permute-start | bytes 884744 | tf_op jit(solution)/shard_map/ppermute | solution.py:269
  27.4 8.9 %collective-permute-start.4 = (bf16[2,72,1024]{2,1,0:T(8,128)(2,1)S(1)}, bf16[2,72,1024]{2,1,0:T(8,128)(2,1)S(1)}, u32[]{:S(2)}, u32[]{:S(2)}) collective-permute-start(bf16[2,72,1024]{2,1,0:T(8,128)(2,1)S(1)} %stack.3), channel_id=1, source_target_pairs={{0,16},{4,20},{8,24},{12,28},{1,17},{5,21},{9,25},{13,29},{2,18},{... | collective-permute-start | bytes 884744 | tf_op jit(solution)/shard_map/ppermute | solution.py:277
  35.0 5.5 %collective-permute-start.6 = (bf16[1,72,1024]{2,1,0:T(8,128)(2,1)S(1)}, bf16[1,72,1024]{2,1,0:T(8,128)(2,1)S(1)}, u32[]{:S(2)}, u32[]{:S(2)}) collective-permute-start(bf16[1,72,1024]{2,1,0:T(8,128)(2,1)S(1)} %stack.5), channel_id=1, source_target_pairs={{0,16},{4,20},{8,24},{12,28},{1,17},{5,21},{9,25},{13,29},{2,18},{... | collective-permute-start | bytes 442376 | tf_op jit(solution)/shard_map/ppermute | solution.py:277
  36.4 13.3 %collective-permute-start.5 = (bf16[3,72,1024]{2,1,0:T(8,128)(2,1)S(1)}, bf16[3,72,1024]{2,1,0:T(8,128)(2,1)S(1)}, u32[]{:S(2)}, u32[]{:S(2)}) collective-permute-start(bf16[3,72,1024]{2,1,0:T(8,128)(2,1)S(1)} %stack.4), channel_id=1, source_target_pairs={{0,16},{4,20},{8,24},{12,28},{1,17},{5,21},{9,25},{13,29},{2,18},{... | collective-permute-start | bytes 1327112 | tf_op jit(solution)/shard_map/ppermute | solution.py:277
  48.4 16.2 %collective-permute-start.8 = (bf16[4,72,1024]{2,1,0:T(8,128)(2,1)S(1)}, bf16[4,72,1024]{2,1,0:T(8,128)(2,1)S(1)}, u32[]{:S(2)}, u32[]{:S(2)}) collective-permute-start(bf16[4,72,1024]{2,1,0:T(8,128)(2,1)S(1)} %get-tuple-element.60), channel_id=1, source_target_pairs={{16,0},{20,4},{24,8},{28,12},{17,1},{21,5},{25,9},{29,13},{18,2},{... | collective-permute-start | bytes 1769480 | tf_op jit(solution)/shard_map/ppermute | solution.py:277
  57.6 17.5 %collective-permute-start.7 = (bf16[4,72,1024]{2,1,0:T(8,128)(2,1)S(1)}, bf16[4,72,1024]{2,1,0:T(8,128)(2,1)S(1)}, u32[]{:S(2)}, u32[]{:S(2)}) collective-permute-start(bf16[4,72,1024]{2,1,0:T(8,128)(2,1)S(1)} %get-tuple-element.58), channel_id=1, source_target_pairs={{16,0},{20,4},{24,8},{28,12},{17,1},{21,5},{25,9},{29,13},{18,2},{... | collective-permute-start | bytes 1769480 | tf_op jit(solution)/shard_map/ppermute | solution.py:277
  64.7 18.1 %collective-permute-start.10 = (bf16[72,1024]{1,0:T(8,128)(2,1)S(1)}, bf16[72,1024]{1,0:T(8,128)(2,1)S(1)}, u32[]{:S(2)}, u32[]{:S(2)}) collective-permute-start(bf16[72,1024]{1,0:T(8,128)(2,1)S(1)} %get-tuple-element.64), channel_id=1, source_target_pairs={{0,8},{4,12},{8,0},{12,4},{24,16},{28,20},{1,9},{5,13},{9,1},{13,5... | collective-permute-start | bytes 442376 | tf_op jit(solution)/shard_map/ppermute | solution.py:269
  70.7 15.6 %collective-permute-start.11 = (bf16[72,1024]{1,0:T(8,128)(2,1)S(1)}, bf16[72,1024]{1,0:T(8,128)(2,1)S(1)}, u32[]{:S(2)}, u32[]{:S(2)}) collective-permute-start(bf16[72,1024]{1,0:T(8,128)(2,1)S(1)} %get-tuple-element.65), channel_id=1, source_target_pairs={{0,12},{4,8},{8,4},{12,0},{24,20},{28,16},{1,13},{5,9},{9,5},{13,1... | collective-permute-start | bytes 442376 | tf_op jit(solution)/shard_map/ppermute | solution.py:269
  72.6 13.6 %collective-permute-start.9 = (bf16[72,1024]{1,0:T(8,128)(2,1)S(1)}, bf16[72,1024]{1,0:T(8,128)(2,1)S(1)}, u32[]{:S(2)}, u32[]{:S(2)}) collective-permute-start(bf16[72,1024]{1,0:T(8,128)(2,1)S(1)} %get-tuple-element.63), channel_id=1, source_target_pairs={{0,4},{4,0},{8,12},{12,8},{20,16},{28,24},{1,5},{5,1},{9,13},{13,9... | collective-permute-start | bytes 442376 | tf_op jit(solution)/shard_map/ppermute | solution.py:269
  75.3 11.0 %collective-permute-start.12 = (bf16[72,1024]{1,0:T(8,128)(2,1)S(1)}, bf16[72,1024]{1,0:T(8,128)(2,1)S(1)}, u32[]{:S(2)}, u32[]{:S(2)}) collective-permute-start(bf16[72,1024]{1,0:T(8,128)(2,1)S(1)} %get-tuple-element.69), channel_id=1, source_target_pairs={{0,4},{4,0},{8,12},{12,8},{20,16},{28,24},{1,5},{5,1},{9,13},{13,9... | collective-permute-start | bytes 442376 | tf_op jit(solution)/shard_map/ppermute | solution.py:269
  78.6 13.6 %collective-permute-start.13 = (bf16[72,1024]{1,0:T(8,128)(2,1)S(1)}, bf16[72,1024]{1,0:T(8,128)(2,1)S(1)}, u32[]{:S(2)}, u32[]{:S(2)}) collective-permute-start(bf16[72,1024]{1,0:T(8,128)(2,1)S(1)} %get-tuple-element.70), channel_id=1, source_target_pairs={{0,8},{4,12},{8,0},{12,4},{24,16},{28,20},{1,9},{5,13},{9,1},{13,5... | collective-permute-start | bytes 442376 | tf_op jit(solution)/shard_map/ppermute | solution.py:269
  82.9 9.3 %collective-permute-start.14 = (bf16[72,1024]{1,0:T(8,128)(2,1)S(1)}, bf16[72,1024]{1,0:T(8,128)(2,1)S(1)}, u32[]{:S(2)}, u32[]{:S(2)}) collective-permute-start(bf16[72,1024]{1,0:T(8,128)(2,1)S(1)} %get-tuple-element.71), channel_id=1, source_target_pairs={{0,12},{4,8},{8,4},{12,0},{24,20},{28,16},{1,13},{5,9},{9,5},{13,1... | collective-permute-start | bytes 442376 | tf_op jit(solution)/shard_map/ppermute | solution.py:269

commit v12 on v7

--- a/solution.py
+++ b/solution.py
@@ -14,6 +14,7 @@
 GROUP = QUERY_HEADS // KEY_VALUE_HEADS
 ROPE_BASE = 500000.0
 SCORE_SCALE = 1.0 / float(np.sqrt(HEAD_WIDTH))
+SCORE_TO_LOG2 = SCORE_SCALE * 1.4426950408889634
 CHUNKS = 2
 HEADS_PER_CHUNK = KEY_VALUE_HEADS // CHUNKS
 CHUNK_COLS = HEADS_PER_CHUNK * HEAD_WIDTH
@@ -152,20 +153,19 @@
     heads = range(STEP_HEADS)
     keys, values = [gathered(0, p) for p in heads], [gathered(HEADS_PER_CHUNK, p) for p in heads]
     bias, live = bias_ref[...], live_ref[0:1, :]
-    scores = [dot(keys[p][0], qt_ref[p]) * SCORE_SCALE + bias for p in heads]
-    dprobs, probs, probs_low = [], [], []
+    scores = [dot(keys[p][0], qt_ref[p]) * SCORE_TO_LOG2 + bias for p in heads]
+    probs_low = []
     for p in heads:
-        weights = jnp.exp(scores[p] - jnp.max(scores[p], 0, keepdims=True))
-        probs.append(weights * (live / jnp.sum(weights, 0, keepdims=True)))
-        probs_low.append(probs[p].astype(jnp.bfloat16))
-        dprobs.append(dot(values[p][0], gt_ref[p]))
+        weights = jnp.exp2(scores[p] - jnp.max(scores[p], 0, keepdims=True))
+        factor = live / jnp.sum(weights, 0, keepdims=True)
+        probs_low.append((weights * factor).astype(jnp.bfloat16))
     outs_t, value_parts, dscores = [], [], []
     for p in heads:
         outs_t.append(dot(values[p][1], probs_low[p]))
         value_parts.append(dot(probs_low[p], g_ref[p]))
         out_low = outs_t[p].astype(jnp.bfloat16).astype(jnp.float32)
         delta = jnp.sum(gt_ref[p].astype(jnp.float32) * out_low, 0, keepdims=True)
-        dscores.append((probs[p] * (dprobs[p] - delta)).astype(jnp.bfloat16))
+        dscores.append(probs_low[p] * (dot(values[p][0], gt_ref[p]) - delta).astype(jnp.bfloat16))
     grads_t = [dot(keys[p][1], dscores[p]) for p in heads]
     key_parts = [dot(dscores[p], q_ref[p]) * SCORE_SCALE for p in heads]
 

time: 93.8 us -> 93.2 us (level)
  Pallas kernels: 22.8 us -> 21.7 us
    pallas_call x2, Pallas kernels: 16 us -> 14.9 us  [shards(): pl.pallas_call(functools.partial(attend, seq_count, head_count, rows, inp...]
  transfers between devices with their start and end apart: 15 -> 15, of which waited for: 5 -> 5; matrix products, arithmetic and copies ran while one was open for 0% -> 0% of each run, Pallas kernels for 21% -> 20%
where the time goes in v12:
time: 93.2 us; the launch traced here: 92.6 us
  starting transfers between devices  43.9 us (47%)
  waiting for transfers between devices  22.9 us (25%)
  Pallas kernels  21.7 us (23%)
  local copies, waits for them, and re-layouts  3.23 us (3%)
    ppermute x9, starting transfers between devices, along_head(): return lax.ppermute(x, ('seq', 'head'), pairs)  33.1 us
    pallas_call x2, Pallas kernels, shards(): pl.pallas_call(functools.partial(attend, seq_count, head_count, rows, inp...  14.9 us
    ppermute x9, waiting for transfers between devices, along_head(): return lax.ppermute(x, ('seq', 'head'), pairs)  14.8 us
    ppermute x6, starting transfers between devices, along_seq(): return lax.ppermute(x, ('seq', 'head'), pairs)  10.9 us
    ppermute x6, waiting for transfers between devices, along_seq(): return lax.ppermute(x, ('seq', 'head'), pairs)  8.1 us
    pallas_call x1, Pallas kernels, shards(): pl.pallas_call(functools.partial(prepare_queries, rows), grid=(KEY_VALUE_...  3.65 us
    unnamed x10, local copies, waits for them, and re-layouts  3.23 us
    pallas_call x1, Pallas kernels, shards(): pl.pallas_call(functools.partial(prepare_keys, rows), out_shape=shape((pa...  1.96 us
  transfers between devices with their start and end apart: 15, of which 5 were waited for; matrix products, arithmetic and copies ran while one was open for 0% of the time, Pallas kernels for 20%

profile of v12, /device:TPU:0, one launch (start us, length us, event | category | flops | bytes accessed | tf_op | source)
XLA Modules:
  0.0 92.6 jit_solution(15572799620951287094)
XLA Ops:
  0.6 2.0 %prepare_keys.1.refs_0_ = bf16[72,2048]{1,0:T(8,128)(2,1)} custom-call(s32[576]{0:T(1024)} %pos_ref.3, bf16[72,1024]{1,0:T(8,128)(2,1)} %key_ref.1, bf16[72,1024]{1,0:T(8,128)(2,1)} %value_ref.1), custom_call_target="tpu_custom_call" | custom-call | tf_op jit(solution)/shard_map/prepare_keys/pallas_call | solution.py:272
  2.6 4.9 %collective-permute-start = (bf16[72,2048]{1,0:T(8,128)(2,1)}, bf16[72,2048]{1,0:T(8,128)(2,1)S(1)}, u32[]{:S(2)}, u32[]{:S(2)}) collective-permute-start(bf16[72,2048]{1,0:T(8,128)(2,1)} %prepare_keys.1.refs_0_), channel_id=1, source_target_pairs={{0,4},{4,0},{8,12},{12,8},{16,20},{24,28},{1,5},{5,1},{9,13},{13,9... | collective-permute-start | bytes 884744 | tf_op jit(solution)/shard_map/ppermute | solution.py:259
  7.5 4.5 %collective-permute-start.1 = (bf16[72,2048]{1,0:T(8,128)(2,1)}, bf16[72,2048]{1,0:T(8,128)(2,1)S(1)}, u32[]{:S(2)}, u32[]{:S(2)}) collective-permute-start(bf16[72,2048]{1,0:T(8,128)(2,1)} %prepare_keys.1.refs_0_), channel_id=1, source_target_pairs={{0,8},{4,12},{8,0},{12,4},{16,24},{20,28},{1,9},{5,13},{9,1},{13,5... | collective-permute-start | bytes 884744 | tf_op jit(solution)/shard_map/ppermute | solution.py:259
  12.0 3.5 %collective-permute-start.2 = (bf16[72,2048]{1,0:T(8,128)(2,1)}, bf16[72,2048]{1,0:T(8,128)(2,1)S(1)}, u32[]{:S(2)}, u32[]{:S(2)}) collective-permute-start(bf16[72,2048]{1,0:T(8,128)(2,1)} %prepare_keys.1.refs_0_), channel_id=1, source_target_pairs={{0,16},{4,20},{8,24},{12,28},{1,17},{5,21},{9,25},{13,29},{2,18},{... | collective-permute-start | bytes 884744 | tf_op jit(solution)/shard_map/ppermute | solution.py:267
  15.5 0.0 copy-start.1
  15.5 0.7 copy-done.1
  16.2 1.3 %copy-done.2 = bf16[72,8192]{1,0:T(8,128)(2,1)S(1)} copy-done((bf16[72,8192]{1,0:T(8,128)(2,1)S(1)}, bf16[72,8192]{1,0:T(8,128)(2,1)}, u32[]{:S(2)}) %copy-start.2) | copy-done | bytes 1179672
  17.5 1.3 %copy-done.3 = bf16[72,8192]{1,0:T(8,128)(2,1)S(1)} copy-done((bf16[72,8192]{1,0:T(8,128)(2,1)S(1)}, bf16[72,8192]{1,0:T(8,128)(2,1)}, u32[]{:S(2)}) %copy-start.3) | copy-done | bytes 1179672
  18.7 3.7 %prepare_queries.1 = (bf16[8,576,128]{2,1,0:T(8,128)(2,1)S(1)}, bf16[8,128,576]{2,1,0:T(8,128)(2,1)S(1)}, bf16[8,576,128]{2,1,0:T(8,128)(2,1)S(1)}, bf16[8,128,5...) custom-call(s32[576]{0:T(1024)S(1)} %copy-done.1, ...), custom_call_target="tpu_custom_call" | custom-call | flops 8071000064 | bytes 25830000 | tf_op jit(solution)/shard_map/prepare_queries/pallas_call | solution.py:289
  22.4 3.0 %collective-permute-done.1.refs_1_.refs_2_ = bf16[72,2048]{1,0:T(8,128)(2,1)S(1)} collective-permute-done((bf16[72,2048]{1,0:T(8,128)(2,1)}, bf16[72,2048]{1,0:T(8,128)(2,1)S(1)}, u32[]{:S(2)}, u32[]{:S(2)}) %collective-permute-start.1) | collective-permute-done | bytes 294944 | tf_op jit(solution)/shard_map/ppermute | solution.py:259
  25.4 2.0 %collective-permute-start.3 = (bf16[72,2048]{1,0:T(8,128)(2,1)S(1)}, bf16[72,2048]{1,0:T(8,128)(2,1)S(1)}, u32[]{:S(2)}, u32[]{:S(2)}) collective-permute-start(bf16[72,2048]{1,0:T(8,128)(2,1)S(1)} %collective-permute-done.1.refs_1_.refs_2_), channel_id=1, source_target_pairs={{0,4},{4,0},{8,12},{12,8},{24,28},{28,24},{1,5},{5,1},{9,13},{13,9... | collective-permute-start | bytes 884744 | tf_op jit(solution)/shard_map/ppermute | solution.py:259
  27.4 1.3 %collective-permute-start.4 = (bf16[2,72,1024]{2,1,0:T(8,128)(2,1)S(1)}, bf16[2,72,1024]{2,1,0:T(8,128)(2,1)S(1)}, u32[]{:S(2)}, u32[]{:S(2)}) collective-permute-start(bf16[2,72,1024]{2,1,0:T(8,128)(2,1)S(1)} %stack.3), channel_id=1, source_target_pairs={{0,16},{4,20},{8,24},{12,28},{1,17},{5,21},{9,25},{13,29},{2,18},{... | collective-permute-start | bytes 884744 | tf_op jit(solution)/shard_map/ppermute | solution.py:267
  28.8 6.2 %collective-permute-done.3.refs_2_.refs_0_.refs_3_ = bf16[72,2048]{1,0:T(8,128)(2,1)S(1)} collective-permute-done((bf16[72,2048]{1,0:T(8,128)(2,1)S(1)}, bf16[72,2048]{1,0:T(8,128)(2,1)S(1)}, u32[]{:S(2)}, u32[]{:S(2)}) %collective-permute-start.3) | collective-permute-done | bytes 294944 | tf_op jit(solution)/shard_map/ppermute | solution.py:259
  35.0 1.3 %collective-permute-start.6 = (bf16[1,72,1024]{2,1,0:T(8,128)(2,1)S(1)}, bf16[1,72,1024]{2,1,0:T(8,128)(2,1)S(1)}, u32[]{:S(2)}, u32[]{:S(2)}) collective-permute-start(bf16[1,72,1024]{2,1,0:T(8,128)(2,1)S(1)} %stack.5), channel_id=1, source_target_pairs={{0,16},{4,20},{8,24},{12,28},{1,17},{5,21},{9,25},{13,29},{2,18},{... | collective-permute-start | bytes 442376 | tf_op jit(solution)/shard_map/ppermute | solution.py:267
  36.3 0.0 collective-permute-done.4.refs_5_
  36.4 2.2 %collective-permute-start.5 = (bf16[3,72,1024]{2,1,0:T(8,128)(2,1)S(1)}, bf16[3,72,1024]{2,1,0:T(8,128)(2,1)S(1)}, u32[]{:S(2)}, u32[]{:S(2)}) collective-permute-start(bf16[3,72,1024]{2,1,0:T(8,128)(2,1)S(1)} %stack.4), channel_id=1, source_target_pairs={{0,16},{4,20},{8,24},{12,28},{1,17},{5,21},{9,25},{13,29},{2,18},{... | collective-permute-start | bytes 1327112 | tf_op jit(solution)/shard_map/ppermute | solution.py:267
  38.6 1.9 %collective-permute-done.6.refs_6_ = bf16[1,72,1024]{2,1,0:T(8,128)(2,1)S(1)} collective-permute-done((bf16[1,72,1024]{2,1,0:T(8,128)(2,1)S(1)}, bf16[1,72,1024]{2,1,0:T(8,128)(2,1)S(1)}, u32[]{:S(2)}, u32[]{:S(2)}) %collective-permute-start.6) | collective-permute-done | bytes 147488 | tf_op jit(solution)/shard_map/ppermute | solution.py:267
  40.5 7.4 %attend.2 = (bf16[72,8192]{1,0:T(8,128)(2,1)}, bf16[72,8192]{1,0:T(8,128)(2,1)}, bf16[4,72,1024]{2,1,0:T(8,128)(2,1)S(1)}, bf16[4,72,1024]{2,1,0:T(8,128)(2,1)S(1)}) custom-call(s32[2]{0:T(128)S(1)} %copy-done.4, bf16[72,2048]{1,0:T(8,128)(2,1)S(1)} %copy-done, bf16[72,2048]{1,0:T(8,128)(2,1)S(1)} %collective-permute-done.refs_0_.refs_1_, ...), custom_call_target="tpu_custom_call" | custom-call | flops 11530000384 | bytes 36900000 | tf_op jit(solution)/shard_map/attend/pallas_call | solution.py:347
  47.9 1.3 %collective-permute-start.8 = (bf16[4,72,1024]{2,1,0:T(8,128)(2,1)S(1)}, bf16[4,72,1024]{2,1,0:T(8,128)(2,1)S(1)}, u32[]{:S(2)}, u32[]{:S(2)}) collective-permute-start(bf16[4,72,1024]{2,1,0:T(8,128)(2,1)S(1)} %get-tuple-element.60), channel_id=1, source_target_pairs={{16,0},{20,4},{24,8},{28,12},{17,1},{21,5},{25,9},{29,13},{18,2},{... | collective-permute-start | bytes 1769480 | tf_op jit(solution)/shard_map/ppermute | solution.py:267
  49.2 7.5 %attend.3 = (bf16[72,8192]{1,0:T(8,128)(2,1)}, bf16[72,8192]{1,0:T(8,128)(2,1)}, bf16[4,72,1024]{2,1,0:T(8,128)(2,1)S(1)}, bf16[4,72,1024]{2,1,0:T(8,128)(2,1)S(1)}) custom-call(s32[2]{0:T(128)S(1)} %copy-done.4, bf16[72,2048]{1,0:T(8,128)(2,1)S(1)} %copy-done, ...), custom_call_target="tpu_custom_call", output_to_operand_aliasing={{0}: (13, {}), {1}: (14, {})} | custom-call | flops 11530000384 | bytes 36900000 | tf_op jit(solution)/shard_map/attend/pallas_call | solution.py:347
  56.7 1.3 %collective-permute-start.7 = (bf16[4,72,1024]{2,1,0:T(8,128)(2,1)S(1)}, bf16[4,72,1024]{2,1,0:T(8,128)(2,1)S(1)}, u32[]{:S(2)}, u32[]{:S(2)}) collective-permute-start(bf16[4,72,1024]{2,1,0:T(8,128)(2,1)S(1)} %get-tuple-element.58), channel_id=1, source_target_pairs={{16,0},{20,4},{24,8},{28,12},{17,1},{21,5},{25,9},{29,13},{18,2},{... | collective-permute-start | bytes 1769480 | tf_op jit(solution)/shard_map/ppermute | solution.py:267
  57.9 6.2 %collective-permute-done.8.refs_1_ = bf16[4,72,1024]{2,1,0:T(8,128)(2,1)S(1)} collective-permute-done((bf16[4,72,1024]{2,1,0:T(8,128)(2,1)S(1)}, bf16[4,72,1024]{2,1,0:T(8,128)(2,1)S(1)}, u32[]{:S(2)}, u32[]{:S(2)}) %collective-permute-start.8) | collective-permute-done | bytes 589856 | tf_op jit(solution)/shard_map/ppermute | solution.py:267
  64.2 0.1 combine.2
  64.3 6.2 %collective-permute-start.10 = (bf16[72,1024]{1,0:T(8,128)(2,1)S(1)}, bf16[72,1024]{1,0:T(8,128)(2,1)S(1)}, u32[]{:S(2)}, u32[]{:S(2)}) collective-permute-start(bf16[72,1024]{1,0:T(8,128)(2,1)S(1)} %get-tuple-element.64), channel_id=1, source_target_pairs={{0,8},{4,12},{8,0},{12,4},{24,16},{28,20},{1,9},{5,13},{9,1},{13,5... | collective-permute-start | bytes 442376 | tf_op jit(solution)/shard_map/ppermute | solution.py:259
  70.5 2.0 %collective-permute-start.11 = (bf16[72,1024]{1,0:T(8,128)(2,1)S(1)}, bf16[72,1024]{1,0:T(8,128)(2,1)S(1)}, u32[]{:S(2)}, u32[]{:S(2)}) collective-permute-start(bf16[72,1024]{1,0:T(8,128)(2,1)S(1)} %get-tuple-element.65), channel_id=1, source_target_pairs={{0,12},{4,8},{8,4},{12,0},{24,20},{28,16},{1,13},{5,9},{9,5},{13,1... | collective-permute-start | bytes 442376 | tf_op jit(solution)/shard_map/ppermute | solution.py:259
  72.5 2.4 %collective-permute-start.9 = (bf16[72,1024]{1,0:T(8,128)(2,1)S(1)}, bf16[72,1024]{1,0:T(8,128)(2,1)S(1)}, u32[]{:S(2)}, u32[]{:S(2)}) collective-permute-start(bf16[72,1024]{1,0:T(8,128)(2,1)S(1)} %get-tuple-element.63), channel_id=1, source_target_pairs={{0,4},{4,0},{8,12},{12,8},{20,16},{28,24},{1,5},{5,1},{9,13},{13,9... | collective-permute-start | bytes 442376 | tf_op jit(solution)/shard_map/ppermute | solution.py:259
  74.9 0.1 combine.3
  75.1 3.4 %collective-permute-start.12 = (bf16[72,1024]{1,0:T(8,128)(2,1)S(1)}, bf16[72,1024]{1,0:T(8,128)(2,1)S(1)}, u32[]{:S(2)}, u32[]{:S(2)}) collective-permute-start(bf16[72,1024]{1,0:T(8,128)(2,1)S(1)} %get-tuple-element.69), channel_id=1, source_target_pairs={{0,4},{4,0},{8,12},{12,8},{20,16},{28,24},{1,5},{5,1},{9,13},{13,9... | collective-permute-start | bytes 442376 | tf_op jit(solution)/shard_map/ppermute | solution.py:259
  78.5 4.2 %collective-permute-start.13 = (bf16[72,1024]{1,0:T(8,128)(2,1)S(1)}, bf16[72,1024]{1,0:T(8,128)(2,1)S(1)}, u32[]{:S(2)}, u32[]{:S(2)}) collective-permute-start(bf16[72,1024]{1,0:T(8,128)(2,1)S(1)} %get-tuple-element.70), channel_id=1, source_target_pairs={{0,8},{4,12},{8,0},{12,4},{24,16},{28,20},{1,9},{5,13},{9,1},{13,5... | collective-permute-start | bytes 442376 | tf_op jit(solution)/shard_map/ppermute | solution.py:259
  82.7 3.4 %collective-permute-start.14 = (bf16[72,1024]{1,0:T(8,128)(2,1)S(1)}, bf16[72,1024]{1,0:T(8,128)(2,1)S(1)}, u32[]{:S(2)}, u32[]{:S(2)}) collective-permute-start(bf16[72,1024]{1,0:T(8,128)(2,1)S(1)} %get-tuple-element.71), channel_id=1, source_target_pairs={{0,12},{4,8},{8,4},{12,0},{24,20},{28,16},{1,13},{5,9},{9,5},{13,1... | collective-permute-start | bytes 442376 | tf_op jit(solution)/shard_map/ppermute | solution.py:259
  86.2 5.6 %collective-permute-done.13.refs_8_ = bf16[72,1024]{1,0:T(8,128)(2,1)S(1)} collective-permute-done((bf16[72,1024]{1,0:T(8,128)(2,1)S(1)}, bf16[72,1024]{1,0:T(8,128)(2,1)S(1)}, u32[]{:S(2)}, u32[]{:S(2)}) %collective-permute-start.13) | collective-permute-done | bytes 147488 | tf_op jit(solution)/shard_map/ppermute | solution.py:259
  91.7 0.9 finish.1
  (18 shorter events, 0.1 us)
Async XLA Ops:
  2.6 19.8 %collective-permute-start = (bf16[72,2048]{1,0:T(8,128)(2,1)}, bf16[72,2048]{1,0:T(8,128)(2,1)S(1)}, u32[]{:S(2)}, u32[]{:S(2)}) collective-permute-start(bf16[72,2048]{1,0:T(8,128)(2,1)} %prepare_keys.1.refs_0_), channel_id=1, source_target_pairs={{0,4},{4,0},{8,12},{12,8},{16,20},{24,28},{1,5},{5,1},{9,13},{13,9... | collective-permute-start | bytes 884744 | tf_op jit(solution)/shard_map/ppermute | solution.py:259
  7.5 17.8 %collective-permute-start.1 = (bf16[72,2048]{1,0:T(8,128)(2,1)}, bf16[72,2048]{1,0:T(8,128)(2,1)S(1)}, u32[]{:S(2)}, u32[]{:S(2)}) collective-permute-start(bf16[72,2048]{1,0:T(8,128)(2,1)} %prepare_keys.1.refs_0_), channel_id=1, source_target_pairs={{0,8},{4,12},{8,0},{12,4},{16,24},{20,28},{1,9},{5,13},{9,1},{13,5... | collective-permute-start | bytes 884744 | tf_op jit(solution)/shard_map/ppermute | solution.py:259
  12.0 13.3 %collective-permute-start.2 = (bf16[72,2048]{1,0:T(8,128)(2,1)}, bf16[72,2048]{1,0:T(8,128)(2,1)S(1)}, u32[]{:S(2)}, u32[]{:S(2)}) collective-permute-start(bf16[72,2048]{1,0:T(8,128)(2,1)} %prepare_keys.1.refs_0_), channel_id=1, source_target_pairs={{0,16},{4,20},{8,24},{12,28},{1,17},{5,21},{9,25},{13,29},{2,18},{... | collective-permute-start | bytes 884744 | tf_op jit(solution)/shard_map/ppermute | solution.py:267
  15.5 0.7 copy-start.1
  16.2 1.3 %copy-start.2 = (bf16[72,8192]{1,0:T(8,128)(2,1)S(1)}, bf16[72,8192]{1,0:T(8,128)(2,1)}, u32[]{:S(2)}) copy-start(bf16[72,8192]{1,0:T(8,128)(2,1)} %query_ref.1) | copy-start | bytes 3538948
  17.5 1.3 %copy-start.3 = (bf16[72,8192]{1,0:T(8,128)(2,1)S(1)}, bf16[72,8192]{1,0:T(8,128)(2,1)}, u32[]{:S(2)}) copy-start(bf16[72,8192]{1,0:T(8,128)(2,1)} %grad_ref.1) | copy-start | bytes 3538948
  25.4 15.1 %copy-start = (bf16[72,2048]{1,0:T(8,128)(2,1)S(1)}, bf16[72,2048]{1,0:T(8,128)(2,1)}, u32[]{:S(2)}) copy-start(bf16[72,2048]{1,0:T(8,128)(2,1)} %prepare_keys.1.refs_0_) | copy-start | bytes 884740
  25.4 15.1 %copy-start.4 = (s32[2]{0:T(128)S(1)}, s32[2]{0:T(128)}, u32[]{:S(2)}) copy-start(s32[2]{0:T(128)} %counts_ref.3) | copy-start | bytes 28
  25.4 9.6 %collective-permute-start.3 = (bf16[72,2048]{1,0:T(8,128)(2,1)S(1)}, bf16[72,2048]{1,0:T(8,128)(2,1)S(1)}, u32[]{:S(2)}, u32[]{:S(2)}) collective-permute-start(bf16[72,2048]{1,0:T(8,128)(2,1)S(1)} %collective-permute-done.1.refs_1_.refs_2_), channel_id=1, source_target_pairs={{0,4},{4,0},{8,12},{12,8},{24,28},{28,24},{1,5},{5,1},{9,13},{13,9... | collective-permute-start | bytes 884744 | tf_op jit(solution)/shard_map/ppermute | solution.py:259
  27.4 8.9 %collective-permute-start.4 = (bf16[2,72,1024]{2,1,0:T(8,128)(2,1)S(1)}, bf16[2,72,1024]{2,1,0:T(8,128)(2,1)S(1)}, u32[]{:S(2)}, u32[]{:S(2)}) collective-permute-start(bf16[2,72,1024]{2,1,0:T(8,128)(2,1)S(1)} %stack.3), channel_id=1, source_target_pairs={{0,16},{4,20},{8,24},{12,28},{1,17},{5,21},{9,25},{13,29},{2,18},{... | collective-permute-start | bytes 884744 | tf_op jit(solution)/shard_map/ppermute | solution.py:267
  35.0 5.5 %collective-permute-start.6 = (bf16[1,72,1024]{2,1,0:T(8,128)(2,1)S(1)}, bf16[1,72,1024]{2,1,0:T(8,128)(2,1)S(1)}, u32[]{:S(2)}, u32[]{:S(2)}) collective-permute-start(bf16[1,72,1024]{2,1,0:T(8,128)(2,1)S(1)} %stack.5), channel_id=1, source_target_pairs={{0,16},{4,20},{8,24},{12,28},{1,17},{5,21},{9,25},{13,29},{2,18},{... | collective-permute-start | bytes 442376 | tf_op jit(solution)/shard_map/ppermute | solution.py:267
  36.4 12.8 %collective-permute-start.5 = (bf16[3,72,1024]{2,1,0:T(8,128)(2,1)S(1)}, bf16[3,72,1024]{2,1,0:T(8,128)(2,1)S(1)}, u32[]{:S(2)}, u32[]{:S(2)}) collective-permute-start(bf16[3,72,1024]{2,1,0:T(8,128)(2,1)S(1)} %stack.4), channel_id=1, source_target_pairs={{0,16},{4,20},{8,24},{12,28},{1,17},{5,21},{9,25},{13,29},{2,18},{... | collective-permute-start | bytes 1327112 | tf_op jit(solution)/shard_map/ppermute | solution.py:267
  47.9 16.3 %collective-permute-start.8 = (bf16[4,72,1024]{2,1,0:T(8,128)(2,1)S(1)}, bf16[4,72,1024]{2,1,0:T(8,128)(2,1)S(1)}, u32[]{:S(2)}, u32[]{:S(2)}) collective-permute-start(bf16[4,72,1024]{2,1,0:T(8,128)(2,1)S(1)} %get-tuple-element.60), channel_id=1, source_target_pairs={{16,0},{20,4},{24,8},{28,12},{17,1},{21,5},{25,9},{29,13},{18,2},{... | collective-permute-start | bytes 1769480 | tf_op jit(solution)/shard_map/ppermute | solution.py:267
  56.7 18.3 %collective-permute-start.7 = (bf16[4,72,1024]{2,1,0:T(8,128)(2,1)S(1)}, bf16[4,72,1024]{2,1,0:T(8,128)(2,1)S(1)}, u32[]{:S(2)}, u32[]{:S(2)}) collective-permute-start(bf16[4,72,1024]{2,1,0:T(8,128)(2,1)S(1)} %get-tuple-element.58), channel_id=1, source_target_pairs={{16,0},{20,4},{24,8},{28,12},{17,1},{21,5},{25,9},{29,13},{18,2},{... | collective-permute-start | bytes 1769480 | tf_op jit(solution)/shard_map/ppermute | solution.py:267
  64.3 18.5 %collective-permute-start.10 = (bf16[72,1024]{1,0:T(8,128)(2,1)S(1)}, bf16[72,1024]{1,0:T(8,128)(2,1)S(1)}, u32[]{:S(2)}, u32[]{:S(2)}) collective-permute-start(bf16[72,1024]{1,0:T(8,128)(2,1)S(1)} %get-tuple-element.64), channel_id=1, source_target_pairs={{0,8},{4,12},{8,0},{12,4},{24,16},{28,20},{1,9},{5,13},{9,1},{13,5... | collective-permute-start | bytes 442376 | tf_op jit(solution)/shard_map/ppermute | solution.py:259
  70.5 15.6 %collective-permute-start.11 = (bf16[72,1024]{1,0:T(8,128)(2,1)S(1)}, bf16[72,1024]{1,0:T(8,128)(2,1)S(1)}, u32[]{:S(2)}, u32[]{:S(2)}) collective-permute-start(bf16[72,1024]{1,0:T(8,128)(2,1)S(1)} %get-tuple-element.65), channel_id=1, source_target_pairs={{0,12},{4,8},{8,4},{12,0},{24,20},{28,16},{1,13},{5,9},{9,5},{13,1... | collective-permute-start | bytes 442376 | tf_op jit(solution)/shard_map/ppermute | solution.py:259
  72.5 13.6 %collective-permute-start.9 = (bf16[72,1024]{1,0:T(8,128)(2,1)S(1)}, bf16[72,1024]{1,0:T(8,128)(2,1)S(1)}, u32[]{:S(2)}, u32[]{:S(2)}) collective-permute-start(bf16[72,1024]{1,0:T(8,128)(2,1)S(1)} %get-tuple-element.63), channel_id=1, source_target_pairs={{0,4},{4,0},{8,12},{12,8},{20,16},{28,24},{1,5},{5,1},{9,13},{13,9... | collective-permute-start | bytes 442376 | tf_op jit(solution)/shard_map/ppermute | solution.py:259
  75.1 11.1 %collective-permute-start.12 = (bf16[72,1024]{1,0:T(8,128)(2,1)S(1)}, bf16[72,1024]{1,0:T(8,128)(2,1)S(1)}, u32[]{:S(2)}, u32[]{:S(2)}) collective-permute-start(bf16[72,1024]{1,0:T(8,128)(2,1)S(1)} %get-tuple-element.69), channel_id=1, source_target_pairs={{0,4},{4,0},{8,12},{12,8},{20,16},{28,24},{1,5},{5,1},{9,13},{13,9... | collective-permute-start | bytes 442376 | tf_op jit(solution)/shard_map/ppermute | solution.py:259
  78.5 13.2 %collective-permute-start.13 = (bf16[72,1024]{1,0:T(8,128)(2,1)S(1)}, bf16[72,1024]{1,0:T(8,128)(2,1)S(1)}, u32[]{:S(2)}, u32[]{:S(2)}) collective-permute-start(bf16[72,1024]{1,0:T(8,128)(2,1)S(1)} %get-tuple-element.70), channel_id=1, source_target_pairs={{0,8},{4,12},{8,0},{12,4},{24,16},{28,20},{1,9},{5,13},{9,1},{13,5... | collective-permute-start | bytes 442376 | tf_op jit(solution)/shard_map/ppermute | solution.py:259
  82.7 9.0 %collective-permute-start.14 = (bf16[72,1024]{1,0:T(8,128)(2,1)S(1)}, bf16[72,1024]{1,0:T(8,128)(2,1)S(1)}, u32[]{:S(2)}, u32[]{:S(2)}) collective-permute-start(bf16[72,1024]{1,0:T(8,128)(2,1)S(1)} %get-tuple-element.71), channel_id=1, source_target_pairs={{0,12},{4,8},{8,4},{12,0},{24,20},{28,16},{1,13},{5,9},{9,5},{13,1... | collective-permute-start | bytes 442376 | tf_op jit(solution)/shard_map/ppermute | solution.py:259

commit v13 on v12

--- a/solution.py
+++ b/solution.py
@@ -381,7 +381,10 @@
             compiler_params=params(8),
             name="combine",
         )(*mine)
-        summed += [base] + [along_head(x, j + 1, False) for j, x in enumerate(sends)]
+        order = [*enumerate(sends, 1)]
+        if mine is parts[-1]:
+            order.reverse()
+        summed += [base] + [along_head(x, j, False) for j, x in order]
 
     narrow = shape((padded, KEY_VALUE_HEADS * HEAD_WIDTH), bf16)
     key_grad, value_grad = pl.pallas_call(

time: 93.2 us -> 93.7 us (level)
  waiting for transfers between devices: 22.9 us -> 24.2 us
    ppermute x9, waiting for transfers between devices: 14.8 us -> 16.1 us  [along_head(): return lax.ppermute(x, ('seq', 'head'), pairs)]
  transfers between devices with their start and end apart: 15 -> 15, of which waited for: 5 -> 7; matrix products, arithmetic and copies ran while one was open for 0% -> 0% of each run, Pallas kernels for 20% -> 20%
where the time goes in v13:
time: 93.7 us; the launch traced here: 93.1 us
  starting transfers between devices  43 us (46%)
  waiting for transfers between devices  24.2 us (26%)
  Pallas kernels  21.7 us (23%)
  local copies, waits for them, and re-layouts  3.23 us (3%)
    ppermute x9, starting transfers between devices, along_head(): return lax.ppermute(x, ('seq', 'head'), pairs)  32.2 us
    ppermute x9, waiting for transfers between devices, along_head(): return lax.ppermute(x, ('seq', 'head'), pairs)  16.1 us
    pallas_call x2, Pallas kernels, shards(): pl.pallas_call(functools.partial(attend, seq_count, head_count, rows, inp...  14.9 us
    ppermute x6, starting transfers between devices, along_seq(): return lax.ppermute(x, ('seq', 'head'), pairs)  10.9 us
    ppermute x6, waiting for transfers between devices, along_seq(): return lax.ppermute(x, ('seq', 'head'), pairs)  8.1 us
    pallas_call x1, Pallas kernels, shards(): pl.pallas_call(functools.partial(prepare_queries, rows), grid=(KEY_VALUE_...  3.65 us
    unnamed x10, local copies, waits for them, and re-layouts  3.23 us
    pallas_call x1, Pallas kernels, shards(): pl.pallas_call(functools.partial(prepare_keys, rows), out_shape=shape((pa...  1.96 us
  transfers between devices with their start and end apart: 15, of which 7 were waited for; matrix products, arithmetic and copies ran while one was open for 0% of the time, Pallas kernels for 20%

profile of v13, /device:TPU:0, one launch (start us, length us, event | category | flops | bytes accessed | tf_op | source)
XLA Modules:
  0.0 93.1 jit_solution(18053757317182439572)
XLA Ops:
  0.6 2.0 %prepare_keys.1.refs_0_ = bf16[72,2048]{1,0:T(8,128)(2,1)} custom-call(s32[576]{0:T(1024)} %pos_ref.3, bf16[72,1024]{1,0:T(8,128)(2,1)} %key_ref.1, bf16[72,1024]{1,0:T(8,128)(2,1)} %value_ref.1), custom_call_target="tpu_custom_call" | custom-call | tf_op jit(solution)/shard_map/prepare_keys/pallas_call | solution.py:272
  2.6 4.9 %collective-permute-start = (bf16[72,2048]{1,0:T(8,128)(2,1)}, bf16[72,2048]{1,0:T(8,128)(2,1)S(1)}, u32[]{:S(2)}, u32[]{:S(2)}) collective-permute-start(bf16[72,2048]{1,0:T(8,128)(2,1)} %prepare_keys.1.refs_0_), channel_id=1, source_target_pairs={{0,4},{4,0},{8,12},{12,8},{16,20},{24,28},{1,5},{5,1},{9,13},{13,9... | collective-permute-start | bytes 884744 | tf_op jit(solution)/shard_map/ppermute | solution.py:259
  7.5 4.5 %collective-permute-start.1 = (bf16[72,2048]{1,0:T(8,128)(2,1)}, bf16[72,2048]{1,0:T(8,128)(2,1)S(1)}, u32[]{:S(2)}, u32[]{:S(2)}) collective-permute-start(bf16[72,2048]{1,0:T(8,128)(2,1)} %prepare_keys.1.refs_0_), channel_id=1, source_target_pairs={{0,8},{4,12},{8,0},{12,4},{16,24},{20,28},{1,9},{5,13},{9,1},{13,5... | collective-permute-start | bytes 884744 | tf_op jit(solution)/shard_map/ppermute | solution.py:259
  12.0 3.5 %collective-permute-start.2 = (bf16[72,2048]{1,0:T(8,128)(2,1)}, bf16[72,2048]{1,0:T(8,128)(2,1)S(1)}, u32[]{:S(2)}, u32[]{:S(2)}) collective-permute-start(bf16[72,2048]{1,0:T(8,128)(2,1)} %prepare_keys.1.refs_0_), channel_id=1, source_target_pairs={{0,16},{4,20},{8,24},{12,28},{1,17},{5,21},{9,25},{13,29},{2,18},{... | collective-permute-start | bytes 884744 | tf_op jit(solution)/shard_map/ppermute | solution.py:267
  15.5 0.7 copy-done.1
  16.2 1.3 %copy-done.2 = bf16[72,8192]{1,0:T(8,128)(2,1)S(1)} copy-done((bf16[72,8192]{1,0:T(8,128)(2,1)S(1)}, bf16[72,8192]{1,0:T(8,128)(2,1)}, u32[]{:S(2)}) %copy-start.2) | copy-done | bytes 1179672
  17.5 1.3 %copy-done.3 = bf16[72,8192]{1,0:T(8,128)(2,1)S(1)} copy-done((bf16[72,8192]{1,0:T(8,128)(2,1)S(1)}, bf16[72,8192]{1,0:T(8,128)(2,1)}, u32[]{:S(2)}) %copy-start.3) | copy-done | bytes 1179672
  18.7 3.7 %prepare_queries.1 = (bf16[8,576,128]{2,1,0:T(8,128)(2,1)S(1)}, bf16[8,128,576]{2,1,0:T(8,128)(2,1)S(1)}, bf16[8,576,128]{2,1,0:T(8,128)(2,1)S(1)}, bf16[8,128,5...) custom-call(s32[576]{0:T(1024)S(1)} %copy-done.1, ...), custom_call_target="tpu_custom_call" | custom-call | flops 8071000064 | bytes 25830000 | tf_op jit(solution)/shard_map/prepare_queries/pallas_call | solution.py:289
  22.4 3.0 %collective-permute-done.1.refs_1_.refs_2_ = bf16[72,2048]{1,0:T(8,128)(2,1)S(1)} collective-permute-done((bf16[72,2048]{1,0:T(8,128)(2,1)}, bf16[72,2048]{1,0:T(8,128)(2,1)S(1)}, u32[]{:S(2)}, u32[]{:S(2)}) %collective-permute-start.1) | collective-permute-done | bytes 294944 | tf_op jit(solution)/shard_map/ppermute | solution.py:259
  25.4 2.0 %collective-permute-start.3 = (bf16[72,2048]{1,0:T(8,128)(2,1)S(1)}, bf16[72,2048]{1,0:T(8,128)(2,1)S(1)}, u32[]{:S(2)}, u32[]{:S(2)}) collective-permute-start(bf16[72,2048]{1,0:T(8,128)(2,1)S(1)} %collective-permute-done.1.refs_1_.refs_2_), channel_id=1, source_target_pairs={{0,4},{4,0},{8,12},{12,8},{24,28},{28,24},{1,5},{5,1},{9,13},{13,9... | collective-permute-start | bytes 884744 | tf_op jit(solution)/shard_map/ppermute | solution.py:259
  27.4 1.3 %collective-permute-start.4 = (bf16[2,72,1024]{2,1,0:T(8,128)(2,1)S(1)}, bf16[2,72,1024]{2,1,0:T(8,128)(2,1)S(1)}, u32[]{:S(2)}, u32[]{:S(2)}) collective-permute-start(bf16[2,72,1024]{2,1,0:T(8,128)(2,1)S(1)} %stack.3), channel_id=1, source_target_pairs={{0,16},{4,20},{8,24},{12,28},{1,17},{5,21},{9,25},{13,29},{2,18},{... | collective-permute-start | bytes 884744 | tf_op jit(solution)/shard_map/ppermute | solution.py:267
  28.8 6.2 %collective-permute-done.3.refs_2_.refs_0_.refs_3_ = bf16[72,2048]{1,0:T(8,128)(2,1)S(1)} collective-permute-done((bf16[72,2048]{1,0:T(8,128)(2,1)S(1)}, bf16[72,2048]{1,0:T(8,128)(2,1)S(1)}, u32[]{:S(2)}, u32[]{:S(2)}) %collective-permute-start.3) | collective-permute-done | bytes 294944 | tf_op jit(solution)/shard_map/ppermute | solution.py:259
  35.0 1.3 %collective-permute-start.6 = (bf16[1,72,1024]{2,1,0:T(8,128)(2,1)S(1)}, bf16[1,72,1024]{2,1,0:T(8,128)(2,1)S(1)}, u32[]{:S(2)}, u32[]{:S(2)}) collective-permute-start(bf16[1,72,1024]{2,1,0:T(8,128)(2,1)S(1)} %stack.5), channel_id=1, source_target_pairs={{0,16},{4,20},{8,24},{12,28},{1,17},{5,21},{9,25},{13,29},{2,18},{... | collective-permute-start | bytes 442376 | tf_op jit(solution)/shard_map/ppermute | solution.py:267
  36.4 2.2 %collective-permute-start.5 = (bf16[3,72,1024]{2,1,0:T(8,128)(2,1)S(1)}, bf16[3,72,1024]{2,1,0:T(8,128)(2,1)S(1)}, u32[]{:S(2)}, u32[]{:S(2)}) collective-permute-start(bf16[3,72,1024]{2,1,0:T(8,128)(2,1)S(1)} %stack.4), channel_id=1, source_target_pairs={{0,16},{4,20},{8,24},{12,28},{1,17},{5,21},{9,25},{13,29},{2,18},{... | collective-permute-start | bytes 1327112 | tf_op jit(solution)/shard_map/ppermute | solution.py:267
  38.6 1.9 %collective-permute-done.6.refs_6_ = bf16[1,72,1024]{2,1,0:T(8,128)(2,1)S(1)} collective-permute-done((bf16[1,72,1024]{2,1,0:T(8,128)(2,1)S(1)}, bf16[1,72,1024]{2,1,0:T(8,128)(2,1)S(1)}, u32[]{:S(2)}, u32[]{:S(2)}) %collective-permute-start.6) | collective-permute-done | bytes 147488 | tf_op jit(solution)/shard_map/ppermute | solution.py:267
  40.5 7.4 %attend.2 = (bf16[72,8192]{1,0:T(8,128)(2,1)}, bf16[72,8192]{1,0:T(8,128)(2,1)}, bf16[4,72,1024]{2,1,0:T(8,128)(2,1)S(1)}, bf16[4,72,1024]{2,1,0:T(8,128)(2,1)S(1)}) custom-call(s32[2]{0:T(128)S(1)} %copy-done.4, bf16[72,2048]{1,0:T(8,128)(2,1)S(1)} %copy-done, bf16[72,2048]{1,0:T(8,128)(2,1)S(1)} %collective-permute-done.refs_0_.refs_1_, ...), custom_call_target="tpu_custom_call" | custom-call | flops 11530000384 | bytes 36900000 | tf_op jit(solution)/shard_map/attend/pallas_call | solution.py:347
  47.9 1.3 %collective-permute-start.8 = (bf16[4,72,1024]{2,1,0:T(8,128)(2,1)S(1)}, bf16[4,72,1024]{2,1,0:T(8,128)(2,1)S(1)}, u32[]{:S(2)}, u32[]{:S(2)}) collective-permute-start(bf16[4,72,1024]{2,1,0:T(8,128)(2,1)S(1)} %get-tuple-element.60), channel_id=1, source_target_pairs={{16,0},{20,4},{24,8},{28,12},{17,1},{21,5},{25,9},{29,13},{18,2},{... | collective-permute-start | bytes 1769480 | tf_op jit(solution)/shard_map/ppermute | solution.py:267
  49.2 7.5 %attend.3 = (bf16[72,8192]{1,0:T(8,128)(2,1)}, bf16[72,8192]{1,0:T(8,128)(2,1)}, bf16[4,72,1024]{2,1,0:T(8,128)(2,1)S(1)}, bf16[4,72,1024]{2,1,0:T(8,128)(2,1)S(1)}) custom-call(s32[2]{0:T(128)S(1)} %copy-done.4, bf16[72,2048]{1,0:T(8,128)(2,1)S(1)} %copy-done, ...), custom_call_target="tpu_custom_call", output_to_operand_aliasing={{0}: (13, {}), {1}: (14, {})} | custom-call | flops 11530000384 | bytes 36900000 | tf_op jit(solution)/shard_map/attend/pallas_call | solution.py:347
  56.7 1.3 %collective-permute-start.7 = (bf16[4,72,1024]{2,1,0:T(8,128)(2,1)S(1)}, bf16[4,72,1024]{2,1,0:T(8,128)(2,1)S(1)}, u32[]{:S(2)}, u32[]{:S(2)}) collective-permute-start(bf16[4,72,1024]{2,1,0:T(8,128)(2,1)S(1)} %get-tuple-element.58), channel_id=1, source_target_pairs={{16,0},{20,4},{24,8},{28,12},{17,1},{21,5},{25,9},{29,13},{18,2},{... | collective-permute-start | bytes 1769480 | tf_op jit(solution)/shard_map/ppermute | solution.py:267
  57.9 6.2 %collective-permute-done.8.refs_1_ = bf16[4,72,1024]{2,1,0:T(8,128)(2,1)S(1)} collective-permute-done((bf16[4,72,1024]{2,1,0:T(8,128)(2,1)S(1)}, bf16[4,72,1024]{2,1,0:T(8,128)(2,1)S(1)}, u32[]{:S(2)}, u32[]{:S(2)}) %collective-permute-start.8) | collective-permute-done | bytes 589856 | tf_op jit(solution)/shard_map/ppermute | solution.py:267
  64.2 0.1 combine.2
  64.3 6.2 %collective-permute-start.10 = (bf16[72,1024]{1,0:T(8,128)(2,1)S(1)}, bf16[72,1024]{1,0:T(8,128)(2,1)S(1)}, u32[]{:S(2)}, u32[]{:S(2)}) collective-permute-start(bf16[72,1024]{1,0:T(8,128)(2,1)S(1)} %get-tuple-element.64), channel_id=1, source_target_pairs={{0,8},{4,12},{8,0},{12,4},{24,16},{28,20},{1,9},{5,13},{9,1},{13,5... | collective-permute-start | bytes 442376 | tf_op jit(solution)/shard_map/ppermute | solution.py:259
  70.5 2.0 %collective-permute-start.11 = (bf16[72,1024]{1,0:T(8,128)(2,1)S(1)}, bf16[72,1024]{1,0:T(8,128)(2,1)S(1)}, u32[]{:S(2)}, u32[]{:S(2)}) collective-permute-start(bf16[72,1024]{1,0:T(8,128)(2,1)S(1)} %get-tuple-element.65), channel_id=1, source_target_pairs={{0,12},{4,8},{8,4},{12,0},{24,20},{28,16},{1,13},{5,9},{9,5},{13,1... | collective-permute-start | bytes 442376 | tf_op jit(solution)/shard_map/ppermute | solution.py:259
  72.5 2.4 %collective-permute-start.9 = (bf16[72,1024]{1,0:T(8,128)(2,1)S(1)}, bf16[72,1024]{1,0:T(8,128)(2,1)S(1)}, u32[]{:S(2)}, u32[]{:S(2)}) collective-permute-start(bf16[72,1024]{1,0:T(8,128)(2,1)S(1)} %get-tuple-element.63), channel_id=1, source_target_pairs={{0,4},{4,0},{8,12},{12,8},{20,16},{28,24},{1,5},{5,1},{9,13},{13,9... | collective-permute-start | bytes 442376 | tf_op jit(solution)/shard_map/ppermute | solution.py:259
  74.9 0.1 combine.3
  75.1 5.2 %collective-permute-start.12 = (bf16[72,1024]{1,0:T(8,128)(2,1)S(1)}, bf16[72,1024]{1,0:T(8,128)(2,1)S(1)}, u32[]{:S(2)}, u32[]{:S(2)}) collective-permute-start(bf16[72,1024]{1,0:T(8,128)(2,1)S(1)} %get-tuple-element.69), channel_id=1, source_target_pairs={{0,12},{4,8},{8,4},{12,0},{24,20},{28,16},{1,13},{5,9},{9,5},{13,1... | collective-permute-start | bytes 442376 | tf_op jit(solution)/shard_map/ppermute | solution.py:259
  80.3 2.5 %collective-permute-start.13 = (bf16[72,1024]{1,0:T(8,128)(2,1)S(1)}, bf16[72,1024]{1,0:T(8,128)(2,1)S(1)}, u32[]{:S(2)}, u32[]{:S(2)}) collective-permute-start(bf16[72,1024]{1,0:T(8,128)(2,1)S(1)} %get-tuple-element.70), channel_id=1, source_target_pairs={{0,8},{4,12},{8,0},{12,4},{24,16},{28,20},{1,9},{5,13},{9,1},{13,5... | collective-permute-start | bytes 442376 | tf_op jit(solution)/shard_map/ppermute | solution.py:259
  82.7 2.5 %collective-permute-start.14 = (bf16[72,1024]{1,0:T(8,128)(2,1)S(1)}, bf16[72,1024]{1,0:T(8,128)(2,1)S(1)}, u32[]{:S(2)}, u32[]{:S(2)}) collective-permute-start(bf16[72,1024]{1,0:T(8,128)(2,1)S(1)} %get-tuple-element.71), channel_id=1, source_target_pairs={{0,4},{4,0},{8,12},{12,8},{20,16},{28,24},{1,5},{5,1},{9,13},{13,9... | collective-permute-start | bytes 442376 | tf_op jit(solution)/shard_map/ppermute | solution.py:259
  85.2 0.3 collective-permute-done.12.refs_7_
  85.5 6.2 %collective-permute-done.13.refs_8_ = bf16[72,1024]{1,0:T(8,128)(2,1)S(1)} collective-permute-done((bf16[72,1024]{1,0:T(8,128)(2,1)S(1)}, bf16[72,1024]{1,0:T(8,128)(2,1)S(1)}, u32[]{:S(2)}, u32[]{:S(2)}) %collective-permute-start.13) | collective-permute-done | bytes 147488 | tf_op jit(solution)/shard_map/ppermute | solution.py:259
  91.8 0.4 collective-permute-done.14.refs_9_
  92.2 0.9 finish.1
  (18 shorter events, 0.1 us)
Async XLA Ops:
  2.6 19.8 %collective-permute-start = (bf16[72,2048]{1,0:T(8,128)(2,1)}, bf16[72,2048]{1,0:T(8,128)(2,1)S(1)}, u32[]{:S(2)}, u32[]{:S(2)}) collective-permute-start(bf16[72,2048]{1,0:T(8,128)(2,1)} %prepare_keys.1.refs_0_), channel_id=1, source_target_pairs={{0,4},{4,0},{8,12},{12,8},{16,20},{24,28},{1,5},{5,1},{9,13},{13,9... | collective-permute-start | bytes 884744 | tf_op jit(solution)/shard_map/ppermute | solution.py:259
  7.5 17.8 %collective-permute-start.1 = (bf16[72,2048]{1,0:T(8,128)(2,1)}, bf16[72,2048]{1,0:T(8,128)(2,1)S(1)}, u32[]{:S(2)}, u32[]{:S(2)}) collective-permute-start(bf16[72,2048]{1,0:T(8,128)(2,1)} %prepare_keys.1.refs_0_), channel_id=1, source_target_pairs={{0,8},{4,12},{8,0},{12,4},{16,24},{20,28},{1,9},{5,13},{9,1},{13,5... | collective-permute-start | bytes 884744 | tf_op jit(solution)/shard_map/ppermute | solution.py:259
  12.0 13.3 %collective-permute-start.2 = (bf16[72,2048]{1,0:T(8,128)(2,1)}, bf16[72,2048]{1,0:T(8,128)(2,1)S(1)}, u32[]{:S(2)}, u32[]{:S(2)}) collective-permute-start(bf16[72,2048]{1,0:T(8,128)(2,1)} %prepare_keys.1.refs_0_), channel_id=1, source_target_pairs={{0,16},{4,20},{8,24},{12,28},{1,17},{5,21},{9,25},{13,29},{2,18},{... | collective-permute-start | bytes 884744 | tf_op jit(solution)/shard_map/ppermute | solution.py:267
  15.5 0.7 copy-start.1
  16.2 1.3 %copy-start.2 = (bf16[72,8192]{1,0:T(8,128)(2,1)S(1)}, bf16[72,8192]{1,0:T(8,128)(2,1)}, u32[]{:S(2)}) copy-start(bf16[72,8192]{1,0:T(8,128)(2,1)} %query_ref.1) | copy-start | bytes 3538948
  17.5 1.3 %copy-start.3 = (bf16[72,8192]{1,0:T(8,128)(2,1)S(1)}, bf16[72,8192]{1,0:T(8,128)(2,1)}, u32[]{:S(2)}) copy-start(bf16[72,8192]{1,0:T(8,128)(2,1)} %grad_ref.1) | copy-start | bytes 3538948
  25.4 15.1 %copy-start = (bf16[72,2048]{1,0:T(8,128)(2,1)S(1)}, bf16[72,2048]{1,0:T(8,128)(2,1)}, u32[]{:S(2)}) copy-start(bf16[72,2048]{1,0:T(8,128)(2,1)} %prepare_keys.1.refs_0_) | copy-start | bytes 884740
  25.4 15.1 %copy-start.4 = (s32[2]{0:T(128)S(1)}, s32[2]{0:T(128)}, u32[]{:S(2)}) copy-start(s32[2]{0:T(128)} %counts_ref.3) | copy-start | bytes 28
  25.4 9.6 %collective-permute-start.3 = (bf16[72,2048]{1,0:T(8,128)(2,1)S(1)}, bf16[72,2048]{1,0:T(8,128)(2,1)S(1)}, u32[]{:S(2)}, u32[]{:S(2)}) collective-permute-start(bf16[72,2048]{1,0:T(8,128)(2,1)S(1)} %collective-permute-done.1.refs_1_.refs_2_), channel_id=1, source_target_pairs={{0,4},{4,0},{8,12},{12,8},{24,28},{28,24},{1,5},{5,1},{9,13},{13,9... | collective-permute-start | bytes 884744 | tf_op jit(solution)/shard_map/ppermute | solution.py:259
  27.4 8.9 %collective-permute-start.4 = (bf16[2,72,1024]{2,1,0:T(8,128)(2,1)S(1)}, bf16[2,72,1024]{2,1,0:T(8,128)(2,1)S(1)}, u32[]{:S(2)}, u32[]{:S(2)}) collective-permute-start(bf16[2,72,1024]{2,1,0:T(8,128)(2,1)S(1)} %stack.3), channel_id=1, source_target_pairs={{0,16},{4,20},{8,24},{12,28},{1,17},{5,21},{9,25},{13,29},{2,18},{... | collective-permute-start | bytes 884744 | tf_op jit(solution)/shard_map/ppermute | solution.py:267
  35.0 5.5 %collective-permute-start.6 = (bf16[1,72,1024]{2,1,0:T(8,128)(2,1)S(1)}, bf16[1,72,1024]{2,1,0:T(8,128)(2,1)S(1)}, u32[]{:S(2)}, u32[]{:S(2)}) collective-permute-start(bf16[1,72,1024]{2,1,0:T(8,128)(2,1)S(1)} %stack.5), channel_id=1, source_target_pairs={{0,16},{4,20},{8,24},{12,28},{1,17},{5,21},{9,25},{13,29},{2,18},{... | collective-permute-start | bytes 442376 | tf_op jit(solution)/shard_map/ppermute | solution.py:267
  36.4 12.8 %collective-permute-start.5 = (bf16[3,72,1024]{2,1,0:T(8,128)(2,1)S(1)}, bf16[3,72,1024]{2,1,0:T(8,128)(2,1)S(1)}, u32[]{:S(2)}, u32[]{:S(2)}) collective-permute-start(bf16[3,72,1024]{2,1,0:T(8,128)(2,1)S(1)} %stack.4), channel_id=1, source_target_pairs={{0,16},{4,20},{8,24},{12,28},{1,17},{5,21},{9,25},{13,29},{2,18},{... | collective-permute-start | bytes 1327112 | tf_op jit(solution)/shard_map/ppermute | solution.py:267
  47.9 16.3 %collective-permute-start.8 = (bf16[4,72,1024]{2,1,0:T(8,128)(2,1)S(1)}, bf16[4,72,1024]{2,1,0:T(8,128)(2,1)S(1)}, u32[]{:S(2)}, u32[]{:S(2)}) collective-permute-start(bf16[4,72,1024]{2,1,0:T(8,128)(2,1)S(1)} %get-tuple-element.60), channel_id=1, source_target_pairs={{16,0},{20,4},{24,8},{28,12},{17,1},{21,5},{25,9},{29,13},{18,2},{... | collective-permute-start | bytes 1769480 | tf_op jit(solution)/shard_map/ppermute | solution.py:267
  56.7 18.3 %collective-permute-start.7 = (bf16[4,72,1024]{2,1,0:T(8,128)(2,1)S(1)}, bf16[4,72,1024]{2,1,0:T(8,128)(2,1)S(1)}, u32[]{:S(2)}, u32[]{:S(2)}) collective-permute-start(bf16[4,72,1024]{2,1,0:T(8,128)(2,1)S(1)} %get-tuple-element.58), channel_id=1, source_target_pairs={{16,0},{20,4},{24,8},{28,12},{17,1},{21,5},{25,9},{29,13},{18,2},{... | collective-permute-start | bytes 1769480 | tf_op jit(solution)/shard_map/ppermute | solution.py:267
  64.3 18.5 %collective-permute-start.10 = (bf16[72,1024]{1,0:T(8,128)(2,1)S(1)}, bf16[72,1024]{1,0:T(8,128)(2,1)S(1)}, u32[]{:S(2)}, u32[]{:S(2)}) collective-permute-start(bf16[72,1024]{1,0:T(8,128)(2,1)S(1)} %get-tuple-element.64), channel_id=1, source_target_pairs={{0,8},{4,12},{8,0},{12,4},{24,16},{28,20},{1,9},{5,13},{9,1},{13,5... | collective-permute-start | bytes 442376 | tf_op jit(solution)/shard_map/ppermute | solution.py:259
  70.5 14.7 %collective-permute-start.11 = (bf16[72,1024]{1,0:T(8,128)(2,1)S(1)}, bf16[72,1024]{1,0:T(8,128)(2,1)S(1)}, u32[]{:S(2)}, u32[]{:S(2)}) collective-permute-start(bf16[72,1024]{1,0:T(8,128)(2,1)S(1)} %get-tuple-element.65), channel_id=1, source_target_pairs={{0,12},{4,8},{8,4},{12,0},{24,20},{28,16},{1,13},{5,9},{9,5},{13,1... | collective-permute-start | bytes 442376 | tf_op jit(solution)/shard_map/ppermute | solution.py:259
  72.5 12.7 %collective-permute-start.9 = (bf16[72,1024]{1,0:T(8,128)(2,1)S(1)}, bf16[72,1024]{1,0:T(8,128)(2,1)S(1)}, u32[]{:S(2)}, u32[]{:S(2)}) collective-permute-start(bf16[72,1024]{1,0:T(8,128)(2,1)S(1)} %get-tuple-element.63), channel_id=1, source_target_pairs={{0,4},{4,0},{8,12},{12,8},{20,16},{28,24},{1,5},{5,1},{9,13},{13,9... | collective-permute-start | bytes 442376 | tf_op jit(solution)/shard_map/ppermute | solution.py:259
  75.1 10.5 %collective-permute-start.12 = (bf16[72,1024]{1,0:T(8,128)(2,1)S(1)}, bf16[72,1024]{1,0:T(8,128)(2,1)S(1)}, u32[]{:S(2)}, u32[]{:S(2)}) collective-permute-start(bf16[72,1024]{1,0:T(8,128)(2,1)S(1)} %get-tuple-element.69), channel_id=1, source_target_pairs={{0,12},{4,8},{8,4},{12,0},{24,20},{28,16},{1,13},{5,9},{9,5},{13,1... | collective-permute-start | bytes 442376 | tf_op jit(solution)/shard_map/ppermute | solution.py:259
  80.3 11.5 %collective-permute-start.13 = (bf16[72,1024]{1,0:T(8,128)(2,1)S(1)}, bf16[72,1024]{1,0:T(8,128)(2,1)S(1)}, u32[]{:S(2)}, u32[]{:S(2)}) collective-permute-start(bf16[72,1024]{1,0:T(8,128)(2,1)S(1)} %get-tuple-element.70), channel_id=1, source_target_pairs={{0,8},{4,12},{8,0},{12,4},{24,16},{28,20},{1,9},{5,13},{9,1},{13,5... | collective-permute-start | bytes 442376 | tf_op jit(solution)/shard_map/ppermute | solution.py:259
  82.7 9.4 %collective-permute-start.14 = (bf16[72,1024]{1,0:T(8,128)(2,1)S(1)}, bf16[72,1024]{1,0:T(8,128)(2,1)S(1)}, u32[]{:S(2)}, u32[]{:S(2)}) collective-permute-start(bf16[72,1024]{1,0:T(8,128)(2,1)S(1)} %get-tuple-element.71), channel_id=1, source_target_pairs={{0,4},{4,0},{8,12},{12,8},{20,16},{28,24},{1,5},{5,1},{9,13},{13,9... | collective-permute-start | bytes 442376 | tf_op jit(solution)/shard_map/ppermute | solution.py:259

commit v14 on v12

--- a/solution.py
+++ b/solution.py
@@ -321,7 +321,7 @@
         return {a: along_seq(held, a, True) for a in later}
 
     crossed = [[cross(0, range(1, last)), cross(0, [last])]]
-    near[last], crossed[0][0] = lax.optimization_barrier((near[last], crossed[0][0]))
+    near[last], crossed[0] = lax.optimization_barrier((near[last], crossed[0]))
     crossed += [[cross(chunk, range(1, head_count))] for chunk in range(1, CHUNKS)]
 
     wide_outs = ()

time: 93.2 us -> 96.9 us (1.040)
  waiting for transfers between devices: 22.9 us -> 25 us
  starting transfers between devices: 43.9 us -> 45.4 us
    ppermute x6, starting transfers between devices: 10.9 us -> 13 us  [along_seq(): return lax.ppermute(x, ('seq', 'head'), pairs)]
    ppermute x6, waiting for transfers between devices: 8.1 us -> 10.1 us  [along_seq(): return lax.ppermute(x, ('seq', 'head'), pairs)]
  transfers between devices with their start and end apart: 15 -> 15, of which waited for: 5 -> 6; matrix products, arithmetic and copies ran while one was open for 0% -> 0% of each run, Pallas kernels for 20% -> 20%
where the time goes in v14:
time: 96.9 us; the launch traced here: 96.3 us
  starting transfers between devices  45.4 us (47%)
  waiting for transfers between devices  25 us (26%)
  Pallas kernels  21.8 us (22%)
  local copies, waits for them, and re-layouts  3.23 us (3%)
    ppermute x9, starting transfers between devices, along_head(): return lax.ppermute(x, ('seq', 'head'), pairs)  32.4 us
    pallas_call x2, Pallas kernels, shards(): pl.pallas_call(functools.partial(attend, seq_count, head_count, rows, inp...  14.9 us
    ppermute x9, waiting for transfers between devices, along_head(): return lax.ppermute(x, ('seq', 'head'), pairs)  14.9 us
    ppermute x6, starting transfers between devices, along_seq(): return lax.ppermute(x, ('seq', 'head'), pairs)  13 us
    ppermute x6, waiting for transfers between devices, along_seq(): return lax.ppermute(x, ('seq', 'head'), pairs)  10.1 us
    pallas_call x1, Pallas kernels, shards(): pl.pallas_call(functools.partial(prepare_queries, rows), grid=(KEY_VALUE_...  3.65 us
    unnamed x10, local copies, waits for them, and re-layouts  3.23 us
    pallas_call x1, Pallas kernels, shards(): pl.pallas_call(functools.partial(prepare_keys, rows), out_shape=shape((pa...  1.96 us
  transfers between devices with their start and end apart: 15, of which 6 were waited for; matrix products, arithmetic and copies ran while one was open for 0% of the time, Pallas kernels for 20%

profile of v14, /device:TPU:0, one launch (start us, length us, event | category | flops | bytes accessed | tf_op | source)
XLA Modules:
  0.0 96.3 jit_solution(5708261333431951766)
XLA Ops:
  0.6 2.0 %prepare_keys.1.refs_0_ = bf16[72,2048]{1,0:T(8,128)(2,1)} custom-call(s32[576]{0:T(1024)} %pos_ref.3, bf16[72,1024]{1,0:T(8,128)(2,1)} %key_ref.1, bf16[72,1024]{1,0:T(8,128)(2,1)} %value_ref.1), custom_call_target="tpu_custom_call" | custom-call | tf_op jit(solution)/shard_map/prepare_keys/pallas_call | solution.py:272
  2.6 4.9 %collective-permute-start = (bf16[72,2048]{1,0:T(8,128)(2,1)}, bf16[72,2048]{1,0:T(8,128)(2,1)S(1)}, u32[]{:S(2)}, u32[]{:S(2)}) collective-permute-start(bf16[72,2048]{1,0:T(8,128)(2,1)} %prepare_keys.1.refs_0_), channel_id=1, source_target_pairs={{0,4},{4,0},{8,12},{12,8},{16,20},{24,28},{1,5},{5,1},{9,13},{13,9... | collective-permute-start | bytes 884744 | tf_op jit(solution)/shard_map/ppermute | solution.py:259
  7.5 4.5 %collective-permute-start.1 = (bf16[72,2048]{1,0:T(8,128)(2,1)}, bf16[72,2048]{1,0:T(8,128)(2,1)S(1)}, u32[]{:S(2)}, u32[]{:S(2)}) collective-permute-start(bf16[72,2048]{1,0:T(8,128)(2,1)} %prepare_keys.1.refs_0_), channel_id=1, source_target_pairs={{0,8},{4,12},{8,0},{12,4},{16,24},{20,28},{1,9},{5,13},{9,1},{13,5... | collective-permute-start | bytes 884744 | tf_op jit(solution)/shard_map/ppermute | solution.py:259
  12.0 3.5 %collective-permute-start.2 = (bf16[72,2048]{1,0:T(8,128)(2,1)}, bf16[72,2048]{1,0:T(8,128)(2,1)S(1)}, u32[]{:S(2)}, u32[]{:S(2)}) collective-permute-start(bf16[72,2048]{1,0:T(8,128)(2,1)} %prepare_keys.1.refs_0_), channel_id=1, source_target_pairs={{0,16},{4,20},{8,24},{12,28},{1,17},{5,21},{9,25},{13,29},{2,18},{... | collective-permute-start | bytes 884744 | tf_op jit(solution)/shard_map/ppermute | solution.py:267
  15.5 0.0 copy-start.1
  15.5 0.7 copy-done.1
  16.2 1.3 %copy-done.2 = bf16[72,8192]{1,0:T(8,128)(2,1)S(1)} copy-done((bf16[72,8192]{1,0:T(8,128)(2,1)S(1)}, bf16[72,8192]{1,0:T(8,128)(2,1)}, u32[]{:S(2)}) %copy-start.2) | copy-done | bytes 1179672
  17.5 1.3 %copy-done.3 = bf16[72,8192]{1,0:T(8,128)(2,1)S(1)} copy-done((bf16[72,8192]{1,0:T(8,128)(2,1)S(1)}, bf16[72,8192]{1,0:T(8,128)(2,1)}, u32[]{:S(2)}) %copy-start.3) | copy-done | bytes 1179672
  18.7 3.7 %prepare_queries.1 = (bf16[8,576,128]{2,1,0:T(8,128)(2,1)S(1)}, bf16[8,128,576]{2,1,0:T(8,128)(2,1)S(1)}, bf16[8,576,128]{2,1,0:T(8,128)(2,1)S(1)}, bf16[8,128,5...) custom-call(s32[576]{0:T(1024)S(1)} %copy-done.1, ...), custom_call_target="tpu_custom_call" | custom-call | flops 8071000064 | bytes 25830000 | tf_op jit(solution)/shard_map/prepare_queries/pallas_call | solution.py:289
  22.4 3.0 %collective-permute-done.1.refs_1_.refs_2_ = bf16[72,2048]{1,0:T(8,128)(2,1)S(1)} collective-permute-done((bf16[72,2048]{1,0:T(8,128)(2,1)}, bf16[72,2048]{1,0:T(8,128)(2,1)S(1)}, u32[]{:S(2)}, u32[]{:S(2)}) %collective-permute-start.1) | collective-permute-done | bytes 294944 | tf_op jit(solution)/shard_map/ppermute | solution.py:259
  25.4 2.0 %collective-permute-start.3 = (bf16[72,2048]{1,0:T(8,128)(2,1)S(1)}, bf16[72,2048]{1,0:T(8,128)(2,1)S(1)}, u32[]{:S(2)}, u32[]{:S(2)}) collective-permute-start(bf16[72,2048]{1,0:T(8,128)(2,1)S(1)} %collective-permute-done.1.refs_1_.refs_2_), channel_id=1, source_target_pairs={{0,4},{4,0},{8,12},{12,8},{24,28},{28,24},{1,5},{5,1},{9,13},{13,9... | collective-permute-start | bytes 884744 | tf_op jit(solution)/shard_map/ppermute | solution.py:259
  27.4 1.3 %collective-permute-start.4 = (bf16[2,72,1024]{2,1,0:T(8,128)(2,1)S(1)}, bf16[2,72,1024]{2,1,0:T(8,128)(2,1)S(1)}, u32[]{:S(2)}, u32[]{:S(2)}) collective-permute-start(bf16[2,72,1024]{2,1,0:T(8,128)(2,1)S(1)} %stack.3), channel_id=1, source_target_pairs={{0,16},{4,20},{8,24},{12,28},{1,17},{5,21},{9,25},{13,29},{2,18},{... | collective-permute-start | bytes 884744 | tf_op jit(solution)/shard_map/ppermute | solution.py:267
  28.8 6.2 %collective-permute-done.3.refs_0_.refs_2_.refs_3_ = bf16[72,2048]{1,0:T(8,128)(2,1)S(1)} collective-permute-done((bf16[72,2048]{1,0:T(8,128)(2,1)S(1)}, bf16[72,2048]{1,0:T(8,128)(2,1)S(1)}, u32[]{:S(2)}, u32[]{:S(2)}) %collective-permute-start.3) | collective-permute-done | bytes 294944 | tf_op jit(solution)/shard_map/ppermute | solution.py:259
  35.0 1.3 %collective-permute-start.5 = (bf16[1,72,1024]{2,1,0:T(8,128)(2,1)S(1)}, bf16[1,72,1024]{2,1,0:T(8,128)(2,1)S(1)}, u32[]{:S(2)}, u32[]{:S(2)}) collective-permute-start(bf16[1,72,1024]{2,1,0:T(8,128)(2,1)S(1)} %stack.4), channel_id=1, source_target_pairs={{0,16},{4,20},{8,24},{12,28},{1,17},{5,21},{9,25},{13,29},{2,18},{... | collective-permute-start | bytes 442376 | tf_op jit(solution)/shard_map/ppermute | solution.py:267
  36.3 2.6 %collective-permute-done.5.refs_6_ = bf16[1,72,1024]{2,1,0:T(8,128)(2,1)S(1)} collective-permute-done((bf16[1,72,1024]{2,1,0:T(8,128)(2,1)S(1)}, bf16[1,72,1024]{2,1,0:T(8,128)(2,1)S(1)}, u32[]{:S(2)}, u32[]{:S(2)}) %collective-permute-start.5) | collective-permute-done | bytes 147488 | tf_op jit(solution)/shard_map/ppermute | solution.py:267
  39.0 4.4 %collective-permute-start.6 = (bf16[3,72,1024]{2,1,0:T(8,128)(2,1)S(1)}, bf16[3,72,1024]{2,1,0:T(8,128)(2,1)S(1)}, u32[]{:S(2)}, u32[]{:S(2)}) collective-permute-start(bf16[3,72,1024]{2,1,0:T(8,128)(2,1)S(1)} %stack.5), channel_id=1, source_target_pairs={{0,16},{4,20},{8,24},{12,28},{1,17},{5,21},{9,25},{13,29},{2,18},{... | collective-permute-start | bytes 1327112 | tf_op jit(solution)/shard_map/ppermute | solution.py:267
  43.4 7.5 %attend.2 = (bf16[72,8192]{1,0:T(8,128)(2,1)}, bf16[72,8192]{1,0:T(8,128)(2,1)}, bf16[4,72,1024]{2,1,0:T(8,128)(2,1)S(1)}, bf16[4,72,1024]{2,1,0:T(8,128)(2,1)S(1)}) custom-call(s32[2]{0:T(128)S(1)} %copy-done.4, bf16[72,2048]{1,0:T(8,128)(2,1)S(1)} %copy-done, bf16[72,2048]{1,0:T(8,128)(2,1)S(1)} %collective-permute-done.refs_0_.refs_1_, ...), custom_call_target="tpu_custom_call" | custom-call | flops 11530000384 | bytes 36900000 | tf_op jit(solution)/shard_map/attend/pallas_call | solution.py:347
  50.9 1.3 %collective-permute-start.8 = (bf16[4,72,1024]{2,1,0:T(8,128)(2,1)S(1)}, bf16[4,72,1024]{2,1,0:T(8,128)(2,1)S(1)}, u32[]{:S(2)}, u32[]{:S(2)}) collective-permute-start(bf16[4,72,1024]{2,1,0:T(8,128)(2,1)S(1)} %get-tuple-element.62), channel_id=1, source_target_pairs={{16,0},{20,4},{24,8},{28,12},{17,1},{21,5},{25,9},{29,13},{18,2},{... | collective-permute-start | bytes 1769480 | tf_op jit(solution)/shard_map/ppermute | solution.py:267
  52.2 7.5 %attend.3 = (bf16[72,8192]{1,0:T(8,128)(2,1)}, bf16[72,8192]{1,0:T(8,128)(2,1)}, bf16[4,72,1024]{2,1,0:T(8,128)(2,1)S(1)}, bf16[4,72,1024]{2,1,0:T(8,128)(2,1)S(1)}) custom-call(s32[2]{0:T(128)S(1)} %copy-done.4, bf16[72,2048]{1,0:T(8,128)(2,1)S(1)} %copy-done, ...), custom_call_target="tpu_custom_call", output_to_operand_aliasing={{0}: (13, {}), {1}: (14, {})} | custom-call | flops 11530000384 | bytes 36900000 | tf_op jit(solution)/shard_map/attend/pallas_call | solution.py:347
  59.7 1.3 %collective-permute-start.7 = (bf16[4,72,1024]{2,1,0:T(8,128)(2,1)S(1)}, bf16[4,72,1024]{2,1,0:T(8,128)(2,1)S(1)}, u32[]{:S(2)}, u32[]{:S(2)}) collective-permute-start(bf16[4,72,1024]{2,1,0:T(8,128)(2,1)S(1)} %get-tuple-element.60), channel_id=1, source_target_pairs={{16,0},{20,4},{24,8},{28,12},{17,1},{21,5},{25,9},{29,13},{18,2},{... | collective-permute-start | bytes 1769480 | tf_op jit(solution)/shard_map/ppermute | solution.py:267
  60.9 7.4 %collective-permute-done.8.refs_1_ = bf16[4,72,1024]{2,1,0:T(8,128)(2,1)S(1)} collective-permute-done((bf16[4,72,1024]{2,1,0:T(8,128)(2,1)S(1)}, bf16[4,72,1024]{2,1,0:T(8,128)(2,1)S(1)}, u32[]{:S(2)}, u32[]{:S(2)}) %collective-permute-start.8) | collective-permute-done | bytes 589856 | tf_op jit(solution)/shard_map/ppermute | solution.py:267
  68.4 0.1 combine.2
  68.5 5.5 %collective-permute-start.10 = (bf16[72,1024]{1,0:T(8,128)(2,1)S(1)}, bf16[72,1024]{1,0:T(8,128)(2,1)S(1)}, u32[]{:S(2)}, u32[]{:S(2)}) collective-permute-start(bf16[72,1024]{1,0:T(8,128)(2,1)S(1)} %get-tuple-element.66), channel_id=1, source_target_pairs={{0,8},{4,12},{8,0},{12,4},{24,16},{28,20},{1,9},{5,13},{9,1},{13,5... | collective-permute-start | bytes 442376 | tf_op jit(solution)/shard_map/ppermute | solution.py:259
  74.0 2.5 %collective-permute-start.11 = (bf16[72,1024]{1,0:T(8,128)(2,1)S(1)}, bf16[72,1024]{1,0:T(8,128)(2,1)S(1)}, u32[]{:S(2)}, u32[]{:S(2)}) collective-permute-start(bf16[72,1024]{1,0:T(8,128)(2,1)S(1)} %get-tuple-element.67), channel_id=1, source_target_pairs={{0,12},{4,8},{8,4},{12,0},{24,20},{28,16},{1,13},{5,9},{9,5},{13,1... | collective-permute-start | bytes 442376 | tf_op jit(solution)/shard_map/ppermute | solution.py:259
  76.5 2.5 %collective-permute-start.9 = (bf16[72,1024]{1,0:T(8,128)(2,1)S(1)}, bf16[72,1024]{1,0:T(8,128)(2,1)S(1)}, u32[]{:S(2)}, u32[]{:S(2)}) collective-permute-start(bf16[72,1024]{1,0:T(8,128)(2,1)S(1)} %get-tuple-element.65), channel_id=1, source_target_pairs={{0,4},{4,0},{8,12},{12,8},{20,16},{28,24},{1,5},{5,1},{9,13},{13,9... | collective-permute-start | bytes 442376 | tf_op jit(solution)/shard_map/ppermute | solution.py:259
  79.0 0.1 combine.3
  79.1 3.4 %collective-permute-start.12 = (bf16[72,1024]{1,0:T(8,128)(2,1)S(1)}, bf16[72,1024]{1,0:T(8,128)(2,1)S(1)}, u32[]{:S(2)}, u32[]{:S(2)}) collective-permute-start(bf16[72,1024]{1,0:T(8,128)(2,1)S(1)} %get-tuple-element.71), channel_id=1, source_target_pairs={{0,4},{4,0},{8,12},{12,8},{20,16},{28,24},{1,5},{5,1},{9,13},{13,9... | collective-permute-start | bytes 442376 | tf_op jit(solution)/shard_map/ppermute | solution.py:259
  82.5 3.9 %collective-permute-start.13 = (bf16[72,1024]{1,0:T(8,128)(2,1)S(1)}, bf16[72,1024]{1,0:T(8,128)(2,1)S(1)}, u32[]{:S(2)}, u32[]{:S(2)}) collective-permute-start(bf16[72,1024]{1,0:T(8,128)(2,1)S(1)} %get-tuple-element.72), channel_id=1, source_target_pairs={{0,8},{4,12},{8,0},{12,4},{24,16},{28,20},{1,9},{5,13},{9,1},{13,5... | collective-permute-start | bytes 442376 | tf_op jit(solution)/shard_map/ppermute | solution.py:259
  86.5 3.2 %collective-permute-start.14 = (bf16[72,1024]{1,0:T(8,128)(2,1)S(1)}, bf16[72,1024]{1,0:T(8,128)(2,1)S(1)}, u32[]{:S(2)}, u32[]{:S(2)}) collective-permute-start(bf16[72,1024]{1,0:T(8,128)(2,1)S(1)} %get-tuple-element.73), channel_id=1, source_target_pairs={{0,12},{4,8},{8,4},{12,0},{24,20},{28,16},{1,13},{5,9},{9,5},{13,1... | collective-permute-start | bytes 442376 | tf_op jit(solution)/shard_map/ppermute | solution.py:259
  89.7 4.1 %collective-permute-done.13.refs_8_ = bf16[72,1024]{1,0:T(8,128)(2,1)S(1)} collective-permute-done((bf16[72,1024]{1,0:T(8,128)(2,1)S(1)}, bf16[72,1024]{1,0:T(8,128)(2,1)S(1)}, u32[]{:S(2)}, u32[]{:S(2)}) %collective-permute-start.13) | collective-permute-done | bytes 147488 | tf_op jit(solution)/shard_map/ppermute | solution.py:259
  93.8 1.6 %collective-permute-done.14.refs_9_ = bf16[72,1024]{1,0:T(8,128)(2,1)S(1)} collective-permute-done((bf16[72,1024]{1,0:T(8,128)(2,1)S(1)}, bf16[72,1024]{1,0:T(8,128)(2,1)S(1)}, u32[]{:S(2)}, u32[]{:S(2)}) %collective-permute-start.14) | collective-permute-done | bytes 147488 | tf_op jit(solution)/shard_map/ppermute | solution.py:259
  95.4 0.9 finish.1
  (18 shorter events, 0.1 us)
Async XLA Ops:
  2.6 19.8 %collective-permute-start = (bf16[72,2048]{1,0:T(8,128)(2,1)}, bf16[72,2048]{1,0:T(8,128)(2,1)S(1)}, u32[]{:S(2)}, u32[]{:S(2)}) collective-permute-start(bf16[72,2048]{1,0:T(8,128)(2,1)} %prepare_keys.1.refs_0_), channel_id=1, source_target_pairs={{0,4},{4,0},{8,12},{12,8},{16,20},{24,28},{1,5},{5,1},{9,13},{13,9... | collective-permute-start | bytes 884744 | tf_op jit(solution)/shard_map/ppermute | solution.py:259
  7.5 17.8 %collective-permute-start.1 = (bf16[72,2048]{1,0:T(8,128)(2,1)}, bf16[72,2048]{1,0:T(8,128)(2,1)S(1)}, u32[]{:S(2)}, u32[]{:S(2)}) collective-permute-start(bf16[72,2048]{1,0:T(8,128)(2,1)} %prepare_keys.1.refs_0_), channel_id=1, source_target_pairs={{0,8},{4,12},{8,0},{12,4},{16,24},{20,28},{1,9},{5,13},{9,1},{13,5... | collective-permute-start | bytes 884744 | tf_op jit(solution)/shard_map/ppermute | solution.py:259
  12.0 13.3 %collective-permute-start.2 = (bf16[72,2048]{1,0:T(8,128)(2,1)}, bf16[72,2048]{1,0:T(8,128)(2,1)S(1)}, u32[]{:S(2)}, u32[]{:S(2)}) collective-permute-start(bf16[72,2048]{1,0:T(8,128)(2,1)} %prepare_keys.1.refs_0_), channel_id=1, source_target_pairs={{0,16},{4,20},{8,24},{12,28},{1,17},{5,21},{9,25},{13,29},{2,18},{... | collective-permute-start | bytes 884744 | tf_op jit(solution)/shard_map/ppermute | solution.py:267
  15.5 0.7 copy-start.1
  16.2 1.3 %copy-start.2 = (bf16[72,8192]{1,0:T(8,128)(2,1)S(1)}, bf16[72,8192]{1,0:T(8,128)(2,1)}, u32[]{:S(2)}) copy-start(bf16[72,8192]{1,0:T(8,128)(2,1)} %query_ref.1) | copy-start | bytes 3538948
  17.5 1.3 %copy-start.3 = (bf16[72,8192]{1,0:T(8,128)(2,1)S(1)}, bf16[72,8192]{1,0:T(8,128)(2,1)}, u32[]{:S(2)}) copy-start(bf16[72,8192]{1,0:T(8,128)(2,1)} %grad_ref.1) | copy-start | bytes 3538948
  25.4 18.0 %copy-start = (bf16[72,2048]{1,0:T(8,128)(2,1)S(1)}, bf16[72,2048]{1,0:T(8,128)(2,1)}, u32[]{:S(2)}) copy-start(bf16[72,2048]{1,0:T(8,128)(2,1)} %prepare_keys.1.refs_0_) | copy-start | bytes 884740
  25.4 18.0 %copy-start.4 = (s32[2]{0:T(128)S(1)}, s32[2]{0:T(128)}, u32[]{:S(2)}) copy-start(s32[2]{0:T(128)} %counts_ref.3) | copy-start | bytes 28
  25.4 9.6 %collective-permute-start.3 = (bf16[72,2048]{1,0:T(8,128)(2,1)S(1)}, bf16[72,2048]{1,0:T(8,128)(2,1)S(1)}, u32[]{:S(2)}, u32[]{:S(2)}) collective-permute-start(bf16[72,2048]{1,0:T(8,128)(2,1)S(1)} %collective-permute-done.1.refs_1_.refs_2_), channel_id=1, source_target_pairs={{0,4},{4,0},{8,12},{12,8},{24,28},{28,24},{1,5},{5,1},{9,13},{13,9... | collective-permute-start | bytes 884744 | tf_op jit(solution)/shard_map/ppermute | solution.py:259
  27.4 8.9 %collective-permute-start.4 = (bf16[2,72,1024]{2,1,0:T(8,128)(2,1)S(1)}, bf16[2,72,1024]{2,1,0:T(8,128)(2,1)S(1)}, u32[]{:S(2)}, u32[]{:S(2)}) collective-permute-start(bf16[2,72,1024]{2,1,0:T(8,128)(2,1)S(1)} %stack.3), channel_id=1, source_target_pairs={{0,16},{4,20},{8,24},{12,28},{1,17},{5,21},{9,25},{13,29},{2,18},{... | collective-permute-start | bytes 884744 | tf_op jit(solution)/shard_map/ppermute | solution.py:267
  35.0 4.0 %collective-permute-start.5 = (bf16[1,72,1024]{2,1,0:T(8,128)(2,1)S(1)}, bf16[1,72,1024]{2,1,0:T(8,128)(2,1)S(1)}, u32[]{:S(2)}, u32[]{:S(2)}) collective-permute-start(bf16[1,72,1024]{2,1,0:T(8,128)(2,1)S(1)} %stack.4), channel_id=1, source_target_pairs={{0,16},{4,20},{8,24},{12,28},{1,17},{5,21},{9,25},{13,29},{2,18},{... | collective-permute-start | bytes 442376 | tf_op jit(solution)/shard_map/ppermute | solution.py:267
  39.0 13.2 %collective-permute-start.6 = (bf16[3,72,1024]{2,1,0:T(8,128)(2,1)S(1)}, bf16[3,72,1024]{2,1,0:T(8,128)(2,1)S(1)}, u32[]{:S(2)}, u32[]{:S(2)}) collective-permute-start(bf16[3,72,1024]{2,1,0:T(8,128)(2,1)S(1)} %stack.5), channel_id=1, source_target_pairs={{0,16},{4,20},{8,24},{12,28},{1,17},{5,21},{9,25},{13,29},{2,18},{... | collective-permute-start | bytes 1327112 | tf_op jit(solution)/shard_map/ppermute | solution.py:267
  50.9 17.5 %collective-permute-start.8 = (bf16[4,72,1024]{2,1,0:T(8,128)(2,1)S(1)}, bf16[4,72,1024]{2,1,0:T(8,128)(2,1)S(1)}, u32[]{:S(2)}, u32[]{:S(2)}) collective-permute-start(bf16[4,72,1024]{2,1,0:T(8,128)(2,1)S(1)} %get-tuple-element.62), channel_id=1, source_target_pairs={{16,0},{20,4},{24,8},{28,12},{17,1},{21,5},{25,9},{29,13},{18,2},{... | collective-permute-start | bytes 1769480 | tf_op jit(solution)/shard_map/ppermute | solution.py:267
  59.7 19.4 %collective-permute-start.7 = (bf16[4,72,1024]{2,1,0:T(8,128)(2,1)S(1)}, bf16[4,72,1024]{2,1,0:T(8,128)(2,1)S(1)}, u32[]{:S(2)}, u32[]{:S(2)}) collective-permute-start(bf16[4,72,1024]{2,1,0:T(8,128)(2,1)S(1)} %get-tuple-element.60), channel_id=1, source_target_pairs={{16,0},{20,4},{24,8},{28,12},{17,1},{21,5},{25,9},{29,13},{18,2},{... | collective-permute-start | bytes 1769480 | tf_op jit(solution)/shard_map/ppermute | solution.py:267
  68.5 18.0 %collective-permute-start.10 = (bf16[72,1024]{1,0:T(8,128)(2,1)S(1)}, bf16[72,1024]{1,0:T(8,128)(2,1)S(1)}, u32[]{:S(2)}, u32[]{:S(2)}) collective-permute-start(bf16[72,1024]{1,0:T(8,128)(2,1)S(1)} %get-tuple-element.66), channel_id=1, source_target_pairs={{0,8},{4,12},{8,0},{12,4},{24,16},{28,20},{1,9},{5,13},{9,1},{13,5... | collective-permute-start | bytes 442376 | tf_op jit(solution)/shard_map/ppermute | solution.py:259
  74.0 15.6 %collective-permute-start.11 = (bf16[72,1024]{1,0:T(8,128)(2,1)S(1)}, bf16[72,1024]{1,0:T(8,128)(2,1)S(1)}, u32[]{:S(2)}, u32[]{:S(2)}) collective-permute-start(bf16[72,1024]{1,0:T(8,128)(2,1)S(1)} %get-tuple-element.67), channel_id=1, source_target_pairs={{0,12},{4,8},{8,4},{12,0},{24,20},{28,16},{1,13},{5,9},{9,5},{13,1... | collective-permute-start | bytes 442376 | tf_op jit(solution)/shard_map/ppermute | solution.py:259
  76.5 13.1 %collective-permute-start.9 = (bf16[72,1024]{1,0:T(8,128)(2,1)S(1)}, bf16[72,1024]{1,0:T(8,128)(2,1)S(1)}, u32[]{:S(2)}, u32[]{:S(2)}) collective-permute-start(bf16[72,1024]{1,0:T(8,128)(2,1)S(1)} %get-tuple-element.65), channel_id=1, source_target_pairs={{0,4},{4,0},{8,12},{12,8},{20,16},{28,24},{1,5},{5,1},{9,13},{13,9... | collective-permute-start | bytes 442376 | tf_op jit(solution)/shard_map/ppermute | solution.py:259
  79.1 10.5 %collective-permute-start.12 = (bf16[72,1024]{1,0:T(8,128)(2,1)S(1)}, bf16[72,1024]{1,0:T(8,128)(2,1)S(1)}, u32[]{:S(2)}, u32[]{:S(2)}) collective-permute-start(bf16[72,1024]{1,0:T(8,128)(2,1)S(1)} %get-tuple-element.71), channel_id=1, source_target_pairs={{0,4},{4,0},{8,12},{12,8},{20,16},{28,24},{1,5},{5,1},{9,13},{13,9... | collective-permute-start | bytes 442376 | tf_op jit(solution)/shard_map/ppermute | solution.py:259
  82.5 11.2 %collective-permute-start.13 = (bf16[72,1024]{1,0:T(8,128)(2,1)S(1)}, bf16[72,1024]{1,0:T(8,128)(2,1)S(1)}, u32[]{:S(2)}, u32[]{:S(2)}) collective-permute-start(bf16[72,1024]{1,0:T(8,128)(2,1)S(1)} %get-tuple-element.72), channel_id=1, source_target_pairs={{0,8},{4,12},{8,0},{12,4},{24,16},{28,20},{1,9},{5,13},{9,1},{13,5... | collective-permute-start | bytes 442376 | tf_op jit(solution)/shard_map/ppermute | solution.py:259
  86.5 8.9 %collective-permute-start.14 = (bf16[72,1024]{1,0:T(8,128)(2,1)S(1)}, bf16[72,1024]{1,0:T(8,128)(2,1)S(1)}, u32[]{:S(2)}, u32[]{:S(2)}) collective-permute-start(bf16[72,1024]{1,0:T(8,128)(2,1)S(1)} %get-tuple-element.73), channel_id=1, source_target_pairs={{0,12},{4,8},{8,4},{12,0},{24,20},{28,16},{1,13},{5,9},{9,5},{13,1... | collective-permute-start | bytes 442376 | tf_op jit(solution)/shard_map/ppermute | solution.py:259

commit v15 on v12

--- a/solution.py
+++ b/solution.py
@@ -301,9 +301,11 @@
     bits = [1 << b for b in reversed(range((head_count - 1).bit_length()))]
     later = range(1, seq_count)
     last = head_count - 1
-    near = {0: own, **{j: along_head(own, j, True) for j in sorted({bits[0], 1}, reverse=True)}}
-    far = {a: along_seq(own, a, True) for a in later}
-    near, cosine_t, far = lax.optimization_barrier((near, cosine_t, far))
+    near = {j: along_head(own, j, True) for j in sorted({bits[0], 1}, reverse=True)}
+    crossing, cosine_t = lax.optimization_barrier((own, cosine_t))
+    far = {a: along_seq(crossing, a, True) for a in later}
+    near[1], far, cosine_t = lax.optimization_barrier((near[1], far, cosine_t))
+    near[0] = own
     for bit in bits[1:]:
         near.update(
             {j ^ bit: along_head(x, bit, True, j) for j, x in near.items() if j ^ bit not in near}

time: 93.2 us -> 98.2 us (1.054)
  starting transfers between devices: 43.9 us -> 46.9 us
  waiting for transfers between devices: 22.9 us -> 24.9 us
    ppermute x9, waiting for transfers between devices: 14.8 us -> 17 us  [along_head(): return lax.ppermute(x, ('seq', 'head'), pairs)]
    ppermute x6, starting transfers between devices: 10.9 us -> 13 us  [along_seq(): return lax.ppermute(x, ('seq', 'head'), pairs)]
  transfers between devices with their start and end apart: 15 -> 15, of which waited for: 5 -> 5; matrix products, arithmetic and copies ran while one was open for 0% -> 0% of each run, Pallas kernels for 20% -> 19%
where the time goes in v15:
time: 98.2 us; the launch traced here: 97.6 us
  starting transfers between devices  46.9 us (48%)
  waiting for transfers between devices  24.9 us (25%)
  Pallas kernels  21.8 us (22%)
  local copies, waits for them, and re-layouts  3.23 us (3%)
    ppermute x9, starting transfers between devices, along_head(): return lax.ppermute(x, ('seq', 'head'), pairs)  33.8 us
    ppermute x9, waiting for transfers between devices, along_head(): return lax.ppermute(x, ('seq', 'head'), pairs)  17 us
    pallas_call x2, Pallas kernels, shards(): pl.pallas_call(functools.partial(attend, seq_count, head_count, rows, inp...  14.9 us
    ppermute x6, starting transfers between devices, along_seq(): return lax.ppermute(x, ('seq', 'head'), pairs)  13 us
    ppermute x6, waiting for transfers between devices, along_seq(): return lax.ppermute(x, ('seq', 'head'), pairs)  7.94 us
    pallas_call x1, Pallas kernels, shards(): pl.pallas_call(functools.partial(prepare_queries, rows), grid=(KEY_VALUE_...  3.65 us
    unnamed x10, local copies, waits for them, and re-layouts  3.23 us
  transfers between devices with their start and end apart: 15, of which 5 were waited for; matrix products, arithmetic and copies ran while one was open for 0% of the time, Pallas kernels for 19%

profile of v15, /device:TPU:0, one launch (start us, length us, event | category | flops | bytes accessed | tf_op | source)
XLA Modules:
  0.0 97.6 jit_solution(2384246937033744639)
XLA Ops:
  0.6 2.0 %prepare_keys.1.refs_0_ = bf16[72,2048]{1,0:T(8,128)(2,1)} custom-call(s32[576]{0:T(1024)} %pos_ref.3, bf16[72,1024]{1,0:T(8,128)(2,1)} %key_ref.1, bf16[72,1024]{1,0:T(8,128)(2,1)} %value_ref.1), custom_call_target="tpu_custom_call" | custom-call | tf_op jit(solution)/shard_map/prepare_keys/pallas_call | solution.py:272
  2.6 6.1 %collective-permute-start.2 = (bf16[72,2048]{1,0:T(8,128)(2,1)}, bf16[72,2048]{1,0:T(8,128)(2,1)S(1)}, u32[]{:S(2)}, u32[]{:S(2)}) collective-permute-start(bf16[72,2048]{1,0:T(8,128)(2,1)} %prepare_keys.1.refs_0_), channel_id=1, source_target_pairs={{0,8},{4,12},{8,0},{12,4},{16,24},{20,28},{1,9},{5,13},{9,1},{13,5... | collective-permute-start | bytes 884744 | tf_op jit(solution)/shard_map/ppermute | solution.py:259
  8.7 0.0 copy-start.1
  8.7 0.7 copy-done.1
  9.4 1.3 %copy-done.2 = bf16[72,8192]{1,0:T(8,128)(2,1)S(1)} copy-done((bf16[72,8192]{1,0:T(8,128)(2,1)S(1)}, bf16[72,8192]{1,0:T(8,128)(2,1)}, u32[]{:S(2)}) %copy-start.2) | copy-done | bytes 1179672
  10.6 1.3 %copy-done.3 = bf16[72,8192]{1,0:T(8,128)(2,1)S(1)} copy-done((bf16[72,8192]{1,0:T(8,128)(2,1)S(1)}, bf16[72,8192]{1,0:T(8,128)(2,1)}, u32[]{:S(2)}) %copy-start.3) | copy-done | bytes 1179672
  11.9 3.7 %prepare_queries.1 = (bf16[8,576,128]{2,1,0:T(8,128)(2,1)S(1)}, bf16[8,128,576]{2,1,0:T(8,128)(2,1)S(1)}, bf16[8,576,128]{2,1,0:T(8,128)(2,1)S(1)}, bf16[8,128,5...) custom-call(s32[576]{0:T(1024)S(1)} %copy-done.1, ...), custom_call_target="tpu_custom_call" | custom-call | flops 8071000064 | bytes 25830000 | tf_op jit(solution)/shard_map/prepare_queries/pallas_call | solution.py:289
  15.6 3.5 %collective-permute-start.1 = (bf16[72,2048]{1,0:T(8,128)(2,1)S(1)}, bf16[72,2048]{1,0:T(8,128)(2,1)S(1)}, u32[]{:S(2)}, u32[]{:S(2)}) collective-permute-start(bf16[72,2048]{1,0:T(8,128)(2,1)S(1)} %copy-done), channel_id=1, source_target_pairs={{0,16},{4,20},{8,24},{12,28},{1,17},{5,21},{9,25},{13,29},{2,18},{... | collective-permute-start | bytes 884744 | tf_op jit(solution)/shard_map/ppermute | solution.py:267
  19.0 3.5 %collective-permute-start = (bf16[72,2048]{1,0:T(8,128)(2,1)S(1)}, bf16[72,2048]{1,0:T(8,128)(2,1)S(1)}, u32[]{:S(2)}, u32[]{:S(2)}) collective-permute-start(bf16[72,2048]{1,0:T(8,128)(2,1)S(1)} %copy-done), channel_id=1, source_target_pairs={{0,4},{4,0},{8,12},{12,8},{16,20},{24,28},{1,5},{5,1},{9,13},{13,9... | collective-permute-start | bytes 884744 | tf_op jit(solution)/shard_map/ppermute | solution.py:259
  22.5 2.4 %collective-permute-start.3 = (bf16[72,2048]{1,0:T(8,128)(2,1)S(1)}, bf16[72,2048]{1,0:T(8,128)(2,1)S(1)}, u32[]{:S(2)}, u32[]{:S(2)}) collective-permute-start(bf16[72,2048]{1,0:T(8,128)(2,1)S(1)} %collective-permute-done.2.refs_1_.refs_2_), channel_id=1, source_target_pairs={{0,4},{4,0},{8,12},{12,8},{24,28},{28,24},{1,5},{5,1},{9,13},{13,9... | collective-permute-start | bytes 884744 | tf_op jit(solution)/shard_map/ppermute | solution.py:259
  25.0 0.0 collective-permute-done.1.refs_4_
  25.0 5.9 %collective-permute-done.refs_0_.refs_1_ = bf16[72,2048]{1,0:T(8,128)(2,1)S(1)} collective-permute-done((bf16[72,2048]{1,0:T(8,128)(2,1)S(1)}, bf16[72,2048]{1,0:T(8,128)(2,1)S(1)}, u32[]{:S(2)}, u32[]{:S(2)}) %collective-permute-start) | collective-permute-done | bytes 294944 | tf_op jit(solution)/shard_map/ppermute | solution.py:259
  30.9 1.3 %collective-permute-start.4 = (bf16[2,72,1024]{2,1,0:T(8,128)(2,1)S(1)}, bf16[2,72,1024]{2,1,0:T(8,128)(2,1)S(1)}, u32[]{:S(2)}, u32[]{:S(2)}) collective-permute-start(bf16[2,72,1024]{2,1,0:T(8,128)(2,1)S(1)} %stack.3), channel_id=1, source_target_pairs={{0,16},{4,20},{8,24},{12,28},{1,17},{5,21},{9,25},{13,29},{2,18},{... | collective-permute-start | bytes 884744 | tf_op jit(solution)/shard_map/ppermute | solution.py:267
  32.2 3.2 %collective-permute-done.3.refs_2_.refs_0_.refs_3_ = bf16[72,2048]{1,0:T(8,128)(2,1)S(1)} collective-permute-done((bf16[72,2048]{1,0:T(8,128)(2,1)S(1)}, bf16[72,2048]{1,0:T(8,128)(2,1)S(1)}, u32[]{:S(2)}, u32[]{:S(2)}) %collective-permute-start.3) | collective-permute-done | bytes 294944 | tf_op jit(solution)/shard_map/ppermute | solution.py:259
  35.5 1.3 %collective-permute-start.6 = (bf16[1,72,1024]{2,1,0:T(8,128)(2,1)S(1)}, bf16[1,72,1024]{2,1,0:T(8,128)(2,1)S(1)}, u32[]{:S(2)}, u32[]{:S(2)}) collective-permute-start(bf16[1,72,1024]{2,1,0:T(8,128)(2,1)S(1)} %stack.5), channel_id=1, source_target_pairs={{0,16},{4,20},{8,24},{12,28},{1,17},{5,21},{9,25},{13,29},{2,18},{... | collective-permute-start | bytes 442376 | tf_op jit(solution)/shard_map/ppermute | solution.py:267
  36.8 0.5 collective-permute-done.4.refs_5_
  37.3 4.4 %collective-permute-start.5 = (bf16[3,72,1024]{2,1,0:T(8,128)(2,1)S(1)}, bf16[3,72,1024]{2,1,0:T(8,128)(2,1)S(1)}, u32[]{:S(2)}, u32[]{:S(2)}) collective-permute-start(bf16[3,72,1024]{2,1,0:T(8,128)(2,1)S(1)} %stack.4), channel_id=1, source_target_pairs={{0,16},{4,20},{8,24},{12,28},{1,17},{5,21},{9,25},{13,29},{2,18},{... | collective-permute-start | bytes 1327112 | tf_op jit(solution)/shard_map/ppermute | solution.py:267
  41.8 7.5 %attend.2 = (bf16[72,8192]{1,0:T(8,128)(2,1)}, bf16[72,8192]{1,0:T(8,128)(2,1)}, bf16[4,72,1024]{2,1,0:T(8,128)(2,1)S(1)}, bf16[4,72,1024]{2,1,0:T(8,128)(2,1)S(1)}) custom-call(s32[2]{0:T(128)S(1)} %copy-done.4, bf16[72,2048]{1,0:T(8,128)(2,1)S(1)} %copy-done, bf16[72,2048]{1,0:T(8,128)(2,1)S(1)} %collective-permute-done.refs_0_.refs_1_, ...), custom_call_target="tpu_custom_call" | custom-call | flops 11530000384 | bytes 36900000 | tf_op jit(solution)/shard_map/attend/pallas_call | solution.py:349
  49.2 1.3 %collective-permute-start.8 = (bf16[4,72,1024]{2,1,0:T(8,128)(2,1)S(1)}, bf16[4,72,1024]{2,1,0:T(8,128)(2,1)S(1)}, u32[]{:S(2)}, u32[]{:S(2)}) collective-permute-start(bf16[4,72,1024]{2,1,0:T(8,128)(2,1)S(1)} %get-tuple-element.60), channel_id=1, source_target_pairs={{16,0},{20,4},{24,8},{28,12},{17,1},{21,5},{25,9},{29,13},{18,2},{... | collective-permute-start | bytes 1769480 | tf_op jit(solution)/shard_map/ppermute | solution.py:267
  50.5 7.5 %attend.3 = (bf16[72,8192]{1,0:T(8,128)(2,1)}, bf16[72,8192]{1,0:T(8,128)(2,1)}, bf16[4,72,1024]{2,1,0:T(8,128)(2,1)S(1)}, bf16[4,72,1024]{2,1,0:T(8,128)(2,1)S(1)}) custom-call(s32[2]{0:T(128)S(1)} %copy-done.4, bf16[72,2048]{1,0:T(8,128)(2,1)S(1)} %copy-done, ...), custom_call_target="tpu_custom_call", output_to_operand_aliasing={{0}: (13, {}), {1}: (14, {})} | custom-call | flops 11530000384 | bytes 36900000 | tf_op jit(solution)/shard_map/attend/pallas_call | solution.py:349
  58.0 1.3 %collective-permute-start.7 = (bf16[4,72,1024]{2,1,0:T(8,128)(2,1)S(1)}, bf16[4,72,1024]{2,1,0:T(8,128)(2,1)S(1)}, u32[]{:S(2)}, u32[]{:S(2)}) collective-permute-start(bf16[4,72,1024]{2,1,0:T(8,128)(2,1)S(1)} %get-tuple-element.58), channel_id=1, source_target_pairs={{16,0},{20,4},{24,8},{28,12},{17,1},{21,5},{25,9},{29,13},{18,2},{... | collective-permute-start | bytes 1769480 | tf_op jit(solution)/shard_map/ppermute | solution.py:267
  59.3 7.3 %collective-permute-done.8.refs_1_ = bf16[4,72,1024]{2,1,0:T(8,128)(2,1)S(1)} collective-permute-done((bf16[4,72,1024]{2,1,0:T(8,128)(2,1)S(1)}, bf16[4,72,1024]{2,1,0:T(8,128)(2,1)S(1)}, u32[]{:S(2)}, u32[]{:S(2)}) %collective-permute-start.8) | collective-permute-done | bytes 589856 | tf_op jit(solution)/shard_map/ppermute | solution.py:267
  66.7 0.1 combine.2
  66.8 5.3 %collective-permute-start.10 = (bf16[72,1024]{1,0:T(8,128)(2,1)S(1)}, bf16[72,1024]{1,0:T(8,128)(2,1)S(1)}, u32[]{:S(2)}, u32[]{:S(2)}) collective-permute-start(bf16[72,1024]{1,0:T(8,128)(2,1)S(1)} %get-tuple-element.64), channel_id=1, source_target_pairs={{0,8},{4,12},{8,0},{12,4},{24,16},{28,20},{1,9},{5,13},{9,1},{13,5... | collective-permute-start | bytes 442376 | tf_op jit(solution)/shard_map/ppermute | solution.py:259
  72.1 3.8 %collective-permute-start.11 = (bf16[72,1024]{1,0:T(8,128)(2,1)S(1)}, bf16[72,1024]{1,0:T(8,128)(2,1)S(1)}, u32[]{:S(2)}, u32[]{:S(2)}) collective-permute-start(bf16[72,1024]{1,0:T(8,128)(2,1)S(1)} %get-tuple-element.65), channel_id=1, source_target_pairs={{0,12},{4,8},{8,4},{12,0},{24,20},{28,16},{1,13},{5,9},{9,5},{13,1... | collective-permute-start | bytes 442376 | tf_op jit(solution)/shard_map/ppermute | solution.py:259
  76.0 2.5 %collective-permute-start.9 = (bf16[72,1024]{1,0:T(8,128)(2,1)S(1)}, bf16[72,1024]{1,0:T(8,128)(2,1)S(1)}, u32[]{:S(2)}, u32[]{:S(2)}) collective-permute-start(bf16[72,1024]{1,0:T(8,128)(2,1)S(1)} %get-tuple-element.63), channel_id=1, source_target_pairs={{0,4},{4,0},{8,12},{12,8},{20,16},{28,24},{1,5},{5,1},{9,13},{13,9... | collective-permute-start | bytes 442376 | tf_op jit(solution)/shard_map/ppermute | solution.py:259
  78.5 0.1 combine.3
  78.6 3.4 %collective-permute-start.12 = (bf16[72,1024]{1,0:T(8,128)(2,1)S(1)}, bf16[72,1024]{1,0:T(8,128)(2,1)S(1)}, u32[]{:S(2)}, u32[]{:S(2)}) collective-permute-start(bf16[72,1024]{1,0:T(8,128)(2,1)S(1)} %get-tuple-element.69), channel_id=1, source_target_pairs={{0,4},{4,0},{8,12},{12,8},{20,16},{28,24},{1,5},{5,1},{9,13},{13,9... | collective-permute-start | bytes 442376 | tf_op jit(solution)/shard_map/ppermute | solution.py:259
  82.0 4.9 %collective-permute-start.13 = (bf16[72,1024]{1,0:T(8,128)(2,1)S(1)}, bf16[72,1024]{1,0:T(8,128)(2,1)S(1)}, u32[]{:S(2)}, u32[]{:S(2)}) collective-permute-start(bf16[72,1024]{1,0:T(8,128)(2,1)S(1)} %get-tuple-element.70), channel_id=1, source_target_pairs={{0,8},{4,12},{8,0},{12,4},{24,16},{28,20},{1,9},{5,13},{9,1},{13,5... | collective-permute-start | bytes 442376 | tf_op jit(solution)/shard_map/ppermute | solution.py:259
  86.9 1.9 %collective-permute-start.14 = (bf16[72,1024]{1,0:T(8,128)(2,1)S(1)}, bf16[72,1024]{1,0:T(8,128)(2,1)S(1)}, u32[]{:S(2)}, u32[]{:S(2)}) collective-permute-start(bf16[72,1024]{1,0:T(8,128)(2,1)S(1)} %get-tuple-element.71), channel_id=1, source_target_pairs={{0,12},{4,8},{8,4},{12,0},{24,20},{28,16},{1,13},{5,9},{9,5},{13,1... | collective-permute-start | bytes 442376 | tf_op jit(solution)/shard_map/ppermute | solution.py:259
  88.9 7.8 %collective-permute-done.13.refs_8_ = bf16[72,1024]{1,0:T(8,128)(2,1)S(1)} collective-permute-done((bf16[72,1024]{1,0:T(8,128)(2,1)S(1)}, bf16[72,1024]{1,0:T(8,128)(2,1)S(1)}, u32[]{:S(2)}, u32[]{:S(2)}) %collective-permute-start.13) | collective-permute-done | bytes 147488 | tf_op jit(solution)/shard_map/ppermute | solution.py:259
  96.7 0.9 finish.1
  (18 shorter events, 0.1 us)
Async XLA Ops:
  2.6 13.0 %copy-start = (bf16[72,2048]{1,0:T(8,128)(2,1)S(1)}, bf16[72,2048]{1,0:T(8,128)(2,1)}, u32[]{:S(2)}) copy-start(bf16[72,2048]{1,0:T(8,128)(2,1)} %prepare_keys.1.refs_0_) | copy-start | bytes 884740
  2.6 19.9 %collective-permute-start.2 = (bf16[72,2048]{1,0:T(8,128)(2,1)}, bf16[72,2048]{1,0:T(8,128)(2,1)S(1)}, u32[]{:S(2)}, u32[]{:S(2)}) collective-permute-start(bf16[72,2048]{1,0:T(8,128)(2,1)} %prepare_keys.1.refs_0_), channel_id=1, source_target_pairs={{0,8},{4,12},{8,0},{12,4},{16,24},{20,28},{1,9},{5,13},{9,1},{13,5... | collective-permute-start | bytes 884744 | tf_op jit(solution)/shard_map/ppermute | solution.py:259
  8.7 0.7 copy-start.1
  9.4 1.3 %copy-start.2 = (bf16[72,8192]{1,0:T(8,128)(2,1)S(1)}, bf16[72,8192]{1,0:T(8,128)(2,1)}, u32[]{:S(2)}) copy-start(bf16[72,8192]{1,0:T(8,128)(2,1)} %query_ref.1) | copy-start | bytes 3538948
  10.6 1.3 %copy-start.3 = (bf16[72,8192]{1,0:T(8,128)(2,1)S(1)}, bf16[72,8192]{1,0:T(8,128)(2,1)}, u32[]{:S(2)}) copy-start(bf16[72,8192]{1,0:T(8,128)(2,1)} %grad_ref.1) | copy-start | bytes 3538948
  15.6 26.2 %copy-start.4 = (s32[2]{0:T(128)S(1)}, s32[2]{0:T(128)}, u32[]{:S(2)}) copy-start(s32[2]{0:T(128)} %counts_ref.3) | copy-start | bytes 28
  15.6 9.4 %collective-permute-start.1 = (bf16[72,2048]{1,0:T(8,128)(2,1)S(1)}, bf16[72,2048]{1,0:T(8,128)(2,1)S(1)}, u32[]{:S(2)}, u32[]{:S(2)}) collective-permute-start(bf16[72,2048]{1,0:T(8,128)(2,1)S(1)} %copy-done), channel_id=1, source_target_pairs={{0,16},{4,20},{8,24},{12,28},{1,17},{5,21},{9,25},{13,29},{2,18},{... | collective-permute-start | bytes 884744 | tf_op jit(solution)/shard_map/ppermute | solution.py:267
  19.0 11.8 %collective-permute-start = (bf16[72,2048]{1,0:T(8,128)(2,1)S(1)}, bf16[72,2048]{1,0:T(8,128)(2,1)S(1)}, u32[]{:S(2)}, u32[]{:S(2)}) collective-permute-start(bf16[72,2048]{1,0:T(8,128)(2,1)S(1)} %copy-done), channel_id=1, source_target_pairs={{0,4},{4,0},{8,12},{12,8},{16,20},{24,28},{1,5},{5,1},{9,13},{13,9... | collective-permute-start | bytes 884744 | tf_op jit(solution)/shard_map/ppermute | solution.py:259
  22.5 12.9 %collective-permute-start.3 = (bf16[72,2048]{1,0:T(8,128)(2,1)S(1)}, bf16[72,2048]{1,0:T(8,128)(2,1)S(1)}, u32[]{:S(2)}, u32[]{:S(2)}) collective-permute-start(bf16[72,2048]{1,0:T(8,128)(2,1)S(1)} %collective-permute-done.2.refs_1_.refs_2_), channel_id=1, source_target_pairs={{0,4},{4,0},{8,12},{12,8},{24,28},{28,24},{1,5},{5,1},{9,13},{13,9... | collective-permute-start | bytes 884744 | tf_op jit(solution)/shard_map/ppermute | solution.py:259
  30.9 6.4 %collective-permute-start.4 = (bf16[2,72,1024]{2,1,0:T(8,128)(2,1)S(1)}, bf16[2,72,1024]{2,1,0:T(8,128)(2,1)S(1)}, u32[]{:S(2)}, u32[]{:S(2)}) collective-permute-start(bf16[2,72,1024]{2,1,0:T(8,128)(2,1)S(1)} %stack.3), channel_id=1, source_target_pairs={{0,16},{4,20},{8,24},{12,28},{1,17},{5,21},{9,25},{13,29},{2,18},{... | collective-permute-start | bytes 884744 | tf_op jit(solution)/shard_map/ppermute | solution.py:267
  35.5 6.3 %collective-permute-start.6 = (bf16[1,72,1024]{2,1,0:T(8,128)(2,1)S(1)}, bf16[1,72,1024]{2,1,0:T(8,128)(2,1)S(1)}, u32[]{:S(2)}, u32[]{:S(2)}) collective-permute-start(bf16[1,72,1024]{2,1,0:T(8,128)(2,1)S(1)} %stack.5), channel_id=1, source_target_pairs={{0,16},{4,20},{8,24},{12,28},{1,17},{5,21},{9,25},{13,29},{2,18},{... | collective-permute-start | bytes 442376 | tf_op jit(solution)/shard_map/ppermute | solution.py:267
  37.3 13.2 %collective-permute-start.5 = (bf16[3,72,1024]{2,1,0:T(8,128)(2,1)S(1)}, bf16[3,72,1024]{2,1,0:T(8,128)(2,1)S(1)}, u32[]{:S(2)}, u32[]{:S(2)}) collective-permute-start(bf16[3,72,1024]{2,1,0:T(8,128)(2,1)S(1)} %stack.4), channel_id=1, source_target_pairs={{0,16},{4,20},{8,24},{12,28},{1,17},{5,21},{9,25},{13,29},{2,18},{... | collective-permute-start | bytes 1327112 | tf_op jit(solution)/shard_map/ppermute | solution.py:267
  49.2 17.4 %collective-permute-start.8 = (bf16[4,72,1024]{2,1,0:T(8,128)(2,1)S(1)}, bf16[4,72,1024]{2,1,0:T(8,128)(2,1)S(1)}, u32[]{:S(2)}, u32[]{:S(2)}) collective-permute-start(bf16[4,72,1024]{2,1,0:T(8,128)(2,1)S(1)} %get-tuple-element.60), channel_id=1, source_target_pairs={{16,0},{20,4},{24,8},{28,12},{17,1},{21,5},{25,9},{29,13},{18,2},{... | collective-permute-start | bytes 1769480 | tf_op jit(solution)/shard_map/ppermute | solution.py:267
  58.0 20.4 %collective-permute-start.7 = (bf16[4,72,1024]{2,1,0:T(8,128)(2,1)S(1)}, bf16[4,72,1024]{2,1,0:T(8,128)(2,1)S(1)}, u32[]{:S(2)}, u32[]{:S(2)}) collective-permute-start(bf16[4,72,1024]{2,1,0:T(8,128)(2,1)S(1)} %get-tuple-element.58), channel_id=1, source_target_pairs={{16,0},{20,4},{24,8},{28,12},{17,1},{21,5},{25,9},{29,13},{18,2},{... | collective-permute-start | bytes 1769480 | tf_op jit(solution)/shard_map/ppermute | solution.py:267
  66.8 20.1 %collective-permute-start.10 = (bf16[72,1024]{1,0:T(8,128)(2,1)S(1)}, bf16[72,1024]{1,0:T(8,128)(2,1)S(1)}, u32[]{:S(2)}, u32[]{:S(2)}) collective-permute-start(bf16[72,1024]{1,0:T(8,128)(2,1)S(1)} %get-tuple-element.64), channel_id=1, source_target_pairs={{0,8},{4,12},{8,0},{12,4},{24,16},{28,20},{1,9},{5,13},{9,1},{13,5... | collective-permute-start | bytes 442376 | tf_op jit(solution)/shard_map/ppermute | solution.py:259
  72.1 16.7 %collective-permute-start.11 = (bf16[72,1024]{1,0:T(8,128)(2,1)S(1)}, bf16[72,1024]{1,0:T(8,128)(2,1)S(1)}, u32[]{:S(2)}, u32[]{:S(2)}) collective-permute-start(bf16[72,1024]{1,0:T(8,128)(2,1)S(1)} %get-tuple-element.65), channel_id=1, source_target_pairs={{0,12},{4,8},{8,4},{12,0},{24,20},{28,16},{1,13},{5,9},{9,5},{13,1... | collective-permute-start | bytes 442376 | tf_op jit(solution)/shard_map/ppermute | solution.py:259
  76.0 12.9 %collective-permute-start.9 = (bf16[72,1024]{1,0:T(8,128)(2,1)S(1)}, bf16[72,1024]{1,0:T(8,128)(2,1)S(1)}, u32[]{:S(2)}, u32[]{:S(2)}) collective-permute-start(bf16[72,1024]{1,0:T(8,128)(2,1)S(1)} %get-tuple-element.63), channel_id=1, source_target_pairs={{0,4},{4,0},{8,12},{12,8},{20,16},{28,24},{1,5},{5,1},{9,13},{13,9... | collective-permute-start | bytes 442376 | tf_op jit(solution)/shard_map/ppermute | solution.py:259
  78.6 10.3 %collective-permute-start.12 = (bf16[72,1024]{1,0:T(8,128)(2,1)S(1)}, bf16[72,1024]{1,0:T(8,128)(2,1)S(1)}, u32[]{:S(2)}, u32[]{:S(2)}) collective-permute-start(bf16[72,1024]{1,0:T(8,128)(2,1)S(1)} %get-tuple-element.69), channel_id=1, source_target_pairs={{0,4},{4,0},{8,12},{12,8},{20,16},{28,24},{1,5},{5,1},{9,13},{13,9... | collective-permute-start | bytes 442376 | tf_op jit(solution)/shard_map/ppermute | solution.py:259
  82.0 14.7 %collective-permute-start.13 = (bf16[72,1024]{1,0:T(8,128)(2,1)S(1)}, bf16[72,1024]{1,0:T(8,128)(2,1)S(1)}, u32[]{:S(2)}, u32[]{:S(2)}) collective-permute-start(bf16[72,1024]{1,0:T(8,128)(2,1)S(1)} %get-tuple-element.70), channel_id=1, source_target_pairs={{0,8},{4,12},{8,0},{12,4},{24,16},{28,20},{1,9},{5,13},{9,1},{13,5... | collective-permute-start | bytes 442376 | tf_op jit(solution)/shard_map/ppermute | solution.py:259
  86.9 9.8 %collective-permute-start.14 = (bf16[72,1024]{1,0:T(8,128)(2,1)S(1)}, bf16[72,1024]{1,0:T(8,128)(2,1)S(1)}, u32[]{:S(2)}, u32[]{:S(2)}) collective-permute-start(bf16[72,1024]{1,0:T(8,128)(2,1)S(1)} %get-tuple-element.71), channel_id=1, source_target_pairs={{0,12},{4,8},{8,4},{12,0},{24,20},{28,16},{1,13},{5,9},{9,5},{13,1... | collective-permute-start | bytes 442376 | tf_op jit(solution)/shard_map/ppermute | solution.py:259

commit v16 on v11

--- a/solution.py
+++ b/solution.py
@@ -18,7 +18,7 @@
 CHUNKS = 2
 HEADS_PER_CHUNK = KEY_VALUE_HEADS // CHUNKS
 CHUNK_COLS = HEADS_PER_CHUNK * HEAD_WIDTH
-STEP_HEADS = 2
+STEP_HEADS = 4
 VMEM = pl.BlockSpec(memory_space=pltpu.VMEM)
 SMEM = pl.BlockSpec(memory_space=pltpu.SMEM)
 
@@ -163,19 +163,20 @@
         keys, values = [gathered(0, p) for p in heads], [gathered(HEADS_PER_CHUNK, p) for p in heads]
         bias, live = bias_ref[...], live_ref[0:1, :]
         scores = [dot(keys[p][0], qt_ref[first_head + p]) * SCORE_TO_LOG2 + bias for p in heads]
-        dprobs, probs, probs_low = [], [], []
+        probs_low = []
         for p in heads:
             weights = jnp.exp2(scores[p] - jnp.max(scores[p], 0, keepdims=True))
-            probs.append(weights * (live / jnp.sum(weights, 0, keepdims=True)))
-            probs_low.append(probs[p].astype(jnp.bfloat16))
-            dprobs.append(dot(values[p][0], gt_ref[first_head + p]))
+            factor = live / jnp.sum(weights, 0, keepdims=True)
+            probs_low.append((weights * factor).astype(jnp.bfloat16))
         outs_t, value_parts, dscores = [], [], []
         for p in heads:
+            grads_in = gt_ref[first_head + p]
             outs_t.append(dot(values[p][1], probs_low[p]))
             value_parts.append(dot(probs_low[p], g_ref[first_head + p]))
             out_low = outs_t[p].astype(jnp.bfloat16).astype(jnp.float32)
-            delta = jnp.sum(gt_ref[first_head + p].astype(jnp.float32) * out_low, 0, keepdims=True)
-            dscores.append((probs[p] * (dprobs[p] - delta)).astype(jnp.bfloat16))
+            delta = jnp.sum(grads_in.astype(jnp.float32) * out_low, 0, keepdims=True)
+            dprob = dot(values[p][0], grads_in) - delta
+            dscores.append(probs_low[p] * dprob.astype(jnp.bfloat16))
         grads_t = [dot(keys[p][1], dscores[p]) for p in heads]
         key_parts = [dot(dscores[p], q_ref[first_head + p]) * SCORE_SCALE for p in heads]
 

time: 93.7 us -> 92.6 us (0.988)
  Pallas kernels: 22.7 us -> 20.4 us
    pallas_call x2, Pallas kernels: 15.9 us -> 13.6 us  [shards(): pl.pallas_call(functools.partial(attend, seq_count, head_count, rows, chu...]
  transfers between devices with their start and end apart: 15 -> 15, of which waited for: 5 -> 5; matrix products, arithmetic and copies ran while one was open for 0% -> 0% of each run, Pallas kernels for 21% -> 19%
where the time goes in v16:
time: 92.6 us; the launch traced here: 92 us
  starting transfers between devices  44.1 us (48%)
  waiting for transfers between devices  23.3 us (25%)
  Pallas kernels  20.4 us (22%)
  local copies, waits for them, and re-layouts  3.23 us (3%)
    ppermute x9, starting transfers between devices, along_head(): return lax.ppermute(x, ('seq', 'head'), pairs)  33.1 us
    ppermute x9, waiting for transfers between devices, along_head(): return lax.ppermute(x, ('seq', 'head'), pairs)  14.8 us
    pallas_call x2, Pallas kernels, shards(): pl.pallas_call(functools.partial(attend, seq_count, head_count, rows, chu...  13.6 us
    ppermute x6, starting transfers between devices, along_seq(): return lax.ppermute(x, ('seq', 'head'), pairs)  11 us
    ppermute x6, waiting for transfers between devices, along_seq(): return lax.ppermute(x, ('seq', 'head'), pairs)  8.5 us
    pallas_call x1, Pallas kernels, shards(): pl.pallas_call(functools.partial(prepare_queries, rows), grid=(KEY_VALUE_...  3.65 us
    unnamed x10, local copies, waits for them, and re-layouts  3.23 us
    pallas_call x1, Pallas kernels, shards(): pl.pallas_call(functools.partial(prepare_keys, rows), out_shape=shape((pa...  1.96 us
  transfers between devices with their start and end apart: 15, of which 5 were waited for; matrix products, arithmetic and copies ran while one was open for 0% of the time, Pallas kernels for 19%

profile of v16, /device:TPU:0, one launch (start us, length us, event | category | flops | bytes accessed | tf_op | source)
XLA Modules:
  0.0 92.0 jit_solution(12457458397158879896)
XLA Ops:
  0.6 2.0 %prepare_keys.1.refs_0_ = bf16[72,2048]{1,0:T(8,128)(2,1)} custom-call(s32[576]{0:T(1024)} %pos_ref.3, bf16[72,1024]{1,0:T(8,128)(2,1)} %key_ref.1, bf16[72,1024]{1,0:T(8,128)(2,1)} %value_ref.1), custom_call_target="tpu_custom_call" | custom-call | tf_op jit(solution)/shard_map/prepare_keys/pallas_call | solution.py:283
  2.6 4.9 %collective-permute-start = (bf16[72,2048]{1,0:T(8,128)(2,1)}, bf16[72,2048]{1,0:T(8,128)(2,1)S(1)}, u32[]{:S(2)}, u32[]{:S(2)}) collective-permute-start(bf16[72,2048]{1,0:T(8,128)(2,1)} %prepare_keys.1.refs_0_), channel_id=1, source_target_pairs={{0,4},{4,0},{8,12},{12,8},{16,20},{24,28},{1,5},{5,1},{9,13},{13,9... | collective-permute-start | bytes 884744 | tf_op jit(solution)/shard_map/ppermute | solution.py:270
  7.5 4.5 %collective-permute-start.1 = (bf16[72,2048]{1,0:T(8,128)(2,1)}, bf16[72,2048]{1,0:T(8,128)(2,1)S(1)}, u32[]{:S(2)}, u32[]{:S(2)}) collective-permute-start(bf16[72,2048]{1,0:T(8,128)(2,1)} %prepare_keys.1.refs_0_), channel_id=1, source_target_pairs={{0,8},{4,12},{8,0},{12,4},{16,24},{20,28},{1,9},{5,13},{9,1},{13,5... | collective-permute-start | bytes 884744 | tf_op jit(solution)/shard_map/ppermute | solution.py:270
  12.0 3.5 %collective-permute-start.2 = (bf16[72,2048]{1,0:T(8,128)(2,1)}, bf16[72,2048]{1,0:T(8,128)(2,1)S(1)}, u32[]{:S(2)}, u32[]{:S(2)}) collective-permute-start(bf16[72,2048]{1,0:T(8,128)(2,1)} %prepare_keys.1.refs_0_), channel_id=1, source_target_pairs={{0,16},{4,20},{8,24},{12,28},{1,17},{5,21},{9,25},{13,29},{2,18},{... | collective-permute-start | bytes 884744 | tf_op jit(solution)/shard_map/ppermute | solution.py:278
  15.5 0.0 copy-start.1
  15.5 0.7 copy-done.1
  16.2 1.3 %copy-done.2 = bf16[72,8192]{1,0:T(8,128)(2,1)S(1)} copy-done((bf16[72,8192]{1,0:T(8,128)(2,1)S(1)}, bf16[72,8192]{1,0:T(8,128)(2,1)}, u32[]{:S(2)}) %copy-start.2) | copy-done | bytes 1179672
  17.5 1.3 %copy-done.3 = bf16[72,8192]{1,0:T(8,128)(2,1)S(1)} copy-done((bf16[72,8192]{1,0:T(8,128)(2,1)S(1)}, bf16[72,8192]{1,0:T(8,128)(2,1)}, u32[]{:S(2)}) %copy-start.3) | copy-done | bytes 1179672
  18.7 3.7 %prepare_queries.1 = (bf16[8,576,128]{2,1,0:T(8,128)(2,1)S(1)}, bf16[8,128,576]{2,1,0:T(8,128)(2,1)S(1)}, bf16[8,576,128]{2,1,0:T(8,128)(2,1)S(1)}, bf16[8,128,5...) custom-call(s32[576]{0:T(1024)S(1)} %copy-done.1, ...), custom_call_target="tpu_custom_call" | custom-call | flops 8071000064 | bytes 25830000 | tf_op jit(solution)/shard_map/prepare_queries/pallas_call | solution.py:300
  22.4 0.0 collective-permute-done.refs_0_.refs_1_
  22.4 3.0 %collective-permute-done.1.refs_1_.refs_2_ = bf16[72,2048]{1,0:T(8,128)(2,1)S(1)} collective-permute-done((bf16[72,2048]{1,0:T(8,128)(2,1)}, bf16[72,2048]{1,0:T(8,128)(2,1)S(1)}, u32[]{:S(2)}, u32[]{:S(2)}) %collective-permute-start.1) | collective-permute-done | bytes 294944 | tf_op jit(solution)/shard_map/ppermute | solution.py:270
  25.4 2.0 %collective-permute-start.3 = (bf16[72,2048]{1,0:T(8,128)(2,1)S(1)}, bf16[72,2048]{1,0:T(8,128)(2,1)S(1)}, u32[]{:S(2)}, u32[]{:S(2)}) collective-permute-start(bf16[72,2048]{1,0:T(8,128)(2,1)S(1)} %collective-permute-done.1.refs_1_.refs_2_), channel_id=1, source_target_pairs={{0,4},{4,0},{8,12},{12,8},{24,28},{28,24},{1,5},{5,1},{9,13},{13,9... | collective-permute-start | bytes 884744 | tf_op jit(solution)/shard_map/ppermute | solution.py:270
  27.4 1.3 %collective-permute-start.4 = (bf16[2,72,1024]{2,1,0:T(8,128)(2,1)S(1)}, bf16[2,72,1024]{2,1,0:T(8,128)(2,1)S(1)}, u32[]{:S(2)}, u32[]{:S(2)}) collective-permute-start(bf16[2,72,1024]{2,1,0:T(8,128)(2,1)S(1)} %stack.3), channel_id=1, source_target_pairs={{0,16},{4,20},{8,24},{12,28},{1,17},{5,21},{9,25},{13,29},{2,18},{... | collective-permute-start | bytes 884744 | tf_op jit(solution)/shard_map/ppermute | solution.py:278
  28.8 6.2 %collective-permute-done.3.refs_2_.refs_0_.refs_3_ = bf16[72,2048]{1,0:T(8,128)(2,1)S(1)} collective-permute-done((bf16[72,2048]{1,0:T(8,128)(2,1)S(1)}, bf16[72,2048]{1,0:T(8,128)(2,1)S(1)}, u32[]{:S(2)}, u32[]{:S(2)}) %collective-permute-start.3) | collective-permute-done | bytes 294944 | tf_op jit(solution)/shard_map/ppermute | solution.py:270
  35.0 1.3 %collective-permute-start.6 = (bf16[1,72,1024]{2,1,0:T(8,128)(2,1)S(1)}, bf16[1,72,1024]{2,1,0:T(8,128)(2,1)S(1)}, u32[]{:S(2)}, u32[]{:S(2)}) collective-permute-start(bf16[1,72,1024]{2,1,0:T(8,128)(2,1)S(1)} %stack.5), channel_id=1, source_target_pairs={{0,16},{4,20},{8,24},{12,28},{1,17},{5,21},{9,25},{13,29},{2,18},{... | collective-permute-start | bytes 442376 | tf_op jit(solution)/shard_map/ppermute | solution.py:278
  36.4 2.2 %collective-permute-start.5 = (bf16[3,72,1024]{2,1,0:T(8,128)(2,1)S(1)}, bf16[3,72,1024]{2,1,0:T(8,128)(2,1)S(1)}, u32[]{:S(2)}, u32[]{:S(2)}) collective-permute-start(bf16[3,72,1024]{2,1,0:T(8,128)(2,1)S(1)} %stack.4), channel_id=1, source_target_pairs={{0,16},{4,20},{8,24},{12,28},{1,17},{5,21},{9,25},{13,29},{2,18},{... | collective-permute-start | bytes 1327112 | tf_op jit(solution)/shard_map/ppermute | solution.py:278
  38.6 1.9 %collective-permute-done.6.refs_6_ = bf16[1,72,1024]{2,1,0:T(8,128)(2,1)S(1)} collective-permute-done((bf16[1,72,1024]{2,1,0:T(8,128)(2,1)S(1)}, bf16[1,72,1024]{2,1,0:T(8,128)(2,1)S(1)}, u32[]{:S(2)}, u32[]{:S(2)}) %collective-permute-start.6) | collective-permute-done | bytes 147488 | tf_op jit(solution)/shard_map/ppermute | solution.py:278
  40.5 6.8 %attend.2 = (bf16[72,8192]{1,0:T(8,128)(2,1)}, bf16[72,8192]{1,0:T(8,128)(2,1)}, bf16[4,72,1024]{2,1,0:T(8,128)(2,1)S(1)}, bf16[4,72,1024]{2,1,0:T(8,128)(2,1)S(1)}) custom-call(s32[2]{0:T(128)S(1)} %copy-done.4, bf16[72,2048]{1,0:T(8,128)(2,1)S(1)} %copy-done, bf16[72,2048]{1,0:T(8,128)(2,1)S(1)} %collective-permute-done.refs_0_.refs_1_, ...), custom_call_target="tpu_custom_call" | custom-call | flops 11530000384 | bytes 36900000 | tf_op jit(solution)/shard_map/attend/pallas_call | solution.py:346
  47.3 1.5 %collective-permute-start.8 = (bf16[4,72,1024]{2,1,0:T(8,128)(2,1)S(1)}, bf16[4,72,1024]{2,1,0:T(8,128)(2,1)S(1)}, u32[]{:S(2)}, u32[]{:S(2)}) collective-permute-start(bf16[4,72,1024]{2,1,0:T(8,128)(2,1)S(1)} %get-tuple-element.60), channel_id=1, source_target_pairs={{16,0},{20,4},{24,8},{28,12},{17,1},{21,5},{25,9},{29,13},{18,2},{... | collective-permute-start | bytes 1769480 | tf_op jit(solution)/shard_map/ppermute | solution.py:278
  48.7 6.8 %attend.3 = (bf16[72,8192]{1,0:T(8,128)(2,1)}, bf16[72,8192]{1,0:T(8,128)(2,1)}, bf16[4,72,1024]{2,1,0:T(8,128)(2,1)S(1)}, bf16[4,72,1024]{2,1,0:T(8,128)(2,1)S(1)}) custom-call(s32[2]{0:T(128)S(1)} %copy-done.4, bf16[72,2048]{1,0:T(8,128)(2,1)S(1)} %copy-done, ...), custom_call_target="tpu_custom_call", output_to_operand_aliasing={{0}: (13, {}), {1}: (14, {})} | custom-call | flops 11530000384 | bytes 36900000 | tf_op jit(solution)/shard_map/attend/pallas_call | solution.py:346
  55.5 1.3 %collective-permute-start.7 = (bf16[4,72,1024]{2,1,0:T(8,128)(2,1)S(1)}, bf16[4,72,1024]{2,1,0:T(8,128)(2,1)S(1)}, u32[]{:S(2)}, u32[]{:S(2)}) collective-permute-start(bf16[4,72,1024]{2,1,0:T(8,128)(2,1)S(1)} %get-tuple-element.58), channel_id=1, source_target_pairs={{16,0},{20,4},{24,8},{28,12},{17,1},{21,5},{25,9},{29,13},{18,2},{... | collective-permute-start | bytes 1769480 | tf_op jit(solution)/shard_map/ppermute | solution.py:278
  56.8 6.6 %collective-permute-done.8.refs_1_ = bf16[4,72,1024]{2,1,0:T(8,128)(2,1)S(1)} collective-permute-done((bf16[4,72,1024]{2,1,0:T(8,128)(2,1)S(1)}, bf16[4,72,1024]{2,1,0:T(8,128)(2,1)S(1)}, u32[]{:S(2)}, u32[]{:S(2)}) %collective-permute-start.8) | collective-permute-done | bytes 589856 | tf_op jit(solution)/shard_map/ppermute | solution.py:278
  63.4 0.1 combine.2
  63.6 6.2 %collective-permute-start.10 = (bf16[72,1024]{1,0:T(8,128)(2,1)S(1)}, bf16[72,1024]{1,0:T(8,128)(2,1)S(1)}, u32[]{:S(2)}, u32[]{:S(2)}) collective-permute-start(bf16[72,1024]{1,0:T(8,128)(2,1)S(1)} %get-tuple-element.64), channel_id=1, source_target_pairs={{0,8},{4,12},{8,0},{12,4},{24,16},{28,20},{1,9},{5,13},{9,1},{13,5... | collective-permute-start | bytes 442376 | tf_op jit(solution)/shard_map/ppermute | solution.py:270
  69.8 2.5 %collective-permute-start.11 = (bf16[72,1024]{1,0:T(8,128)(2,1)S(1)}, bf16[72,1024]{1,0:T(8,128)(2,1)S(1)}, u32[]{:S(2)}, u32[]{:S(2)}) collective-permute-start(bf16[72,1024]{1,0:T(8,128)(2,1)S(1)} %get-tuple-element.65), channel_id=1, source_target_pairs={{0,12},{4,8},{8,4},{12,0},{24,20},{28,16},{1,13},{5,9},{9,5},{13,1... | collective-permute-start | bytes 442376 | tf_op jit(solution)/shard_map/ppermute | solution.py:270
  72.3 1.9 %collective-permute-start.9 = (bf16[72,1024]{1,0:T(8,128)(2,1)S(1)}, bf16[72,1024]{1,0:T(8,128)(2,1)S(1)}, u32[]{:S(2)}, u32[]{:S(2)}) collective-permute-start(bf16[72,1024]{1,0:T(8,128)(2,1)S(1)} %get-tuple-element.63), channel_id=1, source_target_pairs={{0,4},{4,0},{8,12},{12,8},{20,16},{28,24},{1,5},{5,1},{9,13},{13,9... | collective-permute-start | bytes 442376 | tf_op jit(solution)/shard_map/ppermute | solution.py:270
  74.3 0.1 combine.3
  74.4 3.9 %collective-permute-start.12 = (bf16[72,1024]{1,0:T(8,128)(2,1)S(1)}, bf16[72,1024]{1,0:T(8,128)(2,1)S(1)}, u32[]{:S(2)}, u32[]{:S(2)}) collective-permute-start(bf16[72,1024]{1,0:T(8,128)(2,1)S(1)} %get-tuple-element.69), channel_id=1, source_target_pairs={{0,4},{4,0},{8,12},{12,8},{20,16},{28,24},{1,5},{5,1},{9,13},{13,9... | collective-permute-start | bytes 442376 | tf_op jit(solution)/shard_map/ppermute | solution.py:270
  78.3 3.7 %collective-permute-start.13 = (bf16[72,1024]{1,0:T(8,128)(2,1)S(1)}, bf16[72,1024]{1,0:T(8,128)(2,1)S(1)}, u32[]{:S(2)}, u32[]{:S(2)}) collective-permute-start(bf16[72,1024]{1,0:T(8,128)(2,1)S(1)} %get-tuple-element.70), channel_id=1, source_target_pairs={{0,8},{4,12},{8,0},{12,4},{24,16},{28,20},{1,9},{5,13},{9,1},{13,5... | collective-permute-start | bytes 442376 | tf_op jit(solution)/shard_map/ppermute | solution.py:270
  82.0 3.4 %collective-permute-start.14 = (bf16[72,1024]{1,0:T(8,128)(2,1)S(1)}, bf16[72,1024]{1,0:T(8,128)(2,1)S(1)}, u32[]{:S(2)}, u32[]{:S(2)}) collective-permute-start(bf16[72,1024]{1,0:T(8,128)(2,1)S(1)} %get-tuple-element.71), channel_id=1, source_target_pairs={{0,12},{4,8},{8,4},{12,0},{24,20},{28,16},{1,13},{5,9},{9,5},{13,1... | collective-permute-start | bytes 442376 | tf_op jit(solution)/shard_map/ppermute | solution.py:270
  85.4 5.6 %collective-permute-done.13.refs_8_ = bf16[72,1024]{1,0:T(8,128)(2,1)S(1)} collective-permute-done((bf16[72,1024]{1,0:T(8,128)(2,1)S(1)}, bf16[72,1024]{1,0:T(8,128)(2,1)S(1)}, u32[]{:S(2)}, u32[]{:S(2)}) %collective-permute-start.13) | collective-permute-done | bytes 147488 | tf_op jit(solution)/shard_map/ppermute | solution.py:270
  91.1 0.9 finish.1
  (18 shorter events, 0.1 us)
Async XLA Ops:
  2.6 19.8 %collective-permute-start = (bf16[72,2048]{1,0:T(8,128)(2,1)}, bf16[72,2048]{1,0:T(8,128)(2,1)S(1)}, u32[]{:S(2)}, u32[]{:S(2)}) collective-permute-start(bf16[72,2048]{1,0:T(8,128)(2,1)} %prepare_keys.1.refs_0_), channel_id=1, source_target_pairs={{0,4},{4,0},{8,12},{12,8},{16,20},{24,28},{1,5},{5,1},{9,13},{13,9... | collective-permute-start | bytes 884744 | tf_op jit(solution)/shard_map/ppermute | solution.py:270
  7.5 17.8 %collective-permute-start.1 = (bf16[72,2048]{1,0:T(8,128)(2,1)}, bf16[72,2048]{1,0:T(8,128)(2,1)S(1)}, u32[]{:S(2)}, u32[]{:S(2)}) collective-permute-start(bf16[72,2048]{1,0:T(8,128)(2,1)} %prepare_keys.1.refs_0_), channel_id=1, source_target_pairs={{0,8},{4,12},{8,0},{12,4},{16,24},{20,28},{1,9},{5,13},{9,1},{13,5... | collective-permute-start | bytes 884744 | tf_op jit(solution)/shard_map/ppermute | solution.py:270
  12.0 13.3 %collective-permute-start.2 = (bf16[72,2048]{1,0:T(8,128)(2,1)}, bf16[72,2048]{1,0:T(8,128)(2,1)S(1)}, u32[]{:S(2)}, u32[]{:S(2)}) collective-permute-start(bf16[72,2048]{1,0:T(8,128)(2,1)} %prepare_keys.1.refs_0_), channel_id=1, source_target_pairs={{0,16},{4,20},{8,24},{12,28},{1,17},{5,21},{9,25},{13,29},{2,18},{... | collective-permute-start | bytes 884744 | tf_op jit(solution)/shard_map/ppermute | solution.py:278
  15.5 0.7 copy-start.1
  16.2 1.3 %copy-start.2 = (bf16[72,8192]{1,0:T(8,128)(2,1)S(1)}, bf16[72,8192]{1,0:T(8,128)(2,1)}, u32[]{:S(2)}) copy-start(bf16[72,8192]{1,0:T(8,128)(2,1)} %query_ref.1) | copy-start | bytes 3538948
  17.5 1.3 %copy-start.3 = (bf16[72,8192]{1,0:T(8,128)(2,1)S(1)}, bf16[72,8192]{1,0:T(8,128)(2,1)}, u32[]{:S(2)}) copy-start(bf16[72,8192]{1,0:T(8,128)(2,1)} %grad_ref.1) | copy-start | bytes 3538948
  25.4 15.1 %copy-start = (bf16[72,2048]{1,0:T(8,128)(2,1)S(1)}, bf16[72,2048]{1,0:T(8,128)(2,1)}, u32[]{:S(2)}) copy-start(bf16[72,2048]{1,0:T(8,128)(2,1)} %prepare_keys.1.refs_0_) | copy-start | bytes 884740
  25.4 15.1 %copy-start.4 = (s32[2]{0:T(128)S(1)}, s32[2]{0:T(128)}, u32[]{:S(2)}) copy-start(s32[2]{0:T(128)} %counts_ref.3) | copy-start | bytes 28
  25.4 9.6 %collective-permute-start.3 = (bf16[72,2048]{1,0:T(8,128)(2,1)S(1)}, bf16[72,2048]{1,0:T(8,128)(2,1)S(1)}, u32[]{:S(2)}, u32[]{:S(2)}) collective-permute-start(bf16[72,2048]{1,0:T(8,128)(2,1)S(1)} %collective-permute-done.1.refs_1_.refs_2_), channel_id=1, source_target_pairs={{0,4},{4,0},{8,12},{12,8},{24,28},{28,24},{1,5},{5,1},{9,13},{13,9... | collective-permute-start | bytes 884744 | tf_op jit(solution)/shard_map/ppermute | solution.py:270
  27.4 8.9 %collective-permute-start.4 = (bf16[2,72,1024]{2,1,0:T(8,128)(2,1)S(1)}, bf16[2,72,1024]{2,1,0:T(8,128)(2,1)S(1)}, u32[]{:S(2)}, u32[]{:S(2)}) collective-permute-start(bf16[2,72,1024]{2,1,0:T(8,128)(2,1)S(1)} %stack.3), channel_id=1, source_target_pairs={{0,16},{4,20},{8,24},{12,28},{1,17},{5,21},{9,25},{13,29},{2,18},{... | collective-permute-start | bytes 884744 | tf_op jit(solution)/shard_map/ppermute | solution.py:278
  35.0 5.5 %collective-permute-start.6 = (bf16[1,72,1024]{2,1,0:T(8,128)(2,1)S(1)}, bf16[1,72,1024]{2,1,0:T(8,128)(2,1)S(1)}, u32[]{:S(2)}, u32[]{:S(2)}) collective-permute-start(bf16[1,72,1024]{2,1,0:T(8,128)(2,1)S(1)} %stack.5), channel_id=1, source_target_pairs={{0,16},{4,20},{8,24},{12,28},{1,17},{5,21},{9,25},{13,29},{2,18},{... | collective-permute-start | bytes 442376 | tf_op jit(solution)/shard_map/ppermute | solution.py:278
  36.4 12.4 %collective-permute-start.5 = (bf16[3,72,1024]{2,1,0:T(8,128)(2,1)S(1)}, bf16[3,72,1024]{2,1,0:T(8,128)(2,1)S(1)}, u32[]{:S(2)}, u32[]{:S(2)}) collective-permute-start(bf16[3,72,1024]{2,1,0:T(8,128)(2,1)S(1)} %stack.4), channel_id=1, source_target_pairs={{0,16},{4,20},{8,24},{12,28},{1,17},{5,21},{9,25},{13,29},{2,18},{... | collective-permute-start | bytes 1327112 | tf_op jit(solution)/shard_map/ppermute | solution.py:278
  47.3 16.2 %collective-permute-start.8 = (bf16[4,72,1024]{2,1,0:T(8,128)(2,1)S(1)}, bf16[4,72,1024]{2,1,0:T(8,128)(2,1)S(1)}, u32[]{:S(2)}, u32[]{:S(2)}) collective-permute-start(bf16[4,72,1024]{2,1,0:T(8,128)(2,1)S(1)} %get-tuple-element.60), channel_id=1, source_target_pairs={{16,0},{20,4},{24,8},{28,12},{17,1},{21,5},{25,9},{29,13},{18,2},{... | collective-permute-start | bytes 1769480 | tf_op jit(solution)/shard_map/ppermute | solution.py:278
  55.5 18.7 %collective-permute-start.7 = (bf16[4,72,1024]{2,1,0:T(8,128)(2,1)S(1)}, bf16[4,72,1024]{2,1,0:T(8,128)(2,1)S(1)}, u32[]{:S(2)}, u32[]{:S(2)}) collective-permute-start(bf16[4,72,1024]{2,1,0:T(8,128)(2,1)S(1)} %get-tuple-element.58), channel_id=1, source_target_pairs={{16,0},{20,4},{24,8},{28,12},{17,1},{21,5},{25,9},{29,13},{18,2},{... | collective-permute-start | bytes 1769480 | tf_op jit(solution)/shard_map/ppermute | solution.py:278
  63.6 18.5 %collective-permute-start.10 = (bf16[72,1024]{1,0:T(8,128)(2,1)S(1)}, bf16[72,1024]{1,0:T(8,128)(2,1)S(1)}, u32[]{:S(2)}, u32[]{:S(2)}) collective-permute-start(bf16[72,1024]{1,0:T(8,128)(2,1)S(1)} %get-tuple-element.64), channel_id=1, source_target_pairs={{0,8},{4,12},{8,0},{12,4},{24,16},{28,20},{1,9},{5,13},{9,1},{13,5... | collective-permute-start | bytes 442376 | tf_op jit(solution)/shard_map/ppermute | solution.py:270
  69.8 15.6 %collective-permute-start.11 = (bf16[72,1024]{1,0:T(8,128)(2,1)S(1)}, bf16[72,1024]{1,0:T(8,128)(2,1)S(1)}, u32[]{:S(2)}, u32[]{:S(2)}) collective-permute-start(bf16[72,1024]{1,0:T(8,128)(2,1)S(1)} %get-tuple-element.65), channel_id=1, source_target_pairs={{0,12},{4,8},{8,4},{12,0},{24,20},{28,16},{1,13},{5,9},{9,5},{13,1... | collective-permute-start | bytes 442376 | tf_op jit(solution)/shard_map/ppermute | solution.py:270
  72.3 13.1 %collective-permute-start.9 = (bf16[72,1024]{1,0:T(8,128)(2,1)S(1)}, bf16[72,1024]{1,0:T(8,128)(2,1)S(1)}, u32[]{:S(2)}, u32[]{:S(2)}) collective-permute-start(bf16[72,1024]{1,0:T(8,128)(2,1)S(1)} %get-tuple-element.63), channel_id=1, source_target_pairs={{0,4},{4,0},{8,12},{12,8},{20,16},{28,24},{1,5},{5,1},{9,13},{13,9... | collective-permute-start | bytes 442376 | tf_op jit(solution)/shard_map/ppermute | solution.py:270
  74.4 11.0 %collective-permute-start.12 = (bf16[72,1024]{1,0:T(8,128)(2,1)S(1)}, bf16[72,1024]{1,0:T(8,128)(2,1)S(1)}, u32[]{:S(2)}, u32[]{:S(2)}) collective-permute-start(bf16[72,1024]{1,0:T(8,128)(2,1)S(1)} %get-tuple-element.69), channel_id=1, source_target_pairs={{0,4},{4,0},{8,12},{12,8},{20,16},{28,24},{1,5},{5,1},{9,13},{13,9... | collective-permute-start | bytes 442376 | tf_op jit(solution)/shard_map/ppermute | solution.py:270
  78.3 12.7 %collective-permute-start.13 = (bf16[72,1024]{1,0:T(8,128)(2,1)S(1)}, bf16[72,1024]{1,0:T(8,128)(2,1)S(1)}, u32[]{:S(2)}, u32[]{:S(2)}) collective-permute-start(bf16[72,1024]{1,0:T(8,128)(2,1)S(1)} %get-tuple-element.70), channel_id=1, source_target_pairs={{0,8},{4,12},{8,0},{12,4},{24,16},{28,20},{1,9},{5,13},{9,1},{13,5... | collective-permute-start | bytes 442376 | tf_op jit(solution)/shard_map/ppermute | solution.py:270
  82.0 9.0 %collective-permute-start.14 = (bf16[72,1024]{1,0:T(8,128)(2,1)S(1)}, bf16[72,1024]{1,0:T(8,128)(2,1)S(1)}, u32[]{:S(2)}, u32[]{:S(2)}) collective-permute-start(bf16[72,1024]{1,0:T(8,128)(2,1)S(1)} %get-tuple-element.71), channel_id=1, source_target_pairs={{0,12},{4,8},{8,4},{12,0},{24,20},{28,16},{1,13},{5,9},{9,5},{13,1... | collective-permute-start | bytes 442376 | tf_op jit(solution)/shard_map/ppermute | solution.py:270
